TPU v7x, 32 devices: a whole 2x2x4 slice. The times are simulated.
32 devices in a mesh: dp: 4 (over x, core), gx: 4 (over z), gy: 2 (over y).
Axes of the slice: x: 2, y: 2, z: 4, core: 2. Of those that a mesh axis runs over, the one named last changes fastest.
Arguments:
- features: bfloat16 [4, 4, 2, 4, 512, 128], P('dp', 'gx', 'gy'), may hold values from -6 to 6
- weight: bfloat16 [3456, 128], replicated, may hold values from -0.109375 to 0.109375
- cotangent: bfloat16 [4, 4, 2, 4, 512, 128], P('dp', 'gx', 'gy'), may hold values from -6 to 6
- neighbours: int32 [4, 4, 2, 4, 27], P('dp', 'gx', 'gy'), may hold values from -1 to 19, as said below
- send_slots: int32 [4, 4, 2, 8, 2], P('dp', 'gx', 'gy'), may hold values from -1 to 3, as said below
Outputs:
- activations: bfloat16 [4, 4, 2, 4, 512, 128], P('dp', 'gx', 'gy')
- input_grad: bfloat16 [4, 4, 2, 4, 512, 128], P('dp', 'gx', 'gy')
- weight_grad: float32 [3456, 128], replicated
Inputs may be any that keep to these rules, and one draw needn't show every extreme that they name: `neighbours`: occupied slots come first in every tile and hold 1 to 4 bricks; the row of an occupied slot k has k at entry 13, other entries are a slot of the same tile, or 4 + r * 2 + q for the brick in entry q of send list 7 - r of the tile at relative position r, or -1 for an empty brick or one outside the grid; rows of empty slots are all -1. Some tile has all 4 slots occupied. Entries never point outside the grid. `send_slots`: row d lists, in a fixed order of brick positions, the slots of the tile's bricks on its face or corner column toward the tile at relative position d; -1 marks empty positions and unused entries.
All inputs are finite; a program needn't handle non-finite values.
Results may differ from a plain program's by a relative error of at most 0.0051.
Values may be sent and summed in bfloat16 or wider, within the bound.
No kernel may reach another device: no remote copies, remote signals or barrier semaphores. Data moves between devices by JAX's collectives and lax.ppermute only.
A program may use at most 64 MiB of HBM per device.

v0:
```python
import math

import jax
import jax.numpy as jnp
from jax import lax
from jax.sharding import PartitionSpec as P

EDGE = 8


DIRECTIONS = ((-1, -1), (-1, 0), (-1, 1), (0, -1), (0, 1), (1, -1), (1, 0), (1, 1))


def passed_along(x, axis, by):
    count = lax.axis_size(axis)
    pairs = [(i, i + by) for i in range(count) if 0 <= i + by < count]
    return lax.ppermute(x, axis, pairs)


def silu_slope(preact):
    sigmoid_of = jax.nn.sigmoid(preact)
    return sigmoid_of * (1.0 + preact * (1.0 - sigmoid_of))


def brick_columns(store, brick_row):
    channels = store.shape[-1]
    chosen = jnp.where(brick_row < 0, store.shape[0] - 1, brick_row)
    picked = jnp.take(store, chosen, axis=0)
    big_cube = picked.reshape(3, 3, 3, EDGE, EDGE, EDGE, channels)
    big_cube = big_cube.transpose(0, 3, 1, 4, 2, 5, 6).reshape(
        3 * EDGE, 3 * EDGE, 3 * EDGE, channels
    )
    padded = big_cube[EDGE - 1 : 2 * EDGE + 1, EDGE - 1 : 2 * EDGE + 1, EDGE - 1 : 2 * EDGE + 1]
    pieces = []
    for offset_x in range(3):
        for offset_y in range(3):
            for offset_z in range(3):
                window = padded[
                    offset_x : offset_x + EDGE,
                    offset_y : offset_y + EDGE,
                    offset_z : offset_z + EDGE,
                ]
                pieces.append(window.reshape(EDGE * EDGE * EDGE, channels))
    return jnp.concatenate(pieces, axis=1)


def make_outbox(source, send_lists, number, slot_count):
    chosen = jnp.where(send_lists[number] < 0, slot_count, send_lists[number])
    outbox = jnp.take(source, chosen, axis=0)
    return outbox


def widen_inbox(inbox, voxel_count, channels):
    return inbox.reshape(-1, voxel_count, channels)


def neighbour_store(bricks, send_lists):
    slot_count, voxel_count, channels = bricks.shape
    zero_brick = jnp.zeros((1, voxel_count, channels), bricks.dtype)
    source = jnp.concatenate([bricks, zero_brick], axis=0).reshape(
        slot_count + 1, EDGE, EDGE, EDGE, channels
    )
    boxes = [make_outbox(source, send_lists, number, slot_count) for number in range(8)]
    moved = list(boxes)
    for number in range(8):
        step_x, step_y = DIRECTIONS[number]
        outbox = moved[number]
        if step_x != 0:
            outbox = passed_along(outbox, "gx", step_x)
        if step_y != 0:
            outbox = passed_along(outbox, "gy", step_y)
        moved[number] = outbox
    arrived = [zero_brick] * 8
    for number in range(8):
        arrived[7 - number] = widen_inbox(moved[number], voxel_count, channels)
    return jnp.concatenate([bricks] + arrived + [zero_brick], axis=0)


def body(features, weight, cotangent, neighbours, send_slots):
    slot_count = features.shape[3]
    voxel_count = features.shape[4]
    channels = features.shape[5]
    own_bricks = features.reshape(slot_count, voxel_count, channels)
    grads_out = cotangent.reshape(slot_count, voxel_count, channels)
    brick_rows = neighbours.reshape(slot_count, 27)
    send_lists = send_slots.reshape(8, send_slots.shape[-1])
    flipped = (
        weight.reshape(27, channels, channels)[::-1]
        .transpose(0, 2, 1)
        .reshape(27 * channels, channels)
    )
    occupied = jnp.sum((brick_rows[:, 13] >= 0).astype(jnp.int32))
    store = neighbour_store(own_bricks, send_lists)

    def forward_slot(slot_at, state_now):
        activated, grads_pre, summed = state_now
        brick_row = lax.dynamic_index_in_dim(brick_rows, slot_at, 0, keepdims=False)
        columns = brick_columns(store, brick_row)
        preact = jnp.dot(columns, weight, preferred_element_type=jnp.float32)
        grad_out = lax.dynamic_index_in_dim(grads_out, slot_at, 0, keepdims=False).astype(
            jnp.float32
        )
        grad_pre = (grad_out * silu_slope(preact)).astype(jnp.bfloat16)
        activated = lax.dynamic_update_index_in_dim(
            activated, jax.nn.silu(preact).astype(jnp.bfloat16), slot_at, 0
        )
        grads_pre = lax.dynamic_update_index_in_dim(grads_pre, grad_pre, slot_at, 0)
        summed = summed + lax.dot_general(
            columns, grad_pre, (((0,), (0,)), ((), ())), preferred_element_type=jnp.float32
        )
        return (activated, grads_pre, summed)

    initial = (
        jnp.zeros((slot_count, voxel_count, channels), jnp.bfloat16),
        jnp.zeros((slot_count, voxel_count, channels), jnp.bfloat16),
        jnp.zeros((27 * channels, channels), jnp.float32),
    )
    activated, grads_pre, summed = lax.fori_loop(0, occupied, forward_slot, initial)
    grad_store = neighbour_store(grads_pre, send_lists)

    def backward_slot(slot_at, result):
        brick_row = lax.dynamic_index_in_dim(brick_rows, slot_at, 0, keepdims=False)
        grad_in = jnp.dot(
            brick_columns(grad_store, brick_row), flipped, preferred_element_type=jnp.float32
        )
        return lax.dynamic_update_index_in_dim(result, grad_in.astype(jnp.bfloat16), slot_at, 0)

    input_grad = lax.fori_loop(
        0, occupied, backward_slot, jnp.zeros((slot_count, voxel_count, channels), jnp.bfloat16)
    )
    combined = lax.psum(summed, ("dp", "gx", "gy"))
    devices = lax.axis_size("dp") * lax.axis_size("gx") * lax.axis_size("gy")
    factor = 1.0 / math.sqrt(float(devices * slot_count * voxel_count))
    weight_grad = combined * factor
    return (activated.reshape(features.shape), input_grad.reshape(features.shape), weight_grad)


def solution(mesh):
    placed = (
        P("dp", "gx", "gy", None, None, None),
        P(),
        P("dp", "gx", "gy", None, None, None),
        P("dp", "gx", "gy", None, None),
        P("dp", "gx", "gy", None, None),
    )
    return jax.shard_map(
        body,
        mesh=mesh,
        in_specs=placed,
        out_specs=(
            P("dp", "gx", "gy", None, None, None),
            P("dp", "gx", "gy", None, None, None),
            P(),
        ),
        check_vma=False,
    )
```

profile of v0, /device:TPU:0, one launch (start us, length us, event | category | flops | bytes accessed | tf_op | source)
XLA Modules:
  0.0 268.0 jit_solution(7074077392700328531)
XLA Ops:
  10.3 5.7 %collective-permute-start.2 = (bf16[2,8,8,8,128]{4,3,2,1,0:T(8,128)(2,1)S(1)}, bf16[2,8,8,8,128]{4,3,2,1,0:T(8,128)(2,1)}, u32[]{:S(2)}, u32[]{:S(2)}) collective-permute-start(bf16[2,8,8,8,128]{4,3,2,1,0:T(8,128)(2,1)S(1)} %broadcast_select_fusion.15), channel_id=1, source_target_pairs={{0,2},{2,4},{4,6},{1,3},{3,5},{5,7},{8,10},{10,12},{12,14},{9,11},... | collective-permute-start | bytes 786440 | tf_op jit(solution)/shard_map/ppermute | solution.py:17
  16.7 3.5 %collective-permute-start = (bf16[2,8,8,8,128]{4,3,2,1,0:T(8,128)(2,1)S(1)}, bf16[2,8,8,8,128]{4,3,2,1,0:T(8,128)(2,1)}, u32[]{:S(2)}, u32[]{:S(2)}) collective-permute-start(bf16[2,8,8,8,128]{4,3,2,1,0:T(8,128)(2,1)S(1)} %broadcast_select_fusion.17), channel_id=1, source_target_pairs={{0,2},{2,4},{4,6},{1,3},{3,5},{5,7},{8,10},{10,12},{12,14},{9,11},... | collective-permute-start | bytes 786440 | tf_op jit(solution)/shard_map/ppermute | solution.py:17
  21.7 3.5 %collective-permute-start.3 = (bf16[2,8,8,8,128]{4,3,2,1,0:T(8,128)(2,1)}, bf16[2,8,8,8,128]{4,3,2,1,0:T(8,128)(2,1)}, u32[]{:S(2)}, u32[]{:S(2)}) collective-permute-start(bf16[2,8,8,8,128]{4,3,2,1,0:T(8,128)(2,1)} %broadcast_select_fusion.13), channel_id=1, source_target_pairs={{0,2},{2,4},{4,6},{1,3},{3,5},{5,7},{8,10},{10,12},{12,14},{9,11},... | collective-permute-start | bytes 786440 | tf_op jit(solution)/shard_map/ppermute | solution.py:17
  32.3 4.1 %collective-permute-start.1 = (bf16[2,8,8,8,128]{4,3,2,1,0:T(8,128)(2,1)}, bf16[2,8,8,8,128]{4,3,2,1,0:T(8,128)(2,1)}, u32[]{:S(2)}, u32[]{:S(2)}) collective-permute-start(bf16[2,8,8,8,128]{4,3,2,1,0:T(8,128)(2,1)} %collective-permute-done), channel_id=1, source_target_pairs={{0,1},{2,3},{4,5},{6,7},{8,9},{10,11},{12,13},{14,15},{16,17},{18,... | collective-permute-start | bytes 786440 | tf_op jit(solution)/shard_map/ppermute | solution.py:17
  40.9 5.3 %collective-permute-start.5 = (bf16[2,8,8,8,128]{4,3,2,1,0:T(8,128)(2,1)S(1)}, bf16[2,8,8,8,128]{4,3,2,1,0:T(8,128)(2,1)S(1)}, u32[]{:S(2)}, u32[]{:S(2)}) collective-permute-start(bf16[2,8,8,8,128]{4,3,2,1,0:T(8,128)(2,1)S(1)} %broadcast_select_fusion.11), channel_id=1, source_target_pairs={{0,1},{2,3},{4,5},{6,7},{8,9},{10,11},{12,13},{14,15},{16,17},{18,... | collective-permute-start | bytes 786440 | tf_op jit(solution)/shard_map/ppermute | solution.py:17
  52.2 4.6 %collective-permute-start.8 = (bf16[2,8,8,8,128]{4,3,2,1,0:T(8,128)(2,1)}, bf16[2,8,8,8,128]{4,3,2,1,0:T(8,128)(2,1)S(1)}, u32[]{:S(2)}, u32[]{:S(2)}) collective-permute-start(bf16[2,8,8,8,128]{4,3,2,1,0:T(8,128)(2,1)} %collective-permute-done.7), channel_id=1, source_target_pairs={{0,1},{2,3},{4,5},{6,7},{8,9},{10,11},{12,13},{14,15},{16,17},{18,... | collective-permute-start | bytes 786440 | tf_op jit(solution)/shard_map/ppermute | solution.py:17
  62.6 2.6 collective-permute-done.11
  69.6 34.7 %while.24 = (s32[]{:T(128)}, bf16[4,512,128]{2,1,0:T(8,128)(2,1)}, bf16[4,512,128]{2,1,0:T(8,128)(2,1)}, f32[3456,128]{1,0:T(8,128)}, s32[]{:T(128)}, /*index=5*...) while((s32[]{:T(128)}, bf16[4,512,128]{2,1,0:T(8,128)(2,1)}, ...), condition=%wide.region_2.5_spmd, body=%wide.region_1.0_spmd.sunk | while | flops 909624576 | bytes 67736328 | solution.py:118
  70.3 3.0 %gather_fusion = bf16[27,512,128]{2,1,0:T(8,128)(2,1)S(1)} fusion(bf16[21,512,128]{2,1,0:T(8,128)(2,1)} %get-tuple-element.461, s32[1024]{0:T(1024)S(1)} %pad_clamp_fusion.12), kind=kCustom, calls=%fused_computation.1.clone.clone.1 | custom fusion | bytes 7077996 | tf_op jit(solution)/shard_map/while/body/jit(_take)/gather | solution.py:28
  81.7 3.0 %gather_fusion = bf16[27,512,128]{2,1,0:T(8,128)(2,1)S(1)} fusion(bf16[21,512,128]{2,1,0:T(8,128)(2,1)} %get-tuple-element.461, s32[1024]{0:T(1024)S(1)} %pad_clamp_fusion.12), kind=kCustom, calls=%fused_computation.1.clone.clone.1 | custom fusion | bytes 7077996 | tf_op jit(solution)/shard_map/while/body/jit(_take)/gather | solution.py:28
  93.1 3.0 %gather_fusion = bf16[27,512,128]{2,1,0:T(8,128)(2,1)S(1)} fusion(bf16[21,512,128]{2,1,0:T(8,128)(2,1)} %get-tuple-element.461, s32[1024]{0:T(1024)S(1)} %pad_clamp_fusion.12), kind=kCustom, calls=%fused_computation.1.clone.clone.1 | custom fusion | bytes 7077996 | tf_op jit(solution)/shard_map/while/body/jit(_take)/gather | solution.py:28
  110.5 17.9 %collective-permute-start.12 = (bf16[2,8,8,8,128]{4,3,2,1,0:T(8,128)(2,1)S(1)}, bf16[2,8,8,8,128]{4,3,2,1,0:T(8,128)(2,1)}, u32[]{:S(2)}, u32[]{:S(2)}) collective-permute-start(bf16[2,8,8,8,128]{4,3,2,1,0:T(8,128)(2,1)S(1)} %broadcast_select_fusion.16), channel_id=1, source_target_pairs={{0,2},{2,4},{4,6},{1,3},{3,5},{5,7},{8,10},{10,12},{12,14},{9,11},... | collective-permute-start | bytes 786440 | tf_op jit(solution)/shard_map/ppermute | solution.py:17
  129.1 3.9 %collective-permute-start.15 = (bf16[2,8,8,8,128]{4,3,2,1,0:T(8,128)(2,1)S(1)}, bf16[2,8,8,8,128]{4,3,2,1,0:T(8,128)(2,1)}, u32[]{:S(2)}, u32[]{:S(2)}) collective-permute-start(bf16[2,8,8,8,128]{4,3,2,1,0:T(8,128)(2,1)S(1)} %broadcast_select_fusion.12), channel_id=1, source_target_pairs={{0,2},{2,4},{4,6},{1,3},{3,5},{5,7},{8,10},{10,12},{12,14},{9,11},... | collective-permute-start | bytes 786440 | tf_op jit(solution)/shard_map/ppermute | solution.py:17
  142.6 4.6 %collective-permute-start.17 = (bf16[2,8,8,8,128]{4,3,2,1,0:T(8,128)(2,1)S(1)}, bf16[2,8,8,8,128]{4,3,2,1,0:T(8,128)(2,1)S(1)}, u32[]{:S(2)}, u32[]{:S(2)}) collective-permute-start(bf16[2,8,8,8,128]{4,3,2,1,0:T(8,128)(2,1)S(1)} %broadcast_select_fusion.10), channel_id=1, source_target_pairs={{0,1},{2,3},{4,5},{6,7},{8,9},{10,11},{12,13},{14,15},{16,17},{18,... | collective-permute-start | bytes 786440 | tf_op jit(solution)/shard_map/ppermute | solution.py:17
  148.6 4.1 %collective-permute-done.19 = bf16[2,8,8,8,128]{4,3,2,1,0:T(8,128)(2,1)S(1)} collective-permute-done((bf16[2,8,8,8,128]{4,3,2,1,0:T(8,128)(2,1)S(1)}, bf16[2,8,8,8,128]{4,3,2,1,0:T(8,128)(2,1)S(1)}, u32[]{:S(2)}, u32[]{:S(2)}) %collective-permute-start.19) | collective-permute-done | bytes 262176 | tf_op jit(solution)/shard_map/ppermute | solution.py:17
  154.0 4.1 %collective-permute-done.22 = bf16[2,8,8,8,128]{4,3,2,1,0:T(8,128)(2,1)S(1)} collective-permute-done((bf16[2,8,8,8,128]{4,3,2,1,0:T(8,128)(2,1)S(1)}, bf16[2,8,8,8,128]{4,3,2,1,0:T(8,128)(2,1)S(1)}, u32[]{:S(2)}, u32[]{:S(2)}) %collective-permute-start.22) | collective-permute-done | bytes 262176 | tf_op jit(solution)/shard_map/ppermute | solution.py:17
  160.9 3.6 %collective-permute-done.20 = bf16[2,8,8,8,128]{4,3,2,1,0:T(8,128)(2,1)S(1)} collective-permute-done((bf16[2,8,8,8,128]{4,3,2,1,0:T(8,128)(2,1)S(1)}, bf16[2,8,8,8,128]{4,3,2,1,0:T(8,128)(2,1)S(1)}, u32[]{:S(2)}, u32[]{:S(2)}) %collective-permute-start.20) | collective-permute-done | bytes 262176 | tf_op jit(solution)/shard_map/ppermute | solution.py:17
  164.6 3.1 %collective-permute-done.23 = bf16[2,8,8,8,128]{4,3,2,1,0:T(8,128)(2,1)S(1)} collective-permute-done((bf16[2,8,8,8,128]{4,3,2,1,0:T(8,128)(2,1)S(1)}, bf16[2,8,8,8,128]{4,3,2,1,0:T(8,128)(2,1)S(1)}, u32[]{:S(2)}, u32[]{:S(2)}) %collective-permute-start.23) | collective-permute-done | bytes 262176 | tf_op jit(solution)/shard_map/ppermute | solution.py:17
  169.5 26.0 %while.25 = (s32[]{:T(128)}, bf16[4,512,128]{2,1,0:T(8,128)(2,1)}, s32[]{:T(128)}, s32[4,27]{1,0:T(4,128)S(1)}, bf16[21,512,128]{2,1,0:T(8,128)(2,1)}, /*index=5...) while((s32[]{:T(128)}, bf16[4,512,128]{2,1,0:T(8,128)(2,1)}, s32[]{:T(128)}, ...), condition=%wide.region_4.7_spmd, body=%wide.region_3.6_spmd.sunk | while | flops 454821088 | bytes 43487888 | solution.py:128
  170.3 3.0 %gather_fusion.1 = bf16[27,512,128]{2,1,0:T(8,128)(2,1)S(1)} fusion(bf16[21,512,128]{2,1,0:T(8,128)(2,1)} %get-tuple-element.489, s32[1024]{0:T(1024)S(1)} %pad_clamp_fusion.13), kind=kCustom, calls=%fused_computation.17.clone.clone.1 | custom fusion | bytes 7077996 | tf_op jit(solution)/shard_map/while/body/jit(_take)/gather | solution.py:28
  178.7 3.0 %gather_fusion.1 = bf16[27,512,128]{2,1,0:T(8,128)(2,1)S(1)} fusion(bf16[21,512,128]{2,1,0:T(8,128)(2,1)} %get-tuple-element.489, s32[1024]{0:T(1024)S(1)} %pad_clamp_fusion.13), kind=kCustom, calls=%fused_computation.17.clone.clone.1 | custom fusion | bytes 7077996 | tf_op jit(solution)/shard_map/while/body/jit(_take)/gather | solution.py:28
  187.1 3.0 %gather_fusion.1 = bf16[27,512,128]{2,1,0:T(8,128)(2,1)S(1)} fusion(bf16[21,512,128]{2,1,0:T(8,128)(2,1)} %get-tuple-element.489, s32[1024]{0:T(1024)S(1)} %pad_clamp_fusion.13), kind=kCustom, calls=%fused_computation.17.clone.clone.1 | custom fusion | bytes 7077996 | tf_op jit(solution)/shard_map/while/body/jit(_take)/gather | solution.py:28
  195.5 62.9 %all-reduce.4.cloned.1.call-done = f32[3456,128]{1,0:T(8,128)} async-done(((f32[3456,128]{1,0:T(8,128)}), f32[3456,128]{1,0:T(8,128)}) %all-reduce.4.cloned.1.call-update) | async-done | bytes 1769488 | tf_op jit(solution)/shard_map/psum | solution.py:131
  258.4 2.8 %broadcast_multiply_fusion = f32[3456,128]{1,0:T(8,128)} fusion(f32[3456,128]{1,0:T(8,128)} %all-reduce.4.cloned.1.call-done), kind=kLoop, calls=%fused_computation.94 | loop fusion | flops 442368 | bytes 3538944 | tf_op jit(solution)/shard_map/mul | solution.py:134
  (403 shorter events, 91.7 us)
Async XLA Ops:
  7.2 251.2 %all-reduce.4.cloned.1.call-start = ((), (), s32[]{:S(2)}) async-start(), calls=%async_computation | async-start | bytes 3538944 | tf_op jit(solution)/shard_map/psum | solution.py:131
  10.3 37.5 %collective-permute-start.2 = (bf16[2,8,8,8,128]{4,3,2,1,0:T(8,128)(2,1)S(1)}, bf16[2,8,8,8,128]{4,3,2,1,0:T(8,128)(2,1)}, u32[]{:S(2)}, u32[]{:S(2)}) collective-permute-start(bf16[2,8,8,8,128]{4,3,2,1,0:T(8,128)(2,1)S(1)} %broadcast_select_fusion.15), channel_id=1, source_target_pairs={{0,2},{2,4},{4,6},{1,3},{3,5},{5,7},{8,10},{10,12},{12,14},{9,11},... | collective-permute-start | bytes 786440 | tf_op jit(solution)/shard_map/ppermute | solution.py:17
  16.7 15.6 %collective-permute-start = (bf16[2,8,8,8,128]{4,3,2,1,0:T(8,128)(2,1)S(1)}, bf16[2,8,8,8,128]{4,3,2,1,0:T(8,128)(2,1)}, u32[]{:S(2)}, u32[]{:S(2)}) collective-permute-start(bf16[2,8,8,8,128]{4,3,2,1,0:T(8,128)(2,1)S(1)} %broadcast_select_fusion.17), channel_id=1, source_target_pairs={{0,2},{2,4},{4,6},{1,3},{3,5},{5,7},{8,10},{10,12},{12,14},{9,11},... | collective-permute-start | bytes 786440 | tf_op jit(solution)/shard_map/ppermute | solution.py:17
  21.7 14.8 %collective-permute-start.3 = (bf16[2,8,8,8,128]{4,3,2,1,0:T(8,128)(2,1)}, bf16[2,8,8,8,128]{4,3,2,1,0:T(8,128)(2,1)}, u32[]{:S(2)}, u32[]{:S(2)}) collective-permute-start(bf16[2,8,8,8,128]{4,3,2,1,0:T(8,128)(2,1)} %broadcast_select_fusion.13), channel_id=1, source_target_pairs={{0,2},{2,4},{4,6},{1,3},{3,5},{5,7},{8,10},{10,12},{12,14},{9,11},... | collective-permute-start | bytes 786440 | tf_op jit(solution)/shard_map/ppermute | solution.py:17
  26.0 24.9 %collective-permute-start.7 = (bf16[2,8,8,8,128]{4,3,2,1,0:T(8,128)(2,1)S(1)}, bf16[2,8,8,8,128]{4,3,2,1,0:T(8,128)(2,1)}, u32[]{:S(2)}, u32[]{:S(2)}) collective-permute-start(bf16[2,8,8,8,128]{4,3,2,1,0:T(8,128)(2,1)S(1)} %broadcast_select_fusion.7), channel_id=1, source_target_pairs={{2,0},{4,2},{6,4},{3,1},{5,3},{7,5},{10,8},{12,10},{14,12},{11,9},... | collective-permute-start | bytes 786440 | tf_op jit(solution)/shard_map/ppermute | solution.py:17
  28.1 24.1 %collective-permute-start.10 = (bf16[2,8,8,8,128]{4,3,2,1,0:T(8,128)(2,1)S(1)}, bf16[2,8,8,8,128]{4,3,2,1,0:T(8,128)(2,1)}, u32[]{:S(2)}, u32[]{:S(2)}) collective-permute-start(bf16[2,8,8,8,128]{4,3,2,1,0:T(8,128)(2,1)S(1)} %broadcast_select_fusion.3), channel_id=1, source_target_pairs={{2,0},{4,2},{6,4},{3,1},{5,3},{7,5},{10,8},{12,10},{14,12},{11,9},... | collective-permute-start | bytes 786440 | tf_op jit(solution)/shard_map/ppermute | solution.py:17
  32.3 8.6 %collective-permute-start.1 = (bf16[2,8,8,8,128]{4,3,2,1,0:T(8,128)(2,1)}, bf16[2,8,8,8,128]{4,3,2,1,0:T(8,128)(2,1)}, u32[]{:S(2)}, u32[]{:S(2)}) collective-permute-start(bf16[2,8,8,8,128]{4,3,2,1,0:T(8,128)(2,1)} %collective-permute-done), channel_id=1, source_target_pairs={{0,1},{2,3},{4,5},{6,7},{8,9},{10,11},{12,13},{14,15},{16,17},{18,... | collective-permute-start | bytes 786440 | tf_op jit(solution)/shard_map/ppermute | solution.py:17
  36.6 20.2 %collective-permute-start.4 = (bf16[2,8,8,8,128]{4,3,2,1,0:T(8,128)(2,1)}, bf16[2,8,8,8,128]{4,3,2,1,0:T(8,128)(2,1)}, u32[]{:S(2)}, u32[]{:S(2)}) collective-permute-start(bf16[2,8,8,8,128]{4,3,2,1,0:T(8,128)(2,1)} %collective-permute-done.3), channel_id=1, source_target_pairs={{1,0},{3,2},{5,4},{7,6},{9,8},{11,10},{13,12},{15,14},{17,16},{19,... | collective-permute-start | bytes 786440 | tf_op jit(solution)/shard_map/ppermute | solution.py:17
  40.9 18.8 %collective-permute-start.5 = (bf16[2,8,8,8,128]{4,3,2,1,0:T(8,128)(2,1)S(1)}, bf16[2,8,8,8,128]{4,3,2,1,0:T(8,128)(2,1)S(1)}, u32[]{:S(2)}, u32[]{:S(2)}) collective-permute-start(bf16[2,8,8,8,128]{4,3,2,1,0:T(8,128)(2,1)S(1)} %broadcast_select_fusion.11), channel_id=1, source_target_pairs={{0,1},{2,3},{4,5},{6,7},{8,9},{10,11},{12,13},{14,15},{16,17},{18,... | collective-permute-start | bytes 786440 | tf_op jit(solution)/shard_map/ppermute | solution.py:17
  47.9 12.6 %collective-permute-start.6 = (bf16[2,8,8,8,128]{4,3,2,1,0:T(8,128)(2,1)S(1)}, bf16[2,8,8,8,128]{4,3,2,1,0:T(8,128)(2,1)S(1)}, u32[]{:S(2)}, u32[]{:S(2)}) collective-permute-start(bf16[2,8,8,8,128]{4,3,2,1,0:T(8,128)(2,1)S(1)} %broadcast_select_fusion.9), channel_id=1, source_target_pairs={{1,0},{3,2},{5,4},{7,6},{9,8},{11,10},{13,12},{15,14},{17,16},{19,... | collective-permute-start | bytes 786440 | tf_op jit(solution)/shard_map/ppermute | solution.py:17
  50.9 11.0 %collective-permute-start.9 = (bf16[2,8,8,8,128]{4,3,2,1,0:T(8,128)(2,1)S(1)}, bf16[2,8,8,8,128]{4,3,2,1,0:T(8,128)(2,1)S(1)}, u32[]{:S(2)}, u32[]{:S(2)}) collective-permute-start(bf16[2,8,8,8,128]{4,3,2,1,0:T(8,128)(2,1)S(1)} %broadcast_select_fusion.5), channel_id=1, source_target_pairs={{2,0},{4,2},{6,4},{3,1},{5,3},{7,5},{10,8},{12,10},{14,12},{11,9},... | collective-permute-start | bytes 786440 | tf_op jit(solution)/shard_map/ppermute | solution.py:17
  52.2 9.0 %collective-permute-start.8 = (bf16[2,8,8,8,128]{4,3,2,1,0:T(8,128)(2,1)}, bf16[2,8,8,8,128]{4,3,2,1,0:T(8,128)(2,1)S(1)}, u32[]{:S(2)}, u32[]{:S(2)}) collective-permute-start(bf16[2,8,8,8,128]{4,3,2,1,0:T(8,128)(2,1)} %collective-permute-done.7), channel_id=1, source_target_pairs={{0,1},{2,3},{4,5},{6,7},{8,9},{10,11},{12,13},{14,15},{16,17},{18,... | collective-permute-start | bytes 786440 | tf_op jit(solution)/shard_map/ppermute | solution.py:17
  56.7 8.5 %collective-permute-start.11 = (bf16[2,8,8,8,128]{4,3,2,1,0:T(8,128)(2,1)}, bf16[2,8,8,8,128]{4,3,2,1,0:T(8,128)(2,1)S(1)}, u32[]{:S(2)}, u32[]{:S(2)}) collective-permute-start(bf16[2,8,8,8,128]{4,3,2,1,0:T(8,128)(2,1)} %collective-permute-done.10), channel_id=1, source_target_pairs={{1,0},{3,2},{5,4},{7,6},{9,8},{11,10},{13,12},{15,14},{17,16},{19,... | collective-permute-start | bytes 786440 | tf_op jit(solution)/shard_map/ppermute | solution.py:17
  110.5 24.7 %collective-permute-start.12 = (bf16[2,8,8,8,128]{4,3,2,1,0:T(8,128)(2,1)S(1)}, bf16[2,8,8,8,128]{4,3,2,1,0:T(8,128)(2,1)}, u32[]{:S(2)}, u32[]{:S(2)}) collective-permute-start(bf16[2,8,8,8,128]{4,3,2,1,0:T(8,128)(2,1)S(1)} %broadcast_select_fusion.16), channel_id=1, source_target_pairs={{0,2},{2,4},{4,6},{1,3},{3,5},{5,7},{8,10},{10,12},{12,14},{9,11},... | collective-permute-start | bytes 786440 | tf_op jit(solution)/shard_map/ppermute | solution.py:17
  129.1 12.2 %collective-permute-start.15 = (bf16[2,8,8,8,128]{4,3,2,1,0:T(8,128)(2,1)S(1)}, bf16[2,8,8,8,128]{4,3,2,1,0:T(8,128)(2,1)}, u32[]{:S(2)}, u32[]{:S(2)}) collective-permute-start(bf16[2,8,8,8,128]{4,3,2,1,0:T(8,128)(2,1)S(1)} %broadcast_select_fusion.12), channel_id=1, source_target_pairs={{0,2},{2,4},{4,6},{1,3},{3,5},{5,7},{8,10},{10,12},{12,14},{9,11},... | collective-permute-start | bytes 786440 | tf_op jit(solution)/shard_map/ppermute | solution.py:17
  133.8 13.4 %collective-permute-start.14 = (bf16[2,8,8,8,128]{4,3,2,1,0:T(8,128)(2,1)S(1)}, bf16[2,8,8,8,128]{4,3,2,1,0:T(8,128)(2,1)S(1)}, u32[]{:S(2)}, u32[]{:S(2)}) collective-permute-start(bf16[2,8,8,8,128]{4,3,2,1,0:T(8,128)(2,1)S(1)} %broadcast_select_fusion.14), channel_id=1, source_target_pairs={{0,2},{2,4},{4,6},{1,3},{3,5},{5,7},{8,10},{10,12},{12,14},{9,11},... | collective-permute-start | bytes 786440 | tf_op jit(solution)/shard_map/ppermute | solution.py:17
  135.2 7.5 %collective-permute-start.13 = (bf16[2,8,8,8,128]{4,3,2,1,0:T(8,128)(2,1)}, bf16[2,8,8,8,128]{4,3,2,1,0:T(8,128)(2,1)S(1)}, u32[]{:S(2)}, u32[]{:S(2)}) collective-permute-start(bf16[2,8,8,8,128]{4,3,2,1,0:T(8,128)(2,1)} %collective-permute-done.12), channel_id=1, source_target_pairs={{0,1},{2,3},{4,5},{6,7},{8,9},{10,11},{12,13},{14,15},{16,17},{18,... | collective-permute-start | bytes 786440 | tf_op jit(solution)/shard_map/ppermute | solution.py:17
  136.6 16.2 %collective-permute-start.19 = (bf16[2,8,8,8,128]{4,3,2,1,0:T(8,128)(2,1)S(1)}, bf16[2,8,8,8,128]{4,3,2,1,0:T(8,128)(2,1)S(1)}, u32[]{:S(2)}, u32[]{:S(2)}) collective-permute-start(bf16[2,8,8,8,128]{4,3,2,1,0:T(8,128)(2,1)S(1)} %broadcast_select_fusion.6), channel_id=1, source_target_pairs={{2,0},{4,2},{6,4},{3,1},{5,3},{7,5},{10,8},{12,10},{14,12},{11,9},... | collective-permute-start | bytes 786440 | tf_op jit(solution)/shard_map/ppermute | solution.py:17
  137.9 20.2 %collective-permute-start.22 = (bf16[2,8,8,8,128]{4,3,2,1,0:T(8,128)(2,1)S(1)}, bf16[2,8,8,8,128]{4,3,2,1,0:T(8,128)(2,1)S(1)}, u32[]{:S(2)}, u32[]{:S(2)}) collective-permute-start(bf16[2,8,8,8,128]{4,3,2,1,0:T(8,128)(2,1)S(1)} %broadcast_select_fusion.2), channel_id=1, source_target_pairs={{2,0},{4,2},{6,4},{3,1},{5,3},{7,5},{10,8},{12,10},{14,12},{11,9},... | collective-permute-start | bytes 786440 | tf_op jit(solution)/shard_map/ppermute | solution.py:17
  141.3 18.1 %collective-permute-start.16 = (bf16[2,8,8,8,128]{4,3,2,1,0:T(8,128)(2,1)}, bf16[2,8,8,8,128]{4,3,2,1,0:T(8,128)(2,1)S(1)}, u32[]{:S(2)}, u32[]{:S(2)}) collective-permute-start(bf16[2,8,8,8,128]{4,3,2,1,0:T(8,128)(2,1)} %collective-permute-done.15), channel_id=1, source_target_pairs={{1,0},{3,2},{5,4},{7,6},{9,8},{11,10},{13,12},{15,14},{17,16},{19,... | collective-permute-start | bytes 786440 | tf_op jit(solution)/shard_map/ppermute | solution.py:17
  142.6 18.1 %collective-permute-start.17 = (bf16[2,8,8,8,128]{4,3,2,1,0:T(8,128)(2,1)S(1)}, bf16[2,8,8,8,128]{4,3,2,1,0:T(8,128)(2,1)S(1)}, u32[]{:S(2)}, u32[]{:S(2)}) collective-permute-start(bf16[2,8,8,8,128]{4,3,2,1,0:T(8,128)(2,1)S(1)} %broadcast_select_fusion.10), channel_id=1, source_target_pairs={{0,1},{2,3},{4,5},{6,7},{8,9},{10,11},{12,13},{14,15},{16,17},{18,... | collective-permute-start | bytes 786440 | tf_op jit(solution)/shard_map/ppermute | solution.py:17
  147.3 13.6 %collective-permute-start.18 = (bf16[2,8,8,8,128]{4,3,2,1,0:T(8,128)(2,1)S(1)}, bf16[2,8,8,8,128]{4,3,2,1,0:T(8,128)(2,1)S(1)}, u32[]{:S(2)}, u32[]{:S(2)}) collective-permute-start(bf16[2,8,8,8,128]{4,3,2,1,0:T(8,128)(2,1)S(1)} %broadcast_select_fusion.8), channel_id=1, source_target_pairs={{1,0},{3,2},{5,4},{7,6},{9,8},{11,10},{13,12},{15,14},{17,16},{19,... | collective-permute-start | bytes 786440 | tf_op jit(solution)/shard_map/ppermute | solution.py:17
  152.7 11.8 %collective-permute-start.21 = (bf16[2,8,8,8,128]{4,3,2,1,0:T(8,128)(2,1)S(1)}, bf16[2,8,8,8,128]{4,3,2,1,0:T(8,128)(2,1)S(1)}, u32[]{:S(2)}, u32[]{:S(2)}) collective-permute-start(bf16[2,8,8,8,128]{4,3,2,1,0:T(8,128)(2,1)S(1)} %broadcast_select_fusion.4), channel_id=1, source_target_pairs={{2,0},{4,2},{6,4},{3,1},{5,3},{7,5},{10,8},{12,10},{14,12},{11,9},... | collective-permute-start | bytes 786440 | tf_op jit(solution)/shard_map/ppermute | solution.py:17
  159.4 8.3 %collective-permute-start.23 = (bf16[2,8,8,8,128]{4,3,2,1,0:T(8,128)(2,1)S(1)}, bf16[2,8,8,8,128]{4,3,2,1,0:T(8,128)(2,1)S(1)}, u32[]{:S(2)}, u32[]{:S(2)}) collective-permute-start(bf16[2,8,8,8,128]{4,3,2,1,0:T(8,128)(2,1)S(1)} %collective-permute-done.22), channel_id=1, source_target_pairs={{1,0},{3,2},{5,4},{7,6},{9,8},{11,10},{13,12},{15,14},{17,16},{19,... | collective-permute-start | bytes 786440 | tf_op jit(solution)/shard_map/ppermute | solution.py:17
  (44 other events, 399.1 us)
Sparse Core Ops, SparseCore 0:
  110.1 148.2 all-reduce.3
where the time goes:
time: 270 us; the launch traced here: 268 us
  waiting for transfers between devices  82.6 us (31%)
  starting transfers between devices  72.4 us (27%)
  local copies, waits for them, and re-layouts  67.4 us (25%)
  matrix products  15.2 us (6%)
  between operations  15 us (6%)
  other arithmetic  8.34 us (3%)
  loops' own time  7.06 us (3%)
    ppermute x24, starting transfers between devices, passed_along(): return lax.ppermute(x, axis, pairs)  72.4 us
    psum x1, waiting for transfers between devices, body(): combined = lax.psum(summed, ('dp', 'gx', 'gy'))  62.9 us
    ppermute x24, waiting for transfers between devices, passed_along(): return lax.ppermute(x, axis, pairs)  19.7 us
    gather x6, local copies, waits for them, and re-layouts, brick_columns(): picked = jnp.take(store, chosen, axis=0)  18 us
    unnamed x74, local copies, waits for them, and re-layouts  10.6 us
    gather x16, local copies, waits for them, and re-layouts, make_outbox(): outbox = jnp.take(source, chosen, axis=0)  10.4 us
    while x186, local copies, waits for them, and re-layouts  9.58 us
    dot_general x3, matrix products, forward_slot(): preact = jnp.dot(columns, weight, preferred_element_type=jnp.float32)  5.57 us
  transfers between devices with their start and end apart: 25, of which 7 were waited for; matrix products, arithmetic and copies ran while one was open for 16% of the time, Pallas kernels for 0%

commit v1 on v0

v1 whole, which is shorter than its diff:
```python
import functools
import math

import jax
import jax.numpy as jnp
from jax import lax
from jax.experimental import pallas as pl
from jax.experimental.pallas import tpu as pltpu
from jax.sharding import PartitionSpec as P

EDGE = 8
PLANE = EDGE * EDGE
DIRECTIONS = ((-1, -1), (-1, 0), (-1, 1), (0, -1), (0, 1), (1, -1), (1, 0), (1, 1))
VMEM_BYTES = 28 * 2**20
CORES = 2

F32 = jnp.float32
BF16 = jnp.bfloat16


def swap_phases(size):
    return [None] + ([0] if size > 1 else []) + ([1] if size > 2 else [])


def swap_partner(at, size, phase):
    if phase is None:
        return at
    other = at + 1 if at % 2 == phase else at - 1
    return other if 0 <= other < size else None


def routes_of(count_x, count_y):
    both = [(px, py) for px in swap_phases(count_x) for py in swap_phases(count_y)]
    return [route for route in both if route != (None, None)]


def route_pairs(route, count_x, count_y):
    pairs = []
    for x in range(count_x):
        for y in range(count_y):
            to_x = swap_partner(x, count_x, route[0])
            to_y = swap_partner(y, count_y, route[1])
            if to_x is not None and to_y is not None:
                pairs.append((x * count_y + y, to_x * count_y + to_y))
    return pairs


def step_of(at, phase):
    return 0 if phase is None else jnp.where(at % 2 == phase, 1, -1)


def direction_of(route, at_x, at_y):
    step_x, step_y = step_of(at_x, route[0]), step_of(at_y, route[1])
    flat = 3 * (step_x + 1) + step_y + 1
    return flat - jnp.where(flat > 4, 1, 0), step_x, step_y


def box_shape(route, send):
    if route[0] is None or route[1] is None:
        return (send, PLANE, 128)
    return (send * EDGE, 128)


def low_or_high(group, upper):
    wide = group.astype(F32)
    return wide[..., EDGE:, :] if upper else wide[..., :EDGE, :]


def pack_boxes(bricks, lists, boxes, routes, at_x, at_y, send):
    for route, box in zip(routes, boxes):
        number, step_x, step_y = direction_of(route, at_x, at_y)
        pieces = []
        for entry in range(send):
            listed = lists[number, entry]
            slot = jnp.maximum(listed, 0)
            kept = listed >= 0
            if route[1] is None:
                face = bricks[slot, jnp.where(step_x > 0, EDGE - 1, 0)]
                box[entry] = jnp.where(kept, face, jnp.zeros_like(face))
            elif route[0] is None:
                low = low_or_high(bricks[slot, :, 0:16, :], False)
                high = low_or_high(bricks[slot, :, PLANE - 16 : PLANE, :], True)
                face = jnp.where(kept, jnp.where(step_y > 0, high, low), 0.0)
                box[entry] = face.reshape(PLANE, 128).astype(BF16)
            else:
                plane = jnp.where(step_x > 0, EDGE - 1, 0)
                low = low_or_high(bricks[slot, plane, 0:16, :], False)
                high = low_or_high(bricks[slot, plane, PLANE - 16 : PLANE, :], True)
                pieces.append(jnp.where(kept, jnp.where(step_y > 0, high, low), 0.0))
        if pieces:
            box[...] = jnp.concatenate(pieces, axis=0).astype(BF16)


def fill_store(store, bricks, boxes, routes, at_x, at_y, send):
    slots = bricks.shape[0]
    store[0:slots] = bricks[...]
    store[store.shape[0] - 1] = jnp.zeros(store.shape[1:], BF16)
    for route, box in zip(routes, boxes):
        number, _, _ = direction_of(route, at_x, at_y)
        if not (route[0] is None or route[1] is None):
            edges = box[...].astype(F32)
        for entry in range(send):
            at = slots + number * send + entry
            if route[1] is None:
                store[at, 0] = box[entry]
                store[at, EDGE - 1] = box[entry]
            elif route[0] is None:
                rows = box[entry].astype(F32).reshape(EDGE, EDGE, 128)
                twice = jnp.concatenate([rows, rows], axis=1).astype(BF16)
                store[at, :, 0:16, :] = twice
                store[at, :, PLANE - 16 : PLANE, :] = twice
            else:
                rows = edges[entry * EDGE : (entry + 1) * EDGE]
                twice = jnp.concatenate([rows, rows], axis=0).astype(BF16)
                for plane in (0, EDGE - 1):
                    store[at, plane, 0:16, :] = twice
                    store[at, plane, PLANE - 16 : PLANE, :] = twice


def fill_views(views, store, table, slot):
    zero_at = store.shape[0] - 1

    def entry(off_x, off_y):
        listed = table[slot, 9 * (off_x + 1) + 3 * (off_y + 1) + 1]
        return jnp.where(listed < 0, zero_at, listed)

    for off_x, source, target in ((-1, EDGE - 1, 0), (0, slice(0, EDGE), slice(1, EDGE + 1)), (1, 0, EDGE + 1)):
        middle = store[entry(off_x, 0), source]
        before = low_or_high(store[entry(off_x, -1), source, PLANE - 16 : PLANE, :], True)
        after = low_or_high(store[entry(off_x, 1), source, 0:16, :], False)
        wide = middle.astype(F32)
        axis = wide.ndim - 2
        views[target, :, 128:256] = middle
        views[target, :, 0:128] = jnp.concatenate(
            [before, wide[..., : PLANE - EDGE, :]], axis=axis
        ).astype(BF16)
        views[target, :, 256:384] = jnp.concatenate(
            [wide[..., EDGE:, :], after], axis=axis
        ).astype(BF16)


def lhs_of(views):
    return jnp.concatenate(
        [views[dx : dx + EDGE].reshape(EDGE * PLANE, 384) for dx in range(3)], axis=1
    )


def shift_rows(wide, step):
    row = lax.broadcasted_iota(jnp.int32, wide.shape, 1)
    moved = pltpu.roll(wide, (-step) % EDGE, 1)
    return jnp.where(row == (EDGE - 1 if step > 0 else 0), 0.0, moved)


def join_taps(parts):
    blocks = [parts[:, 128 * dz : 128 * dz + 128].reshape(PLANE, EDGE, 128) for dz in range(3)]
    return blocks[1] + shift_rows(blocks[0], -1) + shift_rows(blocks[2], 1)


def pack_kernel(routes, send, lists, bricks, *boxes):
    at_x, at_y = lax.axis_index("gx"), lax.axis_index("gy")
    pack_boxes(bricks, lists, boxes, routes, at_x, at_y, send)


def forward_kernel(routes, send, factor, table, lists, bricks, cotangent, weight, *rest):
    count = len(routes)
    boxes_in, rest = rest[:count], rest[count:]
    activated, grads, kept_term, sent_term = rest[:4]
    boxes_out, rest = rest[4 : 4 + count], rest[4 + count :]
    store, views, taps = rest
    at_x, at_y = lax.axis_index("gx"), lax.axis_index("gy")
    core = lax.axis_index("dp") % CORES
    slots = bricks.shape[0]
    for tap in range(27):
        taps[tap // 3 * 128 : tap // 3 * 128 + 128, tap % 3 * 128 : tap % 3 * 128 + 128] = weight[tap]
    fill_store(store, bricks, boxes_in, routes, at_x, at_y, send)
    for slot in range(slots):
        fill_views(views.at[slot], store, table, slot)
        parts = jnp.dot(lhs_of(views.at[slot]), taps[...], preferred_element_type=F32)
        preact = join_taps(parts)
        sigmoid = jax.nn.sigmoid(preact)
        activated[slot] = (preact * sigmoid).reshape(EDGE, PLANE, 128).astype(BF16)
        slope = sigmoid * (1.0 + preact * (1.0 - sigmoid))
        wide = cotangent[slot].astype(F32).reshape(PLANE, EDGE, 128) * slope
        wide = jnp.where(table[slot, 13] >= 0, wide, 0.0)
        grads[slot] = wide.reshape(EDGE, PLANE, 128).astype(BF16)
    pack_boxes(grads, lists, boxes_out, routes, at_x, at_y, send)
    total = None
    for slot in range(slots):
        grad = grads[slot].astype(F32).reshape(PLANE, EDGE, 128)
        shifted = [shift_rows(grad, 1), grad, shift_rows(grad, -1)]
        rhs = jnp.concatenate([s.reshape(EDGE * PLANE, 128) for s in shifted], axis=1).astype(BF16)
        term = lax.dot_general(
            lhs_of(views.at[slot]), rhs, (((0,), (0,)), ((), ())), preferred_element_type=F32
        )
        total = term if total is None else total + term
    half = 128 // CORES
    for tap in range(27):
        block = total[tap // 3 * 128 : tap // 3 * 128 + 128, tap % 3 * 128 : tap % 3 * 128 + 128]
        block = block * factor
        first, second = block[:half], block[half:]
        kept_term[tap] = jnp.where(core == 0, first, second)
        sent_term[tap] = jnp.where(core == 0, second, first).astype(BF16)


def backward_kernel(routes, send, table, bricks, weight, *rest):
    count = len(routes)
    boxes_in, (result, store, views, taps) = rest[:count], rest[count:]
    at_x, at_y = lax.axis_index("gx"), lax.axis_index("gy")
    for tap in range(27):
        taps[tap % 3 * 128 : tap % 3 * 128 + 128, tap // 3 * 128 : tap // 3 * 128 + 128] = weight[26 - tap]
    fill_store(store, bricks, boxes_in, routes, at_x, at_y, send)
    for slot in range(bricks.shape[0]):
        fill_views(views.at[slot], store, table, slot)
        parts = lax.dot_general(
            lhs_of(views.at[slot]), taps[...], (((1,), (1,)), ((), ())), preferred_element_type=F32
        )
        result[slot] = join_taps(parts).reshape(EDGE, PLANE, 128).astype(BF16)


VMEM = pl.BlockSpec(memory_space=pltpu.VMEM)
SMEM = pl.BlockSpec(memory_space=pltpu.SMEM)
PARAMS = pltpu.CompilerParams(vmem_limit_bytes=VMEM_BYTES)


def xor_swap(x, axes, sizes, masks):
    pairs = []
    total = math.prod(sizes)
    for flat in range(total):
        left, where = flat, []
        for size in reversed(sizes):
            where.append(left % size)
            left //= size
        where.reverse()
        to = 0
        for size, at, mask in zip(sizes, where, masks):
            to = to * size + (at ^ mask)
        pairs.append((flat, to))
    return lax.ppermute(x, axes, pairs)


def tree_sum(terms):
    while len(terms) > 1:
        terms = [a + b for a, b in zip(terms[::2], terms[1::2])]
    return terms[0]


def own_piece(pieces, at):
    return lax.dynamic_index_in_dim(pieces, at, 1, keepdims=False)


def summed_everywhere(kept, sent):
    dp, gx, gy = (lax.axis_size(name) for name in ("dp", "gx", "gy"))
    me = lax.axis_index("dp")
    core = me % CORES
    half = kept + xor_swap(sent, ("dp",), (dp,), (1,)).astype(F32)
    chips = dp // CORES
    group = chips * gy
    mine = (me // CORES) * gy + lax.axis_index("gy")
    shares = half.reshape(half.shape[0], group, half.shape[1] // group, 128)
    masks = [(m // gy * CORES, m % gy) for m in range(group)]
    total = own_piece(shares, mine)
    for m in range(1, group):
        piece = own_piece(shares, mine ^ m).astype(BF16)
        total = total + xor_swap(piece, ("dp", "gy"), (dp, gy), masks[m]).astype(F32)
    rounded = total.astype(BF16)
    terms = [rounded] + [xor_swap(rounded, ("gx",), (gx,), (m,)) for m in range(1, gx)]
    rounded = tree_sum([term.astype(F32) for term in terms]).astype(BF16)
    parts = [rounded] + [xor_swap(rounded, ("dp", "gy"), (dp, gy), masks[m]) for m in range(1, group)]
    stacked = jnp.stack(parts, axis=1)
    order = jnp.arange(group) ^ mine
    half = jnp.take(stacked, order, axis=1).reshape(half.shape)
    other = xor_swap(half, ("dp",), (dp,), (1,))
    first = jnp.where(core == 0, half, other)
    second = jnp.where(core == 0, other, half)
    return jnp.concatenate([first, second], axis=1).astype(F32)


def body(features, weight, cotangent, neighbours, send_slots):
    slots, _, channels = features.shape[3:]
    send = send_slots.shape[-1]
    gx, gy = lax.axis_size("gx"), lax.axis_size("gy")
    devices = lax.axis_size("dp") * gx * gy
    routes = routes_of(gx, gy)
    bricks = features.reshape(slots, EDGE, PLANE, channels)
    cot = cotangent.reshape(slots, EDGE, PLANE, channels)
    table = neighbours.reshape(slots, 27)
    lists = send_slots.reshape(8, send)
    taps = weight.reshape(27, channels, channels)
    factor = 1.0 / math.sqrt(float(devices * slots * EDGE * PLANE))
    box_types = [jax.ShapeDtypeStruct(box_shape(route, send), BF16) for route in routes]
    bricks_type = jax.ShapeDtypeStruct(bricks.shape, BF16)
    entries = slots + 8 * send + 1
    scratch = [
        pltpu.VMEM((entries, EDGE, PLANE, 128), BF16),
        pltpu.VMEM((slots, EDGE + 2, PLANE, 384), BF16),
    ]

    def moved(boxes):
        return [
            lax.ppermute(box, ("gx", "gy"), route_pairs(route, gx, gy))
            for route, box in zip(routes, boxes)
        ]

    boxes = pl.pallas_call(
        functools.partial(pack_kernel, routes, send),
        out_shape=box_types,
        in_specs=[SMEM, VMEM],
        out_specs=[VMEM] * len(routes),
        compiler_params=PARAMS,
        name="pack",
    )(lists, bricks)
    arrived = moved(boxes)
    half_shape = (27, channels // CORES, channels)
    activated, grads, kept, sent, *boxes = pl.pallas_call(
        functools.partial(forward_kernel, routes, send, factor),
        out_shape=[
            bricks_type,
            bricks_type,
            jax.ShapeDtypeStruct(half_shape, F32),
            jax.ShapeDtypeStruct(half_shape, BF16),
            *box_types,
        ],
        in_specs=[SMEM, SMEM, VMEM, VMEM, VMEM] + [VMEM] * len(routes),
        out_specs=[VMEM] * (4 + len(routes)),
        scratch_shapes=scratch + [pltpu.VMEM((1152, 384), BF16)],
        compiler_params=PARAMS,
        name="forward",
    )(table, lists, bricks, cot, taps, *arrived)
    arrived = moved(boxes)
    weight_grad = summed_everywhere(kept, sent)
    input_grad = pl.pallas_call(
        functools.partial(backward_kernel, routes, send),
        out_shape=bricks_type,
        in_specs=[SMEM, VMEM, VMEM] + [VMEM] * len(routes),
        out_specs=VMEM,
        scratch_shapes=scratch + [pltpu.VMEM((384, 1152), BF16)],
        compiler_params=PARAMS,
        name="backward",
    )(table, grads, taps, *arrived)
    return (
        activated.reshape(features.shape),
        input_grad.reshape(features.shape),
        weight_grad.reshape(weight.shape),
    )


def solution(mesh):
    split = P("dp", "gx", "gy", None, None, None)
    table = P("dp", "gx", "gy", None, None)
    return jax.shard_map(
        body,
        mesh=mesh,
        in_specs=(split, P(), split, table, table),
        out_specs=(split, split, P()),
        check_vma=False,
    )
```

time: 270 us -> 76.6 us (0.28)
  the two profiles are of different devices: /device:TPU:0 before, /device:TPU:16 now
where the time goes in v1:
time: 76.6 us; the launch traced here: 76.3 us
  starting transfers between devices  29.2 us (38%)
  waiting for transfers between devices  27.4 us (36%)
  Pallas kernels  11.2 us (15%)
  local copies, waits for them, and re-layouts  5.63 us (7%)
  other arithmetic  2 us (3%)
  between operations  0.87 us (1%)
    ppermute x10, starting transfers between devices, moved(): lax.ppermute(box, ('gx', 'gy'), route_pairs(route, gx, gy))  18.4 us
    ppermute x11, waiting for transfers between devices, xor_swap(): return lax.ppermute(x, axes, pairs)  16.5 us
    ppermute x11, starting transfers between devices, xor_swap(): return lax.ppermute(x, axes, pairs)  10.9 us
    ppermute x10, waiting for transfers between devices, moved(): lax.ppermute(box, ('gx', 'gy'), route_pairs(route, gx, gy))  10.9 us
    pallas_call x1, Pallas kernels, body(): pl.pallas_call(functools.partial(forward_kernel, routes, send, factor), o...  6.24 us
    pallas_call x1, Pallas kernels, body(): pl.pallas_call(functools.partial(backward_kernel, routes, send), out_shap...  4.3 us
    unnamed x12, local copies, waits for them, and re-layouts  3.93 us
  transfers between devices with their start and end apart: 21, of which 13 were waited for; matrix products, arithmetic and copies ran while one was open for 0% of the time, Pallas kernels for 6%

profile of v1, /device:TPU:16, one launch (start us, length us, event | category | flops | bytes accessed | tf_op | source)
XLA Modules:
  0.0 76.3 jit_solution(3694649958790486269)
XLA Ops:
  3.1 1.6 %collective-permute-start = (bf16[2,64,128]{2,1,0:T(8,128)(2,1)S(1)}, bf16[2,64,128]{2,1,0:T(8,128)(2,1)S(1)}, u32[]{:S(2)}, u32[]{:S(2)}) collective-permute-start(bf16[2,64,128]{2,1,0:T(8,128)(2,1)S(1)} %get-tuple-element.17), channel_id=1, source_target_pairs={{0,1},{1,0},{2,3},{3,2},{4,5},{5,4},{6,7},{7,6},{8,9},{9,8},{10,11... | collective-permute-start | bytes 98312 | tf_op jit(solution)/shard_map/ppermute | solution.py:300
  4.7 1.6 %collective-permute-start.1 = (bf16[2,64,128]{2,1,0:T(8,128)(2,1)S(1)}, bf16[2,64,128]{2,1,0:T(8,128)(2,1)S(1)}, u32[]{:S(2)}, u32[]{:S(2)}) collective-permute-start(bf16[2,64,128]{2,1,0:T(8,128)(2,1)S(1)} %get-tuple-element.18), channel_id=1, source_target_pairs={{0,2},{1,3},{2,0},{3,1},{4,6},{5,7},{6,4},{7,5},{8,10},{9,11},{10,... | collective-permute-start | bytes 98312 | tf_op jit(solution)/shard_map/ppermute | solution.py:300
  6.3 1.9 %collective-permute-start.3 = (bf16[2,64,128]{2,1,0:T(8,128)(2,1)S(1)}, bf16[2,64,128]{2,1,0:T(8,128)(2,1)S(1)}, u32[]{:S(2)}, u32[]{:S(2)}) collective-permute-start(bf16[2,64,128]{2,1,0:T(8,128)(2,1)S(1)} %get-tuple-element.20), channel_id=1, source_target_pairs={{2,4},{3,5},{4,2},{5,3},{10,12},{11,13},{12,10},{13,11},{18,20},{1... | collective-permute-start | bytes 98312 | tf_op jit(solution)/shard_map/ppermute | solution.py:300
  8.3 3.9 %collective-permute-start.4 = (bf16[16,128]{1,0:T(8,128)(2,1)S(1)}, bf16[16,128]{1,0:T(8,128)(2,1)S(1)}, u32[]{:S(2)}, u32[]{:S(2)}) collective-permute-start(bf16[16,128]{1,0:T(8,128)(2,1)S(1)} %get-tuple-element.21), channel_id=1, source_target_pairs={{2,5},{3,4},{4,3},{5,2},{10,13},{11,12},{12,11},{13,10},{18,21},{1... | collective-permute-start | bytes 12296 | tf_op jit(solution)/shard_map/ppermute | solution.py:300
  12.8 1.9 %collective-permute-done.4.rest_4_ = bf16[16,128]{1,0:T(8,128)(2,1)S(1)} collective-permute-done((bf16[16,128]{1,0:T(8,128)(2,1)S(1)}, bf16[16,128]{1,0:T(8,128)(2,1)S(1)}, u32[]{:S(2)}, u32[]{:S(2)}) %collective-permute-start.4) | collective-permute-done | bytes 4128 | tf_op jit(solution)/shard_map/ppermute | solution.py:300
  17.6 6.2 %forward.1 = (bf16[4,8,64,128]{3,2,1,0:T(8,128)(2,1)}, bf16[4,8,64,128]{3,2,1,0:T(8,128)(2,1)S(1)}, f32[27,64,128]{2,1,0:T(8,128)S(1)}, bf16[27,64,128]{2,1,0:T(...) custom-call(s32[4,27]{1,0:T(4,128)S(1)} %bitcast.59, ...), custom_call_target="tpu_custom_call" | custom-call | tf_op jit(solution)/shard_map/forward/pallas_call | solution.py:314
  23.9 1.7 %collective-permute-done.10 = bf16[27,64,128]{2,1,0:T(8,128)(2,1)S(1)} collective-permute-done((bf16[27,64,128]{2,1,0:T(8,128)(2,1)S(1)}, bf16[27,64,128]{2,1,0:T(8,128)(2,1)S(1)}, u32[]{:S(2)}, u32[]{:S(2)}) %collective-permute-start.10) | collective-permute-done | bytes 442400 | tf_op jit(solution)/shard_map/ppermute | solution.py:238
  26.6 1.5 %collective-permute-start.12 = (bf16[27,16,128]{2,1,0:T(8,128)(2,1)S(1)}, bf16[27,16,128]{2,1,0:T(8,128)(2,1)S(1)}, u32[]{:S(2)}, u32[]{:S(2)}) collective-permute-start(bf16[27,16,128]{2,1,0:T(8,128)(2,1)S(1)} %get-tuple-element.34), channel_id=1, source_target_pairs={{0,16},{1,17},{8,24},{9,25},{16,0},{17,1},{24,8},{25,9},{2,18},{3,... | collective-permute-start | bytes 331784 | tf_op jit(solution)/shard_map/ppermute | solution.py:238
  28.1 1.4 %collective-permute-start.13 = (bf16[27,16,128]{2,1,0:T(8,128)(2,1)S(1)}, bf16[27,16,128]{2,1,0:T(8,128)(2,1)S(1)}, u32[]{:S(2)}, u32[]{:S(2)}) collective-permute-start(bf16[27,16,128]{2,1,0:T(8,128)(2,1)S(1)} %get-tuple-element.35), channel_id=1, source_target_pairs={{0,17},{1,16},{8,25},{9,24},{16,1},{17,0},{24,9},{25,8},{2,19},{3,... | collective-permute-start | bytes 331784 | tf_op jit(solution)/shard_map/ppermute | solution.py:238
  29.6 1.4 %collective-permute-done.11 = bf16[27,16,128]{2,1,0:T(8,128)(2,1)S(1)} collective-permute-done((bf16[27,16,128]{2,1,0:T(8,128)(2,1)S(1)}, bf16[27,16,128]{2,1,0:T(8,128)(2,1)S(1)}, u32[]{:S(2)}, u32[]{:S(2)}) %collective-permute-start.11) | collective-permute-done | bytes 110624 | tf_op jit(solution)/shard_map/ppermute | solution.py:238
  31.8 2.9 %collective-permute-done.13 = bf16[27,16,128]{2,1,0:T(8,128)(2,1)S(1)} collective-permute-done((bf16[27,16,128]{2,1,0:T(8,128)(2,1)S(1)}, bf16[27,16,128]{2,1,0:T(8,128)(2,1)S(1)}, u32[]{:S(2)}, u32[]{:S(2)}) %collective-permute-start.13) | collective-permute-done | bytes 110624 | tf_op jit(solution)/shard_map/ppermute | solution.py:238
  34.7 2.1 %collective-permute-start.16 = (bf16[27,16,128]{2,1,0:T(8,128)(2,1)S(1)}, bf16[27,16,128]{2,1,0:T(8,128)(2,1)S(1)}, u32[]{:S(2)}, u32[]{:S(2)}) collective-permute-start(bf16[27,16,128]{2,1,0:T(8,128)(2,1)S(1)} %fusion.2), channel_id=1, source_target_pairs={{0,6},{2,4},{4,2},{6,0},{1,7},{3,5},{5,3},{7,1},{8,14},{10,12},{12... | collective-permute-start | bytes 331784 | tf_op jit(solution)/shard_map/ppermute | solution.py:238
  36.7 1.5 %collective-permute-start.14 = (bf16[27,16,128]{2,1,0:T(8,128)(2,1)S(1)}, bf16[27,16,128]{2,1,0:T(8,128)(2,1)S(1)}, u32[]{:S(2)}, u32[]{:S(2)}) collective-permute-start(bf16[27,16,128]{2,1,0:T(8,128)(2,1)S(1)} %fusion.2), channel_id=1, source_target_pairs={{0,2},{2,0},{4,6},{6,4},{1,3},{3,1},{5,7},{7,5},{8,10},{10,8},{12,... | collective-permute-start | bytes 331784 | tf_op jit(solution)/shard_map/ppermute | solution.py:238
  38.3 4.8 %collective-permute-done.16 = bf16[27,16,128]{2,1,0:T(8,128)(2,1)S(1)} collective-permute-done((bf16[27,16,128]{2,1,0:T(8,128)(2,1)S(1)}, bf16[27,16,128]{2,1,0:T(8,128)(2,1)S(1)}, u32[]{:S(2)}, u32[]{:S(2)}) %collective-permute-start.16) | collective-permute-done | bytes 110624 | tf_op jit(solution)/shard_map/ppermute | solution.py:238
  43.7 2.0 %collective-permute-start.19 = (bf16[27,16,128]{2,1,0:T(8,128)(2,1)S(1)}, bf16[27,16,128]{2,1,0:T(8,128)(2,1)S(1)}, u32[]{:S(2)}, u32[]{:S(2)}) collective-permute-start(bf16[27,16,128]{2,1,0:T(8,128)(2,1)S(1)} %add_convert_fusion), channel_id=1, source_target_pairs={{0,17},{1,16},{8,25},{9,24},{16,1},{17,0},{24,9},{25,8},{2,19},{3,... | collective-permute-start | bytes 331784 | tf_op jit(solution)/shard_map/ppermute | solution.py:238
  45.9 1.3 %collective-permute-start.17 = (bf16[27,16,128]{2,1,0:T(8,128)(2,1)S(1)}, bf16[27,16,128]{2,1,0:T(8,128)(2,1)S(1)}, u32[]{:S(2)}, u32[]{:S(2)}) collective-permute-start(bf16[27,16,128]{2,1,0:T(8,128)(2,1)S(1)} %add_convert_fusion), channel_id=1, source_target_pairs={{0,1},{1,0},{8,9},{9,8},{16,17},{17,16},{24,25},{25,24},{2,3},{3,2... | collective-permute-start | bytes 331784 | tf_op jit(solution)/shard_map/ppermute | solution.py:238
  47.3 3.3 %collective-permute-done.19 = bf16[27,16,128]{2,1,0:T(8,128)(2,1)S(1)} collective-permute-done((bf16[27,16,128]{2,1,0:T(8,128)(2,1)S(1)}, bf16[27,16,128]{2,1,0:T(8,128)(2,1)S(1)}, u32[]{:S(2)}, u32[]{:S(2)}) %collective-permute-start.19) | collective-permute-done | bytes 110624 | tf_op jit(solution)/shard_map/ppermute | solution.py:238
  53.5 2.0 %collective-permute-start.6 = (bf16[2,64,128]{2,1,0:T(8,128)(2,1)S(1)}, bf16[2,64,128]{2,1,0:T(8,128)(2,1)S(1)}, u32[]{:S(2)}, u32[]{:S(2)}) collective-permute-start(bf16[2,64,128]{2,1,0:T(8,128)(2,1)S(1)} %get-tuple-element.25), channel_id=1, source_target_pairs={{0,2},{1,3},{2,0},{3,1},{4,6},{5,7},{6,4},{7,5},{8,10},{9,11},{10,... | collective-permute-start | bytes 98312 | tf_op jit(solution)/shard_map/ppermute | solution.py:300
  55.5 3.9 %collective-permute-start.8 = (bf16[2,64,128]{2,1,0:T(8,128)(2,1)S(1)}, bf16[2,64,128]{2,1,0:T(8,128)(2,1)S(1)}, u32[]{:S(2)}, u32[]{:S(2)}) collective-permute-start(bf16[2,64,128]{2,1,0:T(8,128)(2,1)S(1)} %get-tuple-element.27), channel_id=1, source_target_pairs={{2,4},{3,5},{4,2},{5,3},{10,12},{11,13},{12,10},{13,11},{18,20},{1... | collective-permute-start | bytes 98312 | tf_op jit(solution)/shard_map/ppermute | solution.py:300
  59.5 4.5 %collective-permute-done.7.rest_2_ = bf16[16,128]{1,0:T(8,128)(2,1)S(1)} collective-permute-done((bf16[16,128]{1,0:T(8,128)(2,1)S(1)}, bf16[16,128]{1,0:T(8,128)(2,1)S(1)}, u32[]{:S(2)}, u32[]{:S(2)}) %collective-permute-start.7) | collective-permute-done | bytes 4128 | tf_op jit(solution)/shard_map/ppermute | solution.py:300
  64.0 2.5 %collective-permute-start.9 = (bf16[16,128]{1,0:T(8,128)(2,1)S(1)}, bf16[16,128]{1,0:T(8,128)(2,1)S(1)}, u32[]{:S(2)}, u32[]{:S(2)}) collective-permute-start(bf16[16,128]{1,0:T(8,128)(2,1)S(1)} %get-tuple-element.28), channel_id=1, source_target_pairs={{2,5},{3,4},{4,3},{5,2},{10,13},{11,12},{12,11},{13,10},{18,21},{1... | collective-permute-start | bytes 12296 | tf_op jit(solution)/shard_map/ppermute | solution.py:300
  66.5 3.8 %collective-permute-done.9.rest_4_ = bf16[16,128]{1,0:T(8,128)(2,1)S(1)} collective-permute-done((bf16[16,128]{1,0:T(8,128)(2,1)S(1)}, bf16[16,128]{1,0:T(8,128)(2,1)S(1)}, u32[]{:S(2)}, u32[]{:S(2)}) %collective-permute-start.9) | collective-permute-done | bytes 4128 | tf_op jit(solution)/shard_map/ppermute | solution.py:300
  70.4 4.3 %backward.1 = bf16[4,8,64,128]{3,2,1,0:T(8,128)(2,1)} custom-call(s32[4,27]{1,0:T(4,128)S(1)} %bitcast.60, bf16[4,8,64,128]{3,2,1,0:T(8,128)(2,1)S(1)} %get-tuple-element.23.bricks, bf16[27,128,128]{2,1,0:T(8,128)(2,1)S(1)} %bitcast.55, bf16[2,64,128]{2,1,0:T(8,128)(2,1)S(1)} %collective-permute-done.5.rest_0_, ...), custom_call_target="tpu_custom_call" | custom-call | tf_op jit(solution)/shard_map/backward/pallas_call | solution.py:331
  74.9 1.4 %bitcast_convert_fusion = f32[3456,128]{1,0:T(8,128)} fusion(bf16[27,128,128]{2,1,0:T(8,128)(2,1)S(1)} %pad_maximum_fusion), kind=kLoop, calls=%fused_computation.2 | loop fusion | flops 442368 | bytes 2654208 | tf_op jit(solution)/shard_map/convert_element_type | solution.py:275
  (50 shorter events, 12.1 us)
Async XLA Ops:
  3.1 11.6 %collective-permute-start = (bf16[2,64,128]{2,1,0:T(8,128)(2,1)S(1)}, bf16[2,64,128]{2,1,0:T(8,128)(2,1)S(1)}, u32[]{:S(2)}, u32[]{:S(2)}) collective-permute-start(bf16[2,64,128]{2,1,0:T(8,128)(2,1)S(1)} %get-tuple-element.17), channel_id=1, source_target_pairs={{0,1},{1,0},{2,3},{3,2},{4,5},{5,4},{6,7},{7,6},{8,9},{9,8},{10,11... | collective-permute-start | bytes 98312 | tf_op jit(solution)/shard_map/ppermute | solution.py:300
  4.7 10.0 %collective-permute-start.1 = (bf16[2,64,128]{2,1,0:T(8,128)(2,1)S(1)}, bf16[2,64,128]{2,1,0:T(8,128)(2,1)S(1)}, u32[]{:S(2)}, u32[]{:S(2)}) collective-permute-start(bf16[2,64,128]{2,1,0:T(8,128)(2,1)S(1)} %get-tuple-element.18), channel_id=1, source_target_pairs={{0,2},{1,3},{2,0},{3,1},{4,6},{5,7},{6,4},{7,5},{8,10},{9,11},{10,... | collective-permute-start | bytes 98312 | tf_op jit(solution)/shard_map/ppermute | solution.py:300
  6.3 8.4 %collective-permute-start.3 = (bf16[2,64,128]{2,1,0:T(8,128)(2,1)S(1)}, bf16[2,64,128]{2,1,0:T(8,128)(2,1)S(1)}, u32[]{:S(2)}, u32[]{:S(2)}) collective-permute-start(bf16[2,64,128]{2,1,0:T(8,128)(2,1)S(1)} %get-tuple-element.20), channel_id=1, source_target_pairs={{2,4},{3,5},{4,2},{5,3},{10,12},{11,13},{12,10},{13,11},{18,20},{1... | collective-permute-start | bytes 98312 | tf_op jit(solution)/shard_map/ppermute | solution.py:300
  8.2 4.6 %collective-permute-start.2 = (bf16[16,128]{1,0:T(8,128)(2,1)S(1)}, bf16[16,128]{1,0:T(8,128)(2,1)S(1)}, u32[]{:S(2)}, u32[]{:S(2)}) collective-permute-start(bf16[16,128]{1,0:T(8,128)(2,1)S(1)} %get-tuple-element.19), channel_id=1, source_target_pairs={{0,3},{1,2},{2,1},{3,0},{4,7},{5,6},{6,5},{7,4},{8,11},{9,10},{10,... | collective-permute-start | bytes 12296 | tf_op jit(solution)/shard_map/ppermute | solution.py:300
  8.3 6.4 %collective-permute-start.4 = (bf16[16,128]{1,0:T(8,128)(2,1)S(1)}, bf16[16,128]{1,0:T(8,128)(2,1)S(1)}, u32[]{:S(2)}, u32[]{:S(2)}) collective-permute-start(bf16[16,128]{1,0:T(8,128)(2,1)S(1)} %get-tuple-element.21), channel_id=1, source_target_pairs={{2,5},{3,4},{4,3},{5,2},{10,13},{11,12},{12,11},{13,10},{18,21},{1... | collective-permute-start | bytes 12296 | tf_op jit(solution)/shard_map/ppermute | solution.py:300
  14.7 1.2 %copy-start = (bf16[3456,128]{1,0:T(8,128)(2,1)S(1)}, bf16[3456,128]{1,0:T(8,128)(2,1)}, u32[]{:S(2)}) copy-start(bf16[3456,128]{1,0:T(8,128)(2,1)} %param.6) | copy-start | bytes 2654212
  23.8 1.9 %collective-permute-start.10 = (bf16[27,64,128]{2,1,0:T(8,128)(2,1)S(1)}, bf16[27,64,128]{2,1,0:T(8,128)(2,1)S(1)}, u32[]{:S(2)}, u32[]{:S(2)}) collective-permute-start(bf16[27,64,128]{2,1,0:T(8,128)(2,1)S(1)} %get-tuple-element.30), channel_id=1, source_target_pairs={{0,8},{8,0},{16,24},{24,16},{1,9},{9,1},{17,25},{25,17},{2,10},{10... | collective-permute-start | bytes 1327112 | tf_op jit(solution)/shard_map/ppermute | solution.py:238
  25.9 5.2 %collective-permute-start.11 = (bf16[27,16,128]{2,1,0:T(8,128)(2,1)S(1)}, bf16[27,16,128]{2,1,0:T(8,128)(2,1)S(1)}, u32[]{:S(2)}, u32[]{:S(2)}) collective-permute-start(bf16[27,16,128]{2,1,0:T(8,128)(2,1)S(1)} %get-tuple-element.33), channel_id=1, source_target_pairs={{0,1},{1,0},{8,9},{9,8},{16,17},{17,16},{24,25},{25,24},{2,3},{3,2... | collective-permute-start | bytes 331784 | tf_op jit(solution)/shard_map/ppermute | solution.py:238
  26.6 5.2 %collective-permute-start.12 = (bf16[27,16,128]{2,1,0:T(8,128)(2,1)S(1)}, bf16[27,16,128]{2,1,0:T(8,128)(2,1)S(1)}, u32[]{:S(2)}, u32[]{:S(2)}) collective-permute-start(bf16[27,16,128]{2,1,0:T(8,128)(2,1)S(1)} %get-tuple-element.34), channel_id=1, source_target_pairs={{0,16},{1,17},{8,24},{9,25},{16,0},{17,1},{24,8},{25,9},{2,18},{3,... | collective-permute-start | bytes 331784 | tf_op jit(solution)/shard_map/ppermute | solution.py:238
  28.1 6.5 %collective-permute-start.13 = (bf16[27,16,128]{2,1,0:T(8,128)(2,1)S(1)}, bf16[27,16,128]{2,1,0:T(8,128)(2,1)S(1)}, u32[]{:S(2)}, u32[]{:S(2)}) collective-permute-start(bf16[27,16,128]{2,1,0:T(8,128)(2,1)S(1)} %get-tuple-element.35), channel_id=1, source_target_pairs={{0,17},{1,16},{8,25},{9,24},{16,1},{17,0},{24,9},{25,8},{2,19},{3,... | collective-permute-start | bytes 331784 | tf_op jit(solution)/shard_map/ppermute | solution.py:238
  34.7 8.4 %collective-permute-start.16 = (bf16[27,16,128]{2,1,0:T(8,128)(2,1)S(1)}, bf16[27,16,128]{2,1,0:T(8,128)(2,1)S(1)}, u32[]{:S(2)}, u32[]{:S(2)}) collective-permute-start(bf16[27,16,128]{2,1,0:T(8,128)(2,1)S(1)} %fusion.2), channel_id=1, source_target_pairs={{0,6},{2,4},{4,2},{6,0},{1,7},{3,5},{5,3},{7,1},{8,14},{10,12},{12... | collective-permute-start | bytes 331784 | tf_op jit(solution)/shard_map/ppermute | solution.py:238
  36.7 6.9 %collective-permute-start.15 = (bf16[27,16,128]{2,1,0:T(8,128)(2,1)S(1)}, bf16[27,16,128]{2,1,0:T(8,128)(2,1)S(1)}, u32[]{:S(2)}, u32[]{:S(2)}) collective-permute-start(bf16[27,16,128]{2,1,0:T(8,128)(2,1)S(1)} %fusion.2), channel_id=1, source_target_pairs={{0,4},{2,6},{4,0},{6,2},{1,5},{3,7},{5,1},{7,3},{8,12},{10,14},{12... | collective-permute-start | bytes 331784 | tf_op jit(solution)/shard_map/ppermute | solution.py:238
  36.7 6.9 %collective-permute-start.14 = (bf16[27,16,128]{2,1,0:T(8,128)(2,1)S(1)}, bf16[27,16,128]{2,1,0:T(8,128)(2,1)S(1)}, u32[]{:S(2)}, u32[]{:S(2)}) collective-permute-start(bf16[27,16,128]{2,1,0:T(8,128)(2,1)S(1)} %fusion.2), channel_id=1, source_target_pairs={{0,2},{2,0},{4,6},{6,4},{1,3},{3,1},{5,7},{7,5},{8,10},{10,8},{12,... | collective-permute-start | bytes 331784 | tf_op jit(solution)/shard_map/ppermute | solution.py:238
  43.7 6.8 %collective-permute-start.19 = (bf16[27,16,128]{2,1,0:T(8,128)(2,1)S(1)}, bf16[27,16,128]{2,1,0:T(8,128)(2,1)S(1)}, u32[]{:S(2)}, u32[]{:S(2)}) collective-permute-start(bf16[27,16,128]{2,1,0:T(8,128)(2,1)S(1)} %add_convert_fusion), channel_id=1, source_target_pairs={{0,17},{1,16},{8,25},{9,24},{16,1},{17,0},{24,9},{25,8},{2,19},{3,... | collective-permute-start | bytes 331784 | tf_op jit(solution)/shard_map/ppermute | solution.py:238
  45.7 5.3 %collective-permute-start.18 = (bf16[27,16,128]{2,1,0:T(8,128)(2,1)S(1)}, bf16[27,16,128]{2,1,0:T(8,128)(2,1)S(1)}, u32[]{:S(2)}, u32[]{:S(2)}) collective-permute-start(bf16[27,16,128]{2,1,0:T(8,128)(2,1)S(1)} %add_convert_fusion), channel_id=1, source_target_pairs={{0,16},{1,17},{8,24},{9,25},{16,0},{17,1},{24,8},{25,9},{2,18},{3,... | collective-permute-start | bytes 331784 | tf_op jit(solution)/shard_map/ppermute | solution.py:238
  45.9 5.7 %collective-permute-start.17 = (bf16[27,16,128]{2,1,0:T(8,128)(2,1)S(1)}, bf16[27,16,128]{2,1,0:T(8,128)(2,1)S(1)}, u32[]{:S(2)}, u32[]{:S(2)}) collective-permute-start(bf16[27,16,128]{2,1,0:T(8,128)(2,1)S(1)} %add_convert_fusion), channel_id=1, source_target_pairs={{0,1},{1,0},{8,9},{9,8},{16,17},{17,16},{24,25},{25,24},{2,3},{3,2... | collective-permute-start | bytes 331784 | tf_op jit(solution)/shard_map/ppermute | solution.py:238
  51.7 18.7 %copy-start.1 = (bf16[3456,128]{1,0:T(8,128)(2,1)S(1)}, bf16[3456,128]{1,0:T(8,128)(2,1)}, u32[]{:S(2)}) copy-start(bf16[3456,128]{1,0:T(8,128)(2,1)} %param.6) | copy-start | bytes 2654212
  51.7 18.7 %copy-start.5 = (s32[1,1,1,4,27]{4,3,2,1,0:T(4,128)S(1)}, s32[1,1,1,4,27]{4,3,2,1,0:T(4,128)}, u32[]{:S(2)}) copy-start(s32[1,1,1,4,27]{4,3,2,1,0:T(4,128)} %param.8) | copy-start | bytes 1300
  52.6 22.1 %collective-permute-start.20 = (bf16[27,64,128]{2,1,0:T(8,128)(2,1)S(1)}, bf16[27,64,128]{2,1,0:T(8,128)(2,1)S(1)}, u32[]{:S(2)}, u32[]{:S(2)}) collective-permute-start(bf16[27,64,128]{2,1,0:T(8,128)(2,1)S(1)} %bitcast_select_fusion), channel_id=1, source_target_pairs={{0,8},{8,0},{16,24},{24,16},{1,9},{9,1},{17,25},{25,17},{2,10},{10... | collective-permute-start | bytes 1327112 | tf_op jit(solution)/shard_map/ppermute | solution.py:238
  52.7 17.7 %collective-permute-start.5 = (bf16[2,64,128]{2,1,0:T(8,128)(2,1)S(1)}, bf16[2,64,128]{2,1,0:T(8,128)(2,1)S(1)}, u32[]{:S(2)}, u32[]{:S(2)}) collective-permute-start(bf16[2,64,128]{2,1,0:T(8,128)(2,1)S(1)} %get-tuple-element.24), channel_id=1, source_target_pairs={{0,1},{1,0},{2,3},{3,2},{4,5},{5,4},{6,7},{7,6},{8,9},{9,8},{10,11... | collective-permute-start | bytes 98312 | tf_op jit(solution)/shard_map/ppermute | solution.py:300
  53.5 16.8 %collective-permute-start.6 = (bf16[2,64,128]{2,1,0:T(8,128)(2,1)S(1)}, bf16[2,64,128]{2,1,0:T(8,128)(2,1)S(1)}, u32[]{:S(2)}, u32[]{:S(2)}) collective-permute-start(bf16[2,64,128]{2,1,0:T(8,128)(2,1)S(1)} %get-tuple-element.25), channel_id=1, source_target_pairs={{0,2},{1,3},{2,0},{3,1},{4,6},{5,7},{6,4},{7,5},{8,10},{9,11},{10,... | collective-permute-start | bytes 98312 | tf_op jit(solution)/shard_map/ppermute | solution.py:300
  55.5 14.8 %collective-permute-start.8 = (bf16[2,64,128]{2,1,0:T(8,128)(2,1)S(1)}, bf16[2,64,128]{2,1,0:T(8,128)(2,1)S(1)}, u32[]{:S(2)}, u32[]{:S(2)}) collective-permute-start(bf16[2,64,128]{2,1,0:T(8,128)(2,1)S(1)} %get-tuple-element.27), channel_id=1, source_target_pairs={{2,4},{3,5},{4,2},{5,3},{10,12},{11,13},{12,10},{13,11},{18,20},{1... | collective-permute-start | bytes 98312 | tf_op jit(solution)/shard_map/ppermute | solution.py:300
  59.4 4.6 %collective-permute-start.7 = (bf16[16,128]{1,0:T(8,128)(2,1)S(1)}, bf16[16,128]{1,0:T(8,128)(2,1)S(1)}, u32[]{:S(2)}, u32[]{:S(2)}) collective-permute-start(bf16[16,128]{1,0:T(8,128)(2,1)S(1)} %get-tuple-element.26), channel_id=1, source_target_pairs={{0,3},{1,2},{2,1},{3,0},{4,7},{5,6},{6,5},{7,4},{8,11},{9,10},{10,... | collective-permute-start | bytes 12296 | tf_op jit(solution)/shard_map/ppermute | solution.py:300
  64.0 6.4 %collective-permute-start.9 = (bf16[16,128]{1,0:T(8,128)(2,1)S(1)}, bf16[16,128]{1,0:T(8,128)(2,1)S(1)}, u32[]{:S(2)}, u32[]{:S(2)}) collective-permute-start(bf16[16,128]{1,0:T(8,128)(2,1)S(1)} %get-tuple-element.28), channel_id=1, source_target_pairs={{2,5},{3,4},{4,3},{5,2},{10,13},{11,12},{12,11},{13,10},{18,21},{1... | collective-permute-start | bytes 12296 | tf_op jit(solution)/shard_map/ppermute | solution.py:300
  (3 other events, 2.8 us)

commit v2 on v1

v2 whole, which is shorter than its diff:
```python
import functools
import math

import jax
import jax.numpy as jnp
from jax import lax
from jax.experimental import pallas as pl
from jax.experimental.pallas import tpu as pltpu
from jax.sharding import PartitionSpec as P

EDGE = 8
PLANE = EDGE * EDGE
VMEM_BYTES = 28 * 2**20
CORES = 2

F32 = jnp.float32
BF16 = jnp.bfloat16


def swap_phases(size):
    return ([0] if size > 1 else []) + ([1] if size > 2 else [])


def swap_pairs(size, phase):
    pairs = []
    for low in range(phase, size - 1, 2):
        pairs += [(low, low + 1), (low + 1, low)]
    return pairs


def step_of(at, phase):
    return jnp.where(at % 2 == phase, 1, -1)


def direction(step_x, step_y):
    flat = 3 * (step_x + 1) + step_y + 1
    return flat - jnp.where(flat > 4, 1, 0)


def low_or_high(group, upper):
    wide = group.astype(F32)
    return wide[..., EDGE:, :] if upper else wide[..., :EDGE, :]


def y_edge(bricks, slot, plane, step_y):
    low = low_or_high(bricks[slot, plane, 0:16, :], False)
    high = low_or_high(bricks[slot, plane, PLANE - 16 : PLANE, :], True)
    return jnp.where(step_y > 0, high, low)


def pack_along_y(bricks, lists, box, step_y, send):
    number = direction(0, step_y)
    for entry in range(send):
        listed = lists[number, entry]
        face = y_edge(bricks, jnp.maximum(listed, 0), slice(0, EDGE), step_y)
        face = jnp.where(listed >= 0, face, 0.0).reshape(PLANE, 128)
        box[entry * PLANE : (entry + 1) * PLANE] = face.astype(BF16)
    at = send * PLANE
    for step_x in (-1, 1):
        number = direction(step_x, step_y)
        pieces = []
        for entry in range(send):
            listed = lists[number, entry]
            plane = EDGE - 1 if step_x > 0 else 0
            edge = y_edge(bricks, jnp.maximum(listed, 0), plane, step_y)
            pieces.append(jnp.where(listed >= 0, edge, 0.0))
        box[at : at + send * EDGE] = jnp.concatenate(pieces, axis=0).astype(BF16)
        at += send * EDGE


def pack_along_x(bricks, lists, box, y_boxes, step_x, send):
    number = direction(step_x, 0)
    for entry in range(send):
        listed = lists[number, entry]
        face = bricks[jnp.maximum(listed, 0), jnp.where(step_x > 0, EDGE - 1, 0)]
        box[entry * PLANE : (entry + 1) * PLANE] = jnp.where(listed >= 0, face, jnp.zeros_like(face))
    at = send * PLANE
    for y_box in y_boxes:
        first = y_box[send * PLANE : send * PLANE + send * EDGE]
        second = y_box[send * PLANE + send * EDGE : send * PLANE + 2 * send * EDGE]
        box[at : at + send * EDGE] = jnp.where(step_x > 0, second, first)
        at += send * EDGE


def fill_remote(store, base, x_boxes, y_boxes, steps_x, steps_y, send):
    store[store.shape[0] - 1] = jnp.zeros(store.shape[1:], BF16)
    for step_y, box in zip(steps_y, y_boxes):
        number = direction(0, step_y)
        for entry in range(send):
            rows = box[entry * PLANE : (entry + 1) * PLANE].astype(F32).reshape(EDGE, EDGE, 128)
            twice = jnp.concatenate([rows, rows], axis=1).astype(BF16)
            store[base + number * send + entry, :, 0:16, :] = twice
            store[base + number * send + entry, :, PLANE - 16 : PLANE, :] = twice
    for step_x, box in zip(steps_x, x_boxes):
        number = direction(step_x, 0)
        for entry in range(send):
            face = box[entry * PLANE : (entry + 1) * PLANE]
            store[base + number * send + entry, 0] = face
            store[base + number * send + entry, EDGE - 1] = face
        at = send * PLANE
        for step_y in steps_y:
            number = direction(step_x, step_y)
            edges = box[at : at + send * EDGE].astype(F32)
            at += send * EDGE
            for entry in range(send):
                rows = edges[entry * EDGE : (entry + 1) * EDGE]
                twice = jnp.concatenate([rows, rows], axis=0).astype(BF16)
                for plane in (0, EDGE - 1):
                    store[base + number * send + entry, plane, 0:16, :] = twice
                    store[base + number * send + entry, plane, PLANE - 16 : PLANE, :] = twice


def view_of(store, entry, off_x, source):
    middle = store[entry(off_x, 0), source]
    before = low_or_high(store[entry(off_x, -1), source, PLANE - 16 : PLANE, :], True)
    after = low_or_high(store[entry(off_x, 1), source, 0:16, :], False)
    wide = middle.astype(F32)
    axis = wide.ndim - 2
    left = jnp.concatenate([before, wide[..., : PLANE - EDGE, :]], axis=axis).astype(BF16)
    right = jnp.concatenate([wide[..., EDGE:, :], after], axis=axis).astype(BF16)
    return jnp.concatenate([left, middle, right], axis=axis + 1)


def fill_views(views, store, entry):
    views[0] = view_of(store, entry, -1, EDGE - 1)
    views[1 : EDGE + 1] = view_of(store, entry, 0, slice(0, EDGE))
    views[EDGE + 1] = view_of(store, entry, 1, 0)


def lookup(table, slot, first, last, zero_at):
    def entry(off_x, off_y):
        listed = table[slot, 9 * (off_x + 1) + 3 * (off_y + 1) + 1]
        return jnp.where((listed >= first) & (listed < last), listed - first, zero_at)

    return entry


def lhs_of(views):
    return jnp.concatenate(
        [views[dx : dx + EDGE].reshape(EDGE * PLANE, 384) for dx in range(3)], axis=1
    )


def shift_rows(wide, step):
    row = lax.broadcasted_iota(jnp.int32, wide.shape, 1)
    moved = pltpu.roll(wide, (-step) % EDGE, 1)
    return jnp.where(row == (EDGE - 1 if step > 0 else 0), 0.0, moved)


def join_taps(parts):
    shape = (parts.shape[0] // EDGE, EDGE, 128)
    blocks = [parts[:, 128 * dz : 128 * dz + 128].reshape(shape) for dz in range(3)]
    return blocks[1] + shift_rows(blocks[0], -1) + shift_rows(blocks[2], 1)


def steps_here(counts):
    steps_x = [step_of(lax.axis_index("gx"), phase) for phase in swap_phases(counts[0])]
    steps_y = [step_of(lax.axis_index("gy"), phase) for phase in swap_phases(counts[1])]
    return steps_x, steps_y


def pack_y_kernel(counts, send, lists, bricks, *boxes):
    for step_y, box in zip(steps_here(counts)[1], boxes):
        pack_along_y(bricks, lists, box, step_y, send)


def pack_x_kernel(counts, send, lists, bricks, *rest):
    steps_x, steps_y = steps_here(counts)
    y_boxes, x_boxes = rest[: len(steps_y)], rest[len(steps_y) :]
    for step_x, box in zip(steps_x, x_boxes):
        pack_along_x(bricks, lists, box, y_boxes, step_x, send)


def taps_kernel(weight, forward, backward):
    for tap in range(27):
        far, near = tap // 3 * 128, tap % 3 * 128
        forward[far : far + 128, near : near + 128] = weight[tap]
        backward[near : near + 128, far : far + 128] = weight[26 - tap]


def own_kernel(table, bricks, taps, views, preact, store):
    slots = bricks.shape[0]
    store[0:slots] = bricks[...]
    store[slots] = jnp.zeros(store.shape[1:], BF16)
    for slot in range(slots):
        fill_views(views.at[slot], store, lookup(table, slot, 0, slots, slots))
        parts = jnp.dot(lhs_of(views.at[slot]), taps[...], preferred_element_type=F32)
        preact[slot] = join_taps(parts).reshape(EDGE, EDGE, EDGE, 128)


def forward_kernel(counts, send, factor, table, lists, own_views, own_preact, cotangent, taps, *rest):
    steps_x, steps_y = steps_here(counts)
    number_x, number_y = len(steps_x), len(steps_y)
    x_boxes, y_boxes, rest = rest[:number_x], rest[number_x : number_x + number_y], rest[number_x + number_y :]
    views, preacts, activated, grads, kept_term, sent_term = rest[:6]
    boxes_out, (store, sides) = rest[6 : 6 + number_y], rest[6 + number_y :]
    core = lax.axis_index("dp") % CORES
    slots = cotangent.shape[0]
    fill_remote(store, 0, x_boxes, y_boxes, steps_x, steps_y, send)
    nothing = jnp.zeros((EDGE, EDGE, 128), F32)
    for slot in range(slots):
        rows = slice(slot * PLANE, (slot + 1) * PLANE)
        entry = lookup(table, slot, slots, slots + 8 * send, store.shape[0] - 1)
        for side, off_x, source, target in ((0, -1, EDGE - 1, 0), (1, 1, 0, EDGE + 1)):
            plane = view_of(store, entry, off_x, source)
            sides[side, rows] = plane
            views[slot, target] = views[slot, target] + plane
        for side, off_y, base, lanes in ((2, -1, 0, 0), (3, 1, PLANE - 16, 256)):
            group = slice(PLANE - 16, PLANE) if off_y < 0 else slice(0, 16)
            edge = low_or_high(store[entry(0, off_y), :, group, :], off_y < 0)
            padded = jnp.concatenate([nothing[:1], edge, nothing[:1]], axis=0)
            for dx in range(3):
                sides[side, rows, 128 * dx : 128 * dx + 128] = (
                    padded[dx : dx + EDGE].reshape(PLANE, 128).astype(BF16)
                )
            both = [edge, nothing] if off_y < 0 else [nothing, edge]
            wide = jnp.concatenate(both, axis=1).astype(BF16)
            at = (slot, slice(1, EDGE + 1), slice(base, base + 16), slice(lanes, lanes + 128))
            views[at] = views[at] + wide
    added = []
    for side in range(4):
        if side < 2:
            part = taps[768 * side : 768 * side + 384]
        else:
            dy = 0 if side == 2 else 2
            part = jnp.concatenate(
                [taps[(3 * dx + dy) * 128 : (3 * dx + dy) * 128 + 128] for dx in range(3)], axis=0
            )
        product = join_taps(jnp.dot(sides[side], part, preferred_element_type=F32))
        added.append(product.reshape(slots, EDGE, EDGE, 128))
    for slot in range(slots):
        preacts[slot, 0] = preacts[slot, 0] + added[0][slot]
        preacts[slot, EDGE - 1] = preacts[slot, EDGE - 1] + added[1][slot]
        preacts[slot, :, 0] = preacts[slot, :, 0] + added[2][slot]
        preacts[slot, :, EDGE - 1] = preacts[slot, :, EDGE - 1] + added[3][slot]
        preact = preacts[slot].reshape(PLANE, EDGE, 128)
        sigmoid = jax.nn.sigmoid(preact)
        activated[slot] = (preact * sigmoid).reshape(EDGE, PLANE, 128).astype(BF16)
        slope = sigmoid * (1.0 + preact * (1.0 - sigmoid))
        wide = cotangent[slot].astype(F32).reshape(PLANE, EDGE, 128) * slope
        wide = jnp.where(table[slot, 13] >= 0, wide, 0.0)
        grads[slot] = wide.reshape(EDGE, PLANE, 128).astype(BF16)
    for step_y, box in zip(steps_y, boxes_out):
        pack_along_y(grads, lists, box, step_y, send)
    total = None
    for slot in range(slots):
        grad = grads[slot].astype(F32).reshape(PLANE, EDGE, 128)
        shifted = [shift_rows(grad, 1), grad, shift_rows(grad, -1)]
        rhs = jnp.concatenate([s.reshape(EDGE * PLANE, 128) for s in shifted], axis=1).astype(BF16)
        term = lax.dot_general(
            lhs_of(views.at[slot]), rhs, (((0,), (0,)), ((), ())), preferred_element_type=F32
        )
        total = term if total is None else total + term
    half = 128 // CORES
    for tap in range(27):
        far, near = tap // 3 * 128, tap % 3 * 128
        block = total[far : far + 128, near : near + 128] * factor
        first, second = block[:half], block[half:]
        kept_term[tap] = jnp.where(core == 0, first, second)
        sent_term[tap] = jnp.where(core == 0, second, first).astype(BF16)


def backward_kernel(counts, send, table, bricks, taps, *rest):
    steps_x, steps_y = steps_here(counts)
    x_boxes, y_boxes = rest[: len(steps_x)], rest[len(steps_x) : len(steps_x) + len(steps_y)]
    result, store, views = rest[-3:]
    slots = bricks.shape[0]
    store[0:slots] = bricks[...]
    fill_remote(store, slots, x_boxes, y_boxes, steps_x, steps_y, send)
    zero_at = store.shape[0] - 1
    for slot in range(slots):
        fill_views(views.at[slot], store, lookup(table, slot, 0, zero_at, zero_at))
        parts = lax.dot_general(
            lhs_of(views.at[slot]), taps[...], (((1,), (1,)), ((), ())), preferred_element_type=F32
        )
        result[slot] = join_taps(parts).reshape(EDGE, PLANE, 128).astype(BF16)


VMEM = pl.BlockSpec(memory_space=pltpu.VMEM)
SMEM = pl.BlockSpec(memory_space=pltpu.SMEM)
PARAMS = pltpu.CompilerParams(vmem_limit_bytes=VMEM_BYTES)


def xor_swap(x, axes, sizes, masks):
    pairs = []
    total = math.prod(sizes)
    for flat in range(total):
        left, where = flat, []
        for size in reversed(sizes):
            where.append(left % size)
            left //= size
        where.reverse()
        to = 0
        for size, at, mask in zip(sizes, where, masks):
            to = to * size + (at ^ mask)
        pairs.append((flat, to))
    return lax.ppermute(x, axes, pairs)


def tree_sum(terms):
    while len(terms) > 1:
        terms = [a + b for a, b in zip(terms[::2], terms[1::2])]
    return terms[0]


def own_piece(pieces, at):
    return lax.dynamic_index_in_dim(pieces, at, 1, keepdims=False)


def summed_everywhere(kept, sent):
    dp, gx, gy = (lax.axis_size(name) for name in ("dp", "gx", "gy"))
    me = lax.axis_index("dp")
    core = me % CORES
    half = kept + xor_swap(sent, ("dp",), (dp,), (1,)).astype(F32)
    chips = dp // CORES
    group = chips * gy
    mine = (me // CORES) * gy + lax.axis_index("gy")
    shares = half.reshape(half.shape[0], group, half.shape[1] // group, 128)
    masks = [(m // gy * CORES, m % gy) for m in range(group)]
    total = own_piece(shares, mine)
    for m in range(1, group):
        piece = own_piece(shares, mine ^ m).astype(BF16)
        total = total + xor_swap(piece, ("dp", "gy"), (dp, gy), masks[m]).astype(F32)
    rounded = total.astype(BF16)
    terms = [rounded] + [xor_swap(rounded, ("gx",), (gx,), (m,)) for m in range(1, gx)]
    rounded = tree_sum([term.astype(F32) for term in terms]).astype(BF16)
    parts = [rounded] + [xor_swap(rounded, ("dp", "gy"), (dp, gy), masks[m]) for m in range(1, group)]
    stacked = jnp.stack(parts, axis=1)
    order = jnp.arange(group) ^ mine
    half = jnp.take(stacked, order, axis=1).reshape(half.shape)
    other = xor_swap(half, ("dp",), (dp,), (1,))
    first = jnp.where(core == 0, half, other)
    second = jnp.where(core == 0, other, half)
    return jnp.concatenate([first, second], axis=1).astype(F32)


def run(kernel, out_shape, ins, outs, scratch=(), aliases=None, micros=1.0):
    cost = pl.CostEstimate(flops=int(micros * 1e9), bytes_accessed=2**16, transcendentals=0)
    return pl.pallas_call(
        kernel,
        out_shape=out_shape,
        in_specs=ins,
        out_specs=outs,
        scratch_shapes=list(scratch),
        input_output_aliases=aliases or {},
        compiler_params=PARAMS,
        cost_estimate=cost,
    )


def body(features, weight, cotangent, neighbours, send_slots):
    slots, _, channels = features.shape[3:]
    send = send_slots.shape[-1]
    counts = (lax.axis_size("gx"), lax.axis_size("gy"))
    devices = lax.axis_size("dp") * counts[0] * counts[1]
    bricks = features.reshape(slots, EDGE, PLANE, channels)
    cot = cotangent.reshape(slots, EDGE, PLANE, channels)
    table = neighbours.reshape(slots, 27)
    lists = send_slots.reshape(8, send)
    factor = 1.0 / math.sqrt(float(devices * slots * EDGE * PLANE))
    phases_x, phases_y = swap_phases(counts[0]), swap_phases(counts[1])
    number_x, number_y = len(phases_x), len(phases_y)
    y_type = jax.ShapeDtypeStruct((send * (PLANE + 2 * EDGE), 128), BF16)
    x_type = jax.ShapeDtypeStruct((send * (PLANE + number_y * EDGE), 128), BF16)
    bricks_type = jax.ShapeDtypeStruct(bricks.shape, BF16)
    views_type = jax.ShapeDtypeStruct((slots, EDGE + 2, PLANE, 384), BF16)
    preact_type = jax.ShapeDtypeStruct((slots, EDGE, EDGE, EDGE, 128), F32)
    half_shape = (27, channels // CORES, channels)

    def swapped(boxes, axis, phases):
        size = lax.axis_size(axis)
        return [
            lax.ppermute(box, axis, swap_pairs(size, phase)) for box, phase in zip(boxes, phases)
        ]

    def store_of(entries):
        return pltpu.VMEM((entries, EDGE, PLANE, 128), BF16)

    pack_x = run(
        functools.partial(pack_x_kernel, counts, send),
        [x_type] * number_x,
        [SMEM, VMEM] + [VMEM] * number_y,
        [VMEM] * number_x,
    )

    y_boxes = run(
        functools.partial(pack_y_kernel, counts, send), [y_type] * number_y, [SMEM, VMEM], [VMEM] * number_y
    )(lists, bricks)
    y_boxes = swapped(y_boxes, "gy", phases_y)
    taps, back_taps = run(
        taps_kernel,
        [jax.ShapeDtypeStruct((1152, 384), BF16), jax.ShapeDtypeStruct((384, 1152), BF16)],
        [VMEM],
        [VMEM, VMEM],
    )(weight.reshape(27, channels, channels))
    x_boxes = swapped(pack_x(lists, bricks, *y_boxes), "gx", phases_x)
    views, preacts = run(
        own_kernel, [views_type, preact_type], [SMEM, VMEM, VMEM], [VMEM, VMEM], [store_of(slots + 1)], micros=4.0
    )(table, bricks, taps)
    _, _, activated, grads, kept, sent, *y_boxes = run(
        functools.partial(forward_kernel, counts, send, factor),
        [
            views_type,
            preact_type,
            bricks_type,
            bricks_type,
            jax.ShapeDtypeStruct(half_shape, F32),
            jax.ShapeDtypeStruct(half_shape, BF16),
        ]
        + [y_type] * number_y,
        [SMEM, SMEM] + [VMEM] * (4 + number_x + number_y),
        [VMEM] * (6 + number_y),
        [store_of(8 * send + 1), pltpu.VMEM((4, slots * PLANE, 384), BF16)],
        aliases={2: 0, 3: 1},
        micros=5.0,
    )(table, lists, views, preacts, cot, taps, *x_boxes, *y_boxes)
    y_boxes = swapped(y_boxes, "gy", phases_y)
    x_boxes = swapped(pack_x(lists, grads, *y_boxes), "gx", phases_x)
    input_grad = run(
        functools.partial(backward_kernel, counts, send),
        bricks_type,
        [SMEM, VMEM, VMEM] + [VMEM] * (number_x + number_y),
        VMEM,
        [store_of(slots + 8 * send + 1), pltpu.VMEM(views_type.shape, BF16)],
        micros=5.0,
    )(table, grads, back_taps, *x_boxes, *y_boxes)
    weight_grad = summed_everywhere(kept, sent)
    return (
        activated.reshape(features.shape),
        input_grad.reshape(features.shape),
        weight_grad.reshape(weight.shape),
    )


def solution(mesh):
    split = P("dp", "gx", "gy", None, None, None)
    table = P("dp", "gx", "gy", None, None)
    return jax.shard_map(
        body,
        mesh=mesh,
        in_specs=(split, P(), split, table, table),
        out_specs=(split, split, P()),
        check_vma=False,
    )
```

time: 76.6 us -> 59.2 us (0.77)
  the two profiles are of different devices: /device:TPU:16 before, /device:TPU:0 now
where the time goes in v2:
time: 59.2 us; the launch traced here: 58.7 us
  starting transfers between devices  21.3 us (36%)
  waiting for transfers between devices  17.6 us (30%)
  Pallas kernels  14.2 us (24%)
  local copies, waits for them, and re-layouts  2.77 us (5%)
  other arithmetic  2 us (3%)
  between operations  0.91 us (2%)
    ppermute x11, waiting for transfers between devices, xor_swap(): return lax.ppermute(x, axes, pairs)  15.9 us
    ppermute x11, starting transfers between devices, xor_swap(): return lax.ppermute(x, axes, pairs)  13.2 us
    ppermute x6, starting transfers between devices, swapped(): lax.ppermute(box, axis, swap_pairs(size, phase))  8.08 us
    pallas_call x1, Pallas kernels, body(): run(functools.partial(forward_kernel, counts, send, factor), [views_type,...  4.4 us
    pallas_call x1, Pallas kernels, body(): run(functools.partial(backward_kernel, counts, send), bricks_type, [SMEM,...  4.19 us
    pallas_call x1, Pallas kernels, body(): run(own_kernel, [views_type, preact_type], [SMEM, VMEM, VMEM], [VMEM, VME...  3.37 us
    ppermute x6, waiting for transfers between devices, swapped(): lax.ppermute(box, axis, swap_pairs(size, phase))  1.68 us
    convert_element_type x1, other arithmetic, summed_everywhere(): return jnp.concatenate([first, second], axis=1).astype(F32)  1.38 us
  transfers between devices with their start and end apart: 17, of which 8 were waited for; matrix products, arithmetic and copies ran while one was open for 2% of the time, Pallas kernels for 14%

profile of v2, /device:TPU:0, one launch (start us, length us, event | category | flops | bytes accessed | tf_op | source)
XLA Modules:
  0.0 58.7 jit_solution(17122867991467438917)
XLA Ops:
  0.6 0.8 %copy.24.lists = s32[8,2]{1,0:T(8,128)S(1)} copy(s32[8,2]{0,1:T(2,128)} %bitcast.69) | data formatting | bytes 128 | tf_op jit(solution)/shard_map/reshape | solution.py:359
  1.4 1.0 %copy-done.1 = bf16[1,1,1,4,512,128]{5,4,3,2,1,0:T(8,128)(2,1)S(1)} copy-done((bf16[1,1,1,4,512,128]{5,4,3,2,1,0:T(8,128)(2,1)S(1)}, bf16[1,1,1,4,512,128]{5,4,3,2,1,0:T(8,128)(2,1)}, u32[]{:S(2)}) %copy-start.1) | copy-done | bytes 524312
  3.1 3.0 %collective-permute-start = (bf16[160,128]{1,0:T(8,128)(2,1)S(1)}, bf16[160,128]{1,0:T(8,128)(2,1)S(1)}, u32[]{:S(2)}, u32[]{:S(2)}) collective-permute-start(bf16[160,128]{1,0:T(8,128)(2,1)S(1)} %shard_map.78), channel_id=1, source_target_pairs={{0,1},{1,0},{2,3},{3,2},{4,5},{5,4},{6,7},{7,6},{8,9},{9,8},{10,11... | collective-permute-start | bytes 122888 | tf_op jit(solution)/shard_map/ppermute | solution.py:373
  6.4 1.7 %collective-permute-done.rest_0_.rest_2_ = bf16[160,128]{1,0:T(8,128)(2,1)S(1)} collective-permute-done((bf16[160,128]{1,0:T(8,128)(2,1)S(1)}, bf16[160,128]{1,0:T(8,128)(2,1)S(1)}, u32[]{:S(2)}, u32[]{:S(2)}) %collective-permute-start) | collective-permute-done | bytes 40992 | tf_op jit(solution)/shard_map/ppermute | solution.py:373
  8.7 2.1 %collective-permute-start.1 = (bf16[144,128]{1,0:T(8,128)(2,1)S(1)}, bf16[144,128]{1,0:T(8,128)(2,1)S(1)}, u32[]{:S(2)}, u32[]{:S(2)}) collective-permute-start(bf16[144,128]{1,0:T(8,128)(2,1)S(1)} %get-tuple-element.19), channel_id=1, source_target_pairs={{0,2},{2,0},{4,6},{6,4},{1,3},{3,1},{5,7},{7,5},{8,10},{10,8},{12,... | collective-permute-start | bytes 110600 | tf_op jit(solution)/shard_map/ppermute | solution.py:373
  10.9 0.7 %collective-permute-start.2 = (bf16[144,128]{1,0:T(8,128)(2,1)S(1)}, bf16[144,128]{1,0:T(8,128)(2,1)S(1)}, u32[]{:S(2)}, u32[]{:S(2)}) collective-permute-start(bf16[144,128]{1,0:T(8,128)(2,1)S(1)} %get-tuple-element.20), channel_id=1, source_target_pairs={{2,4},{4,2},{3,5},{5,3},{10,12},{12,10},{11,13},{13,11},{18,20},{2... | collective-permute-start | bytes 110600 | tf_op jit(solution)/shard_map/ppermute | solution.py:373
  11.6 3.4 %shard_map.77 = (bf16[4,10,64,384]{3,2,1,0:T(8,128)(2,1)S(1)}, f32[4,8,8,8,128]{4,3,2,1,0:T(8,128)S(1)}) custom-call(s32[4,27]{1,0:T(4,128)S(1)} %bitcast.59, bf16[4,8,64,128]{3,2,1,0:T(8,128)(2,1)S(1)} %bitcast.57, bf16[1152,384]{1,0:T(8,128)(2,1)S(1)} %get-tuple-element.16.taps), custom_call_target="tpu_custom_call" | custom-call | flops 4000000000 | bytes 65536 | tf_op jit(solution)/shard_map/pallas_call | solution.py:397
  15.0 4.4 %shard_map.80 = (bf16[4,10,64,384]{3,2,1,0:T(8,128)(2,1)S(1)}, f32[4,8,8,8,128]{4,3,2,1,0:T(8,128)S(1)}, bf16[4,8,64,128]{3,2,1,0:T(8,128)(2,1)}, bf16[4,8,64,12...) custom-call(s32[4,27]{1,0:T(4,128)S(1)} %bitcast.60, ...), custom_call_target="tpu_custom_call", output_to_operand_aliasing={{0}: (2, {}), {1}: (3, {})} | custom-call | flops 5000000000 | bytes 65536 | tf_op jit(solution)/shard_map/pallas_call | solution.py:400
  19.5 1.7 %collective-permute-done.6 = bf16[27,64,128]{2,1,0:T(8,128)(2,1)S(1)} collective-permute-done((bf16[27,64,128]{2,1,0:T(8,128)(2,1)S(1)}, bf16[27,64,128]{2,1,0:T(8,128)(2,1)S(1)}, u32[]{:S(2)}, u32[]{:S(2)}) %collective-permute-start.6) | collective-permute-done | bytes 442400 | tf_op jit(solution)/shard_map/ppermute | solution.py:297
  21.4 2.5 %collective-permute-start.9 = (bf16[27,16,128]{2,1,0:T(8,128)(2,1)S(1)}, bf16[27,16,128]{2,1,0:T(8,128)(2,1)S(1)}, u32[]{:S(2)}, u32[]{:S(2)}) collective-permute-start(bf16[27,16,128]{2,1,0:T(8,128)(2,1)S(1)} %get-tuple-element.33), channel_id=1, source_target_pairs={{0,17},{1,16},{8,25},{9,24},{16,1},{17,0},{24,9},{25,8},{2,19},{3,... | collective-permute-start | bytes 331784 | tf_op jit(solution)/shard_map/ppermute | solution.py:297
  25.0 3.3 %collective-permute-done.9 = bf16[27,16,128]{2,1,0:T(8,128)(2,1)S(1)} collective-permute-done((bf16[27,16,128]{2,1,0:T(8,128)(2,1)S(1)}, bf16[27,16,128]{2,1,0:T(8,128)(2,1)S(1)}, u32[]{:S(2)}, u32[]{:S(2)}) %collective-permute-start.9) | collective-permute-done | bytes 110624 | tf_op jit(solution)/shard_map/ppermute | solution.py:297
  28.3 1.6 %collective-permute-done.8 = bf16[27,16,128]{2,1,0:T(8,128)(2,1)S(1)} collective-permute-done((bf16[27,16,128]{2,1,0:T(8,128)(2,1)S(1)}, bf16[27,16,128]{2,1,0:T(8,128)(2,1)S(1)}, u32[]{:S(2)}, u32[]{:S(2)}) %collective-permute-start.8) | collective-permute-done | bytes 110624 | tf_op jit(solution)/shard_map/ppermute | solution.py:297
  30.0 2.5 %collective-permute-start.12 = (bf16[27,16,128]{2,1,0:T(8,128)(2,1)S(1)}, bf16[27,16,128]{2,1,0:T(8,128)(2,1)S(1)}, u32[]{:S(2)}, u32[]{:S(2)}) collective-permute-start(bf16[27,16,128]{2,1,0:T(8,128)(2,1)S(1)} %fusion.2), channel_id=1, source_target_pairs={{0,6},{2,4},{4,2},{6,0},{1,7},{3,5},{5,3},{7,1},{8,14},{10,12},{12... | collective-permute-start | bytes 331784 | tf_op jit(solution)/shard_map/ppermute | solution.py:297
  32.6 3.4 %collective-permute-start.11 = (bf16[27,16,128]{2,1,0:T(8,128)(2,1)S(1)}, bf16[27,16,128]{2,1,0:T(8,128)(2,1)S(1)}, u32[]{:S(2)}, u32[]{:S(2)}) collective-permute-start(bf16[27,16,128]{2,1,0:T(8,128)(2,1)S(1)} %fusion.2), channel_id=1, source_target_pairs={{0,4},{2,6},{4,0},{6,2},{1,5},{3,7},{5,1},{7,3},{8,12},{10,14},{12... | collective-permute-start | bytes 331784 | tf_op jit(solution)/shard_map/ppermute | solution.py:297
  36.0 1.5 %collective-permute-start.3 = (bf16[160,128]{1,0:T(8,128)(2,1)S(1)}, bf16[160,128]{1,0:T(8,128)(2,1)S(1)}, u32[]{:S(2)}, u32[]{:S(2)}) collective-permute-start(bf16[160,128]{1,0:T(8,128)(2,1)S(1)} %get-tuple-element.24), channel_id=1, source_target_pairs={{0,1},{1,0},{2,3},{3,2},{4,5},{5,4},{6,7},{7,6},{8,9},{9,8},{10,11... | collective-permute-start | bytes 122888 | tf_op jit(solution)/shard_map/ppermute | solution.py:373
  37.5 6.3 %collective-permute-done.11 = bf16[27,16,128]{2,1,0:T(8,128)(2,1)S(1)} collective-permute-done((bf16[27,16,128]{2,1,0:T(8,128)(2,1)S(1)}, bf16[27,16,128]{2,1,0:T(8,128)(2,1)S(1)}, u32[]{:S(2)}, u32[]{:S(2)}) %collective-permute-start.11) | collective-permute-done | bytes 110624 | tf_op jit(solution)/shard_map/ppermute | solution.py:297
  43.8 2.6 %collective-permute-start.15 = (bf16[27,16,128]{2,1,0:T(8,128)(2,1)S(1)}, bf16[27,16,128]{2,1,0:T(8,128)(2,1)S(1)}, u32[]{:S(2)}, u32[]{:S(2)}) collective-permute-start(bf16[27,16,128]{2,1,0:T(8,128)(2,1)S(1)} %add_convert_fusion), channel_id=1, source_target_pairs={{0,17},{1,16},{8,25},{9,24},{16,1},{17,0},{24,9},{25,8},{2,19},{3,... | collective-permute-start | bytes 331784 | tf_op jit(solution)/shard_map/ppermute | solution.py:297
  47.5 0.7 %shard_map.81 = (bf16[144,128]{1,0:T(8,128)(2,1)S(1)}, bf16[144,128]{1,0:T(8,128)(2,1)S(1)}) custom-call(s32[8,2]{1,0:T(8,128)S(1)} %copy.24.lists, bf16[4,8,64,128]{3,2,1,0:T(8,128)(2,1)S(1)} %get-tuple-element.22.bricks, bf16[160,128]{1,0:T(8,128)(2,1)S(1)} %collective-permute-done.3.rest_0_.rest_2_), custom_call_target="tpu_custom_call" | custom-call | flops 1000000000 | bytes 65536 | tf_op jit(solution)/shard_map/pallas_call | solution.py:418
  48.3 0.7 %collective-permute-start.5 = (bf16[144,128]{1,0:T(8,128)(2,1)S(1)}, bf16[144,128]{1,0:T(8,128)(2,1)S(1)}, u32[]{:S(2)}, u32[]{:S(2)}) collective-permute-start(bf16[144,128]{1,0:T(8,128)(2,1)S(1)} %get-tuple-element.26), channel_id=1, source_target_pairs={{2,4},{4,2},{3,5},{5,3},{10,12},{12,10},{11,13},{13,11},{18,20},{2... | collective-permute-start | bytes 110600 | tf_op jit(solution)/shard_map/ppermute | solution.py:373
  49.0 1.8 %collective-permute-done.15 = bf16[27,16,128]{2,1,0:T(8,128)(2,1)S(1)} collective-permute-done((bf16[27,16,128]{2,1,0:T(8,128)(2,1)S(1)}, bf16[27,16,128]{2,1,0:T(8,128)(2,1)S(1)}, u32[]{:S(2)}, u32[]{:S(2)}) %collective-permute-start.15) | collective-permute-done | bytes 110624 | tf_op jit(solution)/shard_map/ppermute | solution.py:297
  50.7 1.0 %collective-permute-done.14 = bf16[27,16,128]{2,1,0:T(8,128)(2,1)S(1)} collective-permute-done((bf16[27,16,128]{2,1,0:T(8,128)(2,1)S(1)}, bf16[27,16,128]{2,1,0:T(8,128)(2,1)S(1)}, u32[]{:S(2)}, u32[]{:S(2)}) %collective-permute-start.14) | collective-permute-done | bytes 110624 | tf_op jit(solution)/shard_map/ppermute | solution.py:297
  52.0 0.7 %gather_fusion = bf16[4,27,16,128]{3,2,1,0:T(8,128)(2,1)S(1)} fusion(bf16[27,4,16,128]{3,2,1,0:T(8,128)(2,1)S(1)} %pad_maximum_fusion.1, s32[1024]{0:T(1024)S(1)} %pad_clamp_fusion), kind=kCustom, calls=%fused_computation | custom fusion | bytes 884752 | tf_op jit(solution)/shard_map/jit(_take)/gather | solution.py:330
  52.9 4.2 %shard_map.82 = bf16[4,8,64,128]{3,2,1,0:T(8,128)(2,1)} custom-call(s32[4,27]{1,0:T(4,128)S(1)} %bitcast.61, bf16[4,8,64,128]{3,2,1,0:T(8,128)(2,1)S(1)} %get-tuple-element.22.bricks, bf16[384,1152]{1,0:T(8,128)(2,1)S(1)} %get-tuple-element.23.taps, bf16[144,128]{1,0:T(8,128)(2,1)S(1)} %collective-permute-done.4.rest_0_, ...), custom_call_target="tpu_custom_call" | custom-call | flops 5000000000 | bytes 65536 | tf_op jit(solution)/shard_map/pallas_call | solution.py:419
  57.3 1.4 %bitcast_convert_fusion = f32[3456,128]{1,0:T(8,128)} fusion(bf16[27,128,128]{2,1,0:T(8,128)(2,1)S(1)} %pad_maximum_fusion), kind=kLoop, calls=%fused_computation.2 | loop fusion | flops 442368 | bytes 2654208 | tf_op jit(solution)/shard_map/convert_element_type | solution.py:334
  (44 shorter events, 5.0 us)
Async XLA Ops:
  1.4 1.0 %copy-start.1 = (bf16[1,1,1,4,512,128]{5,4,3,2,1,0:T(8,128)(2,1)S(1)}, bf16[1,1,1,4,512,128]{5,4,3,2,1,0:T(8,128)(2,1)}, u32[]{:S(2)}) copy-start(bf16[1,1,1,4,512,128]{5,4,3,2,1,0:T(8,128)(2,1)} %param.5) | copy-start | bytes 1572868
  2.4 3.7 %copy-start = (bf16[3456,128]{1,0:T(8,128)(2,1)S(1)}, bf16[3456,128]{1,0:T(8,128)(2,1)}, u32[]{:S(2)}) copy-start(bf16[3456,128]{1,0:T(8,128)(2,1)} %param.6) | copy-start | bytes 2654212
  3.1 5.0 %collective-permute-start = (bf16[160,128]{1,0:T(8,128)(2,1)S(1)}, bf16[160,128]{1,0:T(8,128)(2,1)S(1)}, u32[]{:S(2)}, u32[]{:S(2)}) collective-permute-start(bf16[160,128]{1,0:T(8,128)(2,1)S(1)} %shard_map.78), channel_id=1, source_target_pairs={{0,1},{1,0},{2,3},{3,2},{4,5},{5,4},{6,7},{7,6},{8,9},{9,8},{10,11... | collective-permute-start | bytes 122888 | tf_op jit(solution)/shard_map/ppermute | solution.py:373
  6.4 5.2 %copy-start.2 = (bf16[1,1,1,4,512,128]{5,4,3,2,1,0:T(8,128)(2,1)S(1)}, bf16[1,1,1,4,512,128]{5,4,3,2,1,0:T(8,128)(2,1)}, u32[]{:S(2)}) copy-start(bf16[1,1,1,4,512,128]{5,4,3,2,1,0:T(8,128)(2,1)} %param.5) | copy-start | bytes 1572868
  6.4 5.2 %copy-start.4 = (s32[1,1,1,4,27]{4,3,2,1,0:T(4,128)S(1)}, s32[1,1,1,4,27]{4,3,2,1,0:T(4,128)}, u32[]{:S(2)}) copy-start(s32[1,1,1,4,27]{4,3,2,1,0:T(4,128)} %param.8) | copy-start | bytes 1300
  8.7 6.2 %collective-permute-start.1 = (bf16[144,128]{1,0:T(8,128)(2,1)S(1)}, bf16[144,128]{1,0:T(8,128)(2,1)S(1)}, u32[]{:S(2)}, u32[]{:S(2)}) collective-permute-start(bf16[144,128]{1,0:T(8,128)(2,1)S(1)} %get-tuple-element.19), channel_id=1, source_target_pairs={{0,2},{2,0},{4,6},{6,4},{1,3},{3,1},{5,7},{7,5},{8,10},{10,8},{12,... | collective-permute-start | bytes 110600 | tf_op jit(solution)/shard_map/ppermute | solution.py:373
  10.9 4.1 %collective-permute-start.2 = (bf16[144,128]{1,0:T(8,128)(2,1)S(1)}, bf16[144,128]{1,0:T(8,128)(2,1)S(1)}, u32[]{:S(2)}, u32[]{:S(2)}) collective-permute-start(bf16[144,128]{1,0:T(8,128)(2,1)S(1)} %get-tuple-element.20), channel_id=1, source_target_pairs={{2,4},{4,2},{3,5},{5,3},{10,12},{12,10},{11,13},{13,11},{18,20},{2... | collective-permute-start | bytes 110600 | tf_op jit(solution)/shard_map/ppermute | solution.py:373
  11.6 3.4 %copy-start.3 = (bf16[1,1,1,4,512,128]{5,4,3,2,1,0:T(8,128)(2,1)S(1)}, bf16[1,1,1,4,512,128]{5,4,3,2,1,0:T(8,128)(2,1)}, u32[]{:S(2)}) copy-start(bf16[1,1,1,4,512,128]{5,4,3,2,1,0:T(8,128)(2,1)} %param.7) | copy-start | bytes 1572868
  19.4 1.9 %collective-permute-start.6 = (bf16[27,64,128]{2,1,0:T(8,128)(2,1)S(1)}, bf16[27,64,128]{2,1,0:T(8,128)(2,1)S(1)}, u32[]{:S(2)}, u32[]{:S(2)}) collective-permute-start(bf16[27,64,128]{2,1,0:T(8,128)(2,1)S(1)} %get-tuple-element.28), channel_id=1, source_target_pairs={{0,8},{8,0},{16,24},{24,16},{1,9},{9,1},{17,25},{25,17},{2,10},{10... | collective-permute-start | bytes 1327112 | tf_op jit(solution)/shard_map/ppermute | solution.py:297
  21.4 6.9 %collective-permute-start.9 = (bf16[27,16,128]{2,1,0:T(8,128)(2,1)S(1)}, bf16[27,16,128]{2,1,0:T(8,128)(2,1)S(1)}, u32[]{:S(2)}, u32[]{:S(2)}) collective-permute-start(bf16[27,16,128]{2,1,0:T(8,128)(2,1)S(1)} %get-tuple-element.33), channel_id=1, source_target_pairs={{0,17},{1,16},{8,25},{9,24},{16,1},{17,0},{24,9},{25,8},{2,19},{3,... | collective-permute-start | bytes 331784 | tf_op jit(solution)/shard_map/ppermute | solution.py:297
  24.0 6.0 %collective-permute-start.8 = (bf16[27,16,128]{2,1,0:T(8,128)(2,1)S(1)}, bf16[27,16,128]{2,1,0:T(8,128)(2,1)S(1)}, u32[]{:S(2)}, u32[]{:S(2)}) collective-permute-start(bf16[27,16,128]{2,1,0:T(8,128)(2,1)S(1)} %get-tuple-element.32), channel_id=1, source_target_pairs={{0,16},{1,17},{8,24},{9,25},{16,0},{17,1},{24,8},{25,9},{2,18},{3,... | collective-permute-start | bytes 331784 | tf_op jit(solution)/shard_map/ppermute | solution.py:297
  24.5 5.4 %collective-permute-start.7 = (bf16[27,16,128]{2,1,0:T(8,128)(2,1)S(1)}, bf16[27,16,128]{2,1,0:T(8,128)(2,1)S(1)}, u32[]{:S(2)}, u32[]{:S(2)}) collective-permute-start(bf16[27,16,128]{2,1,0:T(8,128)(2,1)S(1)} %get-tuple-element.31), channel_id=1, source_target_pairs={{0,1},{1,0},{8,9},{9,8},{16,17},{17,16},{24,25},{25,24},{2,3},{3,2... | collective-permute-start | bytes 331784 | tf_op jit(solution)/shard_map/ppermute | solution.py:297
  30.0 7.5 %collective-permute-start.12 = (bf16[27,16,128]{2,1,0:T(8,128)(2,1)S(1)}, bf16[27,16,128]{2,1,0:T(8,128)(2,1)S(1)}, u32[]{:S(2)}, u32[]{:S(2)}) collective-permute-start(bf16[27,16,128]{2,1,0:T(8,128)(2,1)S(1)} %fusion.2), channel_id=1, source_target_pairs={{0,6},{2,4},{4,2},{6,0},{1,7},{3,5},{5,3},{7,1},{8,14},{10,12},{12... | collective-permute-start | bytes 331784 | tf_op jit(solution)/shard_map/ppermute | solution.py:297
  32.6 11.2 %collective-permute-start.11 = (bf16[27,16,128]{2,1,0:T(8,128)(2,1)S(1)}, bf16[27,16,128]{2,1,0:T(8,128)(2,1)S(1)}, u32[]{:S(2)}, u32[]{:S(2)}) collective-permute-start(bf16[27,16,128]{2,1,0:T(8,128)(2,1)S(1)} %fusion.2), channel_id=1, source_target_pairs={{0,4},{2,6},{4,0},{6,2},{1,5},{3,7},{5,1},{7,3},{8,12},{10,14},{12... | collective-permute-start | bytes 331784 | tf_op jit(solution)/shard_map/ppermute | solution.py:297
  35.9 7.8 %collective-permute-start.10 = (bf16[27,16,128]{2,1,0:T(8,128)(2,1)S(1)}, bf16[27,16,128]{2,1,0:T(8,128)(2,1)S(1)}, u32[]{:S(2)}, u32[]{:S(2)}) collective-permute-start(bf16[27,16,128]{2,1,0:T(8,128)(2,1)S(1)} %fusion.2), channel_id=1, source_target_pairs={{0,2},{2,0},{4,6},{6,4},{1,3},{3,1},{5,7},{7,5},{8,10},{10,8},{12,... | collective-permute-start | bytes 331784 | tf_op jit(solution)/shard_map/ppermute | solution.py:297
  36.0 11.6 %collective-permute-start.3 = (bf16[160,128]{1,0:T(8,128)(2,1)S(1)}, bf16[160,128]{1,0:T(8,128)(2,1)S(1)}, u32[]{:S(2)}, u32[]{:S(2)}) collective-permute-start(bf16[160,128]{1,0:T(8,128)(2,1)S(1)} %get-tuple-element.24), channel_id=1, source_target_pairs={{0,1},{1,0},{2,3},{3,2},{4,5},{5,4},{6,7},{7,6},{8,9},{9,8},{10,11... | collective-permute-start | bytes 122888 | tf_op jit(solution)/shard_map/ppermute | solution.py:373
  43.8 6.9 %collective-permute-start.15 = (bf16[27,16,128]{2,1,0:T(8,128)(2,1)S(1)}, bf16[27,16,128]{2,1,0:T(8,128)(2,1)S(1)}, u32[]{:S(2)}, u32[]{:S(2)}) collective-permute-start(bf16[27,16,128]{2,1,0:T(8,128)(2,1)S(1)} %add_convert_fusion), channel_id=1, source_target_pairs={{0,17},{1,16},{8,25},{9,24},{16,1},{17,0},{24,9},{25,8},{2,19},{3,... | collective-permute-start | bytes 331784 | tf_op jit(solution)/shard_map/ppermute | solution.py:297
  46.4 5.3 %collective-permute-start.14 = (bf16[27,16,128]{2,1,0:T(8,128)(2,1)S(1)}, bf16[27,16,128]{2,1,0:T(8,128)(2,1)S(1)}, u32[]{:S(2)}, u32[]{:S(2)}) collective-permute-start(bf16[27,16,128]{2,1,0:T(8,128)(2,1)S(1)} %add_convert_fusion), channel_id=1, source_target_pairs={{0,16},{1,17},{8,24},{9,25},{16,0},{17,1},{24,8},{25,9},{2,18},{3,... | collective-permute-start | bytes 331784 | tf_op jit(solution)/shard_map/ppermute | solution.py:297
  47.0 5.0 %collective-permute-start.13 = (bf16[27,16,128]{2,1,0:T(8,128)(2,1)S(1)}, bf16[27,16,128]{2,1,0:T(8,128)(2,1)S(1)}, u32[]{:S(2)}, u32[]{:S(2)}) collective-permute-start(bf16[27,16,128]{2,1,0:T(8,128)(2,1)S(1)} %add_convert_fusion), channel_id=1, source_target_pairs={{0,1},{1,0},{8,9},{9,8},{16,17},{17,16},{24,25},{25,24},{2,3},{3,2... | collective-permute-start | bytes 331784 | tf_op jit(solution)/shard_map/ppermute | solution.py:297
  48.2 4.7 %collective-permute-start.4 = (bf16[144,128]{1,0:T(8,128)(2,1)S(1)}, bf16[144,128]{1,0:T(8,128)(2,1)S(1)}, u32[]{:S(2)}, u32[]{:S(2)}) collective-permute-start(bf16[144,128]{1,0:T(8,128)(2,1)S(1)} %get-tuple-element.25), channel_id=1, source_target_pairs={{0,2},{2,0},{4,6},{6,4},{1,3},{3,1},{5,7},{7,5},{8,10},{10,8},{12,... | collective-permute-start | bytes 110600 | tf_op jit(solution)/shard_map/ppermute | solution.py:373
  48.3 4.6 %collective-permute-start.5 = (bf16[144,128]{1,0:T(8,128)(2,1)S(1)}, bf16[144,128]{1,0:T(8,128)(2,1)S(1)}, u32[]{:S(2)}, u32[]{:S(2)}) collective-permute-start(bf16[144,128]{1,0:T(8,128)(2,1)S(1)} %get-tuple-element.26), channel_id=1, source_target_pairs={{2,4},{4,2},{3,5},{5,3},{10,12},{12,10},{11,13},{13,11},{18,20},{2... | collective-permute-start | bytes 110600 | tf_op jit(solution)/shard_map/ppermute | solution.py:373
  52.8 4.3 %collective-permute-start.16 = (bf16[27,64,128]{2,1,0:T(8,128)(2,1)S(1)}, bf16[27,64,128]{2,1,0:T(8,128)(2,1)S(1)}, u32[]{:S(2)}, u32[]{:S(2)}) collective-permute-start(bf16[27,64,128]{2,1,0:T(8,128)(2,1)S(1)} %bitcast_select_fusion), channel_id=1, source_target_pairs={{0,8},{8,0},{16,24},{24,16},{1,9},{9,1},{17,25},{25,17},{2,10},{10... | collective-permute-start | bytes 1327112 | tf_op jit(solution)/shard_map/ppermute | solution.py:297

commit v3 on v2

--- a/solution.py
+++ b/solution.py
@@ -51,7 +51,7 @@
 def pack_along_y(bricks, lists, box, step_y, send):
     number = direction(0, step_y)
     for entry in range(send):
-        listed = lists[number, entry]
+        listed = lists[entry, number]
         face = y_edge(bricks, jnp.maximum(listed, 0), slice(0, EDGE), step_y)
         face = jnp.where(listed >= 0, face, 0.0).reshape(PLANE, 128)
         box[entry * PLANE : (entry + 1) * PLANE] = face.astype(BF16)
@@ -60,7 +60,7 @@
         number = direction(step_x, step_y)
         pieces = []
         for entry in range(send):
-            listed = lists[number, entry]
+            listed = lists[entry, number]
             plane = EDGE - 1 if step_x > 0 else 0
             edge = y_edge(bricks, jnp.maximum(listed, 0), plane, step_y)
             pieces.append(jnp.where(listed >= 0, edge, 0.0))
@@ -71,7 +71,7 @@
 def pack_along_x(bricks, lists, box, y_boxes, step_x, send):
     number = direction(step_x, 0)
     for entry in range(send):
-        listed = lists[number, entry]
+        listed = lists[entry, number]
         face = bricks[jnp.maximum(listed, 0), jnp.where(step_x > 0, EDGE - 1, 0)]
         box[entry * PLANE : (entry + 1) * PLANE] = jnp.where(listed >= 0, face, jnp.zeros_like(face))
     at = send * PLANE
@@ -171,19 +171,20 @@
         pack_along_x(bricks, lists, box, y_boxes, step_x, send)
 
 
-def taps_kernel(weight, forward, backward):
+def layout_kernel(table, bricks, weight, forward, backward, views, store):
+    slots = bricks.shape[0]
     for tap in range(27):
         far, near = tap // 3 * 128, tap % 3 * 128
         forward[far : far + 128, near : near + 128] = weight[tap]
         backward[near : near + 128, far : far + 128] = weight[26 - tap]
-
-
-def own_kernel(table, bricks, taps, views, preact, store):
-    slots = bricks.shape[0]
     store[0:slots] = bricks[...]
     store[slots] = jnp.zeros(store.shape[1:], BF16)
     for slot in range(slots):
         fill_views(views.at[slot], store, lookup(table, slot, 0, slots, slots))
+
+
+def own_kernel(views, taps, preact):
+    for slot in range(views.shape[0]):
         parts = jnp.dot(lhs_of(views.at[slot]), taps[...], preferred_element_type=F32)
         preact[slot] = join_taps(parts).reshape(EDGE, EDGE, EDGE, 128)
 
@@ -256,14 +257,18 @@
         far, near = tap // 3 * 128, tap % 3 * 128
         block = total[far : far + 128, near : near + 128] * factor
         first, second = block[:half], block[half:]
-        kept_term[tap] = jnp.where(core == 0, first, second)
-        sent_term[tap] = jnp.where(core == 0, second, first).astype(BF16)
+        rows = slice(tap * half, (tap + 1) * half)
+        kept_term[rows] = jnp.where(core == 0, first, second)
+        sent_term[rows] = jnp.where(core == 0, second, first).astype(BF16)
+    for term in (kept_term, sent_term):
+        if term.shape[0] > 27 * half:
+            term[27 * half :] = jnp.zeros((term.shape[0] - 27 * half, 128), term.dtype)
 
 
 def backward_kernel(counts, send, table, bricks, taps, *rest):
     steps_x, steps_y = steps_here(counts)
     x_boxes, y_boxes = rest[: len(steps_x)], rest[len(steps_x) : len(steps_x) + len(steps_y)]
-    result, store, views = rest[-3:]
+    result, ready, store, views = rest[-4:]
     slots = bricks.shape[0]
     store[0:slots] = bricks[...]
     fill_remote(store, slots, x_boxes, y_boxes, steps_x, steps_y, send)
@@ -274,64 +279,13 @@
             lhs_of(views.at[slot]), taps[...], (((1,), (1,)), ((), ())), preferred_element_type=F32
         )
         result[slot] = join_taps(parts).reshape(EDGE, PLANE, 128).astype(BF16)
+    ready[...] = jnp.zeros(ready.shape, F32)
 
 
 VMEM = pl.BlockSpec(memory_space=pltpu.VMEM)
 SMEM = pl.BlockSpec(memory_space=pltpu.SMEM)
+ANY = pl.BlockSpec(memory_space=pl.ANY)
 PARAMS = pltpu.CompilerParams(vmem_limit_bytes=VMEM_BYTES)
-
-
-def xor_swap(x, axes, sizes, masks):
-    pairs = []
-    total = math.prod(sizes)
-    for flat in range(total):
-        left, where = flat, []
-        for size in reversed(sizes):
-            where.append(left % size)
-            left //= size
-        where.reverse()
-        to = 0
-        for size, at, mask in zip(sizes, where, masks):
-            to = to * size + (at ^ mask)
-        pairs.append((flat, to))
-    return lax.ppermute(x, axes, pairs)
-
-
-def tree_sum(terms):
-    while len(terms) > 1:
-        terms = [a + b for a, b in zip(terms[::2], terms[1::2])]
-    return terms[0]
-
-
-def own_piece(pieces, at):
-    return lax.dynamic_index_in_dim(pieces, at, 1, keepdims=False)
-
-
-def summed_everywhere(kept, sent):
-    dp, gx, gy = (lax.axis_size(name) for name in ("dp", "gx", "gy"))
-    me = lax.axis_index("dp")
-    core = me % CORES
-    half = kept + xor_swap(sent, ("dp",), (dp,), (1,)).astype(F32)
-    chips = dp // CORES
-    group = chips * gy
-    mine = (me // CORES) * gy + lax.axis_index("gy")
-    shares = half.reshape(half.shape[0], group, half.shape[1] // group, 128)
-    masks = [(m // gy * CORES, m % gy) for m in range(group)]
-    total = own_piece(shares, mine)
-    for m in range(1, group):
-        piece = own_piece(shares, mine ^ m).astype(BF16)
-        total = total + xor_swap(piece, ("dp", "gy"), (dp, gy), masks[m]).astype(F32)
-    rounded = total.astype(BF16)
-    terms = [rounded] + [xor_swap(rounded, ("gx",), (gx,), (m,)) for m in range(1, gx)]
-    rounded = tree_sum([term.astype(F32) for term in terms]).astype(BF16)
-    parts = [rounded] + [xor_swap(rounded, ("dp", "gy"), (dp, gy), masks[m]) for m in range(1, group)]
-    stacked = jnp.stack(parts, axis=1)
-    order = jnp.arange(group) ^ mine
-    half = jnp.take(stacked, order, axis=1).reshape(half.shape)
-    other = xor_swap(half, ("dp",), (dp,), (1,))
-    first = jnp.where(core == 0, half, other)
-    second = jnp.where(core == 0, other, half)
-    return jnp.concatenate([first, second], axis=1).astype(F32)
 
 
 def run(kernel, out_shape, ins, outs, scratch=(), aliases=None, micros=1.0):
@@ -348,6 +302,113 @@
     )
 
 
+class Groups:
+    def __init__(self):
+        self.sizes = tuple(lax.axis_size(name) for name in ("dp", "gx", "gy"))
+        dp, gx, gy = self.sizes
+        self.plane, self.line = dp // CORES * gy, gx
+        self.turned = self.plane == self.line
+        at = lax.axis_index("dp")
+        in_plane = at // CORES * gy + lax.axis_index("gy")
+        self.core = at % CORES
+        if self.turned:
+            first = jnp.where(self.core == 0, in_plane, lax.axis_index("gx"))
+        else:
+            first = in_plane
+        self.mine = first.astype(jnp.int32)
+
+    def pairs(self, place):
+        dp, gx, gy = self.sizes
+        out = []
+        for a in range(dp):
+            for b in range(gx):
+                for c in range(gy):
+                    to = place(a, b, c)
+                    out.append(((a * gx + b) * gy + c, (to[0] * gx + to[1]) * gy + to[2]))
+        return out
+
+    def swap(self, x, stage, mask):
+        gy = self.sizes[2]
+
+        def place(a, b, c):
+            if self.turned and a % CORES == 1:
+                plane = stage == 1
+            else:
+                plane = stage == 0
+            if plane:
+                return a ^ (mask // gy * CORES), b, c ^ (mask % gy)
+            return a, b ^ mask, c
+
+        return lax.ppermute(x, ("dp", "gx", "gy"), self.pairs(place))
+
+    def swap_cores(self, x):
+        return lax.ppermute(x, ("dp", "gx", "gy"), self.pairs(lambda a, b, c: (a ^ 1, b, c)))
+
+
+def tree_sum(terms):
+    while len(terms) > 1:
+        terms = [a + b for a, b in zip(terms[::2], terms[1::2])]
+    return terms[0]
+
+
+def share_kernel(mine, kept, arrived, own, *boxes):
+    own[...] = kept[mine[0]] + arrived[mine[0]].astype(F32)
+    for mask, box in enumerate(boxes, 1):
+        at = mine[0] ^ mask
+        box[...] = (kept[at] + arrived[at].astype(F32)).astype(BF16)
+
+
+def first_sum_kernel(own, *rest):
+    total = own[...]
+    for box in rest[:-2]:
+        total = total + box[...].astype(F32)
+    rest[-1][...] = total.astype(BF16)
+
+
+def second_sum_kernel(*rest):
+    rest[-1][...] = tree_sum([box[...].astype(F32) for box in rest[:-2]]).astype(BF16)
+
+
+def gather_kernel(mine, *rest):
+    for mask, box in enumerate(rest[:-1]):
+        rest[-1][mine[0] ^ mask] = box[...]
+
+
+def spread_kernel(core, own, other, out):
+    half = out.shape[1] // CORES
+    for tap in range(27):
+        rows = slice(tap * half, (tap + 1) * half)
+        out[tap, pl.ds(pl.multiple_of(core[0] * half, half), half)] = own[rows].astype(F32)
+        out[tap, pl.ds(pl.multiple_of((1 - core[0]) * half, half), half)] = other[rows].astype(F32)
+
+
+def summed_everywhere(groups, kept, sent, early, late):
+    group, line = groups.plane, groups.line
+    rows = kept.shape[0] // group
+    shares = (group, rows, 128)
+    share_type = jax.ShapeDtypeStruct((rows, 128), BF16)
+    mine = groups.mine.reshape(1)
+    arrived = groups.swap_cores(sent)
+    own, *boxes = run(
+        share_kernel,
+        [jax.ShapeDtypeStruct((rows, 128), F32)] + [share_type] * (group - 1),
+        [SMEM, VMEM, VMEM],
+        [VMEM] * group,
+    )(mine, kept.reshape(shares), arrived.reshape(shares))
+    boxes = [groups.swap(box, 0, mask) for mask, box in enumerate(boxes, 1)]
+    rounded = run(first_sum_kernel, share_type, [VMEM] * group + [ANY], VMEM)(own, *boxes, early)
+    boxes = [rounded] + [groups.swap(rounded, 1, mask) for mask in range(1, line)]
+    rounded = run(second_sum_kernel, share_type, [VMEM] * line + [ANY], VMEM)(*boxes, late)
+    boxes = [rounded] + [groups.swap(rounded, 0, mask) for mask in range(1, group)]
+    half = run(
+        gather_kernel, jax.ShapeDtypeStruct(shares, BF16), [SMEM] + [VMEM] * group, VMEM
+    )(mine, *boxes).reshape(kept.shape)
+    other = groups.swap_cores(half)
+    return run(
+        spread_kernel, jax.ShapeDtypeStruct((27, 128, 128), F32), [SMEM, VMEM, VMEM], VMEM
+    )(groups.core.astype(jnp.int32).reshape(1), half, other)
+
+
 def body(features, weight, cotangent, neighbours, send_slots):
     slots, _, channels = features.shape[3:]
     send = send_slots.shape[-1]
@@ -356,7 +417,7 @@
     bricks = features.reshape(slots, EDGE, PLANE, channels)
     cot = cotangent.reshape(slots, EDGE, PLANE, channels)
     table = neighbours.reshape(slots, 27)
-    lists = send_slots.reshape(8, send)
+    lists = send_slots.reshape(8, send).T
     factor = 1.0 / math.sqrt(float(devices * slots * EDGE * PLANE))
     phases_x, phases_y = swap_phases(counts[0]), swap_phases(counts[1])
     number_x, number_y = len(phases_x), len(phases_y)
@@ -365,7 +426,9 @@
     bricks_type = jax.ShapeDtypeStruct(bricks.shape, BF16)
     views_type = jax.ShapeDtypeStruct((slots, EDGE + 2, PLANE, 384), BF16)
     preact_type = jax.ShapeDtypeStruct((slots, EDGE, EDGE, EDGE, 128), F32)
-    half_shape = (27, channels // CORES, channels)
+    groups = Groups()
+    block = 16 * groups.plane
+    half_shape = (-(-27 * channels // CORES // block) * block, channels)
 
     def swapped(boxes, axis, phases):
         size = lax.axis_size(axis)
@@ -387,16 +450,20 @@
         functools.partial(pack_y_kernel, counts, send), [y_type] * number_y, [SMEM, VMEM], [VMEM] * number_y
     )(lists, bricks)
     y_boxes = swapped(y_boxes, "gy", phases_y)
-    taps, back_taps = run(
-        taps_kernel,
-        [jax.ShapeDtypeStruct((1152, 384), BF16), jax.ShapeDtypeStruct((384, 1152), BF16)],
-        [VMEM],
-        [VMEM, VMEM],
-    )(weight.reshape(27, channels, channels))
+    taps, back_taps, views = run(
+        layout_kernel,
+        [
+            jax.ShapeDtypeStruct((1152, 384), BF16),
+            jax.ShapeDtypeStruct((384, 1152), BF16),
+            views_type,
+        ],
+        [SMEM, VMEM, VMEM],
+        [VMEM] * 3,
+        [store_of(slots + 1)],
+        micros=2.0,
+    )(table, bricks, weight.reshape(27, channels, channels))
     x_boxes = swapped(pack_x(lists, bricks, *y_boxes), "gx", phases_x)
-    views, preacts = run(
-        own_kernel, [views_type, preact_type], [SMEM, VMEM, VMEM], [VMEM, VMEM], [store_of(slots + 1)], micros=4.0
-    )(table, bricks, taps)
+    preacts = run(own_kernel, preact_type, [VMEM, VMEM], VMEM, micros=4.0)(views, taps)
     _, _, activated, grads, kept, sent, *y_boxes = run(
         functools.partial(forward_kernel, counts, send, factor),
         [
@@ -415,16 +482,17 @@
         micros=5.0,
     )(table, lists, views, preacts, cot, taps, *x_boxes, *y_boxes)
     y_boxes = swapped(y_boxes, "gy", phases_y)
-    x_boxes = swapped(pack_x(lists, grads, *y_boxes), "gx", phases_x)
-    input_grad = run(
+    packed = pack_x(lists, grads, *y_boxes)
+    x_boxes = swapped(packed, "gx", phases_x)
+    input_grad, ready = run(
         functools.partial(backward_kernel, counts, send),
-        bricks_type,
+        [bricks_type, jax.ShapeDtypeStruct((8, 128), F32)],
         [SMEM, VMEM, VMEM] + [VMEM] * (number_x + number_y),
-        VMEM,
+        [VMEM, VMEM],
         [store_of(slots + 8 * send + 1), pltpu.VMEM(views_type.shape, BF16)],
         micros=5.0,
     )(table, grads, back_taps, *x_boxes, *y_boxes)
-    weight_grad = summed_everywhere(kept, sent)
+    weight_grad = summed_everywhere(groups, kept, sent, packed[-1], ready)
     return (
         activated.reshape(features.shape),
         input_grad.reshape(features.shape),

time: 59.2 us -> 52.8 us (0.89)
  waiting for transfers between devices: 17.6 us -> 8.12 us
  starting transfers between devices: 21.3 us -> 26.1 us
  other arithmetic: 2 us -> 0 us
  Pallas kernels: 14.2 us -> 15.7 us
  local copies, waits for them, and re-layouts: 2.77 us -> 1.82 us
    ppermute x11, waiting for transfers between devices: 15.9 us -> 7.24 us  [the longest x9 5.3 us: swap(): return lax.ppermute(x, ('dp', 'gx', 'gy'), self.pairs(place))]
    ppermute x6, starting transfers between devices: 8.08 us -> 12.5 us  [swapped(): lax.ppermute(box, axis, swap_pairs(size, phase))]
    pallas_call x4 -> x9, Pallas kernels: 8.49 us -> 10.2 us  [the longest x1 4.19 us: body(): run(functools.partial(backward_kernel, counts, send), [bricks_type, jax.S...]
    convert_element_type x3 -> x0, other arithmetic: 1.51 us -> none  [the longest x1 1.38 us: summed_everywhere(): return jnp.concatenate([first, second], axis=1).astype(F32)]
    ppermute x6, waiting for transfers between devices: 1.68 us -> 0.88 us  [swapped(): lax.ppermute(box, axis, swap_pairs(size, phase))]
    reshape x1 -> x0, local copies, waits for them, and re-layouts: 0.75 us -> none  [body(): lists = send_slots.reshape(8, send)]
    unnamed x10 -> x14, local copies, waits for them, and re-layouts: 1.06 us -> 1.82 us
    gather x2 -> x0, local copies, waits for them, and re-layouts: 0.7 us -> none  [summed_everywhere(): half = jnp.take(stacked, order, axis=1).reshape(half.shape)]
  transfers between devices with their start and end apart: 17 -> 17, of which waited for: 8 -> 7; matrix products, arithmetic and copies ran while one was open for 2% -> 0% of each run, Pallas kernels for 14% -> 17%
where the time goes in v3:
time: 52.8 us; the launch traced here: 52.6 us
  starting transfers between devices  26.1 us (49%)
  Pallas kernels  15.7 us (30%)
  waiting for transfers between devices  8.12 us (15%)
  local copies, waits for them, and re-layouts  1.82 us (3%)
  between operations  0.85 us (2%)
    ppermute x9, starting transfers between devices, swap(): return lax.ppermute(x, ('dp', 'gx', 'gy'), self.pairs(place))  13.4 us
    ppermute x6, starting transfers between devices, swapped(): lax.ppermute(box, axis, swap_pairs(size, phase))  12.5 us
    ppermute x9, waiting for transfers between devices, swap(): return lax.ppermute(x, ('dp', 'gx', 'gy'), self.pairs(place))  5.3 us
    pallas_call x1, Pallas kernels, body(): run(functools.partial(forward_kernel, counts, send, factor), [views_type,...  4.3 us
    pallas_call x1, Pallas kernels, body(): run(functools.partial(backward_kernel, counts, send), [bricks_type, jax.S...  4.19 us
    pallas_call x1, Pallas kernels, body(): run(own_kernel, preact_type, [VMEM, VMEM], VMEM, micros=4.0)(views, taps)  2.75 us
    ppermute x2, waiting for transfers between devices, swap_cores(): lax.ppermute(x, ('dp', 'gx', 'gy'), self.pairs(lambda a, b, c: (a ^ 1, b,...  1.95 us
    unnamed x14, local copies, waits for them, and re-layouts  1.82 us
  transfers between devices with their start and end apart: 17, of which 7 were waited for; matrix products, arithmetic and copies ran while one was open for 0% of the time, Pallas kernels for 17%

profile of v3, /device:TPU:0, one launch (start us, length us, event | category | flops | bytes accessed | tf_op | source)
XLA Modules:
  0.0 52.6 jit_solution(3190675614463113004)
XLA Ops:
  0.7 1.1 %copy-done.1 = bf16[1,1,1,4,512,128]{5,4,3,2,1,0:T(8,128)(2,1)S(1)} copy-done((bf16[1,1,1,4,512,128]{5,4,3,2,1,0:T(8,128)(2,1)S(1)}, bf16[1,1,1,4,512,128]{5,4,3,2,1,0:T(8,128)(2,1)}, u32[]{:S(2)}) %copy-start.1) | copy-done | bytes 524312
  1.8 0.7 %copy-done.5 = s32[1,1,1,8,2]{3,4,2,1,0:T(2,128)S(1)} copy-done((s32[1,1,1,8,2]{3,4,2,1,0:T(2,128)S(1)}, s32[1,1,1,8,2]{3,4,2,1,0:T(2,128)}, u32[]{:S(2)}) %copy-start.5) | copy-done | bytes 88
  3.0 3.0 %collective-permute-start = (bf16[160,128]{1,0:T(8,128)(2,1)S(1)}, bf16[160,128]{1,0:T(8,128)(2,1)S(1)}, u32[]{:S(2)}, u32[]{:S(2)}) collective-permute-start(bf16[160,128]{1,0:T(8,128)(2,1)S(1)} %shard_map.78), channel_id=1, source_target_pairs={{0,1},{1,0},{2,3},{3,2},{4,5},{5,4},{6,7},{7,6},{8,9},{9,8},{10,11... | collective-permute-start | bytes 122888 | tf_op jit(solution)/shard_map/ppermute | solution.py:436
  6.1 1.1 %shard_map.76 = (bf16[1152,384]{1,0:T(8,128)(2,1)S(1)}, bf16[384,1152]{1,0:T(8,128)(2,1)S(1)}, bf16[4,10,64,384]{3,2,1,0:T(8,128)(2,1)S(1)}) custom-call(s32[4,27]{1,0:T(4,128)S(1)} %bitcast.23, bf16[4,8,64,128]{3,2,1,0:T(8,128)(2,1)S(1)} %bitcast.17, bf16[27,128,128]{2,1,0:T(8,128)(2,1)S(1)} %bitcast.15), custom_call_target="tpu_custom_call" | custom-call | flops 2000000000 | bytes 65536 | tf_op jit(solution)/shard_map/pallas_call | solution.py:453
  7.2 0.9 %collective-permute-done.rest_0_.rest_2_ = bf16[160,128]{1,0:T(8,128)(2,1)S(1)} collective-permute-done((bf16[160,128]{1,0:T(8,128)(2,1)S(1)}, bf16[160,128]{1,0:T(8,128)(2,1)S(1)}, u32[]{:S(2)}, u32[]{:S(2)}) %collective-permute-start) | collective-permute-done | bytes 40992 | tf_op jit(solution)/shard_map/ppermute | solution.py:436
  8.7 2.1 %collective-permute-start.1 = (bf16[144,128]{1,0:T(8,128)(2,1)S(1)}, bf16[144,128]{1,0:T(8,128)(2,1)S(1)}, u32[]{:S(2)}, u32[]{:S(2)}) collective-permute-start(bf16[144,128]{1,0:T(8,128)(2,1)S(1)} %get-tuple-element.23), channel_id=1, source_target_pairs={{0,2},{2,0},{4,6},{6,4},{1,3},{3,1},{5,7},{7,5},{8,10},{10,8},{12,... | collective-permute-start | bytes 110600 | tf_op jit(solution)/shard_map/ppermute | solution.py:436
  10.8 0.7 %collective-permute-start.2 = (bf16[144,128]{1,0:T(8,128)(2,1)S(1)}, bf16[144,128]{1,0:T(8,128)(2,1)S(1)}, u32[]{:S(2)}, u32[]{:S(2)}) collective-permute-start(bf16[144,128]{1,0:T(8,128)(2,1)S(1)} %get-tuple-element.24), channel_id=1, source_target_pairs={{2,4},{4,2},{3,5},{5,3},{10,12},{12,10},{11,13},{13,11},{18,20},{2... | collective-permute-start | bytes 110600 | tf_op jit(solution)/shard_map/ppermute | solution.py:436
  11.5 2.8 %shard_map.77.own_preact = f32[4,8,8,8,128]{4,3,2,1,0:T(8,128)S(1)} custom-call(bf16[4,10,64,384]{3,2,1,0:T(8,128)(2,1)S(1)} %get-tuple-element.21.views.own_views, bf16[1152,384]{1,0:T(8,128)(2,1)S(1)} %get-tuple-element.22.taps), custom_call_target="tpu_custom_call" | custom-call | flops 4000000000 | bytes 65536 | tf_op jit(solution)/shard_map/pallas_call | solution.py:466
  14.3 4.3 %shard_map.80 = (bf16[4,10,64,384]{3,2,1,0:T(8,128)(2,1)S(1)}, f32[4,8,8,8,128]{4,3,2,1,0:T(8,128)S(1)}, bf16[4,8,64,128]{3,2,1,0:T(8,128)(2,1)}, bf16[4,8,64,12...) custom-call(s32[4,27]{1,0:T(4,128)S(1)} %bitcast.24, ...), custom_call_target="tpu_custom_call", output_to_operand_aliasing={{0}: (2, {}), {1}: (3, {})} | custom-call | flops 5000000000 | bytes 65536 | tf_op jit(solution)/shard_map/pallas_call | solution.py:467
  18.7 1.6 %collective-permute-start.3 = (bf16[160,128]{1,0:T(8,128)(2,1)S(1)}, bf16[160,128]{1,0:T(8,128)(2,1)S(1)}, u32[]{:S(2)}, u32[]{:S(2)}) collective-permute-start(bf16[160,128]{1,0:T(8,128)(2,1)S(1)} %get-tuple-element.28), channel_id=1, source_target_pairs={{0,1},{1,0},{2,3},{3,2},{4,5},{5,4},{6,7},{7,6},{8,9},{9,8},{10,11... | collective-permute-start | bytes 122888 | tf_op jit(solution)/shard_map/ppermute | solution.py:436
  20.6 1.6 %collective-permute-start.7 = (bf16[432,128]{1,0:T(8,128)(2,1)S(1)}, bf16[432,128]{1,0:T(8,128)(2,1)S(1)}, u32[]{:S(2)}, u32[]{:S(2)}) collective-permute-start(bf16[432,128]{1,0:T(8,128)(2,1)S(1)} %get-tuple-element.35), channel_id=1, source_target_pairs={{0,1},{1,0},{2,3},{3,2},{4,5},{5,4},{6,7},{7,6},{8,10},{9,11},{10,... | collective-permute-start | bytes 331784 | tf_op jit(solution)/shard_map/ppermute | solution.py:342
  22.1 1.5 %collective-permute-start.8 = (bf16[432,128]{1,0:T(8,128)(2,1)S(1)}, bf16[432,128]{1,0:T(8,128)(2,1)S(1)}, u32[]{:S(2)}, u32[]{:S(2)}) collective-permute-start(bf16[432,128]{1,0:T(8,128)(2,1)S(1)} %get-tuple-element.36), channel_id=1, source_target_pairs={{0,16},{1,17},{2,18},{3,19},{4,20},{5,21},{6,22},{7,23},{8,12},{9,... | collective-permute-start | bytes 331784 | tf_op jit(solution)/shard_map/ppermute | solution.py:342
  24.7 4.5 %collective-permute-start.4 = (bf16[144,128]{1,0:T(8,128)(2,1)S(1)}, bf16[144,128]{1,0:T(8,128)(2,1)S(1)}, u32[]{:S(2)}, u32[]{:S(2)}) collective-permute-start(bf16[144,128]{1,0:T(8,128)(2,1)S(1)} %get-tuple-element.29), channel_id=1, source_target_pairs={{0,2},{2,0},{4,6},{6,4},{1,3},{3,1},{5,7},{7,5},{8,10},{10,8},{12,... | collective-permute-start | bytes 110600 | tf_op jit(solution)/shard_map/ppermute | solution.py:436
  29.2 0.7 %collective-permute-start.5 = (bf16[144,128]{1,0:T(8,128)(2,1)S(1)}, bf16[144,128]{1,0:T(8,128)(2,1)S(1)}, u32[]{:S(2)}, u32[]{:S(2)}) collective-permute-start(bf16[144,128]{1,0:T(8,128)(2,1)S(1)} %get-tuple-element.30.rest_3_), channel_id=1, source_target_pairs={{2,4},{4,2},{3,5},{5,3},{10,12},{12,10},{11,13},{13,11},{18,20},{2... | collective-permute-start | bytes 110600 | tf_op jit(solution)/shard_map/ppermute | solution.py:436
  29.9 3.9 %collective-permute-start.10 = (bf16[432,128]{1,0:T(8,128)(2,1)S(1)}, bf16[432,128]{1,0:T(8,128)(2,1)S(1)}, u32[]{:S(2)}, u32[]{:S(2)}) collective-permute-start(bf16[432,128]{1,0:T(8,128)(2,1)S(1)} %shard_map.84.rest_0_), channel_id=1, source_target_pairs={{0,2},{1,3},{2,0},{3,1},{4,6},{5,7},{6,4},{7,5},{8,9},{9,8},{10,11... | collective-permute-start | bytes 331784 | tf_op jit(solution)/shard_map/ppermute | solution.py:342
  34.4 1.8 %collective-permute-start.12 = (bf16[432,128]{1,0:T(8,128)(2,1)S(1)}, bf16[432,128]{1,0:T(8,128)(2,1)S(1)}, u32[]{:S(2)}, u32[]{:S(2)}) collective-permute-start(bf16[432,128]{1,0:T(8,128)(2,1)S(1)} %shard_map.84.rest_0_), channel_id=1, source_target_pairs={{0,6},{1,7},{2,4},{3,5},{4,2},{5,3},{6,0},{7,1},{8,25},{9,24},{10,... | collective-permute-start | bytes 331784 | tf_op jit(solution)/shard_map/ppermute | solution.py:342
  36.2 4.2 %shard_map.82 = (bf16[4,8,64,128]{3,2,1,0:T(8,128)(2,1)}, f32[8,128]{1,0:T(8,128)S(1)}) custom-call(s32[4,27]{1,0:T(4,128)S(1)} %bitcast.25, bf16[4,8,64,128]{3,2,1,0:T(8,128)(2,1)S(1)} %get-tuple-element.26.bricks, bf16[384,1152]{1,0:T(8,128)(2,1)S(1)} %get-tuple-element.27.taps, bf16[144,128]{1,0:T(8,128)(2,1)S(1)} %collective-permute-done.4.rest_0_, ...), custom_call_target="tpu_custom_call" | custom-call | flops 5000000000 | bytes 65536 | tf_op jit(solution)/shard_map/pallas_call | solution.py:487
  40.4 1.4 %collective-permute-done.11.rest_2_ = bf16[432,128]{1,0:T(8,128)(2,1)S(1)} collective-permute-done((bf16[432,128]{1,0:T(8,128)(2,1)S(1)}, bf16[432,128]{1,0:T(8,128)(2,1)S(1)}, u32[]{:S(2)}, u32[]{:S(2)}) %collective-permute-start.11) | collective-permute-done | bytes 110624 | tf_op jit(solution)/shard_map/ppermute | solution.py:342
  42.5 1.2 %collective-permute-start.14 = (bf16[432,128]{1,0:T(8,128)(2,1)S(1)}, bf16[432,128]{1,0:T(8,128)(2,1)S(1)}, u32[]{:S(2)}, u32[]{:S(2)}) collective-permute-start(bf16[432,128]{1,0:T(8,128)(2,1)S(1)} %shard_map.85.rest_0_), channel_id=1, source_target_pairs={{0,16},{1,17},{2,18},{3,19},{4,20},{5,21},{6,22},{7,23},{8,12},{9,... | collective-permute-start | bytes 331784 | tf_op jit(solution)/shard_map/ppermute | solution.py:342
  43.7 1.7 %collective-permute-start.15 = (bf16[432,128]{1,0:T(8,128)(2,1)S(1)}, bf16[432,128]{1,0:T(8,128)(2,1)S(1)}, u32[]{:S(2)}, u32[]{:S(2)}) collective-permute-start(bf16[432,128]{1,0:T(8,128)(2,1)S(1)} %shard_map.85.rest_0_), channel_id=1, source_target_pairs={{0,17},{1,16},{2,19},{3,18},{4,21},{5,20},{6,23},{7,22},{8,14},{9,... | collective-permute-start | bytes 331784 | tf_op jit(solution)/shard_map/ppermute | solution.py:342
  45.4 1.3 %collective-permute-done.13.rest_1_ = bf16[432,128]{1,0:T(8,128)(2,1)S(1)} collective-permute-done((bf16[432,128]{1,0:T(8,128)(2,1)S(1)}, bf16[432,128]{1,0:T(8,128)(2,1)S(1)}, u32[]{:S(2)}, u32[]{:S(2)}) %collective-permute-start.13) | collective-permute-done | bytes 110624 | tf_op jit(solution)/shard_map/ppermute | solution.py:342
  47.2 2.1 %collective-permute-done.15.rest_3_ = bf16[432,128]{1,0:T(8,128)(2,1)S(1)} collective-permute-done((bf16[432,128]{1,0:T(8,128)(2,1)S(1)}, bf16[432,128]{1,0:T(8,128)(2,1)S(1)}, u32[]{:S(2)}, u32[]{:S(2)}) %collective-permute-start.15) | collective-permute-done | bytes 110624 | tf_op jit(solution)/shard_map/ppermute | solution.py:342
  49.5 1.8 %collective-permute-done.16.other = bf16[1728,128]{1,0:T(8,128)(2,1)S(1)} collective-permute-done((bf16[1728,128]{1,0:T(8,128)(2,1)S(1)}, bf16[1728,128]{1,0:T(8,128)(2,1)S(1)}, u32[]{:S(2)}, u32[]{:S(2)}) %collective-permute-start.16) | collective-permute-done | bytes 442400 | tf_op jit(solution)/shard_map/ppermute | solution.py:345
  51.2 1.3 %shard_map.87 = f32[27,128,128]{2,1,0:T(8,128)} custom-call(s32[1]{0:T(128)} %bitcast.9.core, bf16[1728,128]{1,0:T(8,128)(2,1)S(1)} %bitcast.22, bf16[1728,128]{1,0:T(8,128)(2,1)S(1)} %collective-permute-done.16.other), custom_call_target="tpu_custom_call" | custom-call | flops 1000000000 | bytes 65536 | tf_op jit(solution)/shard_map/pallas_call | solution.py:407
  (36 shorter events, 4.6 us)
Async XLA Ops:
  0.6 5.4 %copy-start = (bf16[3456,128]{1,0:T(8,128)(2,1)S(1)}, bf16[3456,128]{1,0:T(8,128)(2,1)}, u32[]{:S(2)}) copy-start(bf16[3456,128]{1,0:T(8,128)(2,1)} %param.6) | copy-start | bytes 2654212
  0.6 1.1 %copy-start.1 = (bf16[1,1,1,4,512,128]{5,4,3,2,1,0:T(8,128)(2,1)S(1)}, bf16[1,1,1,4,512,128]{5,4,3,2,1,0:T(8,128)(2,1)}, u32[]{:S(2)}) copy-start(bf16[1,1,1,4,512,128]{5,4,3,2,1,0:T(8,128)(2,1)} %param.5) | copy-start | bytes 1572868
  1.8 0.7 %copy-start.5 = (s32[1,1,1,8,2]{3,4,2,1,0:T(2,128)S(1)}, s32[1,1,1,8,2]{3,4,2,1,0:T(2,128)}, u32[]{:S(2)}) copy-start(s32[1,1,1,8,2]{3,4,2,1,0:T(2,128)} %param.9) | copy-start | bytes 196
  2.4 3.6 %copy-start.2 = (bf16[1,1,1,4,512,128]{5,4,3,2,1,0:T(8,128)(2,1)S(1)}, bf16[1,1,1,4,512,128]{5,4,3,2,1,0:T(8,128)(2,1)}, u32[]{:S(2)}) copy-start(bf16[1,1,1,4,512,128]{5,4,3,2,1,0:T(8,128)(2,1)} %param.5) | copy-start | bytes 1572868
  2.4 3.6 %copy-start.4 = (s32[1,1,1,4,27]{4,3,2,1,0:T(4,128)S(1)}, s32[1,1,1,4,27]{4,3,2,1,0:T(4,128)}, u32[]{:S(2)}) copy-start(s32[1,1,1,4,27]{4,3,2,1,0:T(4,128)} %param.8) | copy-start | bytes 1300
  3.0 5.0 %collective-permute-start = (bf16[160,128]{1,0:T(8,128)(2,1)S(1)}, bf16[160,128]{1,0:T(8,128)(2,1)S(1)}, u32[]{:S(2)}, u32[]{:S(2)}) collective-permute-start(bf16[160,128]{1,0:T(8,128)(2,1)S(1)} %shard_map.78), channel_id=1, source_target_pairs={{0,1},{1,0},{2,3},{3,2},{4,5},{5,4},{6,7},{7,6},{8,9},{9,8},{10,11... | collective-permute-start | bytes 122888 | tf_op jit(solution)/shard_map/ppermute | solution.py:436
  8.7 5.6 %collective-permute-start.1 = (bf16[144,128]{1,0:T(8,128)(2,1)S(1)}, bf16[144,128]{1,0:T(8,128)(2,1)S(1)}, u32[]{:S(2)}, u32[]{:S(2)}) collective-permute-start(bf16[144,128]{1,0:T(8,128)(2,1)S(1)} %get-tuple-element.23), channel_id=1, source_target_pairs={{0,2},{2,0},{4,6},{6,4},{1,3},{3,1},{5,7},{7,5},{8,10},{10,8},{12,... | collective-permute-start | bytes 110600 | tf_op jit(solution)/shard_map/ppermute | solution.py:436
  10.8 3.5 %collective-permute-start.2 = (bf16[144,128]{1,0:T(8,128)(2,1)S(1)}, bf16[144,128]{1,0:T(8,128)(2,1)S(1)}, u32[]{:S(2)}, u32[]{:S(2)}) collective-permute-start(bf16[144,128]{1,0:T(8,128)(2,1)S(1)} %get-tuple-element.24), channel_id=1, source_target_pairs={{2,4},{4,2},{3,5},{5,3},{10,12},{12,10},{11,13},{13,11},{18,20},{2... | collective-permute-start | bytes 110600 | tf_op jit(solution)/shard_map/ppermute | solution.py:436
  11.5 2.8 %copy-start.3 = (bf16[1,1,1,4,512,128]{5,4,3,2,1,0:T(8,128)(2,1)S(1)}, bf16[1,1,1,4,512,128]{5,4,3,2,1,0:T(8,128)(2,1)}, u32[]{:S(2)}) copy-start(bf16[1,1,1,4,512,128]{5,4,3,2,1,0:T(8,128)(2,1)} %param.7) | copy-start | bytes 1572868
  11.5 2.8 %copy-start.6 = (s32[1,1,1,8,2]{3,4,2,1,0:T(2,128)S(1)}, s32[1,1,1,8,2]{3,4,2,1,0:T(2,128)}, u32[]{:S(2)}) copy-start(s32[1,1,1,8,2]{3,4,2,1,0:T(2,128)} %param.9) | copy-start | bytes 196
  18.6 1.9 %collective-permute-start.6 = (bf16[1728,128]{1,0:T(8,128)(2,1)S(1)}, bf16[1728,128]{1,0:T(8,128)(2,1)S(1)}, u32[]{:S(2)}, u32[]{:S(2)}) collective-permute-start(bf16[1728,128]{1,0:T(8,128)(2,1)S(1)} %get-tuple-element.33), channel_id=1, source_target_pairs={{0,8},{1,9},{2,10},{3,11},{4,12},{5,13},{6,14},{7,15},{8,0},{9,1},... | collective-permute-start | bytes 1327112 | tf_op jit(solution)/shard_map/ppermute | solution.py:345
  18.7 5.4 %collective-permute-start.3 = (bf16[160,128]{1,0:T(8,128)(2,1)S(1)}, bf16[160,128]{1,0:T(8,128)(2,1)S(1)}, u32[]{:S(2)}, u32[]{:S(2)}) collective-permute-start(bf16[160,128]{1,0:T(8,128)(2,1)S(1)} %get-tuple-element.28), channel_id=1, source_target_pairs={{0,1},{1,0},{2,3},{3,2},{4,5},{5,4},{6,7},{7,6},{8,9},{9,8},{10,11... | collective-permute-start | bytes 122888 | tf_op jit(solution)/shard_map/ppermute | solution.py:436
  20.6 9.3 %collective-permute-start.7 = (bf16[432,128]{1,0:T(8,128)(2,1)S(1)}, bf16[432,128]{1,0:T(8,128)(2,1)S(1)}, u32[]{:S(2)}, u32[]{:S(2)}) collective-permute-start(bf16[432,128]{1,0:T(8,128)(2,1)S(1)} %get-tuple-element.35), channel_id=1, source_target_pairs={{0,1},{1,0},{2,3},{3,2},{4,5},{5,4},{6,7},{7,6},{8,10},{9,11},{10,... | collective-permute-start | bytes 331784 | tf_op jit(solution)/shard_map/ppermute | solution.py:342
  22.1 7.7 %collective-permute-start.8 = (bf16[432,128]{1,0:T(8,128)(2,1)S(1)}, bf16[432,128]{1,0:T(8,128)(2,1)S(1)}, u32[]{:S(2)}, u32[]{:S(2)}) collective-permute-start(bf16[432,128]{1,0:T(8,128)(2,1)S(1)} %get-tuple-element.36), channel_id=1, source_target_pairs={{0,16},{1,17},{2,18},{3,19},{4,20},{5,21},{6,22},{7,23},{8,12},{9,... | collective-permute-start | bytes 331784 | tf_op jit(solution)/shard_map/ppermute | solution.py:342
  23.6 6.2 %collective-permute-start.9 = (bf16[432,128]{1,0:T(8,128)(2,1)S(1)}, bf16[432,128]{1,0:T(8,128)(2,1)S(1)}, u32[]{:S(2)}, u32[]{:S(2)}) collective-permute-start(bf16[432,128]{1,0:T(8,128)(2,1)S(1)} %get-tuple-element.37), channel_id=1, source_target_pairs={{0,17},{1,16},{2,19},{3,18},{4,21},{5,20},{6,23},{7,22},{8,14},{9,... | collective-permute-start | bytes 331784 | tf_op jit(solution)/shard_map/ppermute | solution.py:342
  24.7 11.5 %collective-permute-start.4 = (bf16[144,128]{1,0:T(8,128)(2,1)S(1)}, bf16[144,128]{1,0:T(8,128)(2,1)S(1)}, u32[]{:S(2)}, u32[]{:S(2)}) collective-permute-start(bf16[144,128]{1,0:T(8,128)(2,1)S(1)} %get-tuple-element.29), channel_id=1, source_target_pairs={{0,2},{2,0},{4,6},{6,4},{1,3},{3,1},{5,7},{7,5},{8,10},{10,8},{12,... | collective-permute-start | bytes 110600 | tf_op jit(solution)/shard_map/ppermute | solution.py:436
  29.2 7.1 %collective-permute-start.5 = (bf16[144,128]{1,0:T(8,128)(2,1)S(1)}, bf16[144,128]{1,0:T(8,128)(2,1)S(1)}, u32[]{:S(2)}, u32[]{:S(2)}) collective-permute-start(bf16[144,128]{1,0:T(8,128)(2,1)S(1)} %get-tuple-element.30.rest_3_), channel_id=1, source_target_pairs={{2,4},{4,2},{3,5},{5,3},{10,12},{12,10},{11,13},{13,11},{18,20},{2... | collective-permute-start | bytes 110600 | tf_op jit(solution)/shard_map/ppermute | solution.py:436
  29.9 10.5 %collective-permute-start.10 = (bf16[432,128]{1,0:T(8,128)(2,1)S(1)}, bf16[432,128]{1,0:T(8,128)(2,1)S(1)}, u32[]{:S(2)}, u32[]{:S(2)}) collective-permute-start(bf16[432,128]{1,0:T(8,128)(2,1)S(1)} %shard_map.84.rest_0_), channel_id=1, source_target_pairs={{0,2},{1,3},{2,0},{3,1},{4,6},{5,7},{6,4},{7,5},{8,9},{9,8},{10,11... | collective-permute-start | bytes 331784 | tf_op jit(solution)/shard_map/ppermute | solution.py:342
  33.8 8.0 %collective-permute-start.11 = (bf16[432,128]{1,0:T(8,128)(2,1)S(1)}, bf16[432,128]{1,0:T(8,128)(2,1)S(1)}, u32[]{:S(2)}, u32[]{:S(2)}) collective-permute-start(bf16[432,128]{1,0:T(8,128)(2,1)S(1)} %shard_map.84.rest_0_), channel_id=1, source_target_pairs={{0,4},{1,5},{2,6},{3,7},{4,0},{5,1},{6,2},{7,3},{8,24},{9,25},{10,... | collective-permute-start | bytes 331784 | tf_op jit(solution)/shard_map/ppermute | solution.py:342
  34.4 7.4 %collective-permute-start.12 = (bf16[432,128]{1,0:T(8,128)(2,1)S(1)}, bf16[432,128]{1,0:T(8,128)(2,1)S(1)}, u32[]{:S(2)}, u32[]{:S(2)}) collective-permute-start(bf16[432,128]{1,0:T(8,128)(2,1)S(1)} %shard_map.84.rest_0_), channel_id=1, source_target_pairs={{0,6},{1,7},{2,4},{3,5},{4,2},{5,3},{6,0},{7,1},{8,25},{9,24},{10,... | collective-permute-start | bytes 331784 | tf_op jit(solution)/shard_map/ppermute | solution.py:342
  41.9 4.8 %collective-permute-start.13 = (bf16[432,128]{1,0:T(8,128)(2,1)S(1)}, bf16[432,128]{1,0:T(8,128)(2,1)S(1)}, u32[]{:S(2)}, u32[]{:S(2)}) collective-permute-start(bf16[432,128]{1,0:T(8,128)(2,1)S(1)} %shard_map.85.rest_0_), channel_id=1, source_target_pairs={{0,1},{1,0},{2,3},{3,2},{4,5},{5,4},{6,7},{7,6},{8,10},{9,11},{10,... | collective-permute-start | bytes 331784 | tf_op jit(solution)/shard_map/ppermute | solution.py:342
  42.5 4.7 %collective-permute-start.14 = (bf16[432,128]{1,0:T(8,128)(2,1)S(1)}, bf16[432,128]{1,0:T(8,128)(2,1)S(1)}, u32[]{:S(2)}, u32[]{:S(2)}) collective-permute-start(bf16[432,128]{1,0:T(8,128)(2,1)S(1)} %shard_map.85.rest_0_), channel_id=1, source_target_pairs={{0,16},{1,17},{2,18},{3,19},{4,20},{5,21},{6,22},{7,23},{8,12},{9,... | collective-permute-start | bytes 331784 | tf_op jit(solution)/shard_map/ppermute | solution.py:342
  43.7 5.6 %collective-permute-start.15 = (bf16[432,128]{1,0:T(8,128)(2,1)S(1)}, bf16[432,128]{1,0:T(8,128)(2,1)S(1)}, u32[]{:S(2)}, u32[]{:S(2)}) collective-permute-start(bf16[432,128]{1,0:T(8,128)(2,1)S(1)} %shard_map.85.rest_0_), channel_id=1, source_target_pairs={{0,17},{1,16},{2,19},{3,18},{4,21},{5,20},{6,23},{7,22},{8,14},{9,... | collective-permute-start | bytes 331784 | tf_op jit(solution)/shard_map/ppermute | solution.py:342
  49.4 1.9 %collective-permute-start.16 = (bf16[1728,128]{1,0:T(8,128)(2,1)S(1)}, bf16[1728,128]{1,0:T(8,128)(2,1)S(1)}, u32[]{:S(2)}, u32[]{:S(2)}) collective-permute-start(bf16[1728,128]{1,0:T(8,128)(2,1)S(1)} %bitcast.21), channel_id=1, source_target_pairs={{0,8},{1,9},{2,10},{3,11},{4,12},{5,13},{6,14},{7,15},{8,0},{9,1},... | collective-permute-start | bytes 1327112 | tf_op jit(solution)/shard_map/ppermute | solution.py:345

commit v4 on v3

--- a/solution.py
+++ b/solution.py
@@ -21,11 +21,24 @@
     return ([0] if size > 1 else []) + ([1] if size > 2 else [])
 
 
-def swap_pairs(size, phase):
+def partner_of(at, size, phase):
+    other = at + 1 if at % 2 == phase else at - 1
+    return other if 0 <= other < size else at
+
+
+def swap(x, axis, phase):
+    sizes = [lax.axis_size(name) for name in ("dp", axis)]
     pairs = []
-    for low in range(phase, size - 1, 2):
-        pairs += [(low, low + 1), (low + 1, low)]
-    return pairs
+    for at in range(sizes[0]):
+        for tile in range(sizes[1]):
+            other = partner_of(tile, sizes[1], phase)
+            to = (at ^ 1 if other == tile else at) * sizes[1] + other
+            pairs.append((at * sizes[1] + tile, to))
+    return lax.ppermute(x, ("dp", axis), pairs)
+
+
+def inside(at, size, step):
+    return (at + step >= 0) & (at + step < size)
 
 
 def step_of(at, phase):
@@ -68,13 +81,17 @@
         at += send * EDGE
 
 
-def pack_along_x(bricks, lists, box, y_boxes, step_x, send):
+def pack_along_x(bricks, lists, box, step_x, send):
     number = direction(step_x, 0)
     for entry in range(send):
         listed = lists[entry, number]
         face = bricks[jnp.maximum(listed, 0), jnp.where(step_x > 0, EDGE - 1, 0)]
         box[entry * PLANE : (entry + 1) * PLANE] = jnp.where(listed >= 0, face, jnp.zeros_like(face))
+
+
+def join_along_x(faces, box, y_boxes, step_x, send):
     at = send * PLANE
+    box[:at] = faces[...]
     for y_box in y_boxes:
         first = y_box[send * PLANE : send * PLANE + send * EDGE]
         second = y_box[send * PLANE + send * EDGE : send * PLANE + 2 * send * EDGE]
@@ -82,25 +99,27 @@
         at += send * EDGE
 
 
-def fill_remote(store, base, x_boxes, y_boxes, steps_x, steps_y, send):
+def fill_remote(store, base, x_boxes, y_boxes, tiles_x, tiles_y, send):
     store[store.shape[0] - 1] = jnp.zeros(store.shape[1:], BF16)
-    for step_y, box in zip(steps_y, y_boxes):
+    for (step_y, in_y), box in zip(tiles_y, y_boxes):
         number = direction(0, step_y)
         for entry in range(send):
             rows = box[entry * PLANE : (entry + 1) * PLANE].astype(F32).reshape(EDGE, EDGE, 128)
+            rows = jnp.where(in_y, rows, 0.0)
             twice = jnp.concatenate([rows, rows], axis=1).astype(BF16)
             store[base + number * send + entry, :, 0:16, :] = twice
             store[base + number * send + entry, :, PLANE - 16 : PLANE, :] = twice
-    for step_x, box in zip(steps_x, x_boxes):
+    for (step_x, in_x), box in zip(tiles_x, x_boxes):
         number = direction(step_x, 0)
         for entry in range(send):
             face = box[entry * PLANE : (entry + 1) * PLANE]
+            face = jnp.where(in_x, face, jnp.zeros_like(face))
             store[base + number * send + entry, 0] = face
             store[base + number * send + entry, EDGE - 1] = face
         at = send * PLANE
-        for step_y in steps_y:
+        for step_y, in_y in tiles_y:
             number = direction(step_x, step_y)
-            edges = box[at : at + send * EDGE].astype(F32)
+            edges = jnp.where(in_x & in_y, box[at : at + send * EDGE].astype(F32), 0.0)
             at += send * EDGE
             for entry in range(send):
                 rows = edges[entry * EDGE : (entry + 1) * EDGE]
@@ -153,22 +172,43 @@
     return blocks[1] + shift_rows(blocks[0], -1) + shift_rows(blocks[2], 1)
 
 
-def steps_here(counts):
-    steps_x = [step_of(lax.axis_index("gx"), phase) for phase in swap_phases(counts[0])]
-    steps_y = [step_of(lax.axis_index("gy"), phase) for phase in swap_phases(counts[1])]
-    return steps_x, steps_y
-
-
-def pack_y_kernel(counts, send, lists, bricks, *boxes):
-    for step_y, box in zip(steps_here(counts)[1], boxes):
+def tiles_here(counts):
+    out = []
+    for name, size in zip(("gx", "gy"), counts):
+        at = lax.axis_index(name)
+        steps = [step_of(at, phase) for phase in swap_phases(size)]
+        out.append([(step, inside(at, size, step)) for step in steps])
+    return out
+
+
+def pack_all(bricks, lists, x_boxes, y_boxes, counts, send):
+    tiles_x, tiles_y = tiles_here(counts)
+    for (step_y, _), box in zip(tiles_y, y_boxes):
         pack_along_y(bricks, lists, box, step_y, send)
-
-
-def pack_x_kernel(counts, send, lists, bricks, *rest):
-    steps_x, steps_y = steps_here(counts)
-    y_boxes, x_boxes = rest[: len(steps_y)], rest[len(steps_y) :]
-    for step_x, box in zip(steps_x, x_boxes):
-        pack_along_x(bricks, lists, box, y_boxes, step_x, send)
+    for (step_x, _), box in zip(tiles_x, x_boxes):
+        pack_along_x(bricks, lists, box, step_x, send)
+
+
+def start_kernel(counts, send, lists_hbm, bricks_hbm, bricks, *rest):
+    boxes, (lists, sems) = rest[:-2], rest[-2:]
+    copies = [
+        pltpu.make_async_copy(bricks_hbm, bricks, sems.at[0]),
+        pltpu.make_async_copy(lists_hbm, lists, sems.at[1]),
+    ]
+    for copy in copies:
+        copy.start()
+    for copy in copies:
+        copy.wait()
+    number_x = len(swap_phases(counts[0]))
+    pack_all(bricks, lists, boxes[:number_x], boxes[number_x:], counts, send)
+
+
+def join_kernel(counts, send, *rest):
+    tiles_x, tiles_y = tiles_here(counts)
+    number_x, number_y = len(tiles_x), len(tiles_y)
+    faces, y_boxes, x_boxes = rest[:number_x], rest[number_x : number_x + number_y], rest[number_x + number_y :]
+    for (step_x, _), face, box in zip(tiles_x, faces, x_boxes):
+        join_along_x(face, box, y_boxes, step_x, send)
 
 
 def layout_kernel(table, bricks, weight, forward, backward, views, store):
@@ -189,15 +229,24 @@
         preact[slot] = join_taps(parts).reshape(EDGE, EDGE, EDGE, 128)
 
 
-def forward_kernel(counts, send, factor, table, lists, own_views, own_preact, cotangent, taps, *rest):
-    steps_x, steps_y = steps_here(counts)
-    number_x, number_y = len(steps_x), len(steps_y)
+def forward_kernel(counts, send, factor, table_vmem, lists_vmem, own_views, own_preact, cotangent, taps, *rest):
+    tiles_x, tiles_y = tiles_here(counts)
+    number_x, number_y = len(tiles_x), len(tiles_y)
     x_boxes, y_boxes, rest = rest[:number_x], rest[number_x : number_x + number_y], rest[number_x + number_y :]
     views, preacts, activated, grads, kept_term, sent_term = rest[:6]
-    boxes_out, (store, sides) = rest[6 : 6 + number_y], rest[6 + number_y :]
+    faces_out, boxes_out = rest[6 : 6 + number_x], rest[6 + number_x : 6 + number_x + number_y]
+    store, sides, table, lists, sems = rest[6 + number_x + number_y :]
+    copies = [
+        pltpu.make_async_copy(table_vmem, table, sems.at[0]),
+        pltpu.make_async_copy(lists_vmem, lists, sems.at[1]),
+    ]
+    for copy in copies:
+        copy.start()
     core = lax.axis_index("dp") % CORES
     slots = cotangent.shape[0]
-    fill_remote(store, 0, x_boxes, y_boxes, steps_x, steps_y, send)
+    fill_remote(store, 0, x_boxes, y_boxes, tiles_x, tiles_y, send)
+    for copy in copies:
+        copy.wait()
     nothing = jnp.zeros((EDGE, EDGE, 128), F32)
     for slot in range(slots):
         rows = slice(slot * PLANE, (slot + 1) * PLANE)
@@ -241,8 +290,7 @@
         wide = cotangent[slot].astype(F32).reshape(PLANE, EDGE, 128) * slope
         wide = jnp.where(table[slot, 13] >= 0, wide, 0.0)
         grads[slot] = wide.reshape(EDGE, PLANE, 128).astype(BF16)
-    for step_y, box in zip(steps_y, boxes_out):
-        pack_along_y(grads, lists, box, step_y, send)
+    pack_all(grads, lists, faces_out, boxes_out, counts, send)
     total = None
     for slot in range(slots):
         grad = grads[slot].astype(F32).reshape(PLANE, EDGE, 128)
@@ -266,12 +314,12 @@
 
 
 def backward_kernel(counts, send, table, bricks, taps, *rest):
-    steps_x, steps_y = steps_here(counts)
-    x_boxes, y_boxes = rest[: len(steps_x)], rest[len(steps_x) : len(steps_x) + len(steps_y)]
+    tiles_x, tiles_y = tiles_here(counts)
+    x_boxes, y_boxes = rest[: len(tiles_x)], rest[len(tiles_x) : len(tiles_x) + len(tiles_y)]
     result, ready, store, views = rest[-4:]
     slots = bricks.shape[0]
     store[0:slots] = bricks[...]
-    fill_remote(store, slots, x_boxes, y_boxes, steps_x, steps_y, send)
+    fill_remote(store, slots, x_boxes, y_boxes, tiles_x, tiles_y, send)
     zero_at = store.shape[0] - 1
     for slot in range(slots):
         fill_views(views.at[slot], store, lookup(table, slot, 0, zero_at, zero_at))
@@ -285,6 +333,7 @@
 VMEM = pl.BlockSpec(memory_space=pltpu.VMEM)
 SMEM = pl.BlockSpec(memory_space=pltpu.SMEM)
 ANY = pl.BlockSpec(memory_space=pl.ANY)
+HBM = pl.BlockSpec(memory_space=pltpu.HBM)
 PARAMS = pltpu.CompilerParams(vmem_limit_bytes=VMEM_BYTES)
 
 
@@ -341,6 +390,9 @@
 
         return lax.ppermute(x, ("dp", "gx", "gy"), self.pairs(place))
 
+    def swaps(self, boxes, stage):
+        return [self.swap(box, stage, len(boxes) - at) for at, box in enumerate(boxes)]
+
     def swap_cores(self, x):
         return lax.ppermute(x, ("dp", "gx", "gy"), self.pairs(lambda a, b, c: (a ^ 1, b, c)))
 
@@ -353,7 +405,7 @@
 
 def share_kernel(mine, kept, arrived, own, *boxes):
     own[...] = kept[mine[0]] + arrived[mine[0]].astype(F32)
-    for mask, box in enumerate(boxes, 1):
+    for mask, box in enumerate(reversed(boxes), 1):
         at = mine[0] ^ mask
         box[...] = (kept[at] + arrived[at].astype(F32)).astype(BF16)
 
@@ -366,20 +418,21 @@
 
 
 def second_sum_kernel(*rest):
-    rest[-1][...] = tree_sum([box[...].astype(F32) for box in rest[:-2]]).astype(BF16)
+    terms = [box[...].astype(F32) for box in rest[-3::-1]]
+    rest[-1][...] = tree_sum(terms).astype(BF16)
 
 
 def gather_kernel(mine, *rest):
-    for mask, box in enumerate(rest[:-1]):
+    for mask, box in enumerate(rest[-2::-1]):
         rest[-1][mine[0] ^ mask] = box[...]
 
 
-def spread_kernel(core, own, other, out):
-    half = out.shape[1] // CORES
-    for tap in range(27):
-        rows = slice(tap * half, (tap + 1) * half)
-        out[tap, pl.ds(pl.multiple_of(core[0] * half, half), half)] = own[rows].astype(F32)
-        out[tap, pl.ds(pl.multiple_of((1 - core[0]) * half, half), half)] = other[rows].astype(F32)
+def spread_kernel(at, half, *rest):
+    out, wide, sem = rest[-3:]
+    wide[...] = half[0 : wide.shape[0] * wide.shape[1]].astype(F32).reshape(wide.shape)
+    copy = pltpu.make_async_copy(wide, out.at[:, at[0]], sem)
+    copy.start()
+    copy.wait()
 
 
 def summed_everywhere(groups, kept, sent, early, late):
@@ -395,18 +448,21 @@
         [SMEM, VMEM, VMEM],
         [VMEM] * group,
     )(mine, kept.reshape(shares), arrived.reshape(shares))
-    boxes = [groups.swap(box, 0, mask) for mask, box in enumerate(boxes, 1)]
+    boxes = groups.swaps(boxes, 0)
     rounded = run(first_sum_kernel, share_type, [VMEM] * group + [ANY], VMEM)(own, *boxes, early)
-    boxes = [rounded] + [groups.swap(rounded, 1, mask) for mask in range(1, line)]
+    boxes = groups.swaps([rounded] * (line - 1), 1) + [rounded]
     rounded = run(second_sum_kernel, share_type, [VMEM] * line + [ANY], VMEM)(*boxes, late)
-    boxes = [rounded] + [groups.swap(rounded, 0, mask) for mask in range(1, group)]
+    boxes = groups.swaps([rounded] * (group - 1), 0) + [rounded]
     half = run(
         gather_kernel, jax.ShapeDtypeStruct(shares, BF16), [SMEM] + [VMEM] * group, VMEM
     )(mine, *boxes).reshape(kept.shape)
     other = groups.swap_cores(half)
-    return run(
-        spread_kernel, jax.ShapeDtypeStruct((27, 128, 128), F32), [SMEM, VMEM, VMEM], VMEM
-    )(groups.core.astype(jnp.int32).reshape(1), half, other)
+    rows = 128 // CORES
+    out_type = jax.ShapeDtypeStruct((27, CORES, rows, 128), F32)
+    scratch = [pltpu.VMEM((27, rows, 128), F32), pltpu.SemaphoreType.DMA]
+    core = groups.core.astype(jnp.int32).reshape(1)
+    out = run(spread_kernel, out_type, [SMEM, VMEM], ANY, scratch)(core, half)
+    return run(spread_kernel, out_type, [SMEM, VMEM, ANY], ANY, scratch, aliases={2: 0})(1 - core, other, out)
 
 
 def body(features, weight, cotangent, neighbours, send_slots):
@@ -431,24 +487,27 @@
     half_shape = (-(-27 * channels // CORES // block) * block, channels)
 
     def swapped(boxes, axis, phases):
-        size = lax.axis_size(axis)
-        return [
-            lax.ppermute(box, axis, swap_pairs(size, phase)) for box, phase in zip(boxes, phases)
-        ]
+        return [swap(box, axis, phase) for box, phase in zip(boxes, phases)]
 
     def store_of(entries):
         return pltpu.VMEM((entries, EDGE, PLANE, 128), BF16)
 
-    pack_x = run(
-        functools.partial(pack_x_kernel, counts, send),
+    face_type = jax.ShapeDtypeStruct((send * PLANE, 128), BF16)
+    join = run(
+        functools.partial(join_kernel, counts, send),
         [x_type] * number_x,
-        [SMEM, VMEM] + [VMEM] * number_y,
+        [VMEM] * (number_x + number_y),
         [VMEM] * number_x,
     )
 
-    y_boxes = run(
-        functools.partial(pack_y_kernel, counts, send), [y_type] * number_y, [SMEM, VMEM], [VMEM] * number_y
-    )(lists, bricks)
+    bricks, *boxes = run(
+        functools.partial(start_kernel, counts, send),
+        [bricks_type] + [face_type] * number_x + [y_type] * number_y,
+        [HBM, HBM],
+        [VMEM] * (1 + number_x + number_y),
+        [pltpu.SMEM((send, 8), jnp.int32), pltpu.SemaphoreType.DMA((2,))],
+    )(*[pltpu.with_memory_space_constraint(x, pltpu.HBM) for x in (lists, bricks)])
+    faces, y_boxes = boxes[:number_x], boxes[number_x:]
     y_boxes = swapped(y_boxes, "gy", phases_y)
     taps, back_taps, views = run(
         layout_kernel,
@@ -462,9 +521,9 @@
         [store_of(slots + 1)],
         micros=2.0,
     )(table, bricks, weight.reshape(27, channels, channels))
-    x_boxes = swapped(pack_x(lists, bricks, *y_boxes), "gx", phases_x)
+    x_boxes = swapped(join(*faces, *y_boxes), "gx", phases_x)
     preacts = run(own_kernel, preact_type, [VMEM, VMEM], VMEM, micros=4.0)(views, taps)
-    _, _, activated, grads, kept, sent, *y_boxes = run(
+    _, _, activated, grads, kept, sent, *boxes = run(
         functools.partial(forward_kernel, counts, send, factor),
         [
             views_type,
@@ -474,15 +533,22 @@
             jax.ShapeDtypeStruct(half_shape, F32),
             jax.ShapeDtypeStruct(half_shape, BF16),
         ]
+        + [face_type] * number_x
         + [y_type] * number_y,
-        [SMEM, SMEM] + [VMEM] * (4 + number_x + number_y),
-        [VMEM] * (6 + number_y),
-        [store_of(8 * send + 1), pltpu.VMEM((4, slots * PLANE, 384), BF16)],
+        [VMEM] * (6 + number_x + number_y),
+        [VMEM] * (6 + number_x + number_y),
+        [
+            store_of(8 * send + 1),
+            pltpu.VMEM((4, slots * PLANE, 384), BF16),
+            pltpu.SMEM(table.shape, jnp.int32),
+            pltpu.SMEM(lists.shape, jnp.int32),
+            pltpu.SemaphoreType.DMA((2,)),
+        ],
         aliases={2: 0, 3: 1},
         micros=5.0,
     )(table, lists, views, preacts, cot, taps, *x_boxes, *y_boxes)
-    y_boxes = swapped(y_boxes, "gy", phases_y)
-    packed = pack_x(lists, grads, *y_boxes)
+    faces, y_boxes = boxes[:number_x], swapped(boxes[number_x:], "gy", phases_y)
+    packed = join(*faces, *y_boxes)
     x_boxes = swapped(packed, "gx", phases_x)
     input_grad, ready = run(
         functools.partial(backward_kernel, counts, send),

time: 52.8 us -> 46.7 us (0.88)
  starting transfers between devices: 26.1 us -> 22 us
  local copies, waits for them, and re-layouts: 1.82 us -> 0.02 us
  Pallas kernels: 15.7 us -> 16.3 us
  waiting for transfers between devices: 8.12 us -> 7.55 us
    ppermute x6, starting transfers between devices: 12.5 us -> 9.68 us  [swap(): return lax.ppermute(x, ('dp', axis), pairs)]
    unnamed x14 -> x8, local copies, waits for them, and re-layouts: 1.82 us -> 0.02 us
    ppermute x9, starting transfers between devices: 13.4 us -> 11.7 us  [swap(): return lax.ppermute(x, ('dp', 'gx', 'gy'), self.pairs(place))]
    ppermute x2, waiting for transfers between devices: 1.95 us -> 0.79 us  [swap_cores(): lax.ppermute(x, ('dp', 'gx', 'gy'), self.pairs(lambda a, b, c: (a ^ 1, b,...]
    ppermute x9, waiting for transfers between devices: 5.3 us -> 5.88 us  [swap(): return lax.ppermute(x, ('dp', 'gx', 'gy'), self.pairs(place))]
    pallas_call x4 -> x5, Pallas kernels: 3.11 us -> 3.2 us  [the longest x1 1.22 us: body(): run(functools.partial(start_kernel, counts, send), [bricks_type] + [face_...]
  transfers between devices with their start and end apart: 17 -> 17, of which waited for: 7 -> 8; matrix products, arithmetic and copies ran while one was open for 0% -> 0% of each run, Pallas kernels for 17% -> 20%
where the time goes in v4:
time: 46.7 us; the launch traced here: 46.6 us
  starting transfers between devices  22 us (47%)
  Pallas kernels  16.3 us (35%)
  waiting for transfers between devices  7.55 us (16%)
  between operations  0.77 us (2%)
    ppermute x9, starting transfers between devices, swap(): return lax.ppermute(x, ('dp', 'gx', 'gy'), self.pairs(place))  11.7 us
    ppermute x6, starting transfers between devices, swap(): return lax.ppermute(x, ('dp', axis), pairs)  9.68 us
    ppermute x9, waiting for transfers between devices, swap(): return lax.ppermute(x, ('dp', 'gx', 'gy'), self.pairs(place))  5.88 us
    pallas_call x1, Pallas kernels, body(): run(functools.partial(forward_kernel, counts, send, factor), [views_type,...  4.78 us
    pallas_call x1, Pallas kernels, body(): run(functools.partial(backward_kernel, counts, send), [bricks_type, jax.S...  4.2 us
    pallas_call x1, Pallas kernels, body(): run(own_kernel, preact_type, [VMEM, VMEM], VMEM, micros=4.0)(views, taps)  2.75 us
    pallas_call x1, Pallas kernels, body(): run(functools.partial(start_kernel, counts, send), [bricks_type] + [face_...  1.22 us
    pallas_call x1, Pallas kernels, body(): run(layout_kernel, [jax.ShapeDtypeStruct((1152, 384), BF16), jax.ShapeDty...  1.1 us
  transfers between devices with their start and end apart: 17, of which 8 were waited for; matrix products, arithmetic and copies ran while one was open for 0% of the time, Pallas kernels for 20%

profile of v4, /device:TPU:0, one launch (start us, length us, event | category | flops | bytes accessed | tf_op | source)
XLA Modules:
  0.0 46.6 jit_solution(6329013148863083540)
XLA Ops:
  0.7 1.2 %shard_map.76 = (bf16[4,8,64,128]{3,2,1,0:T(8,128)(2,1)S(1)}, bf16[128,128]{1,0:T(8,128)(2,1)S(1)}, bf16[128,128]{1,0:T(8,128)(2,1)S(1)}, bf16[160,128]{1,0:T(8,128)(2,1)S(1)}) custom-call(s32[2,8]{1,0:T(2,128)} %bitcast.23, bf16[4,8,64,128]{3,2,1,0:T(8,128)(2,1)} %bitcast.27), custom_call_target="tpu_custom_call" | custom-call | flops 1000000000 | bytes 65536 | tf_op jit(solution)/shard_map/pallas_call | solution.py:503
  1.9 3.0 %collective-permute-start = (bf16[160,128]{1,0:T(8,128)(2,1)S(1)}, bf16[160,128]{1,0:T(8,128)(2,1)S(1)}, u32[]{:S(2)}, u32[]{:S(2)}) collective-permute-start(bf16[160,128]{1,0:T(8,128)(2,1)S(1)} %get-tuple-element.32), channel_id=1, source_target_pairs={{0,1},{1,0},{8,9},{9,8},{16,17},{17,16},{24,25},{25,24},{2,3},{3,2... | collective-permute-start | bytes 122888 | tf_op jit(solution)/shard_map/ppermute | solution.py:37
  4.9 1.1 %shard_map.77 = (bf16[1152,384]{1,0:T(8,128)(2,1)S(1)}, bf16[384,1152]{1,0:T(8,128)(2,1)S(1)}, bf16[4,10,64,384]{3,2,1,0:T(8,128)(2,1)S(1)}) custom-call(s32[4,27]{1,0:T(4,128)S(1)} %bitcast.20, bf16[4,8,64,128]{3,2,1,0:T(8,128)(2,1)S(1)} %get-tuple-element.27.bricks, bf16[27,128,128]{2,1,0:T(8,128)(2,1)S(1)} %bitcast.15), custom_call_target="tpu_custom_call" | custom-call | flops 2000000000 | bytes 65536 | tf_op jit(solution)/shard_map/pallas_call | solution.py:512
  6.0 0.9 %collective-permute-done.rest_2_ = bf16[160,128]{1,0:T(8,128)(2,1)S(1)} collective-permute-done((bf16[160,128]{1,0:T(8,128)(2,1)S(1)}, bf16[160,128]{1,0:T(8,128)(2,1)S(1)}, u32[]{:S(2)}, u32[]{:S(2)}) %collective-permute-start) | collective-permute-done | bytes 40992 | tf_op jit(solution)/shard_map/ppermute | solution.py:37
  6.9 2.1 %collective-permute-start.1 = (bf16[144,128]{1,0:T(8,128)(2,1)S(1)}, bf16[144,128]{1,0:T(8,128)(2,1)S(1)}, u32[]{:S(2)}, u32[]{:S(2)}) collective-permute-start(bf16[144,128]{1,0:T(8,128)(2,1)S(1)} %get-tuple-element.33), channel_id=1, source_target_pairs={{0,2},{2,0},{4,6},{6,4},{8,10},{10,8},{12,14},{14,12},{16,18},{18,... | collective-permute-start | bytes 110600 | tf_op jit(solution)/shard_map/ppermute | solution.py:37
  9.1 2.7 %shard_map.78.own_preact = f32[4,8,8,8,128]{4,3,2,1,0:T(8,128)S(1)} custom-call(bf16[4,10,64,384]{3,2,1,0:T(8,128)(2,1)S(1)} %get-tuple-element.28.views.own_views, bf16[1152,384]{1,0:T(8,128)(2,1)S(1)} %get-tuple-element.29.taps), custom_call_target="tpu_custom_call" | custom-call | flops 4000000000 | bytes 65536 | tf_op jit(solution)/shard_map/pallas_call | solution.py:525
  11.9 4.8 %shard_map.80 = (bf16[4,10,64,384]{3,2,1,0:T(8,128)(2,1)S(1)}, f32[4,8,8,8,128]{4,3,2,1,0:T(8,128)S(1)}, bf16[4,8,64,128]{3,2,1,0:T(8,128)(2,1)}, bf16[4,8,64,12...) custom-call(s32[4,27]{1,0:T(4,128)S(1)} %bitcast.21, ...), custom_call_target="tpu_custom_call", output_to_operand_aliasing={{0}: (2, {}), {1}: (3, {})} | custom-call | flops 5000000000 | bytes 65536 | tf_op jit(solution)/shard_map/pallas_call | solution.py:526
  16.6 0.6 %collective-permute-start.6 = (bf16[1728,128]{1,0:T(8,128)(2,1)S(1)}, bf16[1728,128]{1,0:T(8,128)(2,1)S(1)}, u32[]{:S(2)}, u32[]{:S(2)}) collective-permute-start(bf16[1728,128]{1,0:T(8,128)(2,1)S(1)} %get-tuple-element.45), channel_id=1, source_target_pairs={{0,8},{1,9},{2,10},{3,11},{4,12},{5,13},{6,14},{7,15},{8,0},{9,1},... | collective-permute-start | bytes 1327112 | tf_op jit(solution)/shard_map/ppermute | solution.py:397
  17.2 1.5 %collective-permute-start.3 = (bf16[160,128]{1,0:T(8,128)(2,1)S(1)}, bf16[160,128]{1,0:T(8,128)(2,1)S(1)}, u32[]{:S(2)}, u32[]{:S(2)}) collective-permute-start(bf16[160,128]{1,0:T(8,128)(2,1)S(1)} %get-tuple-element.40), channel_id=1, source_target_pairs={{0,1},{1,0},{8,9},{9,8},{16,17},{17,16},{24,25},{25,24},{2,3},{3,2... | collective-permute-start | bytes 122888 | tf_op jit(solution)/shard_map/ppermute | solution.py:37
  18.8 2.4 %collective-permute-start.7 = (bf16[432,128]{1,0:T(8,128)(2,1)S(1)}, bf16[432,128]{1,0:T(8,128)(2,1)S(1)}, u32[]{:S(2)}, u32[]{:S(2)}) collective-permute-start(bf16[432,128]{1,0:T(8,128)(2,1)S(1)} %get-tuple-element.47), channel_id=1, source_target_pairs={{0,17},{1,16},{2,19},{3,18},{4,21},{5,20},{6,23},{7,22},{8,14},{9,... | collective-permute-start | bytes 331784 | tf_op jit(solution)/shard_map/ppermute | solution.py:391
  21.8 0.6 %collective-permute-start.9 = (bf16[432,128]{1,0:T(8,128)(2,1)S(1)}, bf16[432,128]{1,0:T(8,128)(2,1)S(1)}, u32[]{:S(2)}, u32[]{:S(2)}) collective-permute-start(bf16[432,128]{1,0:T(8,128)(2,1)S(1)} %get-tuple-element.49), channel_id=1, source_target_pairs={{0,1},{1,0},{2,3},{3,2},{4,5},{5,4},{6,7},{7,6},{8,10},{9,11},{10,... | collective-permute-start | bytes 331784 | tf_op jit(solution)/shard_map/ppermute | solution.py:391
  22.4 3.0 %collective-permute-start.4 = (bf16[144,128]{1,0:T(8,128)(2,1)S(1)}, bf16[144,128]{1,0:T(8,128)(2,1)S(1)}, u32[]{:S(2)}, u32[]{:S(2)}) collective-permute-start(bf16[144,128]{1,0:T(8,128)(2,1)S(1)} %get-tuple-element.41), channel_id=1, source_target_pairs={{0,2},{2,0},{4,6},{6,4},{8,10},{10,8},{12,14},{14,12},{16,18},{18,... | collective-permute-start | bytes 110600 | tf_op jit(solution)/shard_map/ppermute | solution.py:37
  25.4 0.6 %collective-permute-done.8.rest_1_ = bf16[432,128]{1,0:T(8,128)(2,1)S(1)} collective-permute-done((bf16[432,128]{1,0:T(8,128)(2,1)S(1)}, bf16[432,128]{1,0:T(8,128)(2,1)S(1)}, u32[]{:S(2)}, u32[]{:S(2)}) %collective-permute-start.8) | collective-permute-done | bytes 110624 | tf_op jit(solution)/shard_map/ppermute | solution.py:391
  26.6 3.1 %collective-permute-start.10 = (bf16[432,128]{1,0:T(8,128)(2,1)S(1)}, bf16[432,128]{1,0:T(8,128)(2,1)S(1)}, u32[]{:S(2)}, u32[]{:S(2)}) collective-permute-start(bf16[432,128]{1,0:T(8,128)(2,1)S(1)} %shard_map.84.rest_3_), channel_id=1, source_target_pairs={{0,6},{1,7},{2,4},{3,5},{4,2},{5,3},{6,0},{7,1},{8,25},{9,24},{10,... | collective-permute-start | bytes 331784 | tf_op jit(solution)/shard_map/ppermute | solution.py:391
  29.7 1.4 %collective-permute-start.11 = (bf16[432,128]{1,0:T(8,128)(2,1)S(1)}, bf16[432,128]{1,0:T(8,128)(2,1)S(1)}, u32[]{:S(2)}, u32[]{:S(2)}) collective-permute-start(bf16[432,128]{1,0:T(8,128)(2,1)S(1)} %shard_map.84.rest_3_), channel_id=1, source_target_pairs={{0,4},{1,5},{2,6},{3,7},{4,0},{5,1},{6,2},{7,3},{8,24},{9,25},{10,... | collective-permute-start | bytes 331784 | tf_op jit(solution)/shard_map/ppermute | solution.py:391
  31.2 4.2 %shard_map.82 = (bf16[4,8,64,128]{3,2,1,0:T(8,128)(2,1)}, f32[8,128]{1,0:T(8,128)S(1)}) custom-call(s32[4,27]{1,0:T(4,128)S(1)} %bitcast.22, bf16[4,8,64,128]{3,2,1,0:T(8,128)(2,1)S(1)} %get-tuple-element.36.bricks, bf16[384,1152]{1,0:T(8,128)(2,1)S(1)} %get-tuple-element.37.taps, bf16[144,128]{1,0:T(8,128)(2,1)S(1)} %collective-permute-done.4.rest_0_, ...), custom_call_target="tpu_custom_call" | custom-call | flops 5000000000 | bytes 65536 | tf_op jit(solution)/shard_map/pallas_call | solution.py:553
  35.4 1.4 %collective-permute-done.11.rest_1_ = bf16[432,128]{1,0:T(8,128)(2,1)S(1)} collective-permute-done((bf16[432,128]{1,0:T(8,128)(2,1)S(1)}, bf16[432,128]{1,0:T(8,128)(2,1)S(1)}, u32[]{:S(2)}, u32[]{:S(2)}) %collective-permute-start.11) | collective-permute-done | bytes 110624 | tf_op jit(solution)/shard_map/ppermute | solution.py:391
  36.8 1.6 %collective-permute-start.13 = (bf16[432,128]{1,0:T(8,128)(2,1)S(1)}, bf16[432,128]{1,0:T(8,128)(2,1)S(1)}, u32[]{:S(2)}, u32[]{:S(2)}) collective-permute-start(bf16[432,128]{1,0:T(8,128)(2,1)S(1)} %shard_map.85.rest_3_), channel_id=1, source_target_pairs={{0,17},{1,16},{2,19},{3,18},{4,21},{5,20},{6,23},{7,22},{8,14},{9,... | collective-permute-start | bytes 331784 | tf_op jit(solution)/shard_map/ppermute | solution.py:391
  39.0 1.4 %collective-permute-start.15 = (bf16[432,128]{1,0:T(8,128)(2,1)S(1)}, bf16[432,128]{1,0:T(8,128)(2,1)S(1)}, u32[]{:S(2)}, u32[]{:S(2)}) collective-permute-start(bf16[432,128]{1,0:T(8,128)(2,1)S(1)} %shard_map.85.rest_3_), channel_id=1, source_target_pairs={{0,1},{1,0},{2,3},{3,2},{4,5},{5,4},{6,7},{7,6},{8,10},{9,11},{10,... | collective-permute-start | bytes 331784 | tf_op jit(solution)/shard_map/ppermute | solution.py:391
  40.4 2.2 %collective-permute-done.13.rest_0_ = bf16[432,128]{1,0:T(8,128)(2,1)S(1)} collective-permute-done((bf16[432,128]{1,0:T(8,128)(2,1)S(1)}, bf16[432,128]{1,0:T(8,128)(2,1)S(1)}, u32[]{:S(2)}, u32[]{:S(2)}) %collective-permute-start.13) | collective-permute-done | bytes 110624 | tf_op jit(solution)/shard_map/ppermute | solution.py:391
  42.5 0.6 %collective-permute-done.14.rest_1_ = bf16[432,128]{1,0:T(8,128)(2,1)S(1)} collective-permute-done((bf16[432,128]{1,0:T(8,128)(2,1)S(1)}, bf16[432,128]{1,0:T(8,128)(2,1)S(1)}, u32[]{:S(2)}, u32[]{:S(2)}) %collective-permute-start.14) | collective-permute-done | bytes 110624 | tf_op jit(solution)/shard_map/ppermute | solution.py:391
  43.8 1.0 %shard_map.87.rest_0_ = f32[27,2,64,128]{3,2,1,0:T(8,128)} custom-call(s32[1]{0:T(128)} %bitcast.9.at, bf16[1728,128]{1,0:T(8,128)(2,1)S(1)} %bitcast.19), custom_call_target="tpu_custom_call" | custom-call | flops 1000000000 | bytes 65536 | tf_op jit(solution)/shard_map/pallas_call | solution.py:464
  44.8 0.8 %collective-permute-done.16.half = bf16[1728,128]{1,0:T(8,128)(2,1)S(1)} collective-permute-done((bf16[1728,128]{1,0:T(8,128)(2,1)S(1)}, bf16[1728,128]{1,0:T(8,128)(2,1)S(1)}, u32[]{:S(2)}, u32[]{:S(2)}) %collective-permute-start.16) | collective-permute-done | bytes 442400 | tf_op jit(solution)/shard_map/ppermute | solution.py:397
  45.6 1.0 %shard_map.88 = f32[27,2,64,128]{3,2,1,0:T(8,128)} custom-call(s32[1]{0:T(128)S(6)} %sub.7.at, bf16[1728,128]{1,0:T(8,128)(2,1)S(1)} %collective-permute-done.16.half, f32[27,2,64,128]{3,2,1,0:T(8,128)} %shard_map.87.rest_0_), custom_call_target="tpu_custom_call", output_to_operand_aliasing={{}: (2, {})} | custom-call | flops 1000000000 | bytes 65536 | tf_op jit(solution)/shard_map/pallas_call | solution.py:465
  (31 shorter events, 2.5 us)
Async XLA Ops:
  0.6 4.3 %copy-start.2 = (s32[1,1,1,4,27]{4,3,2,1,0:T(4,128)S(1)}, s32[1,1,1,4,27]{4,3,2,1,0:T(4,128)}, u32[]{:S(2)}) copy-start(s32[1,1,1,4,27]{4,3,2,1,0:T(4,128)} %param.8) | copy-start | bytes 1300
  0.6 4.3 %copy-start = (bf16[3456,128]{1,0:T(8,128)(2,1)S(1)}, bf16[3456,128]{1,0:T(8,128)(2,1)}, u32[]{:S(2)}) copy-start(bf16[3456,128]{1,0:T(8,128)(2,1)} %param.6) | copy-start | bytes 2654212
  1.9 5.0 %collective-permute-start = (bf16[160,128]{1,0:T(8,128)(2,1)S(1)}, bf16[160,128]{1,0:T(8,128)(2,1)S(1)}, u32[]{:S(2)}, u32[]{:S(2)}) collective-permute-start(bf16[160,128]{1,0:T(8,128)(2,1)S(1)} %get-tuple-element.32), channel_id=1, source_target_pairs={{0,1},{1,0},{8,9},{9,8},{16,17},{17,16},{24,25},{25,24},{2,3},{3,2... | collective-permute-start | bytes 122888 | tf_op jit(solution)/shard_map/ppermute | solution.py:37
  6.9 4.9 %collective-permute-start.1 = (bf16[144,128]{1,0:T(8,128)(2,1)S(1)}, bf16[144,128]{1,0:T(8,128)(2,1)S(1)}, u32[]{:S(2)}, u32[]{:S(2)}) collective-permute-start(bf16[144,128]{1,0:T(8,128)(2,1)S(1)} %get-tuple-element.33), channel_id=1, source_target_pairs={{0,2},{2,0},{4,6},{6,4},{8,10},{10,8},{12,14},{14,12},{16,18},{18,... | collective-permute-start | bytes 110600 | tf_op jit(solution)/shard_map/ppermute | solution.py:37
  9.0 2.8 %collective-permute-start.2 = (bf16[144,128]{1,0:T(8,128)(2,1)S(1)}, bf16[144,128]{1,0:T(8,128)(2,1)S(1)}, u32[]{:S(2)}, u32[]{:S(2)}) collective-permute-start(bf16[144,128]{1,0:T(8,128)(2,1)S(1)} %get-tuple-element.34), channel_id=1, source_target_pairs={{0,8},{2,4},{4,2},{6,14},{8,0},{10,12},{12,10},{14,6},{16,24},{18,... | collective-permute-start | bytes 110600 | tf_op jit(solution)/shard_map/ppermute | solution.py:37
  9.1 2.8 %copy-start.1 = (bf16[1,1,1,4,512,128]{5,4,3,2,1,0:T(8,128)(2,1)S(1)}, bf16[1,1,1,4,512,128]{5,4,3,2,1,0:T(8,128)(2,1)}, u32[]{:S(2)}) copy-start(bf16[1,1,1,4,512,128]{5,4,3,2,1,0:T(8,128)(2,1)} %param.7) | copy-start | bytes 1572868
  9.1 2.8 %copy-start.3 = (s32[1,1,1,8,2]{3,4,2,1,0:T(2,128)S(1)}, s32[1,1,1,8,2]{3,4,2,1,0:T(2,128)}, u32[]{:S(2)}) copy-start(s32[1,1,1,8,2]{3,4,2,1,0:T(2,128)} %param.9) | copy-start | bytes 196
  16.6 2.1 %collective-permute-start.6 = (bf16[1728,128]{1,0:T(8,128)(2,1)S(1)}, bf16[1728,128]{1,0:T(8,128)(2,1)S(1)}, u32[]{:S(2)}, u32[]{:S(2)}) collective-permute-start(bf16[1728,128]{1,0:T(8,128)(2,1)S(1)} %get-tuple-element.45), channel_id=1, source_target_pairs={{0,8},{1,9},{2,10},{3,11},{4,12},{5,13},{6,14},{7,15},{8,0},{9,1},... | collective-permute-start | bytes 1327112 | tf_op jit(solution)/shard_map/ppermute | solution.py:397
  17.2 5.2 %collective-permute-start.3 = (bf16[160,128]{1,0:T(8,128)(2,1)S(1)}, bf16[160,128]{1,0:T(8,128)(2,1)S(1)}, u32[]{:S(2)}, u32[]{:S(2)}) collective-permute-start(bf16[160,128]{1,0:T(8,128)(2,1)S(1)} %get-tuple-element.40), channel_id=1, source_target_pairs={{0,1},{1,0},{8,9},{9,8},{16,17},{17,16},{24,25},{25,24},{2,3},{3,2... | collective-permute-start | bytes 122888 | tf_op jit(solution)/shard_map/ppermute | solution.py:37
  18.8 6.6 %collective-permute-start.7 = (bf16[432,128]{1,0:T(8,128)(2,1)S(1)}, bf16[432,128]{1,0:T(8,128)(2,1)S(1)}, u32[]{:S(2)}, u32[]{:S(2)}) collective-permute-start(bf16[432,128]{1,0:T(8,128)(2,1)S(1)} %get-tuple-element.47), channel_id=1, source_target_pairs={{0,17},{1,16},{2,19},{3,18},{4,21},{5,20},{6,23},{7,22},{8,14},{9,... | collective-permute-start | bytes 331784 | tf_op jit(solution)/shard_map/ppermute | solution.py:391
  21.2 4.7 %collective-permute-start.8 = (bf16[432,128]{1,0:T(8,128)(2,1)S(1)}, bf16[432,128]{1,0:T(8,128)(2,1)S(1)}, u32[]{:S(2)}, u32[]{:S(2)}) collective-permute-start(bf16[432,128]{1,0:T(8,128)(2,1)S(1)} %get-tuple-element.48), channel_id=1, source_target_pairs={{0,16},{1,17},{2,18},{3,19},{4,20},{5,21},{6,22},{7,23},{8,12},{9,... | collective-permute-start | bytes 331784 | tf_op jit(solution)/shard_map/ppermute | solution.py:391
  21.8 4.7 %collective-permute-start.9 = (bf16[432,128]{1,0:T(8,128)(2,1)S(1)}, bf16[432,128]{1,0:T(8,128)(2,1)S(1)}, u32[]{:S(2)}, u32[]{:S(2)}) collective-permute-start(bf16[432,128]{1,0:T(8,128)(2,1)S(1)} %get-tuple-element.49), channel_id=1, source_target_pairs={{0,1},{1,0},{2,3},{3,2},{4,5},{5,4},{6,7},{7,6},{8,10},{9,11},{10,... | collective-permute-start | bytes 331784 | tf_op jit(solution)/shard_map/ppermute | solution.py:391
  22.4 8.7 %collective-permute-start.4 = (bf16[144,128]{1,0:T(8,128)(2,1)S(1)}, bf16[144,128]{1,0:T(8,128)(2,1)S(1)}, u32[]{:S(2)}, u32[]{:S(2)}) collective-permute-start(bf16[144,128]{1,0:T(8,128)(2,1)S(1)} %get-tuple-element.41), channel_id=1, source_target_pairs={{0,2},{2,0},{4,6},{6,4},{8,10},{10,8},{12,14},{14,12},{16,18},{18,... | collective-permute-start | bytes 110600 | tf_op jit(solution)/shard_map/ppermute | solution.py:37
  25.4 5.8 %collective-permute-start.5 = (bf16[144,128]{1,0:T(8,128)(2,1)S(1)}, bf16[144,128]{1,0:T(8,128)(2,1)S(1)}, u32[]{:S(2)}, u32[]{:S(2)}) collective-permute-start(bf16[144,128]{1,0:T(8,128)(2,1)S(1)} %get-tuple-element.42.rest_3_), channel_id=1, source_target_pairs={{0,8},{2,4},{4,2},{6,14},{8,0},{10,12},{12,10},{14,6},{16,24},{18,... | collective-permute-start | bytes 110600 | tf_op jit(solution)/shard_map/ppermute | solution.py:37
  26.6 8.8 %collective-permute-start.10 = (bf16[432,128]{1,0:T(8,128)(2,1)S(1)}, bf16[432,128]{1,0:T(8,128)(2,1)S(1)}, u32[]{:S(2)}, u32[]{:S(2)}) collective-permute-start(bf16[432,128]{1,0:T(8,128)(2,1)S(1)} %shard_map.84.rest_3_), channel_id=1, source_target_pairs={{0,6},{1,7},{2,4},{3,5},{4,2},{5,3},{6,0},{7,1},{8,25},{9,24},{10,... | collective-permute-start | bytes 331784 | tf_op jit(solution)/shard_map/ppermute | solution.py:391
  29.7 7.0 %collective-permute-start.11 = (bf16[432,128]{1,0:T(8,128)(2,1)S(1)}, bf16[432,128]{1,0:T(8,128)(2,1)S(1)}, u32[]{:S(2)}, u32[]{:S(2)}) collective-permute-start(bf16[432,128]{1,0:T(8,128)(2,1)S(1)} %shard_map.84.rest_3_), channel_id=1, source_target_pairs={{0,4},{1,5},{2,6},{3,7},{4,0},{5,1},{6,2},{7,3},{8,24},{9,25},{10,... | collective-permute-start | bytes 331784 | tf_op jit(solution)/shard_map/ppermute | solution.py:391
  31.1 5.6 %collective-permute-start.12 = (bf16[432,128]{1,0:T(8,128)(2,1)S(1)}, bf16[432,128]{1,0:T(8,128)(2,1)S(1)}, u32[]{:S(2)}, u32[]{:S(2)}) collective-permute-start(bf16[432,128]{1,0:T(8,128)(2,1)S(1)} %shard_map.84.rest_3_), channel_id=1, source_target_pairs={{0,2},{1,3},{2,0},{3,1},{4,6},{5,7},{6,4},{7,5},{8,9},{9,8},{10,11... | collective-permute-start | bytes 331784 | tf_op jit(solution)/shard_map/ppermute | solution.py:391
  36.8 5.7 %collective-permute-start.13 = (bf16[432,128]{1,0:T(8,128)(2,1)S(1)}, bf16[432,128]{1,0:T(8,128)(2,1)S(1)}, u32[]{:S(2)}, u32[]{:S(2)}) collective-permute-start(bf16[432,128]{1,0:T(8,128)(2,1)S(1)} %shard_map.85.rest_3_), channel_id=1, source_target_pairs={{0,17},{1,16},{2,19},{3,18},{4,21},{5,20},{6,23},{7,22},{8,14},{9,... | collective-permute-start | bytes 331784 | tf_op jit(solution)/shard_map/ppermute | solution.py:391
  38.4 4.7 %collective-permute-start.14 = (bf16[432,128]{1,0:T(8,128)(2,1)S(1)}, bf16[432,128]{1,0:T(8,128)(2,1)S(1)}, u32[]{:S(2)}, u32[]{:S(2)}) collective-permute-start(bf16[432,128]{1,0:T(8,128)(2,1)S(1)} %shard_map.85.rest_3_), channel_id=1, source_target_pairs={{0,16},{1,17},{2,18},{3,19},{4,20},{5,21},{6,22},{7,23},{8,12},{9,... | collective-permute-start | bytes 331784 | tf_op jit(solution)/shard_map/ppermute | solution.py:391
  39.0 4.7 %collective-permute-start.15 = (bf16[432,128]{1,0:T(8,128)(2,1)S(1)}, bf16[432,128]{1,0:T(8,128)(2,1)S(1)}, u32[]{:S(2)}, u32[]{:S(2)}) collective-permute-start(bf16[432,128]{1,0:T(8,128)(2,1)S(1)} %shard_map.85.rest_3_), channel_id=1, source_target_pairs={{0,1},{1,0},{2,3},{3,2},{4,5},{5,4},{6,7},{7,6},{8,10},{9,11},{10,... | collective-permute-start | bytes 331784 | tf_op jit(solution)/shard_map/ppermute | solution.py:391
  43.8 1.9 %collective-permute-start.16 = (bf16[1728,128]{1,0:T(8,128)(2,1)S(1)}, bf16[1728,128]{1,0:T(8,128)(2,1)S(1)}, u32[]{:S(2)}, u32[]{:S(2)}) collective-permute-start(bf16[1728,128]{1,0:T(8,128)(2,1)S(1)} %bitcast.18), channel_id=1, source_target_pairs={{0,8},{1,9},{2,10},{3,11},{4,12},{5,13},{6,14},{7,15},{8,0},{9,1},... | collective-permute-start | bytes 1327112 | tf_op jit(solution)/shard_map/ppermute | solution.py:397

commit v5 on v4

--- a/solution.py
+++ b/solution.py
@@ -211,55 +211,44 @@
         join_along_x(face, box, y_boxes, step_x, send)
 
 
-def layout_kernel(table, bricks, weight, forward, backward, views, store):
+def layout_kernel(table, bricks, weight, forward, views, preact, store):
     slots = bricks.shape[0]
     for tap in range(27):
         far, near = tap // 3 * 128, tap % 3 * 128
         forward[far : far + 128, near : near + 128] = weight[tap]
-        backward[near : near + 128, far : far + 128] = weight[26 - tap]
     store[0:slots] = bricks[...]
     store[slots] = jnp.zeros(store.shape[1:], BF16)
     for slot in range(slots):
         fill_views(views.at[slot], store, lookup(table, slot, 0, slots, slots))
-
-
-def own_kernel(views, taps, preact):
-    for slot in range(views.shape[0]):
+    own_products(views, forward, preact, range(slots // 2))
+
+
+def own_products(views, taps, preact, which):
+    for slot in which:
         parts = jnp.dot(lhs_of(views.at[slot]), taps[...], preferred_element_type=F32)
         preact[slot] = join_taps(parts).reshape(EDGE, EDGE, EDGE, 128)
 
 
-def forward_kernel(counts, send, factor, table_vmem, lists_vmem, own_views, own_preact, cotangent, taps, *rest):
-    tiles_x, tiles_y = tiles_here(counts)
-    number_x, number_y = len(tiles_x), len(tiles_y)
-    x_boxes, y_boxes, rest = rest[:number_x], rest[number_x : number_x + number_y], rest[number_x + number_y :]
-    views, preacts, activated, grads, kept_term, sent_term = rest[:6]
-    faces_out, boxes_out = rest[6 : 6 + number_x], rest[6 + number_x : 6 + number_x + number_y]
-    store, sides, table, lists, sems = rest[6 + number_x + number_y :]
-    copies = [
-        pltpu.make_async_copy(table_vmem, table, sems.at[0]),
-        pltpu.make_async_copy(lists_vmem, lists, sems.at[1]),
-    ]
-    for copy in copies:
-        copy.start()
-    core = lax.axis_index("dp") % CORES
-    slots = cotangent.shape[0]
-    fill_remote(store, 0, x_boxes, y_boxes, tiles_x, tiles_y, send)
-    for copy in copies:
-        copy.wait()
+def own_kernel(views, taps, begun, preact):
+    own_products(views, taps, preact, range(views.shape[0] // 2, views.shape[0]))
+
+
+def add_remote(views, store, table, send, sides=None):
+    slots = views.shape[0]
     nothing = jnp.zeros((EDGE, EDGE, 128), F32)
     for slot in range(slots):
         rows = slice(slot * PLANE, (slot + 1) * PLANE)
         entry = lookup(table, slot, slots, slots + 8 * send, store.shape[0] - 1)
         for side, off_x, source, target in ((0, -1, EDGE - 1, 0), (1, 1, 0, EDGE + 1)):
             plane = view_of(store, entry, off_x, source)
-            sides[side, rows] = plane
+            if sides is not None:
+                sides[side, rows] = plane
             views[slot, target] = views[slot, target] + plane
         for side, off_y, base, lanes in ((2, -1, 0, 0), (3, 1, PLANE - 16, 256)):
             group = slice(PLANE - 16, PLANE) if off_y < 0 else slice(0, 16)
             edge = low_or_high(store[entry(0, off_y), :, group, :], off_y < 0)
             padded = jnp.concatenate([nothing[:1], edge, nothing[:1]], axis=0)
-            for dx in range(3):
+            for dx in range(3 if sides is not None else 0):
                 sides[side, rows, 128 * dx : 128 * dx + 128] = (
                     padded[dx : dx + EDGE].reshape(PLANE, 128).astype(BF16)
                 )
@@ -267,6 +256,19 @@
             wide = jnp.concatenate(both, axis=1).astype(BF16)
             at = (slot, slice(1, EDGE + 1), slice(base, base + 16), slice(lanes, lanes + 128))
             views[at] = views[at] + wide
+
+
+def forward_kernel(counts, send, factor, table, lists, own_views, own_preact, cotangent, taps, *rest):
+    tiles_x, tiles_y = tiles_here(counts)
+    number_x, number_y = len(tiles_x), len(tiles_y)
+    x_boxes, y_boxes, rest = rest[:number_x], rest[number_x : number_x + number_y], rest[number_x + number_y :]
+    views, preacts, activated, grads, kept_term, sent_term = rest[:6]
+    faces_out, boxes_out = rest[6 : 6 + number_x], rest[6 + number_x : 6 + number_x + number_y]
+    store, sides = rest[6 + number_x + number_y :]
+    core = lax.axis_index("dp") % CORES
+    slots = cotangent.shape[0]
+    fill_remote(store, 0, x_boxes, y_boxes, tiles_x, tiles_y, send)
+    add_remote(views, store, table, send, sides)
     added = []
     for side in range(4):
         if side < 2:
@@ -313,19 +315,25 @@
             term[27 * half :] = jnp.zeros((term.shape[0] - 27 * half, 128), term.dtype)
 
 
-def backward_kernel(counts, send, table, bricks, taps, *rest):
+def back_layout_kernel(table, bricks, weight, backward, views, store):
+    slots = bricks.shape[0]
+    for tap in range(27):
+        far, near = tap // 3 * 128, tap % 3 * 128
+        backward[far : far + 128, near : near + 128] = weight[26 - tap].T
+    store[0:slots] = bricks[...]
+    store[slots] = jnp.zeros(store.shape[1:], BF16)
+    for slot in range(slots):
+        fill_views(views.at[slot], store, lookup(table, slot, 0, slots, slots))
+
+
+def backward_kernel(counts, send, table, own_views, taps, *rest):
     tiles_x, tiles_y = tiles_here(counts)
     x_boxes, y_boxes = rest[: len(tiles_x)], rest[len(tiles_x) : len(tiles_x) + len(tiles_y)]
-    result, ready, store, views = rest[-4:]
-    slots = bricks.shape[0]
-    store[0:slots] = bricks[...]
-    fill_remote(store, slots, x_boxes, y_boxes, tiles_x, tiles_y, send)
-    zero_at = store.shape[0] - 1
-    for slot in range(slots):
-        fill_views(views.at[slot], store, lookup(table, slot, 0, zero_at, zero_at))
-        parts = lax.dot_general(
-            lhs_of(views.at[slot]), taps[...], (((1,), (1,)), ((), ())), preferred_element_type=F32
-        )
+    views, result, ready, store = rest[-4:]
+    fill_remote(store, 0, x_boxes, y_boxes, tiles_x, tiles_y, send)
+    add_remote(views, store, table, send)
+    for slot in range(views.shape[0]):
+        parts = jnp.dot(lhs_of(views.at[slot]), taps[...], preferred_element_type=F32)
         result[slot] = join_taps(parts).reshape(EDGE, PLANE, 128).astype(BF16)
     ready[...] = jnp.zeros(ready.shape, F32)
 
@@ -410,9 +418,9 @@
         box[...] = (kept[at] + arrived[at].astype(F32)).astype(BF16)
 
 
-def first_sum_kernel(own, *rest):
+def first_sum_kernel(boxes, own, *rest):
     total = own[...]
-    for box in rest[:-2]:
+    for box in rest[:boxes]:
         total = total + box[...].astype(F32)
     rest[-1][...] = total.astype(BF16)
 
@@ -449,7 +457,10 @@
         [VMEM] * group,
     )(mine, kept.reshape(shares), arrived.reshape(shares))
     boxes = groups.swaps(boxes, 0)
-    rounded = run(first_sum_kernel, share_type, [VMEM] * group + [ANY], VMEM)(own, *boxes, early)
+    first_sum = functools.partial(first_sum_kernel, group - 1)
+    rounded = run(first_sum, share_type, [VMEM] * group + [ANY] * len(early), VMEM)(
+        own, *boxes, *early
+    )
     boxes = groups.swaps([rounded] * (line - 1), 1) + [rounded]
     rounded = run(second_sum_kernel, share_type, [VMEM] * line + [ANY], VMEM)(*boxes, late)
     boxes = groups.swaps([rounded] * (group - 1), 0) + [rounded]
@@ -472,6 +483,7 @@
     devices = lax.axis_size("dp") * counts[0] * counts[1]
     bricks = features.reshape(slots, EDGE, PLANE, channels)
     cot = cotangent.reshape(slots, EDGE, PLANE, channels)
+    blocks = weight.reshape(27, channels, channels)
     table = neighbours.reshape(slots, 27)
     lists = send_slots.reshape(8, send).T
     factor = 1.0 / math.sqrt(float(devices * slots * EDGE * PLANE))
@@ -481,6 +493,7 @@
     x_type = jax.ShapeDtypeStruct((send * (PLANE + number_y * EDGE), 128), BF16)
     bricks_type = jax.ShapeDtypeStruct(bricks.shape, BF16)
     views_type = jax.ShapeDtypeStruct((slots, EDGE + 2, PLANE, 384), BF16)
+    taps_type = jax.ShapeDtypeStruct((1152, 384), BF16)
     preact_type = jax.ShapeDtypeStruct((slots, EDGE, EDGE, EDGE, 128), F32)
     groups = Groups()
     block = 16 * groups.plane
@@ -509,20 +522,22 @@
     )(*[pltpu.with_memory_space_constraint(x, pltpu.HBM) for x in (lists, bricks)])
     faces, y_boxes = boxes[:number_x], boxes[number_x:]
     y_boxes = swapped(y_boxes, "gy", phases_y)
-    taps, back_taps, views = run(
+    taps, views, preacts = run(
         layout_kernel,
         [
-            jax.ShapeDtypeStruct((1152, 384), BF16),
-            jax.ShapeDtypeStruct((384, 1152), BF16),
+            taps_type,
             views_type,
+            preact_type,
         ],
         [SMEM, VMEM, VMEM],
         [VMEM] * 3,
         [store_of(slots + 1)],
         micros=2.0,
-    )(table, bricks, weight.reshape(27, channels, channels))
+    )(table, bricks, blocks)
     x_boxes = swapped(join(*faces, *y_boxes), "gx", phases_x)
-    preacts = run(own_kernel, preact_type, [VMEM, VMEM], VMEM, micros=4.0)(views, taps)
+    preacts = run(own_kernel, preact_type, [VMEM] * 3, VMEM, aliases={2: 0}, micros=4.0)(
+        views, taps, preacts
+    )
     _, _, activated, grads, kept, sent, *boxes = run(
         functools.partial(forward_kernel, counts, send, factor),
         [
@@ -535,30 +550,28 @@
         ]
         + [face_type] * number_x
         + [y_type] * number_y,
+        [SMEM, SMEM] + [VMEM] * (4 + number_x + number_y),
         [VMEM] * (6 + number_x + number_y),
-        [VMEM] * (6 + number_x + number_y),
-        [
-            store_of(8 * send + 1),
-            pltpu.VMEM((4, slots * PLANE, 384), BF16),
-            pltpu.SMEM(table.shape, jnp.int32),
-            pltpu.SMEM(lists.shape, jnp.int32),
-            pltpu.SemaphoreType.DMA((2,)),
-        ],
+        [store_of(8 * send + 1), pltpu.VMEM((4, slots * PLANE, 384), BF16)],
         aliases={2: 0, 3: 1},
         micros=5.0,
     )(table, lists, views, preacts, cot, taps, *x_boxes, *y_boxes)
     faces, y_boxes = boxes[:number_x], swapped(boxes[number_x:], "gy", phases_y)
     packed = join(*faces, *y_boxes)
     x_boxes = swapped(packed, "gx", phases_x)
-    input_grad, ready = run(
+    back_taps, views = run(
+        back_layout_kernel, [taps_type, views_type], [SMEM, VMEM, VMEM], [VMEM, VMEM], [store_of(slots + 1)]
+    )(table, grads, blocks)
+    _, input_grad, ready = run(
         functools.partial(backward_kernel, counts, send),
-        [bricks_type, jax.ShapeDtypeStruct((8, 128), F32)],
+        [views_type, bricks_type, jax.ShapeDtypeStruct((8, 128), F32)],
         [SMEM, VMEM, VMEM] + [VMEM] * (number_x + number_y),
-        [VMEM, VMEM],
-        [store_of(slots + 8 * send + 1), pltpu.VMEM(views_type.shape, BF16)],
+        [VMEM] * 3,
+        [store_of(8 * send + 1)],
+        aliases={1: 0},
         micros=5.0,
-    )(table, grads, back_taps, *x_boxes, *y_boxes)
-    weight_grad = summed_everywhere(groups, kept, sent, packed[-1], ready)
+    )(table, views, back_taps, *x_boxes, *y_boxes)
+    weight_grad = summed_everywhere(groups, kept, sent, [packed[-1], views], ready)
     return (
         activated.reshape(features.shape),
         input_grad.reshape(features.shape),

time: 46.7 us -> 46.1 us (0.987)
  waiting for transfers between devices: 7.55 us -> 6.81 us
  Pallas kernels: 16.3 us -> 16.8 us
  starting transfers between devices: 22 us -> 21.5 us
    pallas_call x4 -> x5, Pallas kernels: 8.11 us -> 9.05 us  [the longest x1 4.17 us: body(): run(functools.partial(backward_kernel, counts, send), [views_type, bricks...]
    ppermute x9, waiting for transfers between devices: 5.88 us -> 5.24 us  [swap(): return lax.ppermute(x, ('dp', 'gx', 'gy'), self.pairs(place))]
    ppermute x2, starting transfers between devices: 0.64 us -> 0.14 us  [swap_cores(): lax.ppermute(x, ('dp', 'gx', 'gy'), self.pairs(lambda a, b, c: (a ^ 1, b,...]
  transfers between devices with their start and end apart: 17 -> 17, of which waited for: 8 -> 7; matrix products, arithmetic and copies ran while one was open for 0% -> 0% of each run, Pallas kernels for 20% -> 22%
where the time goes in v5:
time: 46.1 us; the launch traced here: 45.9 us
  starting transfers between devices  21.5 us (47%)
  Pallas kernels  16.8 us (36%)
  waiting for transfers between devices  6.81 us (15%)
  between operations  0.81 us (2%)
    ppermute x9, starting transfers between devices, swap(): return lax.ppermute(x, ('dp', 'gx', 'gy'), self.pairs(place))  11.9 us
    ppermute x6, starting transfers between devices, swap(): return lax.ppermute(x, ('dp', axis), pairs)  9.48 us
    ppermute x9, waiting for transfers between devices, swap(): return lax.ppermute(x, ('dp', 'gx', 'gy'), self.pairs(place))  5.24 us
    pallas_call x1, Pallas kernels, body(): run(functools.partial(forward_kernel, counts, send, factor), [views_type,...  4.32 us
    pallas_call x1, Pallas kernels, body(): run(functools.partial(backward_kernel, counts, send), [views_type, bricks...  4.17 us
    pallas_call x1, Pallas kernels, body(): run(layout_kernel, [taps_type, views_type, preact_type], [SMEM, VMEM, VME...  2.29 us
    pallas_call x1, Pallas kernels, body(): run(own_kernel, preact_type, [VMEM] * 3, VMEM, aliases={2: 0}, micros=4.0)  1.46 us
    pallas_call x1, Pallas kernels, body(): run(functools.partial(start_kernel, counts, send), [bricks_type] + [face_...  1.22 us
  transfers between devices with their start and end apart: 17, of which 7 were waited for; matrix products, arithmetic and copies ran while one was open for 0% of the time, Pallas kernels for 22%

profile of v5, /device:TPU:0, one launch (start us, length us, event | category | flops | bytes accessed | tf_op | source)
XLA Modules:
  0.0 45.9 jit_solution(13146468037649054411)
XLA Ops:
  0.7 1.2 %shard_map.76 = (bf16[4,8,64,128]{3,2,1,0:T(8,128)(2,1)S(1)}, bf16[128,128]{1,0:T(8,128)(2,1)S(1)}, bf16[128,128]{1,0:T(8,128)(2,1)S(1)}, bf16[160,128]{1,0:T(8,128)(2,1)S(1)}) custom-call(s32[2,8]{1,0:T(2,128)} %bitcast.25, bf16[4,8,64,128]{3,2,1,0:T(8,128)(2,1)} %bitcast.29), custom_call_target="tpu_custom_call" | custom-call | flops 1000000000 | bytes 65536 | tf_op jit(solution)/shard_map/pallas_call | solution.py:516
  1.9 3.0 %collective-permute-start = (bf16[160,128]{1,0:T(8,128)(2,1)S(1)}, bf16[160,128]{1,0:T(8,128)(2,1)S(1)}, u32[]{:S(2)}, u32[]{:S(2)}) collective-permute-start(bf16[160,128]{1,0:T(8,128)(2,1)S(1)} %get-tuple-element.35), channel_id=1, source_target_pairs={{0,1},{1,0},{8,9},{9,8},{16,17},{17,16},{24,25},{25,24},{2,3},{3,2... | collective-permute-start | bytes 122888 | tf_op jit(solution)/shard_map/ppermute | solution.py:37
  4.9 2.3 %shard_map.77 = (bf16[1152,384]{1,0:T(8,128)(2,1)S(1)}, bf16[4,10,64,384]{3,2,1,0:T(8,128)(2,1)S(1)}, f32[4,8,8,8,128]{4,3,2,1,0:T(8,128)S(1)}) custom-call(s32[4,27]{1,0:T(4,128)S(1)} %bitcast.21, bf16[4,8,64,128]{3,2,1,0:T(8,128)(2,1)S(1)} %get-tuple-element.29.bricks, bf16[27,128,128]{2,1,0:T(8,128)(2,1)S(1)} %bitcast.15), custom_call_target="tpu_custom_call" | custom-call | flops 2000000000 | bytes 65536 | tf_op jit(solution)/shard_map/pallas_call | solution.py:525
  7.3 1.8 %collective-permute-start.1 = (bf16[144,128]{1,0:T(8,128)(2,1)S(1)}, bf16[144,128]{1,0:T(8,128)(2,1)S(1)}, u32[]{:S(2)}, u32[]{:S(2)}) collective-permute-start(bf16[144,128]{1,0:T(8,128)(2,1)S(1)} %get-tuple-element.36), channel_id=1, source_target_pairs={{0,2},{2,0},{4,6},{6,4},{8,10},{10,8},{12,14},{14,12},{16,18},{18,... | collective-permute-start | bytes 110600 | tf_op jit(solution)/shard_map/ppermute | solution.py:37
  9.1 1.5 %shard_map.78.own_preact = f32[4,8,8,8,128]{4,3,2,1,0:T(8,128)S(1)} custom-call(bf16[4,10,64,384]{3,2,1,0:T(8,128)(2,1)S(1)} %get-tuple-element.30.views.own_views, bf16[1152,384]{1,0:T(8,128)(2,1)S(1)} %get-tuple-element.31.taps, f32[4,8,8,8,128]{4,3,2,1,0:T(8,128)S(1)} %get-tuple-element.32.begun), custom_call_target="tpu_custom_call", output_to_operand_aliasing={{}: (2, {})} | custom-call | flops 4000000000 | bytes 65536 | tf_op jit(solution)/shard_map/pallas_call | solution.py:538
  10.5 0.8 %collective-permute-done.1.rest_0_ = bf16[144,128]{1,0:T(8,128)(2,1)S(1)} collective-permute-done((bf16[144,128]{1,0:T(8,128)(2,1)S(1)}, bf16[144,128]{1,0:T(8,128)(2,1)S(1)}, u32[]{:S(2)}, u32[]{:S(2)}) %collective-permute-start.1) | collective-permute-done | bytes 36896 | tf_op jit(solution)/shard_map/ppermute | solution.py:37
  11.3 4.3 %shard_map.80 = (bf16[4,10,64,384]{3,2,1,0:T(8,128)(2,1)S(1)}, f32[4,8,8,8,128]{4,3,2,1,0:T(8,128)S(1)}, bf16[4,8,64,128]{3,2,1,0:T(8,128)(2,1)}, bf16[4,8,64,12...) custom-call(s32[4,27]{1,0:T(4,128)S(1)} %bitcast.22, ...), custom_call_target="tpu_custom_call", output_to_operand_aliasing={{0}: (2, {}), {1}: (3, {})} | custom-call | flops 5000000000 | bytes 65536 | tf_op jit(solution)/shard_map/pallas_call | solution.py:541
  15.7 1.7 %collective-permute-start.3 = (bf16[160,128]{1,0:T(8,128)(2,1)S(1)}, bf16[160,128]{1,0:T(8,128)(2,1)S(1)}, u32[]{:S(2)}, u32[]{:S(2)}) collective-permute-start(bf16[160,128]{1,0:T(8,128)(2,1)S(1)} %get-tuple-element.44), channel_id=1, source_target_pairs={{0,1},{1,0},{8,9},{9,8},{16,17},{17,16},{24,25},{25,24},{2,3},{3,2... | collective-permute-start | bytes 122888 | tf_op jit(solution)/shard_map/ppermute | solution.py:37
  17.6 2.7 %collective-permute-start.7 = (bf16[432,128]{1,0:T(8,128)(2,1)S(1)}, bf16[432,128]{1,0:T(8,128)(2,1)S(1)}, u32[]{:S(2)}, u32[]{:S(2)}) collective-permute-start(bf16[432,128]{1,0:T(8,128)(2,1)S(1)} %get-tuple-element.51), channel_id=1, source_target_pairs={{0,17},{1,16},{2,19},{3,18},{4,21},{5,20},{6,23},{7,22},{8,14},{9,... | collective-permute-start | bytes 331784 | tf_op jit(solution)/shard_map/ppermute | solution.py:399
  20.2 0.5 %collective-permute-start.8 = (bf16[432,128]{1,0:T(8,128)(2,1)S(1)}, bf16[432,128]{1,0:T(8,128)(2,1)S(1)}, u32[]{:S(2)}, u32[]{:S(2)}) collective-permute-start(bf16[432,128]{1,0:T(8,128)(2,1)S(1)} %get-tuple-element.52), channel_id=1, source_target_pairs={{0,16},{1,17},{2,18},{3,19},{4,20},{5,21},{6,22},{7,23},{8,12},{9,... | collective-permute-start | bytes 331784 | tf_op jit(solution)/shard_map/ppermute | solution.py:399
  21.1 1.1 %shard_map.81 = (bf16[1152,384]{1,0:T(8,128)(2,1)S(1)}, bf16[4,10,64,384]{3,2,1,0:T(8,128)(2,1)S(1)}) custom-call(s32[4,27]{1,0:T(4,128)S(1)} %bitcast.23, bf16[4,8,64,128]{3,2,1,0:T(8,128)(2,1)S(1)} %get-tuple-element.39.bricks, bf16[27,128,128]{2,1,0:T(8,128)(2,1)S(1)} %bitcast.16), custom_call_target="tpu_custom_call" | custom-call | flops 1000000000 | bytes 65536 | tf_op jit(solution)/shard_map/pallas_call | solution.py:562
  22.3 2.9 %collective-permute-start.4 = (bf16[144,128]{1,0:T(8,128)(2,1)S(1)}, bf16[144,128]{1,0:T(8,128)(2,1)S(1)}, u32[]{:S(2)}, u32[]{:S(2)}) collective-permute-start(bf16[144,128]{1,0:T(8,128)(2,1)S(1)} %get-tuple-element.45), channel_id=1, source_target_pairs={{0,2},{2,0},{4,6},{6,4},{8,10},{10,8},{12,14},{14,12},{16,18},{18,... | collective-permute-start | bytes 110600 | tf_op jit(solution)/shard_map/ppermute | solution.py:37
  25.6 3.7 %collective-permute-start.10 = (bf16[432,128]{1,0:T(8,128)(2,1)S(1)}, bf16[432,128]{1,0:T(8,128)(2,1)S(1)}, u32[]{:S(2)}, u32[]{:S(2)}) collective-permute-start(bf16[432,128]{1,0:T(8,128)(2,1)S(1)} %shard_map.85.rest_3_), channel_id=1, source_target_pairs={{0,6},{1,7},{2,4},{3,5},{4,2},{5,3},{6,0},{7,1},{8,25},{9,24},{10,... | collective-permute-start | bytes 331784 | tf_op jit(solution)/shard_map/ppermute | solution.py:399
  29.3 0.6 %collective-permute-start.11 = (bf16[432,128]{1,0:T(8,128)(2,1)S(1)}, bf16[432,128]{1,0:T(8,128)(2,1)S(1)}, u32[]{:S(2)}, u32[]{:S(2)}) collective-permute-start(bf16[432,128]{1,0:T(8,128)(2,1)S(1)} %shard_map.85.rest_3_), channel_id=1, source_target_pairs={{0,4},{1,5},{2,6},{3,7},{4,0},{5,1},{6,2},{7,3},{8,24},{9,25},{10,... | collective-permute-start | bytes 331784 | tf_op jit(solution)/shard_map/ppermute | solution.py:399
  30.4 4.2 %shard_map.83 = (bf16[4,10,64,384]{3,2,1,0:T(8,128)(2,1)S(1)}, bf16[4,8,64,128]{3,2,1,0:T(8,128)(2,1)}, f32[8,128]{1,0:T(8,128)S(1)}) custom-call(s32[4,27]{1,0:T(4,128)S(1)} %bitcast.24, bf16[4,10,64,384]{3,2,1,0:T(8,128)(2,1)S(1)} %get-tuple-element.40.own_views.rest_4_, ...), custom_call_target="tpu_custom_call", output_to_operand_aliasing={{0}: (1, {})} | custom-call | flops 5000000000 | bytes 65536 | tf_op jit(solution)/shard_map/pallas_call | solution.py:565
  34.6 1.5 %collective-permute-done.11.rest_1_ = bf16[432,128]{1,0:T(8,128)(2,1)S(1)} collective-permute-done((bf16[432,128]{1,0:T(8,128)(2,1)S(1)}, bf16[432,128]{1,0:T(8,128)(2,1)S(1)}, u32[]{:S(2)}, u32[]{:S(2)}) %collective-permute-start.11) | collective-permute-done | bytes 110624 | tf_op jit(solution)/shard_map/ppermute | solution.py:399
  36.2 1.6 %collective-permute-start.13 = (bf16[432,128]{1,0:T(8,128)(2,1)S(1)}, bf16[432,128]{1,0:T(8,128)(2,1)S(1)}, u32[]{:S(2)}, u32[]{:S(2)}) collective-permute-start(bf16[432,128]{1,0:T(8,128)(2,1)S(1)} %shard_map.86.rest_3_), channel_id=1, source_target_pairs={{0,17},{1,16},{2,19},{3,18},{4,21},{5,20},{6,23},{7,22},{8,14},{9,... | collective-permute-start | bytes 331784 | tf_op jit(solution)/shard_map/ppermute | solution.py:399
  37.8 0.5 %collective-permute-start.14 = (bf16[432,128]{1,0:T(8,128)(2,1)S(1)}, bf16[432,128]{1,0:T(8,128)(2,1)S(1)}, u32[]{:S(2)}, u32[]{:S(2)}) collective-permute-start(bf16[432,128]{1,0:T(8,128)(2,1)S(1)} %shard_map.86.rest_3_), channel_id=1, source_target_pairs={{0,16},{1,17},{2,18},{3,19},{4,20},{5,21},{6,22},{7,23},{8,12},{9,... | collective-permute-start | bytes 331784 | tf_op jit(solution)/shard_map/ppermute | solution.py:399
  38.3 1.4 %collective-permute-start.15 = (bf16[432,128]{1,0:T(8,128)(2,1)S(1)}, bf16[432,128]{1,0:T(8,128)(2,1)S(1)}, u32[]{:S(2)}, u32[]{:S(2)}) collective-permute-start(bf16[432,128]{1,0:T(8,128)(2,1)S(1)} %shard_map.86.rest_3_), channel_id=1, source_target_pairs={{0,1},{1,0},{2,3},{3,2},{4,5},{5,4},{6,7},{7,6},{8,10},{9,11},{10,... | collective-permute-start | bytes 331784 | tf_op jit(solution)/shard_map/ppermute | solution.py:399
  39.7 2.2 %collective-permute-done.13.rest_0_ = bf16[432,128]{1,0:T(8,128)(2,1)S(1)} collective-permute-done((bf16[432,128]{1,0:T(8,128)(2,1)S(1)}, bf16[432,128]{1,0:T(8,128)(2,1)S(1)}, u32[]{:S(2)}, u32[]{:S(2)}) %collective-permute-start.13) | collective-permute-done | bytes 110624 | tf_op jit(solution)/shard_map/ppermute | solution.py:399
  41.9 0.6 %collective-permute-done.14.rest_1_ = bf16[432,128]{1,0:T(8,128)(2,1)S(1)} collective-permute-done((bf16[432,128]{1,0:T(8,128)(2,1)S(1)}, bf16[432,128]{1,0:T(8,128)(2,1)S(1)}, u32[]{:S(2)}, u32[]{:S(2)}) %collective-permute-start.14) | collective-permute-done | bytes 110624 | tf_op jit(solution)/shard_map/ppermute | solution.py:399
  43.2 1.0 %shard_map.88.rest_0_ = f32[27,2,64,128]{3,2,1,0:T(8,128)} custom-call(s32[1]{0:T(128)} %bitcast.9.at, bf16[1728,128]{1,0:T(8,128)(2,1)S(1)} %bitcast.20), custom_call_target="tpu_custom_call" | custom-call | flops 1000000000 | bytes 65536 | tf_op jit(solution)/shard_map/pallas_call | solution.py:475
  44.2 0.8 %collective-permute-done.16.half = bf16[1728,128]{1,0:T(8,128)(2,1)S(1)} collective-permute-done((bf16[1728,128]{1,0:T(8,128)(2,1)S(1)}, bf16[1728,128]{1,0:T(8,128)(2,1)S(1)}, u32[]{:S(2)}, u32[]{:S(2)}) %collective-permute-start.16) | collective-permute-done | bytes 442400 | tf_op jit(solution)/shard_map/ppermute | solution.py:405
  45.0 1.0 %shard_map.89 = f32[27,2,64,128]{3,2,1,0:T(8,128)} custom-call(s32[1]{0:T(128)S(6)} %sub.7.at, bf16[1728,128]{1,0:T(8,128)(2,1)S(1)} %collective-permute-done.16.half, f32[27,2,64,128]{3,2,1,0:T(8,128)} %shard_map.88.rest_0_), custom_call_target="tpu_custom_call", output_to_operand_aliasing={{}: (2, {})} | custom-call | flops 1000000000 | bytes 65536 | tf_op jit(solution)/shard_map/pallas_call | solution.py:476
  (32 shorter events, 2.2 us)
Async XLA Ops:
  0.6 4.3 %copy-start.2 = (s32[1,1,1,4,27]{4,3,2,1,0:T(4,128)S(1)}, s32[1,1,1,4,27]{4,3,2,1,0:T(4,128)}, u32[]{:S(2)}) copy-start(s32[1,1,1,4,27]{4,3,2,1,0:T(4,128)} %param.8) | copy-start | bytes 1300
  0.6 4.3 %copy-start = (bf16[3456,128]{1,0:T(8,128)(2,1)S(1)}, bf16[3456,128]{1,0:T(8,128)(2,1)}, u32[]{:S(2)}) copy-start(bf16[3456,128]{1,0:T(8,128)(2,1)} %param.6) | copy-start | bytes 2654212
  1.9 5.3 %collective-permute-start = (bf16[160,128]{1,0:T(8,128)(2,1)S(1)}, bf16[160,128]{1,0:T(8,128)(2,1)S(1)}, u32[]{:S(2)}, u32[]{:S(2)}) collective-permute-start(bf16[160,128]{1,0:T(8,128)(2,1)S(1)} %get-tuple-element.35), channel_id=1, source_target_pairs={{0,1},{1,0},{8,9},{9,8},{16,17},{17,16},{24,25},{25,24},{2,3},{3,2... | collective-permute-start | bytes 122888 | tf_op jit(solution)/shard_map/ppermute | solution.py:37
  7.3 4.0 %collective-permute-start.1 = (bf16[144,128]{1,0:T(8,128)(2,1)S(1)}, bf16[144,128]{1,0:T(8,128)(2,1)S(1)}, u32[]{:S(2)}, u32[]{:S(2)}) collective-permute-start(bf16[144,128]{1,0:T(8,128)(2,1)S(1)} %get-tuple-element.36), channel_id=1, source_target_pairs={{0,2},{2,0},{4,6},{6,4},{8,10},{10,8},{12,14},{14,12},{16,18},{18,... | collective-permute-start | bytes 110600 | tf_op jit(solution)/shard_map/ppermute | solution.py:37
  9.0 2.2 %collective-permute-start.2 = (bf16[144,128]{1,0:T(8,128)(2,1)S(1)}, bf16[144,128]{1,0:T(8,128)(2,1)S(1)}, u32[]{:S(2)}, u32[]{:S(2)}) collective-permute-start(bf16[144,128]{1,0:T(8,128)(2,1)S(1)} %get-tuple-element.37), channel_id=1, source_target_pairs={{0,8},{2,4},{4,2},{6,14},{8,0},{10,12},{12,10},{14,6},{16,24},{18,... | collective-permute-start | bytes 110600 | tf_op jit(solution)/shard_map/ppermute | solution.py:37
  9.1 2.2 %copy-start.1 = (bf16[1,1,1,4,512,128]{5,4,3,2,1,0:T(8,128)(2,1)S(1)}, bf16[1,1,1,4,512,128]{5,4,3,2,1,0:T(8,128)(2,1)}, u32[]{:S(2)}) copy-start(bf16[1,1,1,4,512,128]{5,4,3,2,1,0:T(8,128)(2,1)} %param.7) | copy-start | bytes 1572868
  9.1 2.2 %copy-start.3 = (s32[1,1,1,8,2]{3,4,2,1,0:T(2,128)S(1)}, s32[1,1,1,8,2]{3,4,2,1,0:T(2,128)}, u32[]{:S(2)}) copy-start(s32[1,1,1,8,2]{3,4,2,1,0:T(2,128)} %param.9) | copy-start | bytes 196
  15.6 1.9 %collective-permute-start.6 = (bf16[1728,128]{1,0:T(8,128)(2,1)S(1)}, bf16[1728,128]{1,0:T(8,128)(2,1)S(1)}, u32[]{:S(2)}, u32[]{:S(2)}) collective-permute-start(bf16[1728,128]{1,0:T(8,128)(2,1)S(1)} %get-tuple-element.49), channel_id=1, source_target_pairs={{0,8},{1,9},{2,10},{3,11},{4,12},{5,13},{6,14},{7,15},{8,0},{9,1},... | collective-permute-start | bytes 1327112 | tf_op jit(solution)/shard_map/ppermute | solution.py:405
  15.7 6.5 %collective-permute-start.3 = (bf16[160,128]{1,0:T(8,128)(2,1)S(1)}, bf16[160,128]{1,0:T(8,128)(2,1)S(1)}, u32[]{:S(2)}, u32[]{:S(2)}) collective-permute-start(bf16[160,128]{1,0:T(8,128)(2,1)S(1)} %get-tuple-element.44), channel_id=1, source_target_pairs={{0,1},{1,0},{8,9},{9,8},{16,17},{17,16},{24,25},{25,24},{2,3},{3,2... | collective-permute-start | bytes 122888 | tf_op jit(solution)/shard_map/ppermute | solution.py:37
  17.6 7.6 %collective-permute-start.7 = (bf16[432,128]{1,0:T(8,128)(2,1)S(1)}, bf16[432,128]{1,0:T(8,128)(2,1)S(1)}, u32[]{:S(2)}, u32[]{:S(2)}) collective-permute-start(bf16[432,128]{1,0:T(8,128)(2,1)S(1)} %get-tuple-element.51), channel_id=1, source_target_pairs={{0,17},{1,16},{2,19},{3,18},{4,21},{5,20},{6,23},{7,22},{8,14},{9,... | collective-permute-start | bytes 331784 | tf_op jit(solution)/shard_map/ppermute | solution.py:399
  20.2 4.9 %collective-permute-start.8 = (bf16[432,128]{1,0:T(8,128)(2,1)S(1)}, bf16[432,128]{1,0:T(8,128)(2,1)S(1)}, u32[]{:S(2)}, u32[]{:S(2)}) collective-permute-start(bf16[432,128]{1,0:T(8,128)(2,1)S(1)} %get-tuple-element.52), channel_id=1, source_target_pairs={{0,16},{1,17},{2,18},{3,19},{4,20},{5,21},{6,22},{7,23},{8,12},{9,... | collective-permute-start | bytes 331784 | tf_op jit(solution)/shard_map/ppermute | solution.py:399
  20.8 4.7 %collective-permute-start.9 = (bf16[432,128]{1,0:T(8,128)(2,1)S(1)}, bf16[432,128]{1,0:T(8,128)(2,1)S(1)}, u32[]{:S(2)}, u32[]{:S(2)}) collective-permute-start(bf16[432,128]{1,0:T(8,128)(2,1)S(1)} %get-tuple-element.53), channel_id=1, source_target_pairs={{0,1},{1,0},{2,3},{3,2},{4,5},{5,4},{6,7},{7,6},{8,10},{9,11},{10,... | collective-permute-start | bytes 331784 | tf_op jit(solution)/shard_map/ppermute | solution.py:399
  22.3 8.1 %collective-permute-start.4 = (bf16[144,128]{1,0:T(8,128)(2,1)S(1)}, bf16[144,128]{1,0:T(8,128)(2,1)S(1)}, u32[]{:S(2)}, u32[]{:S(2)}) collective-permute-start(bf16[144,128]{1,0:T(8,128)(2,1)S(1)} %get-tuple-element.45), channel_id=1, source_target_pairs={{0,2},{2,0},{4,6},{6,4},{8,10},{10,8},{12,14},{14,12},{16,18},{18,... | collective-permute-start | bytes 110600 | tf_op jit(solution)/shard_map/ppermute | solution.py:37
  25.2 5.2 %collective-permute-start.5 = (bf16[144,128]{1,0:T(8,128)(2,1)S(1)}, bf16[144,128]{1,0:T(8,128)(2,1)S(1)}, u32[]{:S(2)}, u32[]{:S(2)}) collective-permute-start(bf16[144,128]{1,0:T(8,128)(2,1)S(1)} %get-tuple-element.46.rest_3_), channel_id=1, source_target_pairs={{0,8},{2,4},{4,2},{6,14},{8,0},{10,12},{12,10},{14,6},{16,24},{18,... | collective-permute-start | bytes 110600 | tf_op jit(solution)/shard_map/ppermute | solution.py:37
  25.6 9.0 %collective-permute-start.10 = (bf16[432,128]{1,0:T(8,128)(2,1)S(1)}, bf16[432,128]{1,0:T(8,128)(2,1)S(1)}, u32[]{:S(2)}, u32[]{:S(2)}) collective-permute-start(bf16[432,128]{1,0:T(8,128)(2,1)S(1)} %shard_map.85.rest_3_), channel_id=1, source_target_pairs={{0,6},{1,7},{2,4},{3,5},{4,2},{5,3},{6,0},{7,1},{8,25},{9,24},{10,... | collective-permute-start | bytes 331784 | tf_op jit(solution)/shard_map/ppermute | solution.py:399
  29.3 6.8 %collective-permute-start.11 = (bf16[432,128]{1,0:T(8,128)(2,1)S(1)}, bf16[432,128]{1,0:T(8,128)(2,1)S(1)}, u32[]{:S(2)}, u32[]{:S(2)}) collective-permute-start(bf16[432,128]{1,0:T(8,128)(2,1)S(1)} %shard_map.85.rest_3_), channel_id=1, source_target_pairs={{0,4},{1,5},{2,6},{3,7},{4,0},{5,1},{6,2},{7,3},{8,24},{9,25},{10,... | collective-permute-start | bytes 331784 | tf_op jit(solution)/shard_map/ppermute | solution.py:399
  29.9 6.2 %collective-permute-start.12 = (bf16[432,128]{1,0:T(8,128)(2,1)S(1)}, bf16[432,128]{1,0:T(8,128)(2,1)S(1)}, u32[]{:S(2)}, u32[]{:S(2)}) collective-permute-start(bf16[432,128]{1,0:T(8,128)(2,1)S(1)} %shard_map.85.rest_3_), channel_id=1, source_target_pairs={{0,2},{1,3},{2,0},{3,1},{4,6},{5,7},{6,4},{7,5},{8,9},{9,8},{10,11... | collective-permute-start | bytes 331784 | tf_op jit(solution)/shard_map/ppermute | solution.py:399
  36.2 5.7 %collective-permute-start.13 = (bf16[432,128]{1,0:T(8,128)(2,1)S(1)}, bf16[432,128]{1,0:T(8,128)(2,1)S(1)}, u32[]{:S(2)}, u32[]{:S(2)}) collective-permute-start(bf16[432,128]{1,0:T(8,128)(2,1)S(1)} %shard_map.86.rest_3_), channel_id=1, source_target_pairs={{0,17},{1,16},{2,19},{3,18},{4,21},{5,20},{6,23},{7,22},{8,14},{9,... | collective-permute-start | bytes 331784 | tf_op jit(solution)/shard_map/ppermute | solution.py:399
  37.8 4.7 %collective-permute-start.14 = (bf16[432,128]{1,0:T(8,128)(2,1)S(1)}, bf16[432,128]{1,0:T(8,128)(2,1)S(1)}, u32[]{:S(2)}, u32[]{:S(2)}) collective-permute-start(bf16[432,128]{1,0:T(8,128)(2,1)S(1)} %shard_map.86.rest_3_), channel_id=1, source_target_pairs={{0,16},{1,17},{2,18},{3,19},{4,20},{5,21},{6,22},{7,23},{8,12},{9,... | collective-permute-start | bytes 331784 | tf_op jit(solution)/shard_map/ppermute | solution.py:399
  38.3 4.7 %collective-permute-start.15 = (bf16[432,128]{1,0:T(8,128)(2,1)S(1)}, bf16[432,128]{1,0:T(8,128)(2,1)S(1)}, u32[]{:S(2)}, u32[]{:S(2)}) collective-permute-start(bf16[432,128]{1,0:T(8,128)(2,1)S(1)} %shard_map.86.rest_3_), channel_id=1, source_target_pairs={{0,1},{1,0},{2,3},{3,2},{4,5},{5,4},{6,7},{7,6},{8,10},{9,11},{10,... | collective-permute-start | bytes 331784 | tf_op jit(solution)/shard_map/ppermute | solution.py:399
  43.1 1.9 %collective-permute-start.16 = (bf16[1728,128]{1,0:T(8,128)(2,1)S(1)}, bf16[1728,128]{1,0:T(8,128)(2,1)S(1)}, u32[]{:S(2)}, u32[]{:S(2)}) collective-permute-start(bf16[1728,128]{1,0:T(8,128)(2,1)S(1)} %bitcast.19), channel_id=1, source_target_pairs={{0,8},{1,9},{2,10},{3,11},{4,12},{5,13},{6,14},{7,15},{8,0},{9,1},... | collective-permute-start | bytes 1327112 | tf_op jit(solution)/shard_map/ppermute | solution.py:405

commit v6 on v5

--- a/solution.py
+++ b/solution.py
@@ -303,11 +303,14 @@
         )
         total = term if total is None else total + term
     half = 128 // CORES
-    for tap in range(27):
-        far, near = tap // 3 * 128, tap % 3 * 128
-        block = total[far : far + 128, near : near + 128] * factor
-        first, second = block[:half], block[half:]
-        rows = slice(tap * half, (tap + 1) * half)
+
+    def piece(at):
+        far, near, low = at // CORES // 3 * 128, at // CORES % 3 * 128, at % CORES * half
+        return total[far + low : far + low + half, near : near + 128] * factor
+
+    for at in range(27):
+        first, second = piece(at), piece(27 + at)
+        rows = slice(at * half, (at + 1) * half)
         kept_term[rows] = jnp.where(core == 0, first, second)
         sent_term[rows] = jnp.where(core == 0, second, first).astype(BF16)
     for term in (kept_term, sent_term):
@@ -368,11 +371,14 @@
         at = lax.axis_index("dp")
         in_plane = at // CORES * gy + lax.axis_index("gy")
         self.core = at % CORES
-        if self.turned:
-            first = jnp.where(self.core == 0, in_plane, lax.axis_index("gx"))
-        else:
-            first = in_plane
-        self.mine = first.astype(jnp.int32)
+        in_line = lax.axis_index("gx") if self.turned else in_plane
+        self.mine = jnp.where(self.core == 0, in_plane, in_line).astype(jnp.int32)
+        self.others = jnp.where(self.core == 0, in_line, in_plane).astype(jnp.int32)
+
+    def places(self):
+        masks = [0] + list(range(self.plane - 1, 0, -1))
+        own = [(self.core, self.mine ^ mask) for mask in masks]
+        return own + [(1 - self.core, self.others ^ mask) for mask in masks]
 
     def pairs(self, place):
         dp, gx, gy = self.sizes
@@ -430,17 +436,17 @@
     rest[-1][...] = tree_sum(terms).astype(BF16)
 
 
-def gather_kernel(mine, *rest):
-    for mask, box in enumerate(rest[-2::-1]):
-        rest[-1][mine[0] ^ mask] = box[...]
-
-
-def spread_kernel(at, half, *rest):
-    out, wide, sem = rest[-3:]
-    wide[...] = half[0 : wide.shape[0] * wide.shape[1]].astype(F32).reshape(wide.shape)
-    copy = pltpu.make_async_copy(wide, out.at[:, at[0]], sem)
-    copy.start()
-    copy.wait()
+def spread_kernel(count, first, *rest):
+    out, wide, sems = rest[-3:]
+    places = Groups().places()[first : first + count]
+    copies = []
+    for number, box in enumerate(rest[:count]):
+        wide[number] = box[...].astype(F32)
+        place = out.at[places[number]]
+        copies.append(pltpu.make_async_copy(wide.at[number], place, sems.at[number]))
+        copies[-1].start()
+    for copy in copies:
+        copy.wait()
 
 
 def summed_everywhere(groups, kept, sent, early, late):
@@ -463,17 +469,24 @@
     )
     boxes = groups.swaps([rounded] * (line - 1), 1) + [rounded]
     rounded = run(second_sum_kernel, share_type, [VMEM] * line + [ANY], VMEM)(*boxes, late)
-    boxes = groups.swaps([rounded] * (group - 1), 0) + [rounded]
-    half = run(
-        gather_kernel, jax.ShapeDtypeStruct(shares, BF16), [SMEM] + [VMEM] * group, VMEM
-    )(mine, *boxes).reshape(kept.shape)
-    other = groups.swap_cores(half)
-    rows = 128 // CORES
-    out_type = jax.ShapeDtypeStruct((27, CORES, rows, 128), F32)
-    scratch = [pltpu.VMEM((27, rows, 128), F32), pltpu.SemaphoreType.DMA]
-    core = groups.core.astype(jnp.int32).reshape(1)
-    out = run(spread_kernel, out_type, [SMEM, VMEM], ANY, scratch)(core, half)
-    return run(spread_kernel, out_type, [SMEM, VMEM, ANY], ANY, scratch, aliases={2: 0})(1 - core, other, out)
+    boxes = [rounded] + groups.swaps([rounded] * (group - 1), 0)
+    passed = [groups.swap_cores(box) for box in boxes]
+    out_type = jax.ShapeDtypeStruct((CORES, group, rows, 128), F32)
+
+    def spread(boxes, first, *out):
+        count = len(boxes)
+        return run(
+            functools.partial(spread_kernel, count, first),
+            out_type,
+            [VMEM] * count + [ANY] * len(out),
+            ANY,
+            [pltpu.VMEM((count, rows, 128), F32), pltpu.SemaphoreType.DMA((count,))],
+            aliases={count: 0} if out else None,
+        )(*boxes, *out)
+
+    out = spread(boxes + passed[:-2], 0)
+    out = spread(passed[-2:], len(boxes + passed[:-2]), out)
+    return out.reshape(CORES, group * rows, 128)[:, : 27 * 128 // CORES]
 
 
 def body(features, weight, cotangent, neighbours, send_slots):

time: 46.1 us -> 45.3 us (0.983)
  waiting for transfers between devices: 6.81 us -> 6.19 us
    ppermute x2 -> x5, waiting for transfers between devices: 0.8 us -> 0.19 us  [swap_cores(): lax.ppermute(x, ('dp', 'gx', 'gy'), self.pairs(lambda a, b, c: (a ^ 1, b,...]
    pallas_call x3 -> x2, Pallas kernels: 1.99 us -> 1.91 us  [spread(): run(functools.partial(spread_kernel, count, first), out_type, [VMEM] * co...]
  transfers between devices with their start and end apart: 17 -> 20, of which waited for: 7 -> 7; matrix products, arithmetic and copies ran while one was open for 0% -> 0% of each run, Pallas kernels for 22% -> 23%
where the time goes in v6:
time: 45.3 us; the launch traced here: 45.2 us
  starting transfers between devices  21.4 us (47%)
  Pallas kernels  16.7 us (37%)
  waiting for transfers between devices  6.19 us (14%)
  between operations  0.8 us (2%)
    ppermute x9, starting transfers between devices, swap(): return lax.ppermute(x, ('dp', 'gx', 'gy'), self.pairs(place))  11.9 us
    ppermute x6, starting transfers between devices, swap(): return lax.ppermute(x, ('dp', axis), pairs)  9.47 us
    ppermute x9, waiting for transfers between devices, swap(): return lax.ppermute(x, ('dp', 'gx', 'gy'), self.pairs(place))  5.23 us
    pallas_call x1, Pallas kernels, body(): run(functools.partial(forward_kernel, counts, send, factor), [views_type,...  4.34 us
    pallas_call x1, Pallas kernels, body(): run(functools.partial(backward_kernel, counts, send), [views_type, bricks...  4.17 us
    pallas_call x1, Pallas kernels, body(): run(layout_kernel, [taps_type, views_type, preact_type], [SMEM, VMEM, VME...  2.29 us
    pallas_call x2, Pallas kernels, spread(): run(functools.partial(spread_kernel, count, first), out_type, [VMEM] * co...  1.91 us
    pallas_call x1, Pallas kernels, body(): run(own_kernel, preact_type, [VMEM] * 3, VMEM, aliases={2: 0}, micros=4.0)  1.46 us
  transfers between devices with their start and end apart: 20, of which 7 were waited for; matrix products, arithmetic and copies ran while one was open for 0% of the time, Pallas kernels for 23%

profile of v6, /device:TPU:0, one launch (start us, length us, event | category | flops | bytes accessed | tf_op | source)
XLA Modules:
  0.0 45.2 jit_solution(215504158193257456)
XLA Ops:
  0.7 1.2 %shard_map.76 = (bf16[4,8,64,128]{3,2,1,0:T(8,128)(2,1)S(1)}, bf16[128,128]{1,0:T(8,128)(2,1)S(1)}, bf16[128,128]{1,0:T(8,128)(2,1)S(1)}, bf16[160,128]{1,0:T(8,128)(2,1)S(1)}) custom-call(s32[2,8]{1,0:T(2,128)} %bitcast.21, bf16[4,8,64,128]{3,2,1,0:T(8,128)(2,1)} %bitcast.25), custom_call_target="tpu_custom_call" | custom-call | flops 1000000000 | bytes 65536 | tf_op jit(solution)/shard_map/pallas_call | solution.py:529
  1.9 3.0 %collective-permute-start = (bf16[160,128]{1,0:T(8,128)(2,1)S(1)}, bf16[160,128]{1,0:T(8,128)(2,1)S(1)}, u32[]{:S(2)}, u32[]{:S(2)}) collective-permute-start(bf16[160,128]{1,0:T(8,128)(2,1)S(1)} %get-tuple-element.35), channel_id=1, source_target_pairs={{0,1},{1,0},{8,9},{9,8},{16,17},{17,16},{24,25},{25,24},{2,3},{3,2... | collective-permute-start | bytes 122888 | tf_op jit(solution)/shard_map/ppermute | solution.py:37
  4.9 2.3 %shard_map.77 = (bf16[1152,384]{1,0:T(8,128)(2,1)S(1)}, bf16[4,10,64,384]{3,2,1,0:T(8,128)(2,1)S(1)}, f32[4,8,8,8,128]{4,3,2,1,0:T(8,128)S(1)}) custom-call(s32[4,27]{1,0:T(4,128)S(1)} %bitcast.17, bf16[4,8,64,128]{3,2,1,0:T(8,128)(2,1)S(1)} %get-tuple-element.29.bricks, bf16[27,128,128]{2,1,0:T(8,128)(2,1)S(1)} %bitcast.13), custom_call_target="tpu_custom_call" | custom-call | flops 2000000000 | bytes 65536 | tf_op jit(solution)/shard_map/pallas_call | solution.py:538
  7.3 1.8 %collective-permute-start.1 = (bf16[144,128]{1,0:T(8,128)(2,1)S(1)}, bf16[144,128]{1,0:T(8,128)(2,1)S(1)}, u32[]{:S(2)}, u32[]{:S(2)}) collective-permute-start(bf16[144,128]{1,0:T(8,128)(2,1)S(1)} %get-tuple-element.36), channel_id=1, source_target_pairs={{0,2},{2,0},{4,6},{6,4},{8,10},{10,8},{12,14},{14,12},{16,18},{18,... | collective-permute-start | bytes 110600 | tf_op jit(solution)/shard_map/ppermute | solution.py:37
  9.1 1.5 %shard_map.78.own_preact = f32[4,8,8,8,128]{4,3,2,1,0:T(8,128)S(1)} custom-call(bf16[4,10,64,384]{3,2,1,0:T(8,128)(2,1)S(1)} %get-tuple-element.30.views.own_views, bf16[1152,384]{1,0:T(8,128)(2,1)S(1)} %get-tuple-element.31.taps, f32[4,8,8,8,128]{4,3,2,1,0:T(8,128)S(1)} %get-tuple-element.32.begun), custom_call_target="tpu_custom_call", output_to_operand_aliasing={{}: (2, {})} | custom-call | flops 4000000000 | bytes 65536 | tf_op jit(solution)/shard_map/pallas_call | solution.py:551
  10.5 0.8 %collective-permute-done.1.rest_0_ = bf16[144,128]{1,0:T(8,128)(2,1)S(1)} collective-permute-done((bf16[144,128]{1,0:T(8,128)(2,1)S(1)}, bf16[144,128]{1,0:T(8,128)(2,1)S(1)}, u32[]{:S(2)}, u32[]{:S(2)}) %collective-permute-start.1) | collective-permute-done | bytes 36896 | tf_op jit(solution)/shard_map/ppermute | solution.py:37
  11.3 4.3 %shard_map.80 = (bf16[4,10,64,384]{3,2,1,0:T(8,128)(2,1)S(1)}, f32[4,8,8,8,128]{4,3,2,1,0:T(8,128)S(1)}, bf16[4,8,64,128]{3,2,1,0:T(8,128)(2,1)}, bf16[4,8,64,12...) custom-call(s32[4,27]{1,0:T(4,128)S(1)} %bitcast.18, ...), custom_call_target="tpu_custom_call", output_to_operand_aliasing={{0}: (2, {}), {1}: (3, {})} | custom-call | flops 5000000000 | bytes 65536 | tf_op jit(solution)/shard_map/pallas_call | solution.py:554
  15.7 1.7 %collective-permute-start.3 = (bf16[160,128]{1,0:T(8,128)(2,1)S(1)}, bf16[160,128]{1,0:T(8,128)(2,1)S(1)}, u32[]{:S(2)}, u32[]{:S(2)}) collective-permute-start(bf16[160,128]{1,0:T(8,128)(2,1)S(1)} %get-tuple-element.44), channel_id=1, source_target_pairs={{0,1},{1,0},{8,9},{9,8},{16,17},{17,16},{24,25},{25,24},{2,3},{3,2... | collective-permute-start | bytes 122888 | tf_op jit(solution)/shard_map/ppermute | solution.py:37
  17.6 2.7 %collective-permute-start.7 = (bf16[432,128]{1,0:T(8,128)(2,1)S(1)}, bf16[432,128]{1,0:T(8,128)(2,1)S(1)}, u32[]{:S(2)}, u32[]{:S(2)}) collective-permute-start(bf16[432,128]{1,0:T(8,128)(2,1)S(1)} %get-tuple-element.51), channel_id=1, source_target_pairs={{0,17},{1,16},{2,19},{3,18},{4,21},{5,20},{6,23},{7,22},{8,14},{9,... | collective-permute-start | bytes 331784 | tf_op jit(solution)/shard_map/ppermute | solution.py:405
  20.3 0.5 %collective-permute-start.8 = (bf16[432,128]{1,0:T(8,128)(2,1)S(1)}, bf16[432,128]{1,0:T(8,128)(2,1)S(1)}, u32[]{:S(2)}, u32[]{:S(2)}) collective-permute-start(bf16[432,128]{1,0:T(8,128)(2,1)S(1)} %get-tuple-element.52), channel_id=1, source_target_pairs={{0,16},{1,17},{2,18},{3,19},{4,20},{5,21},{6,22},{7,23},{8,12},{9,... | collective-permute-start | bytes 331784 | tf_op jit(solution)/shard_map/ppermute | solution.py:405
  21.2 1.1 %shard_map.81 = (bf16[1152,384]{1,0:T(8,128)(2,1)S(1)}, bf16[4,10,64,384]{3,2,1,0:T(8,128)(2,1)S(1)}) custom-call(s32[4,27]{1,0:T(4,128)S(1)} %bitcast.19, bf16[4,8,64,128]{3,2,1,0:T(8,128)(2,1)S(1)} %get-tuple-element.39.bricks, bf16[27,128,128]{2,1,0:T(8,128)(2,1)S(1)} %bitcast.14), custom_call_target="tpu_custom_call" | custom-call | flops 1000000000 | bytes 65536 | tf_op jit(solution)/shard_map/pallas_call | solution.py:575
  22.3 2.9 %collective-permute-start.4 = (bf16[144,128]{1,0:T(8,128)(2,1)S(1)}, bf16[144,128]{1,0:T(8,128)(2,1)S(1)}, u32[]{:S(2)}, u32[]{:S(2)}) collective-permute-start(bf16[144,128]{1,0:T(8,128)(2,1)S(1)} %get-tuple-element.45), channel_id=1, source_target_pairs={{0,2},{2,0},{4,6},{6,4},{8,10},{10,8},{12,14},{14,12},{16,18},{18,... | collective-permute-start | bytes 110600 | tf_op jit(solution)/shard_map/ppermute | solution.py:37
  25.6 3.7 %collective-permute-start.10 = (bf16[432,128]{1,0:T(8,128)(2,1)S(1)}, bf16[432,128]{1,0:T(8,128)(2,1)S(1)}, u32[]{:S(2)}, u32[]{:S(2)}) collective-permute-start(bf16[432,128]{1,0:T(8,128)(2,1)S(1)} %shard_map.85.rest_3_), channel_id=1, source_target_pairs={{0,6},{1,7},{2,4},{3,5},{4,2},{5,3},{6,0},{7,1},{8,25},{9,24},{10,... | collective-permute-start | bytes 331784 | tf_op jit(solution)/shard_map/ppermute | solution.py:405
  29.3 0.6 %collective-permute-start.11 = (bf16[432,128]{1,0:T(8,128)(2,1)S(1)}, bf16[432,128]{1,0:T(8,128)(2,1)S(1)}, u32[]{:S(2)}, u32[]{:S(2)}) collective-permute-start(bf16[432,128]{1,0:T(8,128)(2,1)S(1)} %shard_map.85.rest_3_), channel_id=1, source_target_pairs={{0,4},{1,5},{2,6},{3,7},{4,0},{5,1},{6,2},{7,3},{8,24},{9,25},{10,... | collective-permute-start | bytes 331784 | tf_op jit(solution)/shard_map/ppermute | solution.py:405
  30.4 4.2 %shard_map.83 = (bf16[4,10,64,384]{3,2,1,0:T(8,128)(2,1)S(1)}, bf16[4,8,64,128]{3,2,1,0:T(8,128)(2,1)}, f32[8,128]{1,0:T(8,128)S(1)}) custom-call(s32[4,27]{1,0:T(4,128)S(1)} %bitcast.20, bf16[4,10,64,384]{3,2,1,0:T(8,128)(2,1)S(1)} %get-tuple-element.40.own_views.rest_4_, ...), custom_call_target="tpu_custom_call", output_to_operand_aliasing={{0}: (1, {})} | custom-call | flops 5000000000 | bytes 65536 | tf_op jit(solution)/shard_map/pallas_call | solution.py:578
  34.6 1.5 %collective-permute-done.11.rest_1_ = bf16[432,128]{1,0:T(8,128)(2,1)S(1)} collective-permute-done((bf16[432,128]{1,0:T(8,128)(2,1)S(1)}, bf16[432,128]{1,0:T(8,128)(2,1)S(1)}, u32[]{:S(2)}, u32[]{:S(2)}) %collective-permute-start.11) | collective-permute-done | bytes 110624 | tf_op jit(solution)/shard_map/ppermute | solution.py:405
  36.2 1.6 %collective-permute-start.17 = (bf16[432,128]{1,0:T(8,128)(2,1)S(1)}, bf16[432,128]{1,0:T(8,128)(2,1)S(1)}, u32[]{:S(2)}, u32[]{:S(2)}) collective-permute-start(bf16[432,128]{1,0:T(8,128)(2,1)S(1)} %shard_map.86.rest_0_), channel_id=1, source_target_pairs={{0,17},{1,16},{2,19},{3,18},{4,21},{5,20},{6,23},{7,22},{8,14},{9,... | collective-permute-start | bytes 331784 | tf_op jit(solution)/shard_map/ppermute | solution.py:405
  37.8 0.5 %collective-permute-start.13 = (bf16[432,128]{1,0:T(8,128)(2,1)S(1)}, bf16[432,128]{1,0:T(8,128)(2,1)S(1)}, u32[]{:S(2)}, u32[]{:S(2)}) collective-permute-start(bf16[432,128]{1,0:T(8,128)(2,1)S(1)} %shard_map.86.rest_0_), channel_id=1, source_target_pairs={{0,16},{1,17},{2,18},{3,19},{4,20},{5,21},{6,22},{7,23},{8,12},{9,... | collective-permute-start | bytes 331784 | tf_op jit(solution)/shard_map/ppermute | solution.py:405
  38.3 1.4 %collective-permute-start.15 = (bf16[432,128]{1,0:T(8,128)(2,1)S(1)}, bf16[432,128]{1,0:T(8,128)(2,1)S(1)}, u32[]{:S(2)}, u32[]{:S(2)}) collective-permute-start(bf16[432,128]{1,0:T(8,128)(2,1)S(1)} %shard_map.86.rest_0_), channel_id=1, source_target_pairs={{0,1},{1,0},{2,3},{3,2},{4,5},{5,4},{6,7},{7,6},{8,10},{9,11},{10,... | collective-permute-start | bytes 331784 | tf_op jit(solution)/shard_map/ppermute | solution.py:405
  39.7 2.2 %collective-permute-done.17.rest_1_ = bf16[432,128]{1,0:T(8,128)(2,1)S(1)} collective-permute-done((bf16[432,128]{1,0:T(8,128)(2,1)S(1)}, bf16[432,128]{1,0:T(8,128)(2,1)S(1)}, u32[]{:S(2)}, u32[]{:S(2)}) %collective-permute-start.17) | collective-permute-done | bytes 110624 | tf_op jit(solution)/shard_map/ppermute | solution.py:405
  41.9 0.6 %collective-permute-done.13.rest_2_ = bf16[432,128]{1,0:T(8,128)(2,1)S(1)} collective-permute-done((bf16[432,128]{1,0:T(8,128)(2,1)S(1)}, bf16[432,128]{1,0:T(8,128)(2,1)S(1)}, u32[]{:S(2)}, u32[]{:S(2)}) %collective-permute-start.13) | collective-permute-done | bytes 110624 | tf_op jit(solution)/shard_map/ppermute | solution.py:405
  42.5 0.5 %collective-permute-done.15.rest_3_ = bf16[432,128]{1,0:T(8,128)(2,1)S(1)} collective-permute-done((bf16[432,128]{1,0:T(8,128)(2,1)S(1)}, bf16[432,128]{1,0:T(8,128)(2,1)S(1)}, u32[]{:S(2)}, u32[]{:S(2)}) %collective-permute-start.15) | collective-permute-done | bytes 110624 | tf_op jit(solution)/shard_map/ppermute | solution.py:405
  43.2 1.1 %shard_map.87.rest_2_ = f32[2,4,432,128]{3,2,1,0:T(8,128)} custom-call(bf16[432,128]{1,0:T(8,128)(2,1)S(1)} %shard_map.86.rest_0_, bf16[432,128]{1,0:T(8,128)(2,1)S(1)} %collective-permute-done.17.rest_1_, bf16[432,128]{1,0:T(8,128)(2,1)S(1)} %collective-permute-done.13.rest_2_, bf16[432,128]{1,0:T(8,128)(2,1)S(1)} %collective-permute-done.15.rest_3_, ...), custom_call_target="tpu_custom_call" | custom-call | flops 1000000000 | bytes 65536 | tf_op jit(solution)/shard_map/pallas_call | solution.py:478
  44.4 0.8 %shard_map.88 = f32[2,4,432,128]{3,2,1,0:T(8,128)} custom-call(bf16[432,128]{1,0:T(8,128)(2,1)S(1)} %collective-permute-done.14.rest_0_, bf16[432,128]{1,0:T(8,128)(2,1)S(1)} %collective-permute-done.16.rest_1_, f32[2,4,432,128]{3,2,1,0:T(8,128)} %shard_map.87.rest_2_), custom_call_target="tpu_custom_call", output_to_operand_aliasing={{}: (2, {})} | custom-call | flops 1000000000 | bytes 65536 | tf_op jit(solution)/shard_map/pallas_call | solution.py:478
  (37 shorter events, 1.8 us)
Async XLA Ops:
  0.6 4.3 %copy-start.2 = (s32[1,1,1,4,27]{4,3,2,1,0:T(4,128)S(1)}, s32[1,1,1,4,27]{4,3,2,1,0:T(4,128)}, u32[]{:S(2)}) copy-start(s32[1,1,1,4,27]{4,3,2,1,0:T(4,128)} %param.8) | copy-start | bytes 1300
  0.6 4.3 %copy-start = (bf16[3456,128]{1,0:T(8,128)(2,1)S(1)}, bf16[3456,128]{1,0:T(8,128)(2,1)}, u32[]{:S(2)}) copy-start(bf16[3456,128]{1,0:T(8,128)(2,1)} %param.6) | copy-start | bytes 2654212
  1.9 5.3 %collective-permute-start = (bf16[160,128]{1,0:T(8,128)(2,1)S(1)}, bf16[160,128]{1,0:T(8,128)(2,1)S(1)}, u32[]{:S(2)}, u32[]{:S(2)}) collective-permute-start(bf16[160,128]{1,0:T(8,128)(2,1)S(1)} %get-tuple-element.35), channel_id=1, source_target_pairs={{0,1},{1,0},{8,9},{9,8},{16,17},{17,16},{24,25},{25,24},{2,3},{3,2... | collective-permute-start | bytes 122888 | tf_op jit(solution)/shard_map/ppermute | solution.py:37
  7.3 4.0 %collective-permute-start.1 = (bf16[144,128]{1,0:T(8,128)(2,1)S(1)}, bf16[144,128]{1,0:T(8,128)(2,1)S(1)}, u32[]{:S(2)}, u32[]{:S(2)}) collective-permute-start(bf16[144,128]{1,0:T(8,128)(2,1)S(1)} %get-tuple-element.36), channel_id=1, source_target_pairs={{0,2},{2,0},{4,6},{6,4},{8,10},{10,8},{12,14},{14,12},{16,18},{18,... | collective-permute-start | bytes 110600 | tf_op jit(solution)/shard_map/ppermute | solution.py:37
  9.0 2.2 %collective-permute-start.2 = (bf16[144,128]{1,0:T(8,128)(2,1)S(1)}, bf16[144,128]{1,0:T(8,128)(2,1)S(1)}, u32[]{:S(2)}, u32[]{:S(2)}) collective-permute-start(bf16[144,128]{1,0:T(8,128)(2,1)S(1)} %get-tuple-element.37), channel_id=1, source_target_pairs={{0,8},{2,4},{4,2},{6,14},{8,0},{10,12},{12,10},{14,6},{16,24},{18,... | collective-permute-start | bytes 110600 | tf_op jit(solution)/shard_map/ppermute | solution.py:37
  9.1 2.2 %copy-start.1 = (bf16[1,1,1,4,512,128]{5,4,3,2,1,0:T(8,128)(2,1)S(1)}, bf16[1,1,1,4,512,128]{5,4,3,2,1,0:T(8,128)(2,1)}, u32[]{:S(2)}) copy-start(bf16[1,1,1,4,512,128]{5,4,3,2,1,0:T(8,128)(2,1)} %param.7) | copy-start | bytes 1572868
  9.1 2.2 %copy-start.3 = (s32[1,1,1,8,2]{3,4,2,1,0:T(2,128)S(1)}, s32[1,1,1,8,2]{3,4,2,1,0:T(2,128)}, u32[]{:S(2)}) copy-start(s32[1,1,1,8,2]{3,4,2,1,0:T(2,128)} %param.9) | copy-start | bytes 196
  15.6 1.9 %collective-permute-start.6 = (bf16[1728,128]{1,0:T(8,128)(2,1)S(1)}, bf16[1728,128]{1,0:T(8,128)(2,1)S(1)}, u32[]{:S(2)}, u32[]{:S(2)}) collective-permute-start(bf16[1728,128]{1,0:T(8,128)(2,1)S(1)} %get-tuple-element.49), channel_id=1, source_target_pairs={{0,8},{1,9},{2,10},{3,11},{4,12},{5,13},{6,14},{7,15},{8,0},{9,1},... | collective-permute-start | bytes 1327112 | tf_op jit(solution)/shard_map/ppermute | solution.py:411
  15.7 6.5 %collective-permute-start.3 = (bf16[160,128]{1,0:T(8,128)(2,1)S(1)}, bf16[160,128]{1,0:T(8,128)(2,1)S(1)}, u32[]{:S(2)}, u32[]{:S(2)}) collective-permute-start(bf16[160,128]{1,0:T(8,128)(2,1)S(1)} %get-tuple-element.44), channel_id=1, source_target_pairs={{0,1},{1,0},{8,9},{9,8},{16,17},{17,16},{24,25},{25,24},{2,3},{3,2... | collective-permute-start | bytes 122888 | tf_op jit(solution)/shard_map/ppermute | solution.py:37
  17.6 7.6 %collective-permute-start.7 = (bf16[432,128]{1,0:T(8,128)(2,1)S(1)}, bf16[432,128]{1,0:T(8,128)(2,1)S(1)}, u32[]{:S(2)}, u32[]{:S(2)}) collective-permute-start(bf16[432,128]{1,0:T(8,128)(2,1)S(1)} %get-tuple-element.51), channel_id=1, source_target_pairs={{0,17},{1,16},{2,19},{3,18},{4,21},{5,20},{6,23},{7,22},{8,14},{9,... | collective-permute-start | bytes 331784 | tf_op jit(solution)/shard_map/ppermute | solution.py:405
  20.3 4.9 %collective-permute-start.8 = (bf16[432,128]{1,0:T(8,128)(2,1)S(1)}, bf16[432,128]{1,0:T(8,128)(2,1)S(1)}, u32[]{:S(2)}, u32[]{:S(2)}) collective-permute-start(bf16[432,128]{1,0:T(8,128)(2,1)S(1)} %get-tuple-element.52), channel_id=1, source_target_pairs={{0,16},{1,17},{2,18},{3,19},{4,20},{5,21},{6,22},{7,23},{8,12},{9,... | collective-permute-start | bytes 331784 | tf_op jit(solution)/shard_map/ppermute | solution.py:405
  20.8 4.7 %collective-permute-start.9 = (bf16[432,128]{1,0:T(8,128)(2,1)S(1)}, bf16[432,128]{1,0:T(8,128)(2,1)S(1)}, u32[]{:S(2)}, u32[]{:S(2)}) collective-permute-start(bf16[432,128]{1,0:T(8,128)(2,1)S(1)} %get-tuple-element.53), channel_id=1, source_target_pairs={{0,1},{1,0},{2,3},{3,2},{4,5},{5,4},{6,7},{7,6},{8,10},{9,11},{10,... | collective-permute-start | bytes 331784 | tf_op jit(solution)/shard_map/ppermute | solution.py:405
  22.3 8.1 %collective-permute-start.4 = (bf16[144,128]{1,0:T(8,128)(2,1)S(1)}, bf16[144,128]{1,0:T(8,128)(2,1)S(1)}, u32[]{:S(2)}, u32[]{:S(2)}) collective-permute-start(bf16[144,128]{1,0:T(8,128)(2,1)S(1)} %get-tuple-element.45), channel_id=1, source_target_pairs={{0,2},{2,0},{4,6},{6,4},{8,10},{10,8},{12,14},{14,12},{16,18},{18,... | collective-permute-start | bytes 110600 | tf_op jit(solution)/shard_map/ppermute | solution.py:37
  25.2 5.2 %collective-permute-start.5 = (bf16[144,128]{1,0:T(8,128)(2,1)S(1)}, bf16[144,128]{1,0:T(8,128)(2,1)S(1)}, u32[]{:S(2)}, u32[]{:S(2)}) collective-permute-start(bf16[144,128]{1,0:T(8,128)(2,1)S(1)} %get-tuple-element.46.rest_3_), channel_id=1, source_target_pairs={{0,8},{2,4},{4,2},{6,14},{8,0},{10,12},{12,10},{14,6},{16,24},{18,... | collective-permute-start | bytes 110600 | tf_op jit(solution)/shard_map/ppermute | solution.py:37
  25.6 9.0 %collective-permute-start.10 = (bf16[432,128]{1,0:T(8,128)(2,1)S(1)}, bf16[432,128]{1,0:T(8,128)(2,1)S(1)}, u32[]{:S(2)}, u32[]{:S(2)}) collective-permute-start(bf16[432,128]{1,0:T(8,128)(2,1)S(1)} %shard_map.85.rest_3_), channel_id=1, source_target_pairs={{0,6},{1,7},{2,4},{3,5},{4,2},{5,3},{6,0},{7,1},{8,25},{9,24},{10,... | collective-permute-start | bytes 331784 | tf_op jit(solution)/shard_map/ppermute | solution.py:405
  29.3 6.8 %collective-permute-start.11 = (bf16[432,128]{1,0:T(8,128)(2,1)S(1)}, bf16[432,128]{1,0:T(8,128)(2,1)S(1)}, u32[]{:S(2)}, u32[]{:S(2)}) collective-permute-start(bf16[432,128]{1,0:T(8,128)(2,1)S(1)} %shard_map.85.rest_3_), channel_id=1, source_target_pairs={{0,4},{1,5},{2,6},{3,7},{4,0},{5,1},{6,2},{7,3},{8,24},{9,25},{10,... | collective-permute-start | bytes 331784 | tf_op jit(solution)/shard_map/ppermute | solution.py:405
  29.9 6.2 %collective-permute-start.12 = (bf16[432,128]{1,0:T(8,128)(2,1)S(1)}, bf16[432,128]{1,0:T(8,128)(2,1)S(1)}, u32[]{:S(2)}, u32[]{:S(2)}) collective-permute-start(bf16[432,128]{1,0:T(8,128)(2,1)S(1)} %shard_map.85.rest_3_), channel_id=1, source_target_pairs={{0,2},{1,3},{2,0},{3,1},{4,6},{5,7},{6,4},{7,5},{8,9},{9,8},{10,11... | collective-permute-start | bytes 331784 | tf_op jit(solution)/shard_map/ppermute | solution.py:405
  36.2 5.7 %collective-permute-start.17 = (bf16[432,128]{1,0:T(8,128)(2,1)S(1)}, bf16[432,128]{1,0:T(8,128)(2,1)S(1)}, u32[]{:S(2)}, u32[]{:S(2)}) collective-permute-start(bf16[432,128]{1,0:T(8,128)(2,1)S(1)} %shard_map.86.rest_0_), channel_id=1, source_target_pairs={{0,17},{1,16},{2,19},{3,18},{4,21},{5,20},{6,23},{7,22},{8,14},{9,... | collective-permute-start | bytes 331784 | tf_op jit(solution)/shard_map/ppermute | solution.py:405
  37.8 4.7 %collective-permute-start.13 = (bf16[432,128]{1,0:T(8,128)(2,1)S(1)}, bf16[432,128]{1,0:T(8,128)(2,1)S(1)}, u32[]{:S(2)}, u32[]{:S(2)}) collective-permute-start(bf16[432,128]{1,0:T(8,128)(2,1)S(1)} %shard_map.86.rest_0_), channel_id=1, source_target_pairs={{0,16},{1,17},{2,18},{3,19},{4,20},{5,21},{6,22},{7,23},{8,12},{9,... | collective-permute-start | bytes 331784 | tf_op jit(solution)/shard_map/ppermute | solution.py:405
  38.3 4.7 %collective-permute-start.15 = (bf16[432,128]{1,0:T(8,128)(2,1)S(1)}, bf16[432,128]{1,0:T(8,128)(2,1)S(1)}, u32[]{:S(2)}, u32[]{:S(2)}) collective-permute-start(bf16[432,128]{1,0:T(8,128)(2,1)S(1)} %shard_map.86.rest_0_), channel_id=1, source_target_pairs={{0,1},{1,0},{2,3},{3,2},{4,5},{5,4},{6,7},{7,6},{8,10},{9,11},{10,... | collective-permute-start | bytes 331784 | tf_op jit(solution)/shard_map/ppermute | solution.py:405
  39.7 3.4 %collective-permute-start.18 = (bf16[432,128]{1,0:T(8,128)(2,1)S(1)}, bf16[432,128]{1,0:T(8,128)(2,1)S(1)}, u32[]{:S(2)}, u32[]{:S(2)}) collective-permute-start(bf16[432,128]{1,0:T(8,128)(2,1)S(1)} %shard_map.86.rest_0_), channel_id=1, source_target_pairs={{0,8},{1,9},{2,10},{3,11},{4,12},{5,13},{6,14},{7,15},{8,0},{9,1},... | collective-permute-start | bytes 331784 | tf_op jit(solution)/shard_map/ppermute | solution.py:411
  41.9 1.3 %collective-permute-start.19 = (bf16[432,128]{1,0:T(8,128)(2,1)S(1)}, bf16[432,128]{1,0:T(8,128)(2,1)S(1)}, u32[]{:S(2)}, u32[]{:S(2)}) collective-permute-start(bf16[432,128]{1,0:T(8,128)(2,1)S(1)} %collective-permute-done.17.rest_1_), channel_id=1, source_target_pairs={{0,8},{1,9},{2,10},{3,11},{4,12},{5,13},{6,14},{7,15},{8,0},{9,1},... | collective-permute-start | bytes 331784 | tf_op jit(solution)/shard_map/ppermute | solution.py:411
  42.5 1.8 %collective-permute-start.14 = (bf16[432,128]{1,0:T(8,128)(2,1)S(1)}, bf16[432,128]{1,0:T(8,128)(2,1)S(1)}, u32[]{:S(2)}, u32[]{:S(2)}) collective-permute-start(bf16[432,128]{1,0:T(8,128)(2,1)S(1)} %collective-permute-done.13.rest_2_), channel_id=1, source_target_pairs={{0,8},{1,9},{2,10},{3,11},{4,12},{5,13},{6,14},{7,15},{8,0},{9,1},... | collective-permute-start | bytes 331784 | tf_op jit(solution)/shard_map/ppermute | solution.py:411
  43.1 1.3 %collective-permute-start.16 = (bf16[432,128]{1,0:T(8,128)(2,1)S(1)}, bf16[432,128]{1,0:T(8,128)(2,1)S(1)}, u32[]{:S(2)}, u32[]{:S(2)}) collective-permute-start(bf16[432,128]{1,0:T(8,128)(2,1)S(1)} %collective-permute-done.15.rest_3_), channel_id=1, source_target_pairs={{0,8},{1,9},{2,10},{3,11},{4,12},{5,13},{6,14},{7,15},{8,0},{9,1},... | collective-permute-start | bytes 331784 | tf_op jit(solution)/shard_map/ppermute | solution.py:411

commit v7 on v6

--- a/solution.py
+++ b/solution.py
@@ -293,15 +293,19 @@
         wide = jnp.where(table[slot, 13] >= 0, wide, 0.0)
         grads[slot] = wide.reshape(EDGE, PLANE, 128).astype(BF16)
     pack_all(grads, lists, faces_out, boxes_out, counts, send)
-    total = None
+    parts = []
     for slot in range(slots):
         grad = grads[slot].astype(F32).reshape(PLANE, EDGE, 128)
         shifted = [shift_rows(grad, 1), grad, shift_rows(grad, -1)]
-        rhs = jnp.concatenate([s.reshape(EDGE * PLANE, 128) for s in shifted], axis=1).astype(BF16)
-        term = lax.dot_general(
-            lhs_of(views.at[slot]), rhs, (((0,), (0,)), ((), ())), preferred_element_type=F32
+        parts.append(
+            jnp.concatenate([part.reshape(EDGE * PLANE, 128) for part in shifted], axis=1).astype(BF16)
         )
-        total = term if total is None else total + term
+    total = lax.dot_general(
+        jnp.concatenate([lhs_of(views.at[slot]) for slot in range(slots)], axis=0),
+        jnp.concatenate(parts, axis=0),
+        (((0,), (0,)), ((), ())),
+        preferred_element_type=F32,
+    )
     half = 128 // CORES
 
     def piece(at):

time: 45.3 us -> 45.3 us (level)
  transfers between devices with their start and end apart: 20 -> 20, of which waited for: 7 -> 8; matrix products, arithmetic and copies ran while one was open for 0% -> 0% of each run, Pallas kernels for 23% -> 23%
where the time goes in v7:
time: 45.3 us; the launch traced here: 45.2 us
  starting transfers between devices  21.4 us (47%)
  Pallas kernels  16.7 us (37%)
  waiting for transfers between devices  6.2 us (14%)
  between operations  0.8 us (2%)
    ppermute x9, starting transfers between devices, swap(): return lax.ppermute(x, ('dp', 'gx', 'gy'), self.pairs(place))  11.9 us
    ppermute x6, starting transfers between devices, swap(): return lax.ppermute(x, ('dp', axis), pairs)  9.48 us
    ppermute x9, waiting for transfers between devices, swap(): return lax.ppermute(x, ('dp', 'gx', 'gy'), self.pairs(place))  5.24 us
    pallas_call x1, Pallas kernels, body(): run(functools.partial(forward_kernel, counts, send, factor), [views_type,...  4.33 us
    pallas_call x1, Pallas kernels, body(): run(functools.partial(backward_kernel, counts, send), [views_type, bricks...  4.18 us
    pallas_call x1, Pallas kernels, body(): run(layout_kernel, [taps_type, views_type, preact_type], [SMEM, VMEM, VME...  2.29 us
    pallas_call x2, Pallas kernels, spread(): run(functools.partial(spread_kernel, count, first), out_type, [VMEM] * co...  1.91 us
    pallas_call x1, Pallas kernels, body(): run(own_kernel, preact_type, [VMEM] * 3, VMEM, aliases={2: 0}, micros=4.0)  1.46 us
  transfers between devices with their start and end apart: 20, of which 8 were waited for; matrix products, arithmetic and copies ran while one was open for 0% of the time, Pallas kernels for 23%

profile of v7, /device:TPU:0, one launch (start us, length us, event | category | flops | bytes accessed | tf_op | source)
XLA Modules:
  0.0 45.2 jit_solution(8610247675240261173)
XLA Ops:
  0.7 1.2 %shard_map.76 = (bf16[4,8,64,128]{3,2,1,0:T(8,128)(2,1)S(1)}, bf16[128,128]{1,0:T(8,128)(2,1)S(1)}, bf16[128,128]{1,0:T(8,128)(2,1)S(1)}, bf16[160,128]{1,0:T(8,128)(2,1)S(1)}) custom-call(s32[2,8]{1,0:T(2,128)} %bitcast.21, bf16[4,8,64,128]{3,2,1,0:T(8,128)(2,1)} %bitcast.25), custom_call_target="tpu_custom_call" | custom-call | flops 1000000000 | bytes 65536 | tf_op jit(solution)/shard_map/pallas_call | solution.py:533
  1.9 3.0 %collective-permute-start = (bf16[160,128]{1,0:T(8,128)(2,1)S(1)}, bf16[160,128]{1,0:T(8,128)(2,1)S(1)}, u32[]{:S(2)}, u32[]{:S(2)}) collective-permute-start(bf16[160,128]{1,0:T(8,128)(2,1)S(1)} %get-tuple-element.35), channel_id=1, source_target_pairs={{0,1},{1,0},{8,9},{9,8},{16,17},{17,16},{24,25},{25,24},{2,3},{3,2... | collective-permute-start | bytes 122888 | tf_op jit(solution)/shard_map/ppermute | solution.py:37
  4.9 2.3 %shard_map.77 = (bf16[1152,384]{1,0:T(8,128)(2,1)S(1)}, bf16[4,10,64,384]{3,2,1,0:T(8,128)(2,1)S(1)}, f32[4,8,8,8,128]{4,3,2,1,0:T(8,128)S(1)}) custom-call(s32[4,27]{1,0:T(4,128)S(1)} %bitcast.17, bf16[4,8,64,128]{3,2,1,0:T(8,128)(2,1)S(1)} %get-tuple-element.29.bricks, bf16[27,128,128]{2,1,0:T(8,128)(2,1)S(1)} %bitcast.13), custom_call_target="tpu_custom_call" | custom-call | flops 2000000000 | bytes 65536 | tf_op jit(solution)/shard_map/pallas_call | solution.py:542
  7.3 1.8 %collective-permute-start.1 = (bf16[144,128]{1,0:T(8,128)(2,1)S(1)}, bf16[144,128]{1,0:T(8,128)(2,1)S(1)}, u32[]{:S(2)}, u32[]{:S(2)}) collective-permute-start(bf16[144,128]{1,0:T(8,128)(2,1)S(1)} %get-tuple-element.36), channel_id=1, source_target_pairs={{0,2},{2,0},{4,6},{6,4},{8,10},{10,8},{12,14},{14,12},{16,18},{18,... | collective-permute-start | bytes 110600 | tf_op jit(solution)/shard_map/ppermute | solution.py:37
  9.1 1.5 %shard_map.78.own_preact = f32[4,8,8,8,128]{4,3,2,1,0:T(8,128)S(1)} custom-call(bf16[4,10,64,384]{3,2,1,0:T(8,128)(2,1)S(1)} %get-tuple-element.30.views.own_views, bf16[1152,384]{1,0:T(8,128)(2,1)S(1)} %get-tuple-element.31.taps, f32[4,8,8,8,128]{4,3,2,1,0:T(8,128)S(1)} %get-tuple-element.32.begun), custom_call_target="tpu_custom_call", output_to_operand_aliasing={{}: (2, {})} | custom-call | flops 4000000000 | bytes 65536 | tf_op jit(solution)/shard_map/pallas_call | solution.py:555
  10.5 0.8 %collective-permute-done.1.rest_0_ = bf16[144,128]{1,0:T(8,128)(2,1)S(1)} collective-permute-done((bf16[144,128]{1,0:T(8,128)(2,1)S(1)}, bf16[144,128]{1,0:T(8,128)(2,1)S(1)}, u32[]{:S(2)}, u32[]{:S(2)}) %collective-permute-start.1) | collective-permute-done | bytes 36896 | tf_op jit(solution)/shard_map/ppermute | solution.py:37
  11.3 4.3 %shard_map.80 = (bf16[4,10,64,384]{3,2,1,0:T(8,128)(2,1)S(1)}, f32[4,8,8,8,128]{4,3,2,1,0:T(8,128)S(1)}, bf16[4,8,64,128]{3,2,1,0:T(8,128)(2,1)}, bf16[4,8,64,12...) custom-call(s32[4,27]{1,0:T(4,128)S(1)} %bitcast.18, ...), custom_call_target="tpu_custom_call", output_to_operand_aliasing={{0}: (2, {}), {1}: (3, {})} | custom-call | flops 5000000000 | bytes 65536 | tf_op jit(solution)/shard_map/pallas_call | solution.py:558
  15.7 1.7 %collective-permute-start.3 = (bf16[160,128]{1,0:T(8,128)(2,1)S(1)}, bf16[160,128]{1,0:T(8,128)(2,1)S(1)}, u32[]{:S(2)}, u32[]{:S(2)}) collective-permute-start(bf16[160,128]{1,0:T(8,128)(2,1)S(1)} %get-tuple-element.44), channel_id=1, source_target_pairs={{0,1},{1,0},{8,9},{9,8},{16,17},{17,16},{24,25},{25,24},{2,3},{3,2... | collective-permute-start | bytes 122888 | tf_op jit(solution)/shard_map/ppermute | solution.py:37
  17.6 2.6 %collective-permute-start.7 = (bf16[432,128]{1,0:T(8,128)(2,1)S(1)}, bf16[432,128]{1,0:T(8,128)(2,1)S(1)}, u32[]{:S(2)}, u32[]{:S(2)}) collective-permute-start(bf16[432,128]{1,0:T(8,128)(2,1)S(1)} %get-tuple-element.51), channel_id=1, source_target_pairs={{0,17},{1,16},{2,19},{3,18},{4,21},{5,20},{6,23},{7,22},{8,14},{9,... | collective-permute-start | bytes 331784 | tf_op jit(solution)/shard_map/ppermute | solution.py:409
  20.2 0.6 %collective-permute-start.8 = (bf16[432,128]{1,0:T(8,128)(2,1)S(1)}, bf16[432,128]{1,0:T(8,128)(2,1)S(1)}, u32[]{:S(2)}, u32[]{:S(2)}) collective-permute-start(bf16[432,128]{1,0:T(8,128)(2,1)S(1)} %get-tuple-element.52), channel_id=1, source_target_pairs={{0,16},{1,17},{2,18},{3,19},{4,20},{5,21},{6,22},{7,23},{8,12},{9,... | collective-permute-start | bytes 331784 | tf_op jit(solution)/shard_map/ppermute | solution.py:409
  21.1 1.1 %shard_map.81 = (bf16[1152,384]{1,0:T(8,128)(2,1)S(1)}, bf16[4,10,64,384]{3,2,1,0:T(8,128)(2,1)S(1)}) custom-call(s32[4,27]{1,0:T(4,128)S(1)} %bitcast.19, bf16[4,8,64,128]{3,2,1,0:T(8,128)(2,1)S(1)} %get-tuple-element.39.bricks, bf16[27,128,128]{2,1,0:T(8,128)(2,1)S(1)} %bitcast.14), custom_call_target="tpu_custom_call" | custom-call | flops 1000000000 | bytes 65536 | tf_op jit(solution)/shard_map/pallas_call | solution.py:579
  22.3 2.9 %collective-permute-start.4 = (bf16[144,128]{1,0:T(8,128)(2,1)S(1)}, bf16[144,128]{1,0:T(8,128)(2,1)S(1)}, u32[]{:S(2)}, u32[]{:S(2)}) collective-permute-start(bf16[144,128]{1,0:T(8,128)(2,1)S(1)} %get-tuple-element.45), channel_id=1, source_target_pairs={{0,2},{2,0},{4,6},{6,4},{8,10},{10,8},{12,14},{14,12},{16,18},{18,... | collective-permute-start | bytes 110600 | tf_op jit(solution)/shard_map/ppermute | solution.py:37
  25.6 3.7 %collective-permute-start.10 = (bf16[432,128]{1,0:T(8,128)(2,1)S(1)}, bf16[432,128]{1,0:T(8,128)(2,1)S(1)}, u32[]{:S(2)}, u32[]{:S(2)}) collective-permute-start(bf16[432,128]{1,0:T(8,128)(2,1)S(1)} %shard_map.85.rest_3_), channel_id=1, source_target_pairs={{0,6},{1,7},{2,4},{3,5},{4,2},{5,3},{6,0},{7,1},{8,25},{9,24},{10,... | collective-permute-start | bytes 331784 | tf_op jit(solution)/shard_map/ppermute | solution.py:409
  29.3 0.6 %collective-permute-start.11 = (bf16[432,128]{1,0:T(8,128)(2,1)S(1)}, bf16[432,128]{1,0:T(8,128)(2,1)S(1)}, u32[]{:S(2)}, u32[]{:S(2)}) collective-permute-start(bf16[432,128]{1,0:T(8,128)(2,1)S(1)} %shard_map.85.rest_3_), channel_id=1, source_target_pairs={{0,4},{1,5},{2,6},{3,7},{4,0},{5,1},{6,2},{7,3},{8,24},{9,25},{10,... | collective-permute-start | bytes 331784 | tf_op jit(solution)/shard_map/ppermute | solution.py:409
  30.4 4.2 %shard_map.83 = (bf16[4,10,64,384]{3,2,1,0:T(8,128)(2,1)S(1)}, bf16[4,8,64,128]{3,2,1,0:T(8,128)(2,1)}, f32[8,128]{1,0:T(8,128)S(1)}) custom-call(s32[4,27]{1,0:T(4,128)S(1)} %bitcast.20, bf16[4,10,64,384]{3,2,1,0:T(8,128)(2,1)S(1)} %get-tuple-element.40.own_views.rest_4_, ...), custom_call_target="tpu_custom_call", output_to_operand_aliasing={{0}: (1, {})} | custom-call | flops 5000000000 | bytes 65536 | tf_op jit(solution)/shard_map/pallas_call | solution.py:582
  34.6 1.5 %collective-permute-done.11.rest_1_ = bf16[432,128]{1,0:T(8,128)(2,1)S(1)} collective-permute-done((bf16[432,128]{1,0:T(8,128)(2,1)S(1)}, bf16[432,128]{1,0:T(8,128)(2,1)S(1)}, u32[]{:S(2)}, u32[]{:S(2)}) %collective-permute-start.11) | collective-permute-done | bytes 110624 | tf_op jit(solution)/shard_map/ppermute | solution.py:409
  36.2 1.6 %collective-permute-start.17 = (bf16[432,128]{1,0:T(8,128)(2,1)S(1)}, bf16[432,128]{1,0:T(8,128)(2,1)S(1)}, u32[]{:S(2)}, u32[]{:S(2)}) collective-permute-start(bf16[432,128]{1,0:T(8,128)(2,1)S(1)} %shard_map.86.rest_0_), channel_id=1, source_target_pairs={{0,17},{1,16},{2,19},{3,18},{4,21},{5,20},{6,23},{7,22},{8,14},{9,... | collective-permute-start | bytes 331784 | tf_op jit(solution)/shard_map/ppermute | solution.py:409
  37.8 0.5 %collective-permute-start.13 = (bf16[432,128]{1,0:T(8,128)(2,1)S(1)}, bf16[432,128]{1,0:T(8,128)(2,1)S(1)}, u32[]{:S(2)}, u32[]{:S(2)}) collective-permute-start(bf16[432,128]{1,0:T(8,128)(2,1)S(1)} %shard_map.86.rest_0_), channel_id=1, source_target_pairs={{0,16},{1,17},{2,18},{3,19},{4,20},{5,21},{6,22},{7,23},{8,12},{9,... | collective-permute-start | bytes 331784 | tf_op jit(solution)/shard_map/ppermute | solution.py:409
  38.3 1.4 %collective-permute-start.15 = (bf16[432,128]{1,0:T(8,128)(2,1)S(1)}, bf16[432,128]{1,0:T(8,128)(2,1)S(1)}, u32[]{:S(2)}, u32[]{:S(2)}) collective-permute-start(bf16[432,128]{1,0:T(8,128)(2,1)S(1)} %shard_map.86.rest_0_), channel_id=1, source_target_pairs={{0,1},{1,0},{2,3},{3,2},{4,5},{5,4},{6,7},{7,6},{8,10},{9,11},{10,... | collective-permute-start | bytes 331784 | tf_op jit(solution)/shard_map/ppermute | solution.py:409
  39.7 2.2 %collective-permute-done.17.rest_1_ = bf16[432,128]{1,0:T(8,128)(2,1)S(1)} collective-permute-done((bf16[432,128]{1,0:T(8,128)(2,1)S(1)}, bf16[432,128]{1,0:T(8,128)(2,1)S(1)}, u32[]{:S(2)}, u32[]{:S(2)}) %collective-permute-start.17) | collective-permute-done | bytes 110624 | tf_op jit(solution)/shard_map/ppermute | solution.py:409
  41.9 0.6 %collective-permute-done.13.rest_2_ = bf16[432,128]{1,0:T(8,128)(2,1)S(1)} collective-permute-done((bf16[432,128]{1,0:T(8,128)(2,1)S(1)}, bf16[432,128]{1,0:T(8,128)(2,1)S(1)}, u32[]{:S(2)}, u32[]{:S(2)}) %collective-permute-start.13) | collective-permute-done | bytes 110624 | tf_op jit(solution)/shard_map/ppermute | solution.py:409
  42.5 0.5 %collective-permute-done.15.rest_3_ = bf16[432,128]{1,0:T(8,128)(2,1)S(1)} collective-permute-done((bf16[432,128]{1,0:T(8,128)(2,1)S(1)}, bf16[432,128]{1,0:T(8,128)(2,1)S(1)}, u32[]{:S(2)}, u32[]{:S(2)}) %collective-permute-start.15) | collective-permute-done | bytes 110624 | tf_op jit(solution)/shard_map/ppermute | solution.py:409
  43.2 1.1 %shard_map.87.rest_2_ = f32[2,4,432,128]{3,2,1,0:T(8,128)} custom-call(bf16[432,128]{1,0:T(8,128)(2,1)S(1)} %shard_map.86.rest_0_, bf16[432,128]{1,0:T(8,128)(2,1)S(1)} %collective-permute-done.17.rest_1_, bf16[432,128]{1,0:T(8,128)(2,1)S(1)} %collective-permute-done.13.rest_2_, bf16[432,128]{1,0:T(8,128)(2,1)S(1)} %collective-permute-done.15.rest_3_, ...), custom_call_target="tpu_custom_call" | custom-call | flops 1000000000 | bytes 65536 | tf_op jit(solution)/shard_map/pallas_call | solution.py:482
  44.4 0.8 %shard_map.88 = f32[2,4,432,128]{3,2,1,0:T(8,128)} custom-call(bf16[432,128]{1,0:T(8,128)(2,1)S(1)} %collective-permute-done.14.rest_0_, bf16[432,128]{1,0:T(8,128)(2,1)S(1)} %collective-permute-done.16.rest_1_, f32[2,4,432,128]{3,2,1,0:T(8,128)} %shard_map.87.rest_2_), custom_call_target="tpu_custom_call", output_to_operand_aliasing={{}: (2, {})} | custom-call | flops 1000000000 | bytes 65536 | tf_op jit(solution)/shard_map/pallas_call | solution.py:482
  (37 shorter events, 1.8 us)
Async XLA Ops:
  0.6 4.3 %copy-start.2 = (s32[1,1,1,4,27]{4,3,2,1,0:T(4,128)S(1)}, s32[1,1,1,4,27]{4,3,2,1,0:T(4,128)}, u32[]{:S(2)}) copy-start(s32[1,1,1,4,27]{4,3,2,1,0:T(4,128)} %param.8) | copy-start | bytes 1300
  0.6 4.3 %copy-start = (bf16[3456,128]{1,0:T(8,128)(2,1)S(1)}, bf16[3456,128]{1,0:T(8,128)(2,1)}, u32[]{:S(2)}) copy-start(bf16[3456,128]{1,0:T(8,128)(2,1)} %param.6) | copy-start | bytes 2654212
  1.9 5.3 %collective-permute-start = (bf16[160,128]{1,0:T(8,128)(2,1)S(1)}, bf16[160,128]{1,0:T(8,128)(2,1)S(1)}, u32[]{:S(2)}, u32[]{:S(2)}) collective-permute-start(bf16[160,128]{1,0:T(8,128)(2,1)S(1)} %get-tuple-element.35), channel_id=1, source_target_pairs={{0,1},{1,0},{8,9},{9,8},{16,17},{17,16},{24,25},{25,24},{2,3},{3,2... | collective-permute-start | bytes 122888 | tf_op jit(solution)/shard_map/ppermute | solution.py:37
  7.3 4.0 %collective-permute-start.1 = (bf16[144,128]{1,0:T(8,128)(2,1)S(1)}, bf16[144,128]{1,0:T(8,128)(2,1)S(1)}, u32[]{:S(2)}, u32[]{:S(2)}) collective-permute-start(bf16[144,128]{1,0:T(8,128)(2,1)S(1)} %get-tuple-element.36), channel_id=1, source_target_pairs={{0,2},{2,0},{4,6},{6,4},{8,10},{10,8},{12,14},{14,12},{16,18},{18,... | collective-permute-start | bytes 110600 | tf_op jit(solution)/shard_map/ppermute | solution.py:37
  9.0 2.2 %collective-permute-start.2 = (bf16[144,128]{1,0:T(8,128)(2,1)S(1)}, bf16[144,128]{1,0:T(8,128)(2,1)S(1)}, u32[]{:S(2)}, u32[]{:S(2)}) collective-permute-start(bf16[144,128]{1,0:T(8,128)(2,1)S(1)} %get-tuple-element.37), channel_id=1, source_target_pairs={{0,8},{2,4},{4,2},{6,14},{8,0},{10,12},{12,10},{14,6},{16,24},{18,... | collective-permute-start | bytes 110600 | tf_op jit(solution)/shard_map/ppermute | solution.py:37
  9.1 2.2 %copy-start.1 = (bf16[1,1,1,4,512,128]{5,4,3,2,1,0:T(8,128)(2,1)S(1)}, bf16[1,1,1,4,512,128]{5,4,3,2,1,0:T(8,128)(2,1)}, u32[]{:S(2)}) copy-start(bf16[1,1,1,4,512,128]{5,4,3,2,1,0:T(8,128)(2,1)} %param.7) | copy-start | bytes 1572868
  9.1 2.2 %copy-start.3 = (s32[1,1,1,8,2]{3,4,2,1,0:T(2,128)S(1)}, s32[1,1,1,8,2]{3,4,2,1,0:T(2,128)}, u32[]{:S(2)}) copy-start(s32[1,1,1,8,2]{3,4,2,1,0:T(2,128)} %param.9) | copy-start | bytes 196
  15.6 1.9 %collective-permute-start.6 = (bf16[1728,128]{1,0:T(8,128)(2,1)S(1)}, bf16[1728,128]{1,0:T(8,128)(2,1)S(1)}, u32[]{:S(2)}, u32[]{:S(2)}) collective-permute-start(bf16[1728,128]{1,0:T(8,128)(2,1)S(1)} %get-tuple-element.49), channel_id=1, source_target_pairs={{0,8},{1,9},{2,10},{3,11},{4,12},{5,13},{6,14},{7,15},{8,0},{9,1},... | collective-permute-start | bytes 1327112 | tf_op jit(solution)/shard_map/ppermute | solution.py:415
  15.7 6.5 %collective-permute-start.3 = (bf16[160,128]{1,0:T(8,128)(2,1)S(1)}, bf16[160,128]{1,0:T(8,128)(2,1)S(1)}, u32[]{:S(2)}, u32[]{:S(2)}) collective-permute-start(bf16[160,128]{1,0:T(8,128)(2,1)S(1)} %get-tuple-element.44), channel_id=1, source_target_pairs={{0,1},{1,0},{8,9},{9,8},{16,17},{17,16},{24,25},{25,24},{2,3},{3,2... | collective-permute-start | bytes 122888 | tf_op jit(solution)/shard_map/ppermute | solution.py:37
  17.6 7.6 %collective-permute-start.7 = (bf16[432,128]{1,0:T(8,128)(2,1)S(1)}, bf16[432,128]{1,0:T(8,128)(2,1)S(1)}, u32[]{:S(2)}, u32[]{:S(2)}) collective-permute-start(bf16[432,128]{1,0:T(8,128)(2,1)S(1)} %get-tuple-element.51), channel_id=1, source_target_pairs={{0,17},{1,16},{2,19},{3,18},{4,21},{5,20},{6,23},{7,22},{8,14},{9,... | collective-permute-start | bytes 331784 | tf_op jit(solution)/shard_map/ppermute | solution.py:409
  20.2 4.9 %collective-permute-start.8 = (bf16[432,128]{1,0:T(8,128)(2,1)S(1)}, bf16[432,128]{1,0:T(8,128)(2,1)S(1)}, u32[]{:S(2)}, u32[]{:S(2)}) collective-permute-start(bf16[432,128]{1,0:T(8,128)(2,1)S(1)} %get-tuple-element.52), channel_id=1, source_target_pairs={{0,16},{1,17},{2,18},{3,19},{4,20},{5,21},{6,22},{7,23},{8,12},{9,... | collective-permute-start | bytes 331784 | tf_op jit(solution)/shard_map/ppermute | solution.py:409
  20.8 4.7 %collective-permute-start.9 = (bf16[432,128]{1,0:T(8,128)(2,1)S(1)}, bf16[432,128]{1,0:T(8,128)(2,1)S(1)}, u32[]{:S(2)}, u32[]{:S(2)}) collective-permute-start(bf16[432,128]{1,0:T(8,128)(2,1)S(1)} %get-tuple-element.53), channel_id=1, source_target_pairs={{0,1},{1,0},{2,3},{3,2},{4,5},{5,4},{6,7},{7,6},{8,10},{9,11},{10,... | collective-permute-start | bytes 331784 | tf_op jit(solution)/shard_map/ppermute | solution.py:409
  22.3 8.1 %collective-permute-start.4 = (bf16[144,128]{1,0:T(8,128)(2,1)S(1)}, bf16[144,128]{1,0:T(8,128)(2,1)S(1)}, u32[]{:S(2)}, u32[]{:S(2)}) collective-permute-start(bf16[144,128]{1,0:T(8,128)(2,1)S(1)} %get-tuple-element.45), channel_id=1, source_target_pairs={{0,2},{2,0},{4,6},{6,4},{8,10},{10,8},{12,14},{14,12},{16,18},{18,... | collective-permute-start | bytes 110600 | tf_op jit(solution)/shard_map/ppermute | solution.py:37
  25.2 5.2 %collective-permute-start.5 = (bf16[144,128]{1,0:T(8,128)(2,1)S(1)}, bf16[144,128]{1,0:T(8,128)(2,1)S(1)}, u32[]{:S(2)}, u32[]{:S(2)}) collective-permute-start(bf16[144,128]{1,0:T(8,128)(2,1)S(1)} %get-tuple-element.46.rest_3_), channel_id=1, source_target_pairs={{0,8},{2,4},{4,2},{6,14},{8,0},{10,12},{12,10},{14,6},{16,24},{18,... | collective-permute-start | bytes 110600 | tf_op jit(solution)/shard_map/ppermute | solution.py:37
  25.6 9.0 %collective-permute-start.10 = (bf16[432,128]{1,0:T(8,128)(2,1)S(1)}, bf16[432,128]{1,0:T(8,128)(2,1)S(1)}, u32[]{:S(2)}, u32[]{:S(2)}) collective-permute-start(bf16[432,128]{1,0:T(8,128)(2,1)S(1)} %shard_map.85.rest_3_), channel_id=1, source_target_pairs={{0,6},{1,7},{2,4},{3,5},{4,2},{5,3},{6,0},{7,1},{8,25},{9,24},{10,... | collective-permute-start | bytes 331784 | tf_op jit(solution)/shard_map/ppermute | solution.py:409
  29.3 6.8 %collective-permute-start.11 = (bf16[432,128]{1,0:T(8,128)(2,1)S(1)}, bf16[432,128]{1,0:T(8,128)(2,1)S(1)}, u32[]{:S(2)}, u32[]{:S(2)}) collective-permute-start(bf16[432,128]{1,0:T(8,128)(2,1)S(1)} %shard_map.85.rest_3_), channel_id=1, source_target_pairs={{0,4},{1,5},{2,6},{3,7},{4,0},{5,1},{6,2},{7,3},{8,24},{9,25},{10,... | collective-permute-start | bytes 331784 | tf_op jit(solution)/shard_map/ppermute | solution.py:409
  29.9 6.2 %collective-permute-start.12 = (bf16[432,128]{1,0:T(8,128)(2,1)S(1)}, bf16[432,128]{1,0:T(8,128)(2,1)S(1)}, u32[]{:S(2)}, u32[]{:S(2)}) collective-permute-start(bf16[432,128]{1,0:T(8,128)(2,1)S(1)} %shard_map.85.rest_3_), channel_id=1, source_target_pairs={{0,2},{1,3},{2,0},{3,1},{4,6},{5,7},{6,4},{7,5},{8,9},{9,8},{10,11... | collective-permute-start | bytes 331784 | tf_op jit(solution)/shard_map/ppermute | solution.py:409
  36.2 5.7 %collective-permute-start.17 = (bf16[432,128]{1,0:T(8,128)(2,1)S(1)}, bf16[432,128]{1,0:T(8,128)(2,1)S(1)}, u32[]{:S(2)}, u32[]{:S(2)}) collective-permute-start(bf16[432,128]{1,0:T(8,128)(2,1)S(1)} %shard_map.86.rest_0_), channel_id=1, source_target_pairs={{0,17},{1,16},{2,19},{3,18},{4,21},{5,20},{6,23},{7,22},{8,14},{9,... | collective-permute-start | bytes 331784 | tf_op jit(solution)/shard_map/ppermute | solution.py:409
  37.8 4.7 %collective-permute-start.13 = (bf16[432,128]{1,0:T(8,128)(2,1)S(1)}, bf16[432,128]{1,0:T(8,128)(2,1)S(1)}, u32[]{:S(2)}, u32[]{:S(2)}) collective-permute-start(bf16[432,128]{1,0:T(8,128)(2,1)S(1)} %shard_map.86.rest_0_), channel_id=1, source_target_pairs={{0,16},{1,17},{2,18},{3,19},{4,20},{5,21},{6,22},{7,23},{8,12},{9,... | collective-permute-start | bytes 331784 | tf_op jit(solution)/shard_map/ppermute | solution.py:409
  38.3 4.7 %collective-permute-start.15 = (bf16[432,128]{1,0:T(8,128)(2,1)S(1)}, bf16[432,128]{1,0:T(8,128)(2,1)S(1)}, u32[]{:S(2)}, u32[]{:S(2)}) collective-permute-start(bf16[432,128]{1,0:T(8,128)(2,1)S(1)} %shard_map.86.rest_0_), channel_id=1, source_target_pairs={{0,1},{1,0},{2,3},{3,2},{4,5},{5,4},{6,7},{7,6},{8,10},{9,11},{10,... | collective-permute-start | bytes 331784 | tf_op jit(solution)/shard_map/ppermute | solution.py:409
  39.7 3.4 %collective-permute-start.18 = (bf16[432,128]{1,0:T(8,128)(2,1)S(1)}, bf16[432,128]{1,0:T(8,128)(2,1)S(1)}, u32[]{:S(2)}, u32[]{:S(2)}) collective-permute-start(bf16[432,128]{1,0:T(8,128)(2,1)S(1)} %shard_map.86.rest_0_), channel_id=1, source_target_pairs={{0,8},{1,9},{2,10},{3,11},{4,12},{5,13},{6,14},{7,15},{8,0},{9,1},... | collective-permute-start | bytes 331784 | tf_op jit(solution)/shard_map/ppermute | solution.py:415
  41.9 1.3 %collective-permute-start.19 = (bf16[432,128]{1,0:T(8,128)(2,1)S(1)}, bf16[432,128]{1,0:T(8,128)(2,1)S(1)}, u32[]{:S(2)}, u32[]{:S(2)}) collective-permute-start(bf16[432,128]{1,0:T(8,128)(2,1)S(1)} %collective-permute-done.17.rest_1_), channel_id=1, source_target_pairs={{0,8},{1,9},{2,10},{3,11},{4,12},{5,13},{6,14},{7,15},{8,0},{9,1},... | collective-permute-start | bytes 331784 | tf_op jit(solution)/shard_map/ppermute | solution.py:415
  42.5 1.8 %collective-permute-start.14 = (bf16[432,128]{1,0:T(8,128)(2,1)S(1)}, bf16[432,128]{1,0:T(8,128)(2,1)S(1)}, u32[]{:S(2)}, u32[]{:S(2)}) collective-permute-start(bf16[432,128]{1,0:T(8,128)(2,1)S(1)} %collective-permute-done.13.rest_2_), channel_id=1, source_target_pairs={{0,8},{1,9},{2,10},{3,11},{4,12},{5,13},{6,14},{7,15},{8,0},{9,1},... | collective-permute-start | bytes 331784 | tf_op jit(solution)/shard_map/ppermute | solution.py:415
  43.1 1.3 %collective-permute-start.16 = (bf16[432,128]{1,0:T(8,128)(2,1)S(1)}, bf16[432,128]{1,0:T(8,128)(2,1)S(1)}, u32[]{:S(2)}, u32[]{:S(2)}) collective-permute-start(bf16[432,128]{1,0:T(8,128)(2,1)S(1)} %collective-permute-done.15.rest_3_), channel_id=1, source_target_pairs={{0,8},{1,9},{2,10},{3,11},{4,12},{5,13},{6,14},{7,15},{8,0},{9,1},... | collective-permute-start | bytes 331784 | tf_op jit(solution)/shard_map/ppermute | solution.py:415

commit v8 on v6

--- a/solution.py
+++ b/solution.py
@@ -229,22 +229,39 @@
         preact[slot] = join_taps(parts).reshape(EDGE, EDGE, EDGE, 128)
 
 
-def own_kernel(views, taps, begun, preact):
-    own_products(views, taps, preact, range(views.shape[0] // 2, views.shape[0]))
-
-
-def add_remote(views, store, table, send, sides=None):
+def own_kernel(counts, send, table, own_views, taps, begun, *rest):
+    tiles_y = tiles_here(counts)[1]
+    y_boxes, (views, preacts, store, sides) = rest[: len(tiles_y)], rest[len(tiles_y) :]
+    slots = views.shape[0]
+    own_products(views, taps, preacts, range(slots // 2, slots))
+    fill_remote(store, 0, [], y_boxes, [], tiles_y, send)
+    add_remote(views, store, table, send, sides, "y")
+    for side, at in ((0, 0), (1, EDGE - 1)):
+        part = jnp.concatenate(
+            [taps[(3 * dx + 2 * side) * 128 : (3 * dx + 2 * side) * 128 + 128] for dx in range(3)], axis=0
+        )
+        product = join_taps(jnp.dot(sides[side], part, preferred_element_type=F32))
+        product = product.reshape(slots, EDGE, EDGE, 128)
+        for slot in range(slots):
+            preacts[slot, :, at] = preacts[slot, :, at] + product[slot]
+
+
+PLANES = ((0, -1, EDGE - 1, 0), (1, 1, 0, EDGE + 1))
+ROWS = ((0, -1, 0, 0), (1, 1, PLANE - 16, 256))
+
+
+def add_remote(views, store, table, send, sides=None, along="xy"):
     slots = views.shape[0]
     nothing = jnp.zeros((EDGE, EDGE, 128), F32)
     for slot in range(slots):
         rows = slice(slot * PLANE, (slot + 1) * PLANE)
         entry = lookup(table, slot, slots, slots + 8 * send, store.shape[0] - 1)
-        for side, off_x, source, target in ((0, -1, EDGE - 1, 0), (1, 1, 0, EDGE + 1)):
+        for side, off_x, source, target in PLANES if "x" in along else ():
             plane = view_of(store, entry, off_x, source)
             if sides is not None:
                 sides[side, rows] = plane
             views[slot, target] = views[slot, target] + plane
-        for side, off_y, base, lanes in ((2, -1, 0, 0), (3, 1, PLANE - 16, 256)):
+        for side, off_y, base, lanes in ROWS if "y" in along else ():
             group = slice(PLANE - 16, PLANE) if off_y < 0 else slice(0, 16)
             edge = low_or_high(store[entry(0, off_y), :, group, :], off_y < 0)
             padded = jnp.concatenate([nothing[:1], edge, nothing[:1]], axis=0)
@@ -268,23 +285,15 @@
     core = lax.axis_index("dp") % CORES
     slots = cotangent.shape[0]
     fill_remote(store, 0, x_boxes, y_boxes, tiles_x, tiles_y, send)
-    add_remote(views, store, table, send, sides)
+    add_remote(views, store, table, send, sides, "x")
     added = []
-    for side in range(4):
-        if side < 2:
-            part = taps[768 * side : 768 * side + 384]
-        else:
-            dy = 0 if side == 2 else 2
-            part = jnp.concatenate(
-                [taps[(3 * dx + dy) * 128 : (3 * dx + dy) * 128 + 128] for dx in range(3)], axis=0
-            )
+    for side in range(2):
+        part = taps[768 * side : 768 * side + 384]
         product = join_taps(jnp.dot(sides[side], part, preferred_element_type=F32))
         added.append(product.reshape(slots, EDGE, EDGE, 128))
     for slot in range(slots):
         preacts[slot, 0] = preacts[slot, 0] + added[0][slot]
         preacts[slot, EDGE - 1] = preacts[slot, EDGE - 1] + added[1][slot]
-        preacts[slot, :, 0] = preacts[slot, :, 0] + added[2][slot]
-        preacts[slot, :, EDGE - 1] = preacts[slot, :, EDGE - 1] + added[3][slot]
         preact = preacts[slot].reshape(PLANE, EDGE, 128)
         sigmoid = jax.nn.sigmoid(preact)
         activated[slot] = (preact * sigmoid).reshape(EDGE, PLANE, 128).astype(BF16)
@@ -515,6 +524,8 @@
     def swapped(boxes, axis, phases):
         return [swap(box, axis, phase) for box, phase in zip(boxes, phases)]
 
+    sides_of = pltpu.VMEM((2, slots * PLANE, 384), BF16)
+
     def store_of(entries):
         return pltpu.VMEM((entries, EDGE, PLANE, 128), BF16)
 
@@ -548,9 +559,15 @@
         micros=2.0,
     )(table, bricks, blocks)
     x_boxes = swapped(join(*faces, *y_boxes), "gx", phases_x)
-    preacts = run(own_kernel, preact_type, [VMEM] * 3, VMEM, aliases={2: 0}, micros=4.0)(
-        views, taps, preacts
-    )
+    views, preacts = run(
+        functools.partial(own_kernel, counts, send),
+        [views_type, preact_type],
+        [SMEM] + [VMEM] * (3 + number_y),
+        [VMEM, VMEM],
+        [store_of(8 * send + 1), sides_of],
+        aliases={1: 0, 3: 1},
+        micros=4.0,
+    )(table, views, taps, preacts, *y_boxes)
     _, _, activated, grads, kept, sent, *boxes = run(
         functools.partial(forward_kernel, counts, send, factor),
         [
@@ -565,7 +582,7 @@
         + [y_type] * number_y,
         [SMEM, SMEM] + [VMEM] * (4 + number_x + number_y),
         [VMEM] * (6 + number_x + number_y),
-        [store_of(8 * send + 1), pltpu.VMEM((4, slots * PLANE, 384), BF16)],
+        [store_of(8 * send + 1), sides_of],
         aliases={2: 0, 3: 1},
         micros=5.0,
     )(table, lists, views, preacts, cot, taps, *x_boxes, *y_boxes)

time: 45.3 us -> 45.4 us (level)
  waiting for transfers between devices: 6.19 us -> 5.5 us
  Pallas kernels: 16.7 us -> 17.2 us
    pallas_call x1, Pallas kernels: 1.46 us -> 2.28 us  [body(): run(functools.partial(own_kernel, counts, send), [views_type, preact_type...]
    ppermute x6, waiting for transfers between devices: 0.77 us -> 0.02 us  [swap(): return lax.ppermute(x, ('dp', axis), pairs)]
    ppermute x5, starting transfers between devices: 0.08 us -> 0.58 us  [swap_cores(): lax.ppermute(x, ('dp', 'gx', 'gy'), self.pairs(lambda a, b, c: (a ^ 1, b,...]
  transfers between devices with their start and end apart: 20 -> 20, of which waited for: 7 -> 5; matrix products, arithmetic and copies ran while one was open for 0% -> 0% of each run, Pallas kernels for 23% -> 25%
where the time goes in v8:
time: 45.4 us; the launch traced here: 45.2 us
  starting transfers between devices  21.7 us (48%)
  Pallas kernels  17.2 us (38%)
  waiting for transfers between devices  5.5 us (12%)
  between operations  0.8 us (2%)
    ppermute x9, starting transfers between devices, swap(): return lax.ppermute(x, ('dp', 'gx', 'gy'), self.pairs(place))  11.8 us
    ppermute x6, starting transfers between devices, swap(): return lax.ppermute(x, ('dp', axis), pairs)  9.32 us
    ppermute x9, waiting for transfers between devices, swap(): return lax.ppermute(x, ('dp', 'gx', 'gy'), self.pairs(place))  5.31 us
    pallas_call x1, Pallas kernels, body(): run(functools.partial(backward_kernel, counts, send), [views_type, bricks...  4.17 us
    pallas_call x1, Pallas kernels, body(): run(functools.partial(forward_kernel, counts, send, factor), [views_type,...  4.02 us
    pallas_call x1, Pallas kernels, body(): run(layout_kernel, [taps_type, views_type, preact_type], [SMEM, VMEM, VME...  2.3 us
    pallas_call x1, Pallas kernels, body(): run(functools.partial(own_kernel, counts, send), [views_type, preact_type...  2.28 us
    pallas_call x2, Pallas kernels, spread(): run(functools.partial(spread_kernel, count, first), out_type, [VMEM] * co...  1.91 us
  transfers between devices with their start and end apart: 20, of which 5 were waited for; matrix products, arithmetic and copies ran while one was open for 0% of the time, Pallas kernels for 25%

profile of v8, /device:TPU:0, one launch (start us, length us, event | category | flops | bytes accessed | tf_op | source)
XLA Modules:
  0.0 45.2 jit_solution(6686080000351536458)
XLA Ops:
  0.7 1.2 %shard_map.76 = (bf16[4,8,64,128]{3,2,1,0:T(8,128)(2,1)S(1)}, bf16[128,128]{1,0:T(8,128)(2,1)S(1)}, bf16[128,128]{1,0:T(8,128)(2,1)S(1)}, bf16[160,128]{1,0:T(8,128)(2,1)S(1)}) custom-call(s32[2,8]{1,0:T(2,128)} %bitcast.22, bf16[4,8,64,128]{3,2,1,0:T(8,128)(2,1)} %bitcast.26), custom_call_target="tpu_custom_call" | custom-call | flops 1000000000 | bytes 65536 | tf_op jit(solution)/shard_map/pallas_call | solution.py:540
  1.9 3.0 %collective-permute-start = (bf16[160,128]{1,0:T(8,128)(2,1)S(1)}, bf16[160,128]{1,0:T(8,128)(2,1)S(1)}, u32[]{:S(2)}, u32[]{:S(2)}) collective-permute-start(bf16[160,128]{1,0:T(8,128)(2,1)S(1)} %get-tuple-element.35), channel_id=1, source_target_pairs={{0,1},{1,0},{8,9},{9,8},{16,17},{17,16},{24,25},{25,24},{2,3},{3,2... | collective-permute-start | bytes 122888 | tf_op jit(solution)/shard_map/ppermute | solution.py:37
  4.9 2.3 %shard_map.77 = (bf16[1152,384]{1,0:T(8,128)(2,1)S(1)}, bf16[4,10,64,384]{3,2,1,0:T(8,128)(2,1)S(1)}, f32[4,8,8,8,128]{4,3,2,1,0:T(8,128)S(1)}) custom-call(s32[4,27]{1,0:T(4,128)S(1)} %bitcast.17, bf16[4,8,64,128]{3,2,1,0:T(8,128)(2,1)S(1)} %get-tuple-element.31.bricks, bf16[27,128,128]{2,1,0:T(8,128)(2,1)S(1)} %bitcast.13), custom_call_target="tpu_custom_call" | custom-call | flops 2000000000 | bytes 65536 | tf_op jit(solution)/shard_map/pallas_call | solution.py:549
  7.3 1.8 %collective-permute-start.1 = (bf16[144,128]{1,0:T(8,128)(2,1)S(1)}, bf16[144,128]{1,0:T(8,128)(2,1)S(1)}, u32[]{:S(2)}, u32[]{:S(2)}) collective-permute-start(bf16[144,128]{1,0:T(8,128)(2,1)S(1)} %get-tuple-element.40), channel_id=1, source_target_pairs={{0,2},{2,0},{4,6},{6,4},{8,10},{10,8},{12,14},{14,12},{16,18},{18,... | collective-permute-start | bytes 110600 | tf_op jit(solution)/shard_map/ppermute | solution.py:37
  9.1 2.3 %shard_map.78 = (bf16[4,10,64,384]{3,2,1,0:T(8,128)(2,1)S(1)}, f32[4,8,8,8,128]{4,3,2,1,0:T(8,128)S(1)}) custom-call(s32[4,27]{1,0:T(4,128)S(1)} %bitcast.18, bf16[4,10,64,384]{3,2,1,0:T(8,128)(2,1)S(1)} %get-tuple-element.32.own_views, bf16[1152,384]{1,0:T(8,128)(2,1)S(1)} %get-tuple-element.33.taps, ...), custom_call_target="tpu_custom_call", output_to_operand_aliasing={{0}: (1, {}), {1}: (3, {})} | custom-call | flops 4000000000 | bytes 65536 | tf_op jit(solution)/shard_map/pallas_call | solution.py:562
  11.4 4.0 %shard_map.80 = (bf16[4,10,64,384]{3,2,1,0:T(8,128)(2,1)S(1)}, f32[4,8,8,8,128]{4,3,2,1,0:T(8,128)S(1)}, bf16[4,8,64,128]{3,2,1,0:T(8,128)(2,1)}, bf16[4,8,64,12...) custom-call(s32[4,27]{1,0:T(4,128)S(1)} %bitcast.19, ...), custom_call_target="tpu_custom_call", output_to_operand_aliasing={{0}: (2, {}), {1}: (3, {})} | custom-call | flops 5000000000 | bytes 65536 | tf_op jit(solution)/shard_map/pallas_call | solution.py:571
  15.4 0.6 %collective-permute-start.6 = (bf16[1728,128]{1,0:T(8,128)(2,1)S(1)}, bf16[1728,128]{1,0:T(8,128)(2,1)S(1)}, u32[]{:S(2)}, u32[]{:S(2)}) collective-permute-start(bf16[1728,128]{1,0:T(8,128)(2,1)S(1)} %get-tuple-element.53), channel_id=1, source_target_pairs={{0,8},{1,9},{2,10},{3,11},{4,12},{5,13},{6,14},{7,15},{8,0},{9,1},... | collective-permute-start | bytes 1327112 | tf_op jit(solution)/shard_map/ppermute | solution.py:420
  16.0 1.5 %collective-permute-start.3 = (bf16[160,128]{1,0:T(8,128)(2,1)S(1)}, bf16[160,128]{1,0:T(8,128)(2,1)S(1)}, u32[]{:S(2)}, u32[]{:S(2)}) collective-permute-start(bf16[160,128]{1,0:T(8,128)(2,1)S(1)} %get-tuple-element.48), channel_id=1, source_target_pairs={{0,1},{1,0},{8,9},{9,8},{16,17},{17,16},{24,25},{25,24},{2,3},{3,2... | collective-permute-start | bytes 122888 | tf_op jit(solution)/shard_map/ppermute | solution.py:37
  17.6 2.4 %collective-permute-start.7 = (bf16[432,128]{1,0:T(8,128)(2,1)S(1)}, bf16[432,128]{1,0:T(8,128)(2,1)S(1)}, u32[]{:S(2)}, u32[]{:S(2)}) collective-permute-start(bf16[432,128]{1,0:T(8,128)(2,1)S(1)} %get-tuple-element.55), channel_id=1, source_target_pairs={{0,17},{1,16},{2,19},{3,18},{4,21},{5,20},{6,23},{7,22},{8,14},{9,... | collective-permute-start | bytes 331784 | tf_op jit(solution)/shard_map/ppermute | solution.py:414
  20.0 0.5 %collective-permute-start.8 = (bf16[432,128]{1,0:T(8,128)(2,1)S(1)}, bf16[432,128]{1,0:T(8,128)(2,1)S(1)}, u32[]{:S(2)}, u32[]{:S(2)}) collective-permute-start(bf16[432,128]{1,0:T(8,128)(2,1)S(1)} %get-tuple-element.56), channel_id=1, source_target_pairs={{0,16},{1,17},{2,18},{3,19},{4,20},{5,21},{6,22},{7,23},{8,12},{9,... | collective-permute-start | bytes 331784 | tf_op jit(solution)/shard_map/ppermute | solution.py:414
  20.5 0.6 %collective-permute-start.9 = (bf16[432,128]{1,0:T(8,128)(2,1)S(1)}, bf16[432,128]{1,0:T(8,128)(2,1)S(1)}, u32[]{:S(2)}, u32[]{:S(2)}) collective-permute-start(bf16[432,128]{1,0:T(8,128)(2,1)S(1)} %get-tuple-element.57), channel_id=1, source_target_pairs={{0,1},{1,0},{2,3},{3,2},{4,5},{5,4},{6,7},{7,6},{8,10},{9,11},{10,... | collective-permute-start | bytes 331784 | tf_op jit(solution)/shard_map/ppermute | solution.py:414
  21.2 1.1 %shard_map.81 = (bf16[1152,384]{1,0:T(8,128)(2,1)S(1)}, bf16[4,10,64,384]{3,2,1,0:T(8,128)(2,1)S(1)}) custom-call(s32[4,27]{1,0:T(4,128)S(1)} %bitcast.20, bf16[4,8,64,128]{3,2,1,0:T(8,128)(2,1)S(1)} %get-tuple-element.43.bricks, bf16[27,128,128]{2,1,0:T(8,128)(2,1)S(1)} %bitcast.14), custom_call_target="tpu_custom_call" | custom-call | flops 1000000000 | bytes 65536 | tf_op jit(solution)/shard_map/pallas_call | solution.py:592
  22.3 3.0 %collective-permute-start.4 = (bf16[144,128]{1,0:T(8,128)(2,1)S(1)}, bf16[144,128]{1,0:T(8,128)(2,1)S(1)}, u32[]{:S(2)}, u32[]{:S(2)}) collective-permute-start(bf16[144,128]{1,0:T(8,128)(2,1)S(1)} %get-tuple-element.49), channel_id=1, source_target_pairs={{0,2},{2,0},{4,6},{6,4},{8,10},{10,8},{12,14},{14,12},{16,18},{18,... | collective-permute-start | bytes 110600 | tf_op jit(solution)/shard_map/ppermute | solution.py:37
  25.4 3.6 %collective-permute-start.10 = (bf16[432,128]{1,0:T(8,128)(2,1)S(1)}, bf16[432,128]{1,0:T(8,128)(2,1)S(1)}, u32[]{:S(2)}, u32[]{:S(2)}) collective-permute-start(bf16[432,128]{1,0:T(8,128)(2,1)S(1)} %shard_map.85.rest_3_), channel_id=1, source_target_pairs={{0,6},{1,7},{2,4},{3,5},{4,2},{5,3},{6,0},{7,1},{8,25},{9,24},{10,... | collective-permute-start | bytes 331784 | tf_op jit(solution)/shard_map/ppermute | solution.py:414
  28.9 1.0 %collective-permute-start.11 = (bf16[432,128]{1,0:T(8,128)(2,1)S(1)}, bf16[432,128]{1,0:T(8,128)(2,1)S(1)}, u32[]{:S(2)}, u32[]{:S(2)}) collective-permute-start(bf16[432,128]{1,0:T(8,128)(2,1)S(1)} %shard_map.85.rest_3_), channel_id=1, source_target_pairs={{0,4},{1,5},{2,6},{3,7},{4,0},{5,1},{6,2},{7,3},{8,24},{9,25},{10,... | collective-permute-start | bytes 331784 | tf_op jit(solution)/shard_map/ppermute | solution.py:414
  30.1 4.2 %shard_map.83 = (bf16[4,10,64,384]{3,2,1,0:T(8,128)(2,1)S(1)}, bf16[4,8,64,128]{3,2,1,0:T(8,128)(2,1)}, f32[8,128]{1,0:T(8,128)S(1)}) custom-call(s32[4,27]{1,0:T(4,128)S(1)} %bitcast.21, bf16[4,10,64,384]{3,2,1,0:T(8,128)(2,1)S(1)} %get-tuple-element.44.own_views.rest_4_, ...), custom_call_target="tpu_custom_call", output_to_operand_aliasing={{0}: (1, {})} | custom-call | flops 5000000000 | bytes 65536 | tf_op jit(solution)/shard_map/pallas_call | solution.py:595
  34.2 1.5 %collective-permute-done.11.rest_1_ = bf16[432,128]{1,0:T(8,128)(2,1)S(1)} collective-permute-done((bf16[432,128]{1,0:T(8,128)(2,1)S(1)}, bf16[432,128]{1,0:T(8,128)(2,1)S(1)}, u32[]{:S(2)}, u32[]{:S(2)}) %collective-permute-start.11) | collective-permute-done | bytes 110624 | tf_op jit(solution)/shard_map/ppermute | solution.py:414
  35.8 2.0 %collective-permute-start.17 = (bf16[432,128]{1,0:T(8,128)(2,1)S(1)}, bf16[432,128]{1,0:T(8,128)(2,1)S(1)}, u32[]{:S(2)}, u32[]{:S(2)}) collective-permute-start(bf16[432,128]{1,0:T(8,128)(2,1)S(1)} %shard_map.86.rest_0_), channel_id=1, source_target_pairs={{0,17},{1,16},{2,19},{3,18},{4,21},{5,20},{6,23},{7,22},{8,14},{9,... | collective-permute-start | bytes 331784 | tf_op jit(solution)/shard_map/ppermute | solution.py:414
  37.8 0.5 %collective-permute-start.13 = (bf16[432,128]{1,0:T(8,128)(2,1)S(1)}, bf16[432,128]{1,0:T(8,128)(2,1)S(1)}, u32[]{:S(2)}, u32[]{:S(2)}) collective-permute-start(bf16[432,128]{1,0:T(8,128)(2,1)S(1)} %shard_map.86.rest_0_), channel_id=1, source_target_pairs={{0,16},{1,17},{2,18},{3,19},{4,20},{5,21},{6,22},{7,23},{8,12},{9,... | collective-permute-start | bytes 331784 | tf_op jit(solution)/shard_map/ppermute | solution.py:414
  38.4 1.0 %collective-permute-start.15 = (bf16[432,128]{1,0:T(8,128)(2,1)S(1)}, bf16[432,128]{1,0:T(8,128)(2,1)S(1)}, u32[]{:S(2)}, u32[]{:S(2)}) collective-permute-start(bf16[432,128]{1,0:T(8,128)(2,1)S(1)} %shard_map.86.rest_0_), channel_id=1, source_target_pairs={{0,1},{1,0},{2,3},{3,2},{4,5},{5,4},{6,7},{7,6},{8,10},{9,11},{10,... | collective-permute-start | bytes 331784 | tf_op jit(solution)/shard_map/ppermute | solution.py:414
  39.4 2.2 %collective-permute-done.17.rest_1_ = bf16[432,128]{1,0:T(8,128)(2,1)S(1)} collective-permute-done((bf16[432,128]{1,0:T(8,128)(2,1)S(1)}, bf16[432,128]{1,0:T(8,128)(2,1)S(1)}, u32[]{:S(2)}, u32[]{:S(2)}) %collective-permute-start.17) | collective-permute-done | bytes 110624 | tf_op jit(solution)/shard_map/ppermute | solution.py:414
  41.5 1.0 %collective-permute-done.13.rest_2_ = bf16[432,128]{1,0:T(8,128)(2,1)S(1)} collective-permute-done((bf16[432,128]{1,0:T(8,128)(2,1)S(1)}, bf16[432,128]{1,0:T(8,128)(2,1)S(1)}, u32[]{:S(2)}, u32[]{:S(2)}) %collective-permute-start.13) | collective-permute-done | bytes 110624 | tf_op jit(solution)/shard_map/ppermute | solution.py:414
  43.2 1.1 %shard_map.87.rest_2_ = f32[2,4,432,128]{3,2,1,0:T(8,128)} custom-call(bf16[432,128]{1,0:T(8,128)(2,1)S(1)} %shard_map.86.rest_0_, bf16[432,128]{1,0:T(8,128)(2,1)S(1)} %collective-permute-done.17.rest_1_, bf16[432,128]{1,0:T(8,128)(2,1)S(1)} %collective-permute-done.13.rest_2_, bf16[432,128]{1,0:T(8,128)(2,1)S(1)} %collective-permute-done.15.rest_3_, ...), custom_call_target="tpu_custom_call" | custom-call | flops 1000000000 | bytes 65536 | tf_op jit(solution)/shard_map/pallas_call | solution.py:487
  44.5 0.8 %shard_map.88 = f32[2,4,432,128]{3,2,1,0:T(8,128)} custom-call(bf16[432,128]{1,0:T(8,128)(2,1)S(1)} %collective-permute-done.14.rest_0_, bf16[432,128]{1,0:T(8,128)(2,1)S(1)} %collective-permute-done.16.rest_1_, f32[2,4,432,128]{3,2,1,0:T(8,128)} %shard_map.87.rest_2_), custom_call_target="tpu_custom_call", output_to_operand_aliasing={{}: (2, {})} | custom-call | flops 1000000000 | bytes 65536 | tf_op jit(solution)/shard_map/pallas_call | solution.py:487
  (37 shorter events, 1.2 us)
Async XLA Ops:
  0.6 4.3 %copy-start.2 = (s32[1,1,1,4,27]{4,3,2,1,0:T(4,128)S(1)}, s32[1,1,1,4,27]{4,3,2,1,0:T(4,128)}, u32[]{:S(2)}) copy-start(s32[1,1,1,4,27]{4,3,2,1,0:T(4,128)} %param.8) | copy-start | bytes 1300
  0.6 4.3 %copy-start = (bf16[3456,128]{1,0:T(8,128)(2,1)S(1)}, bf16[3456,128]{1,0:T(8,128)(2,1)}, u32[]{:S(2)}) copy-start(bf16[3456,128]{1,0:T(8,128)(2,1)} %param.6) | copy-start | bytes 2654212
  1.9 5.3 %collective-permute-start = (bf16[160,128]{1,0:T(8,128)(2,1)S(1)}, bf16[160,128]{1,0:T(8,128)(2,1)S(1)}, u32[]{:S(2)}, u32[]{:S(2)}) collective-permute-start(bf16[160,128]{1,0:T(8,128)(2,1)S(1)} %get-tuple-element.35), channel_id=1, source_target_pairs={{0,1},{1,0},{8,9},{9,8},{16,17},{17,16},{24,25},{25,24},{2,3},{3,2... | collective-permute-start | bytes 122888 | tf_op jit(solution)/shard_map/ppermute | solution.py:37
  7.3 4.1 %collective-permute-start.1 = (bf16[144,128]{1,0:T(8,128)(2,1)S(1)}, bf16[144,128]{1,0:T(8,128)(2,1)S(1)}, u32[]{:S(2)}, u32[]{:S(2)}) collective-permute-start(bf16[144,128]{1,0:T(8,128)(2,1)S(1)} %get-tuple-element.40), channel_id=1, source_target_pairs={{0,2},{2,0},{4,6},{6,4},{8,10},{10,8},{12,14},{14,12},{16,18},{18,... | collective-permute-start | bytes 110600 | tf_op jit(solution)/shard_map/ppermute | solution.py:37
  9.0 2.3 %collective-permute-start.2 = (bf16[144,128]{1,0:T(8,128)(2,1)S(1)}, bf16[144,128]{1,0:T(8,128)(2,1)S(1)}, u32[]{:S(2)}, u32[]{:S(2)}) collective-permute-start(bf16[144,128]{1,0:T(8,128)(2,1)S(1)} %get-tuple-element.41), channel_id=1, source_target_pairs={{0,8},{2,4},{4,2},{6,14},{8,0},{10,12},{12,10},{14,6},{16,24},{18,... | collective-permute-start | bytes 110600 | tf_op jit(solution)/shard_map/ppermute | solution.py:37
  9.1 2.3 %copy-start.1 = (bf16[1,1,1,4,512,128]{5,4,3,2,1,0:T(8,128)(2,1)S(1)}, bf16[1,1,1,4,512,128]{5,4,3,2,1,0:T(8,128)(2,1)}, u32[]{:S(2)}) copy-start(bf16[1,1,1,4,512,128]{5,4,3,2,1,0:T(8,128)(2,1)} %param.7) | copy-start | bytes 1572868
  9.1 2.3 %copy-start.3 = (s32[1,1,1,8,2]{3,4,2,1,0:T(2,128)S(1)}, s32[1,1,1,8,2]{3,4,2,1,0:T(2,128)}, u32[]{:S(2)}) copy-start(s32[1,1,1,8,2]{3,4,2,1,0:T(2,128)} %param.9) | copy-start | bytes 196
  15.4 2.1 %collective-permute-start.6 = (bf16[1728,128]{1,0:T(8,128)(2,1)S(1)}, bf16[1728,128]{1,0:T(8,128)(2,1)S(1)}, u32[]{:S(2)}, u32[]{:S(2)}) collective-permute-start(bf16[1728,128]{1,0:T(8,128)(2,1)S(1)} %get-tuple-element.53), channel_id=1, source_target_pairs={{0,8},{1,9},{2,10},{3,11},{4,12},{5,13},{6,14},{7,15},{8,0},{9,1},... | collective-permute-start | bytes 1327112 | tf_op jit(solution)/shard_map/ppermute | solution.py:420
  16.0 6.3 %collective-permute-start.3 = (bf16[160,128]{1,0:T(8,128)(2,1)S(1)}, bf16[160,128]{1,0:T(8,128)(2,1)S(1)}, u32[]{:S(2)}, u32[]{:S(2)}) collective-permute-start(bf16[160,128]{1,0:T(8,128)(2,1)S(1)} %get-tuple-element.48), channel_id=1, source_target_pairs={{0,1},{1,0},{8,9},{9,8},{16,17},{17,16},{24,25},{25,24},{2,3},{3,2... | collective-permute-start | bytes 122888 | tf_op jit(solution)/shard_map/ppermute | solution.py:37
  17.6 7.7 %collective-permute-start.7 = (bf16[432,128]{1,0:T(8,128)(2,1)S(1)}, bf16[432,128]{1,0:T(8,128)(2,1)S(1)}, u32[]{:S(2)}, u32[]{:S(2)}) collective-permute-start(bf16[432,128]{1,0:T(8,128)(2,1)S(1)} %get-tuple-element.55), channel_id=1, source_target_pairs={{0,17},{1,16},{2,19},{3,18},{4,21},{5,20},{6,23},{7,22},{8,14},{9,... | collective-permute-start | bytes 331784 | tf_op jit(solution)/shard_map/ppermute | solution.py:414
  20.0 5.3 %collective-permute-start.8 = (bf16[432,128]{1,0:T(8,128)(2,1)S(1)}, bf16[432,128]{1,0:T(8,128)(2,1)S(1)}, u32[]{:S(2)}, u32[]{:S(2)}) collective-permute-start(bf16[432,128]{1,0:T(8,128)(2,1)S(1)} %get-tuple-element.56), channel_id=1, source_target_pairs={{0,16},{1,17},{2,18},{3,19},{4,20},{5,21},{6,22},{7,23},{8,12},{9,... | collective-permute-start | bytes 331784 | tf_op jit(solution)/shard_map/ppermute | solution.py:414
  20.5 4.7 %collective-permute-start.9 = (bf16[432,128]{1,0:T(8,128)(2,1)S(1)}, bf16[432,128]{1,0:T(8,128)(2,1)S(1)}, u32[]{:S(2)}, u32[]{:S(2)}) collective-permute-start(bf16[432,128]{1,0:T(8,128)(2,1)S(1)} %get-tuple-element.57), channel_id=1, source_target_pairs={{0,1},{1,0},{2,3},{3,2},{4,5},{5,4},{6,7},{7,6},{8,10},{9,11},{10,... | collective-permute-start | bytes 331784 | tf_op jit(solution)/shard_map/ppermute | solution.py:414
  22.3 7.8 %collective-permute-start.4 = (bf16[144,128]{1,0:T(8,128)(2,1)S(1)}, bf16[144,128]{1,0:T(8,128)(2,1)S(1)}, u32[]{:S(2)}, u32[]{:S(2)}) collective-permute-start(bf16[144,128]{1,0:T(8,128)(2,1)S(1)} %get-tuple-element.49), channel_id=1, source_target_pairs={{0,2},{2,0},{4,6},{6,4},{8,10},{10,8},{12,14},{14,12},{16,18},{18,... | collective-permute-start | bytes 110600 | tf_op jit(solution)/shard_map/ppermute | solution.py:37
  25.3 4.8 %collective-permute-start.5 = (bf16[144,128]{1,0:T(8,128)(2,1)S(1)}, bf16[144,128]{1,0:T(8,128)(2,1)S(1)}, u32[]{:S(2)}, u32[]{:S(2)}) collective-permute-start(bf16[144,128]{1,0:T(8,128)(2,1)S(1)} %get-tuple-element.50.rest_3_), channel_id=1, source_target_pairs={{0,8},{2,4},{4,2},{6,14},{8,0},{10,12},{12,10},{14,6},{16,24},{18,... | collective-permute-start | bytes 110600 | tf_op jit(solution)/shard_map/ppermute | solution.py:37
  25.4 8.9 %collective-permute-start.10 = (bf16[432,128]{1,0:T(8,128)(2,1)S(1)}, bf16[432,128]{1,0:T(8,128)(2,1)S(1)}, u32[]{:S(2)}, u32[]{:S(2)}) collective-permute-start(bf16[432,128]{1,0:T(8,128)(2,1)S(1)} %shard_map.85.rest_3_), channel_id=1, source_target_pairs={{0,6},{1,7},{2,4},{3,5},{4,2},{5,3},{6,0},{7,1},{8,25},{9,24},{10,... | collective-permute-start | bytes 331784 | tf_op jit(solution)/shard_map/ppermute | solution.py:414
  28.9 6.8 %collective-permute-start.11 = (bf16[432,128]{1,0:T(8,128)(2,1)S(1)}, bf16[432,128]{1,0:T(8,128)(2,1)S(1)}, u32[]{:S(2)}, u32[]{:S(2)}) collective-permute-start(bf16[432,128]{1,0:T(8,128)(2,1)S(1)} %shard_map.85.rest_3_), channel_id=1, source_target_pairs={{0,4},{1,5},{2,6},{3,7},{4,0},{5,1},{6,2},{7,3},{8,24},{9,25},{10,... | collective-permute-start | bytes 331784 | tf_op jit(solution)/shard_map/ppermute | solution.py:414
  29.9 5.9 %collective-permute-start.12 = (bf16[432,128]{1,0:T(8,128)(2,1)S(1)}, bf16[432,128]{1,0:T(8,128)(2,1)S(1)}, u32[]{:S(2)}, u32[]{:S(2)}) collective-permute-start(bf16[432,128]{1,0:T(8,128)(2,1)S(1)} %shard_map.85.rest_3_), channel_id=1, source_target_pairs={{0,2},{1,3},{2,0},{3,1},{4,6},{5,7},{6,4},{7,5},{8,9},{9,8},{10,11... | collective-permute-start | bytes 331784 | tf_op jit(solution)/shard_map/ppermute | solution.py:414
  35.8 5.7 %collective-permute-start.17 = (bf16[432,128]{1,0:T(8,128)(2,1)S(1)}, bf16[432,128]{1,0:T(8,128)(2,1)S(1)}, u32[]{:S(2)}, u32[]{:S(2)}) collective-permute-start(bf16[432,128]{1,0:T(8,128)(2,1)S(1)} %shard_map.86.rest_0_), channel_id=1, source_target_pairs={{0,17},{1,16},{2,19},{3,18},{4,21},{5,20},{6,23},{7,22},{8,14},{9,... | collective-permute-start | bytes 331784 | tf_op jit(solution)/shard_map/ppermute | solution.py:414
  37.8 4.7 %collective-permute-start.13 = (bf16[432,128]{1,0:T(8,128)(2,1)S(1)}, bf16[432,128]{1,0:T(8,128)(2,1)S(1)}, u32[]{:S(2)}, u32[]{:S(2)}) collective-permute-start(bf16[432,128]{1,0:T(8,128)(2,1)S(1)} %shard_map.86.rest_0_), channel_id=1, source_target_pairs={{0,16},{1,17},{2,18},{3,19},{4,20},{5,21},{6,22},{7,23},{8,12},{9,... | collective-permute-start | bytes 331784 | tf_op jit(solution)/shard_map/ppermute | solution.py:414
  38.4 4.7 %collective-permute-start.15 = (bf16[432,128]{1,0:T(8,128)(2,1)S(1)}, bf16[432,128]{1,0:T(8,128)(2,1)S(1)}, u32[]{:S(2)}, u32[]{:S(2)}) collective-permute-start(bf16[432,128]{1,0:T(8,128)(2,1)S(1)} %shard_map.86.rest_0_), channel_id=1, source_target_pairs={{0,1},{1,0},{2,3},{3,2},{4,5},{5,4},{6,7},{7,6},{8,10},{9,11},{10,... | collective-permute-start | bytes 331784 | tf_op jit(solution)/shard_map/ppermute | solution.py:414
  39.4 3.8 %collective-permute-start.18 = (bf16[432,128]{1,0:T(8,128)(2,1)S(1)}, bf16[432,128]{1,0:T(8,128)(2,1)S(1)}, u32[]{:S(2)}, u32[]{:S(2)}) collective-permute-start(bf16[432,128]{1,0:T(8,128)(2,1)S(1)} %shard_map.86.rest_0_), channel_id=1, source_target_pairs={{0,8},{1,9},{2,10},{3,11},{4,12},{5,13},{6,14},{7,15},{8,0},{9,1},... | collective-permute-start | bytes 331784 | tf_op jit(solution)/shard_map/ppermute | solution.py:420
  41.5 1.6 %collective-permute-start.19 = (bf16[432,128]{1,0:T(8,128)(2,1)S(1)}, bf16[432,128]{1,0:T(8,128)(2,1)S(1)}, u32[]{:S(2)}, u32[]{:S(2)}) collective-permute-start(bf16[432,128]{1,0:T(8,128)(2,1)S(1)} %collective-permute-done.17.rest_1_), channel_id=1, source_target_pairs={{0,8},{1,9},{2,10},{3,11},{4,12},{5,13},{6,14},{7,15},{8,0},{9,1},... | collective-permute-start | bytes 331784 | tf_op jit(solution)/shard_map/ppermute | solution.py:420
  42.6 1.7 %collective-permute-start.14 = (bf16[432,128]{1,0:T(8,128)(2,1)S(1)}, bf16[432,128]{1,0:T(8,128)(2,1)S(1)}, u32[]{:S(2)}, u32[]{:S(2)}) collective-permute-start(bf16[432,128]{1,0:T(8,128)(2,1)S(1)} %collective-permute-done.13.rest_2_), channel_id=1, source_target_pairs={{0,8},{1,9},{2,10},{3,11},{4,12},{5,13},{6,14},{7,15},{8,0},{9,1},... | collective-permute-start | bytes 331784 | tf_op jit(solution)/shard_map/ppermute | solution.py:420
  43.1 1.3 %collective-permute-start.16 = (bf16[432,128]{1,0:T(8,128)(2,1)S(1)}, bf16[432,128]{1,0:T(8,128)(2,1)S(1)}, u32[]{:S(2)}, u32[]{:S(2)}) collective-permute-start(bf16[432,128]{1,0:T(8,128)(2,1)S(1)} %collective-permute-done.15.rest_3_), channel_id=1, source_target_pairs={{0,8},{1,9},{2,10},{3,11},{4,12},{5,13},{6,14},{7,15},{8,0},{9,1},... | collective-permute-start | bytes 331784 | tf_op jit(solution)/shard_map/ppermute | solution.py:420

commit v9 on v6

--- a/solution.py
+++ b/solution.py
@@ -318,7 +318,7 @@
             term[27 * half :] = jnp.zeros((term.shape[0] - 27 * half, 128), term.dtype)
 
 
-def back_layout_kernel(table, bricks, weight, backward, views, store):
+def back_layout_kernel(table, bricks, weight, joined, backward, views, store):
     slots = bricks.shape[0]
     for tap in range(27):
         far, near = tap // 3 * 128, tap % 3 * 128
@@ -573,8 +573,8 @@
     packed = join(*faces, *y_boxes)
     x_boxes = swapped(packed, "gx", phases_x)
     back_taps, views = run(
-        back_layout_kernel, [taps_type, views_type], [SMEM, VMEM, VMEM], [VMEM, VMEM], [store_of(slots + 1)]
-    )(table, grads, blocks)
+        back_layout_kernel, [taps_type, views_type], [SMEM, VMEM, VMEM, ANY], [VMEM, VMEM], [store_of(slots + 1)]
+    )(table, grads, blocks, packed[-1])
     _, input_grad, ready = run(
         functools.partial(backward_kernel, counts, send),
         [views_type, bricks_type, jax.ShapeDtypeStruct((8, 128), F32)],

time: 45.3 us -> 45.3 us (level)
  no operation moved by 1% of the time
where the time goes in v9:
time: 45.3 us; the launch traced here: 45.2 us
  starting transfers between devices  21.4 us (47%)
  Pallas kernels  16.7 us (37%)
  waiting for transfers between devices  6.18 us (14%)
  between operations  0.81 us (2%)
    ppermute x9, starting transfers between devices, swap(): return lax.ppermute(x, ('dp', 'gx', 'gy'), self.pairs(place))  11.9 us
    ppermute x6, starting transfers between devices, swap(): return lax.ppermute(x, ('dp', axis), pairs)  9.47 us
    ppermute x9, waiting for transfers between devices, swap(): return lax.ppermute(x, ('dp', 'gx', 'gy'), self.pairs(place))  5.22 us
    pallas_call x1, Pallas kernels, body(): run(functools.partial(forward_kernel, counts, send, factor), [views_type,...  4.34 us
    pallas_call x1, Pallas kernels, body(): run(functools.partial(backward_kernel, counts, send), [views_type, bricks...  4.19 us
    pallas_call x1, Pallas kernels, body(): run(layout_kernel, [taps_type, views_type, preact_type], [SMEM, VMEM, VME...  2.29 us
    pallas_call x2, Pallas kernels, spread(): run(functools.partial(spread_kernel, count, first), out_type, [VMEM] * co...  1.91 us
    pallas_call x1, Pallas kernels, body(): run(own_kernel, preact_type, [VMEM] * 3, VMEM, aliases={2: 0}, micros=4.0)  1.46 us
  transfers between devices with their start and end apart: 20, of which 7 were waited for; matrix products, arithmetic and copies ran while one was open for 0% of the time, Pallas kernels for 23%

profile of v9, /device:TPU:0, one launch (start us, length us, event | category | flops | bytes accessed | tf_op | source)
XLA Modules:
  0.0 45.2 jit_solution(3808916169212579627)
XLA Ops:
  0.7 1.2 %shard_map.76 = (bf16[4,8,64,128]{3,2,1,0:T(8,128)(2,1)S(1)}, bf16[128,128]{1,0:T(8,128)(2,1)S(1)}, bf16[128,128]{1,0:T(8,128)(2,1)S(1)}, bf16[160,128]{1,0:T(8,128)(2,1)S(1)}) custom-call(s32[2,8]{1,0:T(2,128)} %bitcast.21, bf16[4,8,64,128]{3,2,1,0:T(8,128)(2,1)} %bitcast.25), custom_call_target="tpu_custom_call" | custom-call | flops 1000000000 | bytes 65536 | tf_op jit(solution)/shard_map/pallas_call | solution.py:529
  1.9 3.0 %collective-permute-start = (bf16[160,128]{1,0:T(8,128)(2,1)S(1)}, bf16[160,128]{1,0:T(8,128)(2,1)S(1)}, u32[]{:S(2)}, u32[]{:S(2)}) collective-permute-start(bf16[160,128]{1,0:T(8,128)(2,1)S(1)} %get-tuple-element.35), channel_id=1, source_target_pairs={{0,1},{1,0},{8,9},{9,8},{16,17},{17,16},{24,25},{25,24},{2,3},{3,2... | collective-permute-start | bytes 122888 | tf_op jit(solution)/shard_map/ppermute | solution.py:37
  4.9 2.3 %shard_map.77 = (bf16[1152,384]{1,0:T(8,128)(2,1)S(1)}, bf16[4,10,64,384]{3,2,1,0:T(8,128)(2,1)S(1)}, f32[4,8,8,8,128]{4,3,2,1,0:T(8,128)S(1)}) custom-call(s32[4,27]{1,0:T(4,128)S(1)} %bitcast.17, bf16[4,8,64,128]{3,2,1,0:T(8,128)(2,1)S(1)} %get-tuple-element.29.bricks, bf16[27,128,128]{2,1,0:T(8,128)(2,1)S(1)} %bitcast.13), custom_call_target="tpu_custom_call" | custom-call | flops 2000000000 | bytes 65536 | tf_op jit(solution)/shard_map/pallas_call | solution.py:538
  7.3 1.8 %collective-permute-start.1 = (bf16[144,128]{1,0:T(8,128)(2,1)S(1)}, bf16[144,128]{1,0:T(8,128)(2,1)S(1)}, u32[]{:S(2)}, u32[]{:S(2)}) collective-permute-start(bf16[144,128]{1,0:T(8,128)(2,1)S(1)} %get-tuple-element.36), channel_id=1, source_target_pairs={{0,2},{2,0},{4,6},{6,4},{8,10},{10,8},{12,14},{14,12},{16,18},{18,... | collective-permute-start | bytes 110600 | tf_op jit(solution)/shard_map/ppermute | solution.py:37
  9.1 1.5 %shard_map.78.own_preact = f32[4,8,8,8,128]{4,3,2,1,0:T(8,128)S(1)} custom-call(bf16[4,10,64,384]{3,2,1,0:T(8,128)(2,1)S(1)} %get-tuple-element.30.views.own_views, bf16[1152,384]{1,0:T(8,128)(2,1)S(1)} %get-tuple-element.31.taps, f32[4,8,8,8,128]{4,3,2,1,0:T(8,128)S(1)} %get-tuple-element.32.begun), custom_call_target="tpu_custom_call", output_to_operand_aliasing={{}: (2, {})} | custom-call | flops 4000000000 | bytes 65536 | tf_op jit(solution)/shard_map/pallas_call | solution.py:551
  10.5 0.8 %collective-permute-done.1.rest_0_ = bf16[144,128]{1,0:T(8,128)(2,1)S(1)} collective-permute-done((bf16[144,128]{1,0:T(8,128)(2,1)S(1)}, bf16[144,128]{1,0:T(8,128)(2,1)S(1)}, u32[]{:S(2)}, u32[]{:S(2)}) %collective-permute-start.1) | collective-permute-done | bytes 36896 | tf_op jit(solution)/shard_map/ppermute | solution.py:37
  11.3 4.3 %shard_map.80 = (bf16[4,10,64,384]{3,2,1,0:T(8,128)(2,1)S(1)}, f32[4,8,8,8,128]{4,3,2,1,0:T(8,128)S(1)}, bf16[4,8,64,128]{3,2,1,0:T(8,128)(2,1)}, bf16[4,8,64,12...) custom-call(s32[4,27]{1,0:T(4,128)S(1)} %bitcast.18, ...), custom_call_target="tpu_custom_call", output_to_operand_aliasing={{0}: (2, {}), {1}: (3, {})} | custom-call | flops 5000000000 | bytes 65536 | tf_op jit(solution)/shard_map/pallas_call | solution.py:554
  15.7 1.7 %collective-permute-start.3 = (bf16[160,128]{1,0:T(8,128)(2,1)S(1)}, bf16[160,128]{1,0:T(8,128)(2,1)S(1)}, u32[]{:S(2)}, u32[]{:S(2)}) collective-permute-start(bf16[160,128]{1,0:T(8,128)(2,1)S(1)} %get-tuple-element.42), channel_id=1, source_target_pairs={{0,1},{1,0},{8,9},{9,8},{16,17},{17,16},{24,25},{25,24},{2,3},{3,2... | collective-permute-start | bytes 122888 | tf_op jit(solution)/shard_map/ppermute | solution.py:37
  17.6 2.7 %collective-permute-start.7 = (bf16[432,128]{1,0:T(8,128)(2,1)S(1)}, bf16[432,128]{1,0:T(8,128)(2,1)S(1)}, u32[]{:S(2)}, u32[]{:S(2)}) collective-permute-start(bf16[432,128]{1,0:T(8,128)(2,1)S(1)} %get-tuple-element.51), channel_id=1, source_target_pairs={{0,17},{1,16},{2,19},{3,18},{4,21},{5,20},{6,23},{7,22},{8,14},{9,... | collective-permute-start | bytes 331784 | tf_op jit(solution)/shard_map/ppermute | solution.py:405
  20.3 0.5 %collective-permute-start.8 = (bf16[432,128]{1,0:T(8,128)(2,1)S(1)}, bf16[432,128]{1,0:T(8,128)(2,1)S(1)}, u32[]{:S(2)}, u32[]{:S(2)}) collective-permute-start(bf16[432,128]{1,0:T(8,128)(2,1)S(1)} %get-tuple-element.52), channel_id=1, source_target_pairs={{0,16},{1,17},{2,18},{3,19},{4,20},{5,21},{6,22},{7,23},{8,12},{9,... | collective-permute-start | bytes 331784 | tf_op jit(solution)/shard_map/ppermute | solution.py:405
  21.2 2.9 %collective-permute-start.4 = (bf16[144,128]{1,0:T(8,128)(2,1)S(1)}, bf16[144,128]{1,0:T(8,128)(2,1)S(1)}, u32[]{:S(2)}, u32[]{:S(2)}) collective-permute-start(bf16[144,128]{1,0:T(8,128)(2,1)S(1)} %get-tuple-element.46), channel_id=1, source_target_pairs={{0,2},{2,0},{4,6},{6,4},{8,10},{10,8},{12,14},{14,12},{16,18},{18,... | collective-permute-start | bytes 110600 | tf_op jit(solution)/shard_map/ppermute | solution.py:37
  24.1 1.1 %shard_map.82 = (bf16[1152,384]{1,0:T(8,128)(2,1)S(1)}, bf16[4,10,64,384]{3,2,1,0:T(8,128)(2,1)S(1)}) custom-call(s32[4,27]{1,0:T(4,128)S(1)} %bitcast.19, bf16[4,8,64,128]{3,2,1,0:T(8,128)(2,1)S(1)} %get-tuple-element.39.bricks, bf16[27,128,128]{2,1,0:T(8,128)(2,1)S(1)} %bitcast.14, bf16[144,128]{1,0:T(8,128)(2,1)S(1)} %get-tuple-element.43.joined.rest_3_), custom_call_target="tpu_custom_call" | custom-call | flops 1000000000 | bytes 65536 | tf_op jit(solution)/shard_map/pallas_call | solution.py:575
  25.6 3.7 %collective-permute-start.10 = (bf16[432,128]{1,0:T(8,128)(2,1)S(1)}, bf16[432,128]{1,0:T(8,128)(2,1)S(1)}, u32[]{:S(2)}, u32[]{:S(2)}) collective-permute-start(bf16[432,128]{1,0:T(8,128)(2,1)S(1)} %shard_map.85.rest_3_), channel_id=1, source_target_pairs={{0,6},{1,7},{2,4},{3,5},{4,2},{5,3},{6,0},{7,1},{8,25},{9,24},{10,... | collective-permute-start | bytes 331784 | tf_op jit(solution)/shard_map/ppermute | solution.py:405
  29.3 0.6 %collective-permute-start.11 = (bf16[432,128]{1,0:T(8,128)(2,1)S(1)}, bf16[432,128]{1,0:T(8,128)(2,1)S(1)}, u32[]{:S(2)}, u32[]{:S(2)}) collective-permute-start(bf16[432,128]{1,0:T(8,128)(2,1)S(1)} %shard_map.85.rest_3_), channel_id=1, source_target_pairs={{0,4},{1,5},{2,6},{3,7},{4,0},{5,1},{6,2},{7,3},{8,24},{9,25},{10,... | collective-permute-start | bytes 331784 | tf_op jit(solution)/shard_map/ppermute | solution.py:405
  30.4 4.2 %shard_map.83 = (bf16[4,10,64,384]{3,2,1,0:T(8,128)(2,1)S(1)}, bf16[4,8,64,128]{3,2,1,0:T(8,128)(2,1)}, f32[8,128]{1,0:T(8,128)S(1)}) custom-call(s32[4,27]{1,0:T(4,128)S(1)} %bitcast.20, bf16[4,10,64,384]{3,2,1,0:T(8,128)(2,1)S(1)} %get-tuple-element.44.own_views.rest_4_, ...), custom_call_target="tpu_custom_call", output_to_operand_aliasing={{0}: (1, {})} | custom-call | flops 5000000000 | bytes 65536 | tf_op jit(solution)/shard_map/pallas_call | solution.py:578
  34.6 1.5 %collective-permute-done.11.rest_1_ = bf16[432,128]{1,0:T(8,128)(2,1)S(1)} collective-permute-done((bf16[432,128]{1,0:T(8,128)(2,1)S(1)}, bf16[432,128]{1,0:T(8,128)(2,1)S(1)}, u32[]{:S(2)}, u32[]{:S(2)}) %collective-permute-start.11) | collective-permute-done | bytes 110624 | tf_op jit(solution)/shard_map/ppermute | solution.py:405
  36.2 1.6 %collective-permute-start.17 = (bf16[432,128]{1,0:T(8,128)(2,1)S(1)}, bf16[432,128]{1,0:T(8,128)(2,1)S(1)}, u32[]{:S(2)}, u32[]{:S(2)}) collective-permute-start(bf16[432,128]{1,0:T(8,128)(2,1)S(1)} %shard_map.86.rest_0_), channel_id=1, source_target_pairs={{0,17},{1,16},{2,19},{3,18},{4,21},{5,20},{6,23},{7,22},{8,14},{9,... | collective-permute-start | bytes 331784 | tf_op jit(solution)/shard_map/ppermute | solution.py:405
  37.8 0.5 %collective-permute-start.13 = (bf16[432,128]{1,0:T(8,128)(2,1)S(1)}, bf16[432,128]{1,0:T(8,128)(2,1)S(1)}, u32[]{:S(2)}, u32[]{:S(2)}) collective-permute-start(bf16[432,128]{1,0:T(8,128)(2,1)S(1)} %shard_map.86.rest_0_), channel_id=1, source_target_pairs={{0,16},{1,17},{2,18},{3,19},{4,20},{5,21},{6,22},{7,23},{8,12},{9,... | collective-permute-start | bytes 331784 | tf_op jit(solution)/shard_map/ppermute | solution.py:405
  38.3 1.4 %collective-permute-start.15 = (bf16[432,128]{1,0:T(8,128)(2,1)S(1)}, bf16[432,128]{1,0:T(8,128)(2,1)S(1)}, u32[]{:S(2)}, u32[]{:S(2)}) collective-permute-start(bf16[432,128]{1,0:T(8,128)(2,1)S(1)} %shard_map.86.rest_0_), channel_id=1, source_target_pairs={{0,1},{1,0},{2,3},{3,2},{4,5},{5,4},{6,7},{7,6},{8,10},{9,11},{10,... | collective-permute-start | bytes 331784 | tf_op jit(solution)/shard_map/ppermute | solution.py:405
  39.7 2.2 %collective-permute-done.17.rest_1_ = bf16[432,128]{1,0:T(8,128)(2,1)S(1)} collective-permute-done((bf16[432,128]{1,0:T(8,128)(2,1)S(1)}, bf16[432,128]{1,0:T(8,128)(2,1)S(1)}, u32[]{:S(2)}, u32[]{:S(2)}) %collective-permute-start.17) | collective-permute-done | bytes 110624 | tf_op jit(solution)/shard_map/ppermute | solution.py:405
  41.9 0.6 %collective-permute-done.13.rest_2_ = bf16[432,128]{1,0:T(8,128)(2,1)S(1)} collective-permute-done((bf16[432,128]{1,0:T(8,128)(2,1)S(1)}, bf16[432,128]{1,0:T(8,128)(2,1)S(1)}, u32[]{:S(2)}, u32[]{:S(2)}) %collective-permute-start.13) | collective-permute-done | bytes 110624 | tf_op jit(solution)/shard_map/ppermute | solution.py:405
  42.5 0.5 %collective-permute-done.15.rest_3_ = bf16[432,128]{1,0:T(8,128)(2,1)S(1)} collective-permute-done((bf16[432,128]{1,0:T(8,128)(2,1)S(1)}, bf16[432,128]{1,0:T(8,128)(2,1)S(1)}, u32[]{:S(2)}, u32[]{:S(2)}) %collective-permute-start.15) | collective-permute-done | bytes 110624 | tf_op jit(solution)/shard_map/ppermute | solution.py:405
  43.2 1.1 %shard_map.87.rest_2_ = f32[2,4,432,128]{3,2,1,0:T(8,128)} custom-call(bf16[432,128]{1,0:T(8,128)(2,1)S(1)} %shard_map.86.rest_0_, bf16[432,128]{1,0:T(8,128)(2,1)S(1)} %collective-permute-done.17.rest_1_, bf16[432,128]{1,0:T(8,128)(2,1)S(1)} %collective-permute-done.13.rest_2_, bf16[432,128]{1,0:T(8,128)(2,1)S(1)} %collective-permute-done.15.rest_3_, ...), custom_call_target="tpu_custom_call" | custom-call | flops 1000000000 | bytes 65536 | tf_op jit(solution)/shard_map/pallas_call | solution.py:478
  44.4 0.8 %shard_map.88 = f32[2,4,432,128]{3,2,1,0:T(8,128)} custom-call(bf16[432,128]{1,0:T(8,128)(2,1)S(1)} %collective-permute-done.14.rest_0_, bf16[432,128]{1,0:T(8,128)(2,1)S(1)} %collective-permute-done.16.rest_1_, f32[2,4,432,128]{3,2,1,0:T(8,128)} %shard_map.87.rest_2_), custom_call_target="tpu_custom_call", output_to_operand_aliasing={{}: (2, {})} | custom-call | flops 1000000000 | bytes 65536 | tf_op jit(solution)/shard_map/pallas_call | solution.py:478
  (37 shorter events, 1.8 us)
Async XLA Ops:
  0.6 4.3 %copy-start.2 = (s32[1,1,1,4,27]{4,3,2,1,0:T(4,128)S(1)}, s32[1,1,1,4,27]{4,3,2,1,0:T(4,128)}, u32[]{:S(2)}) copy-start(s32[1,1,1,4,27]{4,3,2,1,0:T(4,128)} %param.8) | copy-start | bytes 1300
  0.6 4.3 %copy-start = (bf16[3456,128]{1,0:T(8,128)(2,1)S(1)}, bf16[3456,128]{1,0:T(8,128)(2,1)}, u32[]{:S(2)}) copy-start(bf16[3456,128]{1,0:T(8,128)(2,1)} %param.6) | copy-start | bytes 2654212
  1.9 5.3 %collective-permute-start = (bf16[160,128]{1,0:T(8,128)(2,1)S(1)}, bf16[160,128]{1,0:T(8,128)(2,1)S(1)}, u32[]{:S(2)}, u32[]{:S(2)}) collective-permute-start(bf16[160,128]{1,0:T(8,128)(2,1)S(1)} %get-tuple-element.35), channel_id=1, source_target_pairs={{0,1},{1,0},{8,9},{9,8},{16,17},{17,16},{24,25},{25,24},{2,3},{3,2... | collective-permute-start | bytes 122888 | tf_op jit(solution)/shard_map/ppermute | solution.py:37
  7.3 4.0 %collective-permute-start.1 = (bf16[144,128]{1,0:T(8,128)(2,1)S(1)}, bf16[144,128]{1,0:T(8,128)(2,1)S(1)}, u32[]{:S(2)}, u32[]{:S(2)}) collective-permute-start(bf16[144,128]{1,0:T(8,128)(2,1)S(1)} %get-tuple-element.36), channel_id=1, source_target_pairs={{0,2},{2,0},{4,6},{6,4},{8,10},{10,8},{12,14},{14,12},{16,18},{18,... | collective-permute-start | bytes 110600 | tf_op jit(solution)/shard_map/ppermute | solution.py:37
  9.0 2.2 %collective-permute-start.2 = (bf16[144,128]{1,0:T(8,128)(2,1)S(1)}, bf16[144,128]{1,0:T(8,128)(2,1)S(1)}, u32[]{:S(2)}, u32[]{:S(2)}) collective-permute-start(bf16[144,128]{1,0:T(8,128)(2,1)S(1)} %get-tuple-element.37), channel_id=1, source_target_pairs={{0,8},{2,4},{4,2},{6,14},{8,0},{10,12},{12,10},{14,6},{16,24},{18,... | collective-permute-start | bytes 110600 | tf_op jit(solution)/shard_map/ppermute | solution.py:37
  9.1 2.2 %copy-start.1 = (bf16[1,1,1,4,512,128]{5,4,3,2,1,0:T(8,128)(2,1)S(1)}, bf16[1,1,1,4,512,128]{5,4,3,2,1,0:T(8,128)(2,1)}, u32[]{:S(2)}) copy-start(bf16[1,1,1,4,512,128]{5,4,3,2,1,0:T(8,128)(2,1)} %param.7) | copy-start | bytes 1572868
  9.1 2.2 %copy-start.3 = (s32[1,1,1,8,2]{3,4,2,1,0:T(2,128)S(1)}, s32[1,1,1,8,2]{3,4,2,1,0:T(2,128)}, u32[]{:S(2)}) copy-start(s32[1,1,1,8,2]{3,4,2,1,0:T(2,128)} %param.9) | copy-start | bytes 196
  15.6 1.9 %collective-permute-start.6 = (bf16[1728,128]{1,0:T(8,128)(2,1)S(1)}, bf16[1728,128]{1,0:T(8,128)(2,1)S(1)}, u32[]{:S(2)}, u32[]{:S(2)}) collective-permute-start(bf16[1728,128]{1,0:T(8,128)(2,1)S(1)} %get-tuple-element.49), channel_id=1, source_target_pairs={{0,8},{1,9},{2,10},{3,11},{4,12},{5,13},{6,14},{7,15},{8,0},{9,1},... | collective-permute-start | bytes 1327112 | tf_op jit(solution)/shard_map/ppermute | solution.py:411
  15.7 5.4 %collective-permute-start.3 = (bf16[160,128]{1,0:T(8,128)(2,1)S(1)}, bf16[160,128]{1,0:T(8,128)(2,1)S(1)}, u32[]{:S(2)}, u32[]{:S(2)}) collective-permute-start(bf16[160,128]{1,0:T(8,128)(2,1)S(1)} %get-tuple-element.42), channel_id=1, source_target_pairs={{0,1},{1,0},{8,9},{9,8},{16,17},{17,16},{24,25},{25,24},{2,3},{3,2... | collective-permute-start | bytes 122888 | tf_op jit(solution)/shard_map/ppermute | solution.py:37
  17.6 7.6 %collective-permute-start.7 = (bf16[432,128]{1,0:T(8,128)(2,1)S(1)}, bf16[432,128]{1,0:T(8,128)(2,1)S(1)}, u32[]{:S(2)}, u32[]{:S(2)}) collective-permute-start(bf16[432,128]{1,0:T(8,128)(2,1)S(1)} %get-tuple-element.51), channel_id=1, source_target_pairs={{0,17},{1,16},{2,19},{3,18},{4,21},{5,20},{6,23},{7,22},{8,14},{9,... | collective-permute-start | bytes 331784 | tf_op jit(solution)/shard_map/ppermute | solution.py:405
  20.3 4.9 %collective-permute-start.8 = (bf16[432,128]{1,0:T(8,128)(2,1)S(1)}, bf16[432,128]{1,0:T(8,128)(2,1)S(1)}, u32[]{:S(2)}, u32[]{:S(2)}) collective-permute-start(bf16[432,128]{1,0:T(8,128)(2,1)S(1)} %get-tuple-element.52), channel_id=1, source_target_pairs={{0,16},{1,17},{2,18},{3,19},{4,20},{5,21},{6,22},{7,23},{8,12},{9,... | collective-permute-start | bytes 331784 | tf_op jit(solution)/shard_map/ppermute | solution.py:405
  20.8 4.7 %collective-permute-start.9 = (bf16[432,128]{1,0:T(8,128)(2,1)S(1)}, bf16[432,128]{1,0:T(8,128)(2,1)S(1)}, u32[]{:S(2)}, u32[]{:S(2)}) collective-permute-start(bf16[432,128]{1,0:T(8,128)(2,1)S(1)} %get-tuple-element.53), channel_id=1, source_target_pairs={{0,1},{1,0},{2,3},{3,2},{4,5},{5,4},{6,7},{7,6},{8,10},{9,11},{10,... | collective-permute-start | bytes 331784 | tf_op jit(solution)/shard_map/ppermute | solution.py:405
  21.2 9.2 %collective-permute-start.4 = (bf16[144,128]{1,0:T(8,128)(2,1)S(1)}, bf16[144,128]{1,0:T(8,128)(2,1)S(1)}, u32[]{:S(2)}, u32[]{:S(2)}) collective-permute-start(bf16[144,128]{1,0:T(8,128)(2,1)S(1)} %get-tuple-element.46), channel_id=1, source_target_pairs={{0,2},{2,0},{4,6},{6,4},{8,10},{10,8},{12,14},{14,12},{16,18},{18,... | collective-permute-start | bytes 110600 | tf_op jit(solution)/shard_map/ppermute | solution.py:37
  24.1 6.3 %collective-permute-start.5 = (bf16[144,128]{1,0:T(8,128)(2,1)S(1)}, bf16[144,128]{1,0:T(8,128)(2,1)S(1)}, u32[]{:S(2)}, u32[]{:S(2)}) collective-permute-start(bf16[144,128]{1,0:T(8,128)(2,1)S(1)} %get-tuple-element.43.joined.rest_3_), channel_id=1, source_target_pairs={{0,8},{2,4},{4,2},{6,14},{8,0},{10,12},{12,10},{14,6},{16,24},{18,... | collective-permute-start | bytes 110600 | tf_op jit(solution)/shard_map/ppermute | solution.py:37
  25.6 9.0 %collective-permute-start.10 = (bf16[432,128]{1,0:T(8,128)(2,1)S(1)}, bf16[432,128]{1,0:T(8,128)(2,1)S(1)}, u32[]{:S(2)}, u32[]{:S(2)}) collective-permute-start(bf16[432,128]{1,0:T(8,128)(2,1)S(1)} %shard_map.85.rest_3_), channel_id=1, source_target_pairs={{0,6},{1,7},{2,4},{3,5},{4,2},{5,3},{6,0},{7,1},{8,25},{9,24},{10,... | collective-permute-start | bytes 331784 | tf_op jit(solution)/shard_map/ppermute | solution.py:405
  29.3 6.8 %collective-permute-start.11 = (bf16[432,128]{1,0:T(8,128)(2,1)S(1)}, bf16[432,128]{1,0:T(8,128)(2,1)S(1)}, u32[]{:S(2)}, u32[]{:S(2)}) collective-permute-start(bf16[432,128]{1,0:T(8,128)(2,1)S(1)} %shard_map.85.rest_3_), channel_id=1, source_target_pairs={{0,4},{1,5},{2,6},{3,7},{4,0},{5,1},{6,2},{7,3},{8,24},{9,25},{10,... | collective-permute-start | bytes 331784 | tf_op jit(solution)/shard_map/ppermute | solution.py:405
  29.9 6.2 %collective-permute-start.12 = (bf16[432,128]{1,0:T(8,128)(2,1)S(1)}, bf16[432,128]{1,0:T(8,128)(2,1)S(1)}, u32[]{:S(2)}, u32[]{:S(2)}) collective-permute-start(bf16[432,128]{1,0:T(8,128)(2,1)S(1)} %shard_map.85.rest_3_), channel_id=1, source_target_pairs={{0,2},{1,3},{2,0},{3,1},{4,6},{5,7},{6,4},{7,5},{8,9},{9,8},{10,11... | collective-permute-start | bytes 331784 | tf_op jit(solution)/shard_map/ppermute | solution.py:405
  36.2 5.7 %collective-permute-start.17 = (bf16[432,128]{1,0:T(8,128)(2,1)S(1)}, bf16[432,128]{1,0:T(8,128)(2,1)S(1)}, u32[]{:S(2)}, u32[]{:S(2)}) collective-permute-start(bf16[432,128]{1,0:T(8,128)(2,1)S(1)} %shard_map.86.rest_0_), channel_id=1, source_target_pairs={{0,17},{1,16},{2,19},{3,18},{4,21},{5,20},{6,23},{7,22},{8,14},{9,... | collective-permute-start | bytes 331784 | tf_op jit(solution)/shard_map/ppermute | solution.py:405
  37.8 4.7 %collective-permute-start.13 = (bf16[432,128]{1,0:T(8,128)(2,1)S(1)}, bf16[432,128]{1,0:T(8,128)(2,1)S(1)}, u32[]{:S(2)}, u32[]{:S(2)}) collective-permute-start(bf16[432,128]{1,0:T(8,128)(2,1)S(1)} %shard_map.86.rest_0_), channel_id=1, source_target_pairs={{0,16},{1,17},{2,18},{3,19},{4,20},{5,21},{6,22},{7,23},{8,12},{9,... | collective-permute-start | bytes 331784 | tf_op jit(solution)/shard_map/ppermute | solution.py:405
  38.3 4.7 %collective-permute-start.15 = (bf16[432,128]{1,0:T(8,128)(2,1)S(1)}, bf16[432,128]{1,0:T(8,128)(2,1)S(1)}, u32[]{:S(2)}, u32[]{:S(2)}) collective-permute-start(bf16[432,128]{1,0:T(8,128)(2,1)S(1)} %shard_map.86.rest_0_), channel_id=1, source_target_pairs={{0,1},{1,0},{2,3},{3,2},{4,5},{5,4},{6,7},{7,6},{8,10},{9,11},{10,... | collective-permute-start | bytes 331784 | tf_op jit(solution)/shard_map/ppermute | solution.py:405
  39.7 3.3 %collective-permute-start.18 = (bf16[432,128]{1,0:T(8,128)(2,1)S(1)}, bf16[432,128]{1,0:T(8,128)(2,1)S(1)}, u32[]{:S(2)}, u32[]{:S(2)}) collective-permute-start(bf16[432,128]{1,0:T(8,128)(2,1)S(1)} %shard_map.86.rest_0_), channel_id=1, source_target_pairs={{0,8},{1,9},{2,10},{3,11},{4,12},{5,13},{6,14},{7,15},{8,0},{9,1},... | collective-permute-start | bytes 331784 | tf_op jit(solution)/shard_map/ppermute | solution.py:411
  41.9 1.3 %collective-permute-start.19 = (bf16[432,128]{1,0:T(8,128)(2,1)S(1)}, bf16[432,128]{1,0:T(8,128)(2,1)S(1)}, u32[]{:S(2)}, u32[]{:S(2)}) collective-permute-start(bf16[432,128]{1,0:T(8,128)(2,1)S(1)} %collective-permute-done.17.rest_1_), channel_id=1, source_target_pairs={{0,8},{1,9},{2,10},{3,11},{4,12},{5,13},{6,14},{7,15},{8,0},{9,1},... | collective-permute-start | bytes 331784 | tf_op jit(solution)/shard_map/ppermute | solution.py:411
  42.5 1.8 %collective-permute-start.14 = (bf16[432,128]{1,0:T(8,128)(2,1)S(1)}, bf16[432,128]{1,0:T(8,128)(2,1)S(1)}, u32[]{:S(2)}, u32[]{:S(2)}) collective-permute-start(bf16[432,128]{1,0:T(8,128)(2,1)S(1)} %collective-permute-done.13.rest_2_), channel_id=1, source_target_pairs={{0,8},{1,9},{2,10},{3,11},{4,12},{5,13},{6,14},{7,15},{8,0},{9,1},... | collective-permute-start | bytes 331784 | tf_op jit(solution)/shard_map/ppermute | solution.py:411
  43.1 1.3 %collective-permute-start.16 = (bf16[432,128]{1,0:T(8,128)(2,1)S(1)}, bf16[432,128]{1,0:T(8,128)(2,1)S(1)}, u32[]{:S(2)}, u32[]{:S(2)}) collective-permute-start(bf16[432,128]{1,0:T(8,128)(2,1)S(1)} %collective-permute-done.15.rest_3_), channel_id=1, source_target_pairs={{0,8},{1,9},{2,10},{3,11},{4,12},{5,13},{6,14},{7,15},{8,0},{9,1},... | collective-permute-start | bytes 331784 | tf_op jit(solution)/shard_map/ppermute | solution.py:411

commit v10 on v8

--- a/solution.py
+++ b/solution.py
@@ -327,7 +327,7 @@
             term[27 * half :] = jnp.zeros((term.shape[0] - 27 * half, 128), term.dtype)
 
 
-def back_layout_kernel(table, bricks, weight, backward, views, store):
+def back_layout_kernel(table, bricks, weight, joined, backward, views, store):
     slots = bricks.shape[0]
     for tap in range(27):
         far, near = tap // 3 * 128, tap % 3 * 128
@@ -590,8 +590,8 @@
     packed = join(*faces, *y_boxes)
     x_boxes = swapped(packed, "gx", phases_x)
     back_taps, views = run(
-        back_layout_kernel, [taps_type, views_type], [SMEM, VMEM, VMEM], [VMEM, VMEM], [store_of(slots + 1)]
-    )(table, grads, blocks)
+        back_layout_kernel, [taps_type, views_type], [SMEM, VMEM, VMEM, ANY], [VMEM, VMEM], [store_of(slots + 1)]
+    )(table, grads, blocks, packed[-1])
     _, input_grad, ready = run(
         functools.partial(backward_kernel, counts, send),
         [views_type, bricks_type, jax.ShapeDtypeStruct((8, 128), F32)],

time: 45.4 us -> 45.4 us (level)
  no operation moved by 1% of the time
where the time goes in v10:
time: 45.4 us; the launch traced here: 45.3 us
  starting transfers between devices  21.7 us (48%)
  Pallas kernels  17.2 us (38%)
  waiting for transfers between devices  5.49 us (12%)
  between operations  0.8 us (2%)
    ppermute x9, starting transfers between devices, swap(): return lax.ppermute(x, ('dp', 'gx', 'gy'), self.pairs(place))  11.8 us
    ppermute x6, starting transfers between devices, swap(): return lax.ppermute(x, ('dp', axis), pairs)  9.33 us
    ppermute x9, waiting for transfers between devices, swap(): return lax.ppermute(x, ('dp', 'gx', 'gy'), self.pairs(place))  5.3 us
    pallas_call x1, Pallas kernels, body(): run(functools.partial(backward_kernel, counts, send), [views_type, bricks...  4.19 us
    pallas_call x1, Pallas kernels, body(): run(functools.partial(forward_kernel, counts, send, factor), [views_type,...  4.02 us
    pallas_call x1, Pallas kernels, body(): run(layout_kernel, [taps_type, views_type, preact_type], [SMEM, VMEM, VME...  2.29 us
    pallas_call x1, Pallas kernels, body(): run(functools.partial(own_kernel, counts, send), [views_type, preact_type...  2.28 us
    pallas_call x2, Pallas kernels, spread(): run(functools.partial(spread_kernel, count, first), out_type, [VMEM] * co...  1.91 us
  transfers between devices with their start and end apart: 20, of which 5 were waited for; matrix products, arithmetic and copies ran while one was open for 0% of the time, Pallas kernels for 25%

profile of v10, /device:TPU:0, one launch (start us, length us, event | category | flops | bytes accessed | tf_op | source)
XLA Modules:
  0.0 45.3 jit_solution(4449966603816265312)
XLA Ops:
  0.7 1.2 %shard_map.76 = (bf16[4,8,64,128]{3,2,1,0:T(8,128)(2,1)S(1)}, bf16[128,128]{1,0:T(8,128)(2,1)S(1)}, bf16[128,128]{1,0:T(8,128)(2,1)S(1)}, bf16[160,128]{1,0:T(8,128)(2,1)S(1)}) custom-call(s32[2,8]{1,0:T(2,128)} %bitcast.22, bf16[4,8,64,128]{3,2,1,0:T(8,128)(2,1)} %bitcast.26), custom_call_target="tpu_custom_call" | custom-call | flops 1000000000 | bytes 65536 | tf_op jit(solution)/shard_map/pallas_call | solution.py:540
  1.9 3.0 %collective-permute-start = (bf16[160,128]{1,0:T(8,128)(2,1)S(1)}, bf16[160,128]{1,0:T(8,128)(2,1)S(1)}, u32[]{:S(2)}, u32[]{:S(2)}) collective-permute-start(bf16[160,128]{1,0:T(8,128)(2,1)S(1)} %get-tuple-element.35), channel_id=1, source_target_pairs={{0,1},{1,0},{8,9},{9,8},{16,17},{17,16},{24,25},{25,24},{2,3},{3,2... | collective-permute-start | bytes 122888 | tf_op jit(solution)/shard_map/ppermute | solution.py:37
  4.9 2.3 %shard_map.77 = (bf16[1152,384]{1,0:T(8,128)(2,1)S(1)}, bf16[4,10,64,384]{3,2,1,0:T(8,128)(2,1)S(1)}, f32[4,8,8,8,128]{4,3,2,1,0:T(8,128)S(1)}) custom-call(s32[4,27]{1,0:T(4,128)S(1)} %bitcast.17, bf16[4,8,64,128]{3,2,1,0:T(8,128)(2,1)S(1)} %get-tuple-element.31.bricks, bf16[27,128,128]{2,1,0:T(8,128)(2,1)S(1)} %bitcast.13), custom_call_target="tpu_custom_call" | custom-call | flops 2000000000 | bytes 65536 | tf_op jit(solution)/shard_map/pallas_call | solution.py:549
  7.3 1.8 %collective-permute-start.1 = (bf16[144,128]{1,0:T(8,128)(2,1)S(1)}, bf16[144,128]{1,0:T(8,128)(2,1)S(1)}, u32[]{:S(2)}, u32[]{:S(2)}) collective-permute-start(bf16[144,128]{1,0:T(8,128)(2,1)S(1)} %get-tuple-element.40), channel_id=1, source_target_pairs={{0,2},{2,0},{4,6},{6,4},{8,10},{10,8},{12,14},{14,12},{16,18},{18,... | collective-permute-start | bytes 110600 | tf_op jit(solution)/shard_map/ppermute | solution.py:37
  9.1 2.3 %shard_map.78 = (bf16[4,10,64,384]{3,2,1,0:T(8,128)(2,1)S(1)}, f32[4,8,8,8,128]{4,3,2,1,0:T(8,128)S(1)}) custom-call(s32[4,27]{1,0:T(4,128)S(1)} %bitcast.18, bf16[4,10,64,384]{3,2,1,0:T(8,128)(2,1)S(1)} %get-tuple-element.32.own_views, bf16[1152,384]{1,0:T(8,128)(2,1)S(1)} %get-tuple-element.33.taps, ...), custom_call_target="tpu_custom_call", output_to_operand_aliasing={{0}: (1, {}), {1}: (3, {})} | custom-call | flops 4000000000 | bytes 65536 | tf_op jit(solution)/shard_map/pallas_call | solution.py:562
  11.4 4.0 %shard_map.80 = (bf16[4,10,64,384]{3,2,1,0:T(8,128)(2,1)S(1)}, f32[4,8,8,8,128]{4,3,2,1,0:T(8,128)S(1)}, bf16[4,8,64,128]{3,2,1,0:T(8,128)(2,1)}, bf16[4,8,64,12...) custom-call(s32[4,27]{1,0:T(4,128)S(1)} %bitcast.19, ...), custom_call_target="tpu_custom_call", output_to_operand_aliasing={{0}: (2, {}), {1}: (3, {})} | custom-call | flops 5000000000 | bytes 65536 | tf_op jit(solution)/shard_map/pallas_call | solution.py:571
  15.4 0.6 %collective-permute-start.6 = (bf16[1728,128]{1,0:T(8,128)(2,1)S(1)}, bf16[1728,128]{1,0:T(8,128)(2,1)S(1)}, u32[]{:S(2)}, u32[]{:S(2)}) collective-permute-start(bf16[1728,128]{1,0:T(8,128)(2,1)S(1)} %get-tuple-element.53), channel_id=1, source_target_pairs={{0,8},{1,9},{2,10},{3,11},{4,12},{5,13},{6,14},{7,15},{8,0},{9,1},... | collective-permute-start | bytes 1327112 | tf_op jit(solution)/shard_map/ppermute | solution.py:420
  16.0 1.5 %collective-permute-start.3 = (bf16[160,128]{1,0:T(8,128)(2,1)S(1)}, bf16[160,128]{1,0:T(8,128)(2,1)S(1)}, u32[]{:S(2)}, u32[]{:S(2)}) collective-permute-start(bf16[160,128]{1,0:T(8,128)(2,1)S(1)} %get-tuple-element.46), channel_id=1, source_target_pairs={{0,1},{1,0},{8,9},{9,8},{16,17},{17,16},{24,25},{25,24},{2,3},{3,2... | collective-permute-start | bytes 122888 | tf_op jit(solution)/shard_map/ppermute | solution.py:37
  17.6 2.4 %collective-permute-start.7 = (bf16[432,128]{1,0:T(8,128)(2,1)S(1)}, bf16[432,128]{1,0:T(8,128)(2,1)S(1)}, u32[]{:S(2)}, u32[]{:S(2)}) collective-permute-start(bf16[432,128]{1,0:T(8,128)(2,1)S(1)} %get-tuple-element.55), channel_id=1, source_target_pairs={{0,17},{1,16},{2,19},{3,18},{4,21},{5,20},{6,23},{7,22},{8,14},{9,... | collective-permute-start | bytes 331784 | tf_op jit(solution)/shard_map/ppermute | solution.py:414
  20.0 0.5 %collective-permute-start.8 = (bf16[432,128]{1,0:T(8,128)(2,1)S(1)}, bf16[432,128]{1,0:T(8,128)(2,1)S(1)}, u32[]{:S(2)}, u32[]{:S(2)}) collective-permute-start(bf16[432,128]{1,0:T(8,128)(2,1)S(1)} %get-tuple-element.56), channel_id=1, source_target_pairs={{0,16},{1,17},{2,18},{3,19},{4,20},{5,21},{6,22},{7,23},{8,12},{9,... | collective-permute-start | bytes 331784 | tf_op jit(solution)/shard_map/ppermute | solution.py:414
  20.5 0.6 %collective-permute-start.9 = (bf16[432,128]{1,0:T(8,128)(2,1)S(1)}, bf16[432,128]{1,0:T(8,128)(2,1)S(1)}, u32[]{:S(2)}, u32[]{:S(2)}) collective-permute-start(bf16[432,128]{1,0:T(8,128)(2,1)S(1)} %get-tuple-element.57), channel_id=1, source_target_pairs={{0,1},{1,0},{2,3},{3,2},{4,5},{5,4},{6,7},{7,6},{8,10},{9,11},{10,... | collective-permute-start | bytes 331784 | tf_op jit(solution)/shard_map/ppermute | solution.py:414
  21.2 3.0 %collective-permute-start.4 = (bf16[144,128]{1,0:T(8,128)(2,1)S(1)}, bf16[144,128]{1,0:T(8,128)(2,1)S(1)}, u32[]{:S(2)}, u32[]{:S(2)}) collective-permute-start(bf16[144,128]{1,0:T(8,128)(2,1)S(1)} %get-tuple-element.50), channel_id=1, source_target_pairs={{0,2},{2,0},{4,6},{6,4},{8,10},{10,8},{12,14},{14,12},{16,18},{18,... | collective-permute-start | bytes 110600 | tf_op jit(solution)/shard_map/ppermute | solution.py:37
  24.2 1.1 %shard_map.82 = (bf16[1152,384]{1,0:T(8,128)(2,1)S(1)}, bf16[4,10,64,384]{3,2,1,0:T(8,128)(2,1)S(1)}) custom-call(s32[4,27]{1,0:T(4,128)S(1)} %bitcast.20, bf16[4,8,64,128]{3,2,1,0:T(8,128)(2,1)S(1)} %get-tuple-element.43.bricks, bf16[27,128,128]{2,1,0:T(8,128)(2,1)S(1)} %bitcast.14, bf16[144,128]{1,0:T(8,128)(2,1)S(1)} %get-tuple-element.47.joined.rest_3_), custom_call_target="tpu_custom_call" | custom-call | flops 1000000000 | bytes 65536 | tf_op jit(solution)/shard_map/pallas_call | solution.py:592
  25.4 3.6 %collective-permute-start.10 = (bf16[432,128]{1,0:T(8,128)(2,1)S(1)}, bf16[432,128]{1,0:T(8,128)(2,1)S(1)}, u32[]{:S(2)}, u32[]{:S(2)}) collective-permute-start(bf16[432,128]{1,0:T(8,128)(2,1)S(1)} %shard_map.85.rest_3_), channel_id=1, source_target_pairs={{0,6},{1,7},{2,4},{3,5},{4,2},{5,3},{6,0},{7,1},{8,25},{9,24},{10,... | collective-permute-start | bytes 331784 | tf_op jit(solution)/shard_map/ppermute | solution.py:414
  28.9 1.0 %collective-permute-start.11 = (bf16[432,128]{1,0:T(8,128)(2,1)S(1)}, bf16[432,128]{1,0:T(8,128)(2,1)S(1)}, u32[]{:S(2)}, u32[]{:S(2)}) collective-permute-start(bf16[432,128]{1,0:T(8,128)(2,1)S(1)} %shard_map.85.rest_3_), channel_id=1, source_target_pairs={{0,4},{1,5},{2,6},{3,7},{4,0},{5,1},{6,2},{7,3},{8,24},{9,25},{10,... | collective-permute-start | bytes 331784 | tf_op jit(solution)/shard_map/ppermute | solution.py:414
  30.1 4.2 %shard_map.83 = (bf16[4,10,64,384]{3,2,1,0:T(8,128)(2,1)S(1)}, bf16[4,8,64,128]{3,2,1,0:T(8,128)(2,1)}, f32[8,128]{1,0:T(8,128)S(1)}) custom-call(s32[4,27]{1,0:T(4,128)S(1)} %bitcast.21, bf16[4,10,64,384]{3,2,1,0:T(8,128)(2,1)S(1)} %get-tuple-element.48.own_views.rest_4_, ...), custom_call_target="tpu_custom_call", output_to_operand_aliasing={{0}: (1, {})} | custom-call | flops 5000000000 | bytes 65536 | tf_op jit(solution)/shard_map/pallas_call | solution.py:595
  34.3 1.5 %collective-permute-done.11.rest_1_ = bf16[432,128]{1,0:T(8,128)(2,1)S(1)} collective-permute-done((bf16[432,128]{1,0:T(8,128)(2,1)S(1)}, bf16[432,128]{1,0:T(8,128)(2,1)S(1)}, u32[]{:S(2)}, u32[]{:S(2)}) %collective-permute-start.11) | collective-permute-done | bytes 110624 | tf_op jit(solution)/shard_map/ppermute | solution.py:414
  35.8 2.0 %collective-permute-start.17 = (bf16[432,128]{1,0:T(8,128)(2,1)S(1)}, bf16[432,128]{1,0:T(8,128)(2,1)S(1)}, u32[]{:S(2)}, u32[]{:S(2)}) collective-permute-start(bf16[432,128]{1,0:T(8,128)(2,1)S(1)} %shard_map.86.rest_0_), channel_id=1, source_target_pairs={{0,17},{1,16},{2,19},{3,18},{4,21},{5,20},{6,23},{7,22},{8,14},{9,... | collective-permute-start | bytes 331784 | tf_op jit(solution)/shard_map/ppermute | solution.py:414
  37.9 0.5 %collective-permute-start.13 = (bf16[432,128]{1,0:T(8,128)(2,1)S(1)}, bf16[432,128]{1,0:T(8,128)(2,1)S(1)}, u32[]{:S(2)}, u32[]{:S(2)}) collective-permute-start(bf16[432,128]{1,0:T(8,128)(2,1)S(1)} %shard_map.86.rest_0_), channel_id=1, source_target_pairs={{0,16},{1,17},{2,18},{3,19},{4,20},{5,21},{6,22},{7,23},{8,12},{9,... | collective-permute-start | bytes 331784 | tf_op jit(solution)/shard_map/ppermute | solution.py:414
  38.4 1.0 %collective-permute-start.15 = (bf16[432,128]{1,0:T(8,128)(2,1)S(1)}, bf16[432,128]{1,0:T(8,128)(2,1)S(1)}, u32[]{:S(2)}, u32[]{:S(2)}) collective-permute-start(bf16[432,128]{1,0:T(8,128)(2,1)S(1)} %shard_map.86.rest_0_), channel_id=1, source_target_pairs={{0,1},{1,0},{2,3},{3,2},{4,5},{5,4},{6,7},{7,6},{8,10},{9,11},{10,... | collective-permute-start | bytes 331784 | tf_op jit(solution)/shard_map/ppermute | solution.py:414
  39.4 2.2 %collective-permute-done.17.rest_1_ = bf16[432,128]{1,0:T(8,128)(2,1)S(1)} collective-permute-done((bf16[432,128]{1,0:T(8,128)(2,1)S(1)}, bf16[432,128]{1,0:T(8,128)(2,1)S(1)}, u32[]{:S(2)}, u32[]{:S(2)}) %collective-permute-start.17) | collective-permute-done | bytes 110624 | tf_op jit(solution)/shard_map/ppermute | solution.py:414
  41.6 1.0 %collective-permute-done.13.rest_2_ = bf16[432,128]{1,0:T(8,128)(2,1)S(1)} collective-permute-done((bf16[432,128]{1,0:T(8,128)(2,1)S(1)}, bf16[432,128]{1,0:T(8,128)(2,1)S(1)}, u32[]{:S(2)}, u32[]{:S(2)}) %collective-permute-start.13) | collective-permute-done | bytes 110624 | tf_op jit(solution)/shard_map/ppermute | solution.py:414
  43.2 1.1 %shard_map.87.rest_2_ = f32[2,4,432,128]{3,2,1,0:T(8,128)} custom-call(bf16[432,128]{1,0:T(8,128)(2,1)S(1)} %shard_map.86.rest_0_, bf16[432,128]{1,0:T(8,128)(2,1)S(1)} %collective-permute-done.17.rest_1_, bf16[432,128]{1,0:T(8,128)(2,1)S(1)} %collective-permute-done.13.rest_2_, bf16[432,128]{1,0:T(8,128)(2,1)S(1)} %collective-permute-done.15.rest_3_, ...), custom_call_target="tpu_custom_call" | custom-call | flops 1000000000 | bytes 65536 | tf_op jit(solution)/shard_map/pallas_call | solution.py:487
  44.5 0.8 %shard_map.88 = f32[2,4,432,128]{3,2,1,0:T(8,128)} custom-call(bf16[432,128]{1,0:T(8,128)(2,1)S(1)} %collective-permute-done.14.rest_0_, bf16[432,128]{1,0:T(8,128)(2,1)S(1)} %collective-permute-done.16.rest_1_, f32[2,4,432,128]{3,2,1,0:T(8,128)} %shard_map.87.rest_2_), custom_call_target="tpu_custom_call", output_to_operand_aliasing={{}: (2, {})} | custom-call | flops 1000000000 | bytes 65536 | tf_op jit(solution)/shard_map/pallas_call | solution.py:487
  (37 shorter events, 1.2 us)
Async XLA Ops:
  0.6 4.3 %copy-start.2 = (s32[1,1,1,4,27]{4,3,2,1,0:T(4,128)S(1)}, s32[1,1,1,4,27]{4,3,2,1,0:T(4,128)}, u32[]{:S(2)}) copy-start(s32[1,1,1,4,27]{4,3,2,1,0:T(4,128)} %param.8) | copy-start | bytes 1300
  0.6 4.3 %copy-start = (bf16[3456,128]{1,0:T(8,128)(2,1)S(1)}, bf16[3456,128]{1,0:T(8,128)(2,1)}, u32[]{:S(2)}) copy-start(bf16[3456,128]{1,0:T(8,128)(2,1)} %param.6) | copy-start | bytes 2654212
  1.9 5.3 %collective-permute-start = (bf16[160,128]{1,0:T(8,128)(2,1)S(1)}, bf16[160,128]{1,0:T(8,128)(2,1)S(1)}, u32[]{:S(2)}, u32[]{:S(2)}) collective-permute-start(bf16[160,128]{1,0:T(8,128)(2,1)S(1)} %get-tuple-element.35), channel_id=1, source_target_pairs={{0,1},{1,0},{8,9},{9,8},{16,17},{17,16},{24,25},{25,24},{2,3},{3,2... | collective-permute-start | bytes 122888 | tf_op jit(solution)/shard_map/ppermute | solution.py:37
  7.3 4.1 %collective-permute-start.1 = (bf16[144,128]{1,0:T(8,128)(2,1)S(1)}, bf16[144,128]{1,0:T(8,128)(2,1)S(1)}, u32[]{:S(2)}, u32[]{:S(2)}) collective-permute-start(bf16[144,128]{1,0:T(8,128)(2,1)S(1)} %get-tuple-element.40), channel_id=1, source_target_pairs={{0,2},{2,0},{4,6},{6,4},{8,10},{10,8},{12,14},{14,12},{16,18},{18,... | collective-permute-start | bytes 110600 | tf_op jit(solution)/shard_map/ppermute | solution.py:37
  9.0 2.3 %collective-permute-start.2 = (bf16[144,128]{1,0:T(8,128)(2,1)S(1)}, bf16[144,128]{1,0:T(8,128)(2,1)S(1)}, u32[]{:S(2)}, u32[]{:S(2)}) collective-permute-start(bf16[144,128]{1,0:T(8,128)(2,1)S(1)} %get-tuple-element.41), channel_id=1, source_target_pairs={{0,8},{2,4},{4,2},{6,14},{8,0},{10,12},{12,10},{14,6},{16,24},{18,... | collective-permute-start | bytes 110600 | tf_op jit(solution)/shard_map/ppermute | solution.py:37
  9.1 2.3 %copy-start.1 = (bf16[1,1,1,4,512,128]{5,4,3,2,1,0:T(8,128)(2,1)S(1)}, bf16[1,1,1,4,512,128]{5,4,3,2,1,0:T(8,128)(2,1)}, u32[]{:S(2)}) copy-start(bf16[1,1,1,4,512,128]{5,4,3,2,1,0:T(8,128)(2,1)} %param.7) | copy-start | bytes 1572868
  9.1 2.3 %copy-start.3 = (s32[1,1,1,8,2]{3,4,2,1,0:T(2,128)S(1)}, s32[1,1,1,8,2]{3,4,2,1,0:T(2,128)}, u32[]{:S(2)}) copy-start(s32[1,1,1,8,2]{3,4,2,1,0:T(2,128)} %param.9) | copy-start | bytes 196
  15.4 2.1 %collective-permute-start.6 = (bf16[1728,128]{1,0:T(8,128)(2,1)S(1)}, bf16[1728,128]{1,0:T(8,128)(2,1)S(1)}, u32[]{:S(2)}, u32[]{:S(2)}) collective-permute-start(bf16[1728,128]{1,0:T(8,128)(2,1)S(1)} %get-tuple-element.53), channel_id=1, source_target_pairs={{0,8},{1,9},{2,10},{3,11},{4,12},{5,13},{6,14},{7,15},{8,0},{9,1},... | collective-permute-start | bytes 1327112 | tf_op jit(solution)/shard_map/ppermute | solution.py:420
  16.0 5.2 %collective-permute-start.3 = (bf16[160,128]{1,0:T(8,128)(2,1)S(1)}, bf16[160,128]{1,0:T(8,128)(2,1)S(1)}, u32[]{:S(2)}, u32[]{:S(2)}) collective-permute-start(bf16[160,128]{1,0:T(8,128)(2,1)S(1)} %get-tuple-element.46), channel_id=1, source_target_pairs={{0,1},{1,0},{8,9},{9,8},{16,17},{17,16},{24,25},{25,24},{2,3},{3,2... | collective-permute-start | bytes 122888 | tf_op jit(solution)/shard_map/ppermute | solution.py:37
  17.6 7.6 %collective-permute-start.7 = (bf16[432,128]{1,0:T(8,128)(2,1)S(1)}, bf16[432,128]{1,0:T(8,128)(2,1)S(1)}, u32[]{:S(2)}, u32[]{:S(2)}) collective-permute-start(bf16[432,128]{1,0:T(8,128)(2,1)S(1)} %get-tuple-element.55), channel_id=1, source_target_pairs={{0,17},{1,16},{2,19},{3,18},{4,21},{5,20},{6,23},{7,22},{8,14},{9,... | collective-permute-start | bytes 331784 | tf_op jit(solution)/shard_map/ppermute | solution.py:414
  20.0 5.3 %collective-permute-start.8 = (bf16[432,128]{1,0:T(8,128)(2,1)S(1)}, bf16[432,128]{1,0:T(8,128)(2,1)S(1)}, u32[]{:S(2)}, u32[]{:S(2)}) collective-permute-start(bf16[432,128]{1,0:T(8,128)(2,1)S(1)} %get-tuple-element.56), channel_id=1, source_target_pairs={{0,16},{1,17},{2,18},{3,19},{4,20},{5,21},{6,22},{7,23},{8,12},{9,... | collective-permute-start | bytes 331784 | tf_op jit(solution)/shard_map/ppermute | solution.py:414
  20.5 4.7 %collective-permute-start.9 = (bf16[432,128]{1,0:T(8,128)(2,1)S(1)}, bf16[432,128]{1,0:T(8,128)(2,1)S(1)}, u32[]{:S(2)}, u32[]{:S(2)}) collective-permute-start(bf16[432,128]{1,0:T(8,128)(2,1)S(1)} %get-tuple-element.57), channel_id=1, source_target_pairs={{0,1},{1,0},{2,3},{3,2},{4,5},{5,4},{6,7},{7,6},{8,10},{9,11},{10,... | collective-permute-start | bytes 331784 | tf_op jit(solution)/shard_map/ppermute | solution.py:414
  21.2 8.9 %collective-permute-start.4 = (bf16[144,128]{1,0:T(8,128)(2,1)S(1)}, bf16[144,128]{1,0:T(8,128)(2,1)S(1)}, u32[]{:S(2)}, u32[]{:S(2)}) collective-permute-start(bf16[144,128]{1,0:T(8,128)(2,1)S(1)} %get-tuple-element.50), channel_id=1, source_target_pairs={{0,2},{2,0},{4,6},{6,4},{8,10},{10,8},{12,14},{14,12},{16,18},{18,... | collective-permute-start | bytes 110600 | tf_op jit(solution)/shard_map/ppermute | solution.py:37
  24.2 5.9 %collective-permute-start.5 = (bf16[144,128]{1,0:T(8,128)(2,1)S(1)}, bf16[144,128]{1,0:T(8,128)(2,1)S(1)}, u32[]{:S(2)}, u32[]{:S(2)}) collective-permute-start(bf16[144,128]{1,0:T(8,128)(2,1)S(1)} %get-tuple-element.47.joined.rest_3_), channel_id=1, source_target_pairs={{0,8},{2,4},{4,2},{6,14},{8,0},{10,12},{12,10},{14,6},{16,24},{18,... | collective-permute-start | bytes 110600 | tf_op jit(solution)/shard_map/ppermute | solution.py:37
  25.4 8.9 %collective-permute-start.10 = (bf16[432,128]{1,0:T(8,128)(2,1)S(1)}, bf16[432,128]{1,0:T(8,128)(2,1)S(1)}, u32[]{:S(2)}, u32[]{:S(2)}) collective-permute-start(bf16[432,128]{1,0:T(8,128)(2,1)S(1)} %shard_map.85.rest_3_), channel_id=1, source_target_pairs={{0,6},{1,7},{2,4},{3,5},{4,2},{5,3},{6,0},{7,1},{8,25},{9,24},{10,... | collective-permute-start | bytes 331784 | tf_op jit(solution)/shard_map/ppermute | solution.py:414
  28.9 6.8 %collective-permute-start.11 = (bf16[432,128]{1,0:T(8,128)(2,1)S(1)}, bf16[432,128]{1,0:T(8,128)(2,1)S(1)}, u32[]{:S(2)}, u32[]{:S(2)}) collective-permute-start(bf16[432,128]{1,0:T(8,128)(2,1)S(1)} %shard_map.85.rest_3_), channel_id=1, source_target_pairs={{0,4},{1,5},{2,6},{3,7},{4,0},{5,1},{6,2},{7,3},{8,24},{9,25},{10,... | collective-permute-start | bytes 331784 | tf_op jit(solution)/shard_map/ppermute | solution.py:414
  29.9 5.9 %collective-permute-start.12 = (bf16[432,128]{1,0:T(8,128)(2,1)S(1)}, bf16[432,128]{1,0:T(8,128)(2,1)S(1)}, u32[]{:S(2)}, u32[]{:S(2)}) collective-permute-start(bf16[432,128]{1,0:T(8,128)(2,1)S(1)} %shard_map.85.rest_3_), channel_id=1, source_target_pairs={{0,2},{1,3},{2,0},{3,1},{4,6},{5,7},{6,4},{7,5},{8,9},{9,8},{10,11... | collective-permute-start | bytes 331784 | tf_op jit(solution)/shard_map/ppermute | solution.py:414
  35.8 5.7 %collective-permute-start.17 = (bf16[432,128]{1,0:T(8,128)(2,1)S(1)}, bf16[432,128]{1,0:T(8,128)(2,1)S(1)}, u32[]{:S(2)}, u32[]{:S(2)}) collective-permute-start(bf16[432,128]{1,0:T(8,128)(2,1)S(1)} %shard_map.86.rest_0_), channel_id=1, source_target_pairs={{0,17},{1,16},{2,19},{3,18},{4,21},{5,20},{6,23},{7,22},{8,14},{9,... | collective-permute-start | bytes 331784 | tf_op jit(solution)/shard_map/ppermute | solution.py:414
  37.9 4.7 %collective-permute-start.13 = (bf16[432,128]{1,0:T(8,128)(2,1)S(1)}, bf16[432,128]{1,0:T(8,128)(2,1)S(1)}, u32[]{:S(2)}, u32[]{:S(2)}) collective-permute-start(bf16[432,128]{1,0:T(8,128)(2,1)S(1)} %shard_map.86.rest_0_), channel_id=1, source_target_pairs={{0,16},{1,17},{2,18},{3,19},{4,20},{5,21},{6,22},{7,23},{8,12},{9,... | collective-permute-start | bytes 331784 | tf_op jit(solution)/shard_map/ppermute | solution.py:414
  38.4 4.7 %collective-permute-start.15 = (bf16[432,128]{1,0:T(8,128)(2,1)S(1)}, bf16[432,128]{1,0:T(8,128)(2,1)S(1)}, u32[]{:S(2)}, u32[]{:S(2)}) collective-permute-start(bf16[432,128]{1,0:T(8,128)(2,1)S(1)} %shard_map.86.rest_0_), channel_id=1, source_target_pairs={{0,1},{1,0},{2,3},{3,2},{4,5},{5,4},{6,7},{7,6},{8,10},{9,11},{10,... | collective-permute-start | bytes 331784 | tf_op jit(solution)/shard_map/ppermute | solution.py:414
  39.4 3.8 %collective-permute-start.18 = (bf16[432,128]{1,0:T(8,128)(2,1)S(1)}, bf16[432,128]{1,0:T(8,128)(2,1)S(1)}, u32[]{:S(2)}, u32[]{:S(2)}) collective-permute-start(bf16[432,128]{1,0:T(8,128)(2,1)S(1)} %shard_map.86.rest_0_), channel_id=1, source_target_pairs={{0,8},{1,9},{2,10},{3,11},{4,12},{5,13},{6,14},{7,15},{8,0},{9,1},... | collective-permute-start | bytes 331784 | tf_op jit(solution)/shard_map/ppermute | solution.py:420
  41.6 1.6 %collective-permute-start.19 = (bf16[432,128]{1,0:T(8,128)(2,1)S(1)}, bf16[432,128]{1,0:T(8,128)(2,1)S(1)}, u32[]{:S(2)}, u32[]{:S(2)}) collective-permute-start(bf16[432,128]{1,0:T(8,128)(2,1)S(1)} %collective-permute-done.17.rest_1_), channel_id=1, source_target_pairs={{0,8},{1,9},{2,10},{3,11},{4,12},{5,13},{6,14},{7,15},{8,0},{9,1},... | collective-permute-start | bytes 331784 | tf_op jit(solution)/shard_map/ppermute | solution.py:420
  42.6 1.7 %collective-permute-start.14 = (bf16[432,128]{1,0:T(8,128)(2,1)S(1)}, bf16[432,128]{1,0:T(8,128)(2,1)S(1)}, u32[]{:S(2)}, u32[]{:S(2)}) collective-permute-start(bf16[432,128]{1,0:T(8,128)(2,1)S(1)} %collective-permute-done.13.rest_2_), channel_id=1, source_target_pairs={{0,8},{1,9},{2,10},{3,11},{4,12},{5,13},{6,14},{7,15},{8,0},{9,1},... | collective-permute-start | bytes 331784 | tf_op jit(solution)/shard_map/ppermute | solution.py:420
  43.1 1.3 %collective-permute-start.16 = (bf16[432,128]{1,0:T(8,128)(2,1)S(1)}, bf16[432,128]{1,0:T(8,128)(2,1)S(1)}, u32[]{:S(2)}, u32[]{:S(2)}) collective-permute-start(bf16[432,128]{1,0:T(8,128)(2,1)S(1)} %collective-permute-done.15.rest_3_), channel_id=1, source_target_pairs={{0,8},{1,9},{2,10},{3,11},{4,12},{5,13},{6,14},{7,15},{8,0},{9,1},... | collective-permute-start | bytes 331784 | tf_op jit(solution)/shard_map/ppermute | solution.py:420
